TPU v7x, 32 devices: a whole 2x2x4 slice. The times are simulated.
32 devices in a mesh: dp: 16 (over z, x, core), node: 2 (over y).
Axes of the slice: x: 2, y: 2, z: 4, core: 2. Of those that a mesh axis runs over, the one named last changes fastest.
Arguments:
- tokens: bfloat16 [384, 5120], P('node'), may hold values from -6 to 6
- cotangent: bfloat16 [384, 5120], P('node'), may hold values from -6 to 6
- gate_codes: bfloat16 [5120, 8192], P('node', 'dp'), may hold values from -4 to 4
- up_codes: bfloat16 [5120, 8192], P('node', 'dp'), may hold values from -4 to 4
- down_codes: bfloat16 [8192, 5120], P('dp', 'node'), may hold values from -4 to 4
- gate_scales: float32 [40, 8192], P(None, 'dp'), may hold values from 0.00559017 to 0.034938563
- up_scales: float32 [40, 8192], P(None, 'dp'), may hold values from 0.00559017 to 0.034938563
- down_scales: float32 [8192, 40], P('dp'), may hold values from 0.0044194176 to 0.027621359
Outputs:
- token_grad: bfloat16 [384, 5120], P('node', 'dp')
- gate_grad: bfloat16 [5120, 8192], P('node', 'dp')
- up_grad: bfloat16 [5120, 8192], P('node', 'dp')
- down_grad: bfloat16 [8192, 5120], P('dp', 'node')
All inputs are finite; a program needn't handle non-finite values.
Results may differ from a plain program's by a relative error of at most 0.0077.
Values may be sent and summed in bfloat16 or wider, within the bound.
No kernel may reach another device: no remote copies, remote signals or barrier semaphores. Data moves between devices by JAX's collectives and lax.ppermute only.
A program may use at most 128 MiB of HBM per device.

v0:
```python
import jax
import jax.numpy as jnp
from jax import lax
from jax.sharding import PartitionSpec as P

QB = 128


def shortened(value):
    return jax.tree.map(lambda a: a.astype(jnp.bfloat16) if a.dtype == jnp.float32 else a, value)


def scale_rows(codes, scales):
    blocks = codes.astype(jnp.float32).reshape(scales.shape[0], QB, codes.shape[1])
    return (blocks * scales[:, None, :]).reshape(codes.shape).astype(jnp.bfloat16)


def contract(left, right):
    return lax.dot_general(
        left, right, (((0,), (0,)), ((), ())), preferred_element_type=jnp.float32
    )


def against(left, right):
    return lax.dot_general(
        left, right, (((1,), (1,)), ((), ())), preferred_element_type=jnp.float32
    )


def body(tokens, cotangent, gate_codes, up_codes, down_codes, gate_scales, up_scales, down_scales):
    node_count = lax.axis_size("node")
    full_codes = (
        lax.all_gather(gate_codes, "node", axis=0, tiled=True),
        lax.all_gather(up_codes, "node", axis=0, tiled=True),
        lax.all_gather(down_codes, "node", axis=1, tiled=True),
    )
    w_gate = scale_rows(full_codes[0], gate_scales)
    w_up = scale_rows(full_codes[1], up_scales)
    w_down_t = scale_rows(full_codes[2].T, down_scales.T)
    gate = jnp.dot(tokens, w_gate, preferred_element_type=jnp.float32)
    upper = jnp.dot(tokens, w_up, preferred_element_type=jnp.float32)
    sig = jax.nn.sigmoid(gate)
    silu_val = gate * sig
    act = (silu_val * upper).astype(jnp.bfloat16)
    d_act = jnp.dot(cotangent, w_down_t, preferred_element_type=jnp.float32)
    d_gate = (d_act * upper * sig * (1.0 + gate * (1.0 - sig))).astype(jnp.bfloat16)
    d_up = (d_act * silu_val).astype(jnp.bfloat16)
    token_terms = against(d_gate, w_gate) + against(d_up, w_up)
    token_grad = lax.psum_scatter(token_terms, "dp", scatter_dimension=1, tiled=True).astype(
        jnp.bfloat16
    )
    width = d_gate.shape[1]
    partials = (contract(tokens, d_gate), contract(tokens, d_up), contract(cotangent, act))
    rounded = tuple((p.astype(jnp.bfloat16).reshape(node_count, -1, width) for p in partials))
    received = jax.tree.map(
        lambda part, own: part.astype(own.dtype),
        lax.all_to_all(shortened(rounded), "node", split_axis=0, concat_axis=0, tiled=True),
        rounded,
    )
    sums = tuple((r.astype(jnp.float32).sum(axis=0).astype(jnp.bfloat16) for r in received))
    return (token_grad, sums[0], sums[1], sums[2].T)


def solution(mesh):
    return jax.shard_map(
        body,
        mesh=mesh,
        in_specs=(
            P("node", None),
            P("node", None),
            P("node", "dp"),
            P("node", "dp"),
            P("dp", "node"),
            P(None, "dp"),
            P(None, "dp"),
            P("dp", None),
        ),
        out_specs=(P("node", "dp"), P("node", "dp"), P("node", "dp"), P("dp", "node")),
        check_vma=False,
    )
```

profile of v0, /device:TPU:0, one launch (start us, length us, event | category | flops | bytes accessed | tf_op | source)
XLA Modules:
  0.0 437.1 jit_solution(16675051946922043496)
XLA Ops:
  7.2 0.0 copy-start
  7.2 0.0 copy-start.7
  7.2 0.0 copy-start.5
  7.2 0.0 all-gather.8.cloned.1.call-start
  7.2 0.7 all-gather.8.cloned.1.call-update
  7.9 0.0 all-gather.6.cloned.1.call-start
  8.0 0.7 all-gather.6.cloned.1.call-update
  8.7 0.0 all-gather.4.cloned.1.call-start
  8.7 0.7 all-gather.4.cloned.1.call-update
  9.4 0.0 copy-done.7
  9.4 0.1 copy.13
  9.6 0.0 copy-start.6
  9.6 71.3 %all-gather.8.cloned.1.call-done = bf16[5120,512]{1,0:T(8,128)(2,1)} async-done(((bf16[2560,512]{1,0:T(8,128)(2,1)}), bf16[5120,512]{1,0:T(8,128)(2,1)}) %all-gather.8.cloned.1.call-update) | async-done | bytes 5242896 | tf_op jit(solution)/shard_map/all_gather | solution.py:33
  80.9 0.0 copy-done.5
  80.9 5.9 %fusion.1 = bf16[5120,512]{1,0:T(8,128)(2,1)} fusion(bf16[5120,512]{1,0:T(8,128)(2,1)} %all-gather.8.cloned.1.call-done, f32[40,512]{1,0:T(8,128)S(1)} %copy-done.5), kind=kLoop, calls=%fused_computation.3 | loop fusion | flops 7864320 | bytes 10567680 | tf_op jit(solution)/shard_map/convert_element_type | solution.py:15
  86.8 64.2 %all-gather.6.cloned.1.call-done = bf16[5120,512]{1,0:T(8,128)(2,1)} async-done(((bf16[2560,512]{1,0:T(8,128)(2,1)}), bf16[5120,512]{1,0:T(8,128)(2,1)}) %all-gather.6.cloned.1.call-update) | async-done | bytes 5242896 | tf_op jit(solution)/shard_map/all_gather | solution.py:34
  151.0 0.0 copy-done.6
  151.0 0.0 copy-start.2
  151.0 3.7 fusion.2
  154.7 0.0 copy-done
  154.7 0.3 copy-done.2
  155.1 0.0 copy-start.1
  155.1 1.2 convolution_bitcast_fusion
  156.3 1.0 copy-done.1
  157.3 1.2 convolution_bitcast_fusion.1
  158.5 62.6 %all-gather.4.cloned.1.call-done = bf16[512,5120]{1,0:T(8,128)(2,1)} async-done(((bf16[512,2560]{1,0:T(8,128)(2,1)}), bf16[512,5120]{1,0:T(8,128)(2,1)}) %all-gather.4.cloned.1.call-update) | async-done | bytes 5242896 | tf_op jit(solution)/shard_map/all_gather | solution.py:35
  221.2 0.0 copy-start.3
  221.2 0.0 copy-start.4
  221.2 3.0 mul.54
  224.1 0.0 copy-done.3
  224.1 0.1 copy-done.4
  224.3 2.5 multiply_convert_fusion.1
  226.8 1.6 convolution_convert_fusion.2
  228.4 2.8 copy.40
  231.1 5.9 %all-to-all-start = ((bf16[2,2560,512]{1,2,0:T(8,128)(2,1)}), bf16[2,2560,512]{1,2,0:T(8,128)(2,1)}, u32[]{:S(2)}, u32[]{:S(2)}) async-start(bf16[2,2560,512]{1,2,0:T(8,128)(2,1)} %bitcast.68), calls=%async_computation | async-start | bytes 10485760 | tf_op jit(solution)/shard_map/all_to_all | solution.py:57
  237.1 0.2 reduce-scatter.4.cloned.1.call-start
  237.3 4.3 fusion.11
  241.7 6.2 %convolution_add_fusion = f32[192,5120]{1,0:T(8,128)} fusion(f32[192,5120]{1,0:T(8,128)S(1)} %fusion.11, bf16[192,512]{1,0:T(8,128)(2,1)S(1)} %get-tuple-element.8, bf16[5120,512]{1,0:T(8,128)(2,1)} %copy-done.1), kind=kOutput, calls=%fused_computation.9 | convolution fusion | flops 1007616000 | bytes 13303808 | tf_op jit(solution)/shard_map/dot_general | solution.py:25
  247.9 5.6 %copy.21 = f32[192,5120]{0,1:T(8,128)} copy(f32[192,5120]{1,0:T(8,128)} %convolution_add_fusion) | data formatting | bytes 7864320
  253.5 0.0 reduce-scatter.4.cloned.1.call-update
  253.5 1.6 convolution_convert_fusion.1
  255.1 2.7 copy.39
  257.8 38.2 %all-to-all-done = bf16[2,2560,512]{1,2,0:T(8,128)(2,1)} async-done(((bf16[2,2560,512]{1,2,0:T(8,128)(2,1)}), bf16[2,2560,512]{1,2,0:T(8,128)(2,1)}, u32[]{:S(2)}, u32[]{:S(2)}) %all-to-all-start) | async-done | bytes 5242912 | tf_op jit(solution)/shard_map/all_to_all | solution.py:57
  296.0 6.0 %all-to-all-start.1 = ((bf16[2,2560,512]{1,2,0:T(8,128)(2,1)}), bf16[2,2560,512]{1,2,0:T(8,128)(2,1)}, u32[]{:S(2)}, u32[]{:S(2)}) async-start(bf16[2,2560,512]{1,2,0:T(8,128)(2,1)} %bitcast.70), calls=%async_computation.1 | async-start | bytes 10485760 | tf_op jit(solution)/shard_map/all_to_all | solution.py:57
  302.0 3.2 convolution_convert_fusion
  305.3 2.7 copy.38
  307.9 52.1 %all-to-all-done.1 = bf16[2,2560,512]{1,2,0:T(8,128)(2,1)} async-done(((bf16[2,2560,512]{1,2,0:T(8,128)(2,1)}), bf16[2,2560,512]{1,2,0:T(8,128)(2,1)}, u32[]{:S(2)}, u32[]{:S(2)}) %all-to-all-start.1) | async-done | bytes 5242912 | tf_op jit(solution)/shard_map/all_to_all | solution.py:57
  360.0 6.2 %all-to-all-start.2 = ((bf16[2,2560,512]{1,2,0:T(8,128)(2,1)}), bf16[2,2560,512]{1,2,0:T(8,128)(2,1)}, u32[]{:S(2)}, u32[]{:S(2)}) async-start(bf16[2,2560,512]{1,2,0:T(8,128)(2,1)} %bitcast.69), calls=%async_computation.2 | async-start | bytes 10485760 | tf_op jit(solution)/shard_map/all_to_all | solution.py:57
  366.2 5.7 %reduce_sum.36 = bf16[2560,512]{0,1:T(8,128)(2,1)} reduce(bf16[2,2560,512]{1,2,0:T(8,128)(2,1)} %all-to-all-done, bf16[]{:T(256)} %constant.6.clone.1), dimensions={0}, to_apply=%region_1.0 | reduce | flops 1310720 | bytes 7864322 | tf_op jit(solution)/shard_map/reduce_sum | solution.py:60
  371.9 4.4 %copy.19 = bf16[2560,512]{1,0:T(8,128)(2,1)} copy(bf16[2560,512]{0,1:T(8,128)(2,1)} %reduce_sum.36) | data formatting | bytes 5242880
  376.3 5.7 %reduce_sum.37 = bf16[2560,512]{0,1:T(8,128)(2,1)} reduce(bf16[2,2560,512]{1,2,0:T(8,128)(2,1)} %all-to-all-done.1, bf16[]{:T(256)} %constant.6.clone.1), dimensions={0}, to_apply=%region_2.0 | reduce | flops 1310720 | bytes 7864322 | tf_op jit(solution)/shard_map/reduce_sum | solution.py:60
  382.0 4.4 %copy.20 = bf16[2560,512]{1,0:T(8,128)(2,1)} copy(bf16[2560,512]{0,1:T(8,128)(2,1)} %reduce_sum.37) | data formatting | bytes 5242880
  386.4 36.7 %all-to-all-done.2 = bf16[2,2560,512]{1,2,0:T(8,128)(2,1)} async-done(((bf16[2,2560,512]{1,2,0:T(8,128)(2,1)}), bf16[2,2560,512]{1,2,0:T(8,128)(2,1)}, u32[]{:S(2)}, u32[]{:S(2)}) %all-to-all-start.2) | async-done | bytes 5242912 | tf_op jit(solution)/shard_map/all_to_all | solution.py:57
  423.1 5.7 %reduce_sum.38 = bf16[2560,512]{0,1:T(8,128)(2,1)} reduce(bf16[2,2560,512]{1,2,0:T(8,128)(2,1)} %all-to-all-done.2, bf16[]{:T(256)} %constant.6.clone.1), dimensions={0}, to_apply=%region_3.0 | reduce | flops 1310720 | bytes 7864322 | tf_op jit(solution)/shard_map/reduce_sum | solution.py:60
  428.8 0.0 reduce-scatter.4.cloned.1.call-done
  428.8 1.8 copy.22
Async XLA Ops:
  7.2 147.5 %copy-start = (bf16[192,5120]{1,0:T(8,128)(2,1)S(1)}, bf16[192,5120]{1,0:T(8,128)(2,1)}, u32[]{:S(2)}) copy-start(bf16[192,5120]{1,0:T(8,128)(2,1)} %param.8) | copy-start | bytes 5898244
  7.2 2.2 copy-start.7
  7.2 73.7 %copy-start.5 = (f32[40,512]{1,0:T(8,128)S(1)}, f32[40,512]{1,0:T(8,128)}, u32[]{:S(2)}) copy-start(f32[40,512]{1,0:T(8,128)} %param.13) | copy-start | bytes 245764
  7.2 73.7 %all-gather.8.cloned.1.call-start = ((), (), s32[]{:S(2)}) async-start(), calls=%async_computation.6 | async-start | bytes 7864320 | tf_op jit(solution)/shard_map/all_gather | solution.py:33
  7.9 143.1 %all-gather.6.cloned.1.call-start = ((), (), s32[]{:S(2)}) async-start(), calls=%async_computation.5 | async-start | bytes 7864320 | tf_op jit(solution)/shard_map/all_gather | solution.py:34
  8.7 212.5 %all-gather.4.cloned.1.call-start = ((), (), s32[]{:S(2)}) async-start(), calls=%async_computation.4 | async-start | bytes 7864320 | tf_op jit(solution)/shard_map/all_gather | solution.py:35
  9.6 141.5 %copy-start.6 = (f32[40,512]{1,0:T(8,128)S(1)}, f32[40,512]{1,0:T(8,128)}, u32[]{:S(2)}) copy-start(f32[40,512]{1,0:T(8,128)} %param.14) | copy-start | bytes 245764
  151.0 4.0 copy-start.2
  155.1 2.3 copy-start.1
  221.2 3.0 copy-start.3
  221.2 3.1 copy-start.4
  231.1 64.8 %all-to-all-start = ((bf16[2,2560,512]{1,2,0:T(8,128)(2,1)}), bf16[2,2560,512]{1,2,0:T(8,128)(2,1)}, u32[]{:S(2)}, u32[]{:S(2)}) async-start(bf16[2,2560,512]{1,2,0:T(8,128)(2,1)} %bitcast.68), calls=%async_computation | async-start | bytes 10485760 | tf_op jit(solution)/shard_map/all_to_all | solution.py:57
  237.1 191.7 %reduce-scatter.4.cloned.1.call-start = ((), (), s32[]{:S(2)}) async-start(), calls=%async_computation.7 | async-start | bytes 5570560
  296.0 64.0 %all-to-all-start.1 = ((bf16[2,2560,512]{1,2,0:T(8,128)(2,1)}), bf16[2,2560,512]{1,2,0:T(8,128)(2,1)}, u32[]{:S(2)}, u32[]{:S(2)}) async-start(bf16[2,2560,512]{1,2,0:T(8,128)(2,1)} %bitcast.70), calls=%async_computation.1 | async-start | bytes 10485760 | tf_op jit(solution)/shard_map/all_to_all | solution.py:57
  360.0 63.1 %all-to-all-start.2 = ((bf16[2,2560,512]{1,2,0:T(8,128)(2,1)}), bf16[2,2560,512]{1,2,0:T(8,128)(2,1)}, u32[]{:S(2)}, u32[]{:S(2)}) async-start(bf16[2,2560,512]{1,2,0:T(8,128)(2,1)} %bitcast.69), calls=%async_computation.2 | async-start | bytes 10485760 | tf_op jit(solution)/shard_map/all_to_all | solution.py:57
Sparse Core Ops, SparseCore 0:
  9.6 71.2 all-gather.7
  82.4 68.5 all-gather.5
  152.6 68.5 all-gather.3
  253.6 79.6 reduce-scatter.3
where the time goes:
time: 438 us; the launch traced here: 437 us
  waiting for transfers between devices  327 us (75%)
  local copies, waits for them, and re-layouts  28.9 us (7%)
  other arithmetic  26.7 us (6%)
  matrix products  21.9 us (5%)
  starting transfers between devices  18.5 us (4%)
  between operations  13.9 us (3%)
    all_to_all x3, waiting for transfers between devices, body(): lax.all_to_all(shortened(rounded), 'node', split_axis=0, concat_axis=0, t...  127 us
    all_gather x1, waiting for transfers between devices, body(): lax.all_gather(gate_codes, 'node', axis=0, tiled=True)  71.3 us
    all_gather x1, waiting for transfers between devices, body(): lax.all_gather(up_codes, 'node', axis=0, tiled=True)  64.2 us
    all_gather x1, waiting for transfers between devices, body(): lax.all_gather(down_codes, 'node', axis=1, tiled=True)  62.6 us
    all_to_all x3, starting transfers between devices, body(): lax.all_to_all(shortened(rounded), 'node', split_axis=0, concat_axis=0, t...  18.2 us
    unnamed x20, local copies, waits for them, and re-layouts  17.6 us
    reduce_sum x3, other arithmetic, body(): r.astype(jnp.float32).sum(axis=0).astype(jnp.bfloat16)  17.1 us
    dot_general x2, matrix products, against(): lax.dot_general(left, right, (((1,), (1,)), ((), ())), preferred_element_...  10.6 us
  transfers between devices with their start and end apart: 7, of which 6 were waited for; matrix products, arithmetic and copies ran while one was open for 15% of the time, Pallas kernels for 0%

commit v1 on v0

v1 whole, which is shorter than its diff:
```python
import functools

import jax
import jax.numpy as jnp
from jax import lax
from jax.experimental import pallas as pl
from jax.experimental.pallas import tpu as pltpu
from jax.sharding import PartitionSpec as P

QB = 128
STEP = 640
SIDE_BIT = 2
IN_HBM = pl.BlockSpec(memory_space=pltpu.HBM)
IN_VMEM = pl.BlockSpec(memory_space=pltpu.VMEM)
IN_SMEM = pl.BlockSpec(memory_space=pltpu.SMEM)


def contract(left, right):
    return lax.dot_general(
        left, right, (((0,), (0,)), ((), ())), preferred_element_type=jnp.float32
    )


def against(left, right):
    return lax.dot_general(
        left, right, (((1,), (1,)), ((), ())), preferred_element_type=jnp.float32
    )


def flipped(size, mask):
    return [(i, i ^ mask) for i in range(size)]


def swap(value, axis, size, mask):
    return lax.ppermute(value, axis, flipped(size, mask))


def in_hbm(array):
    return pltpu.with_memory_space_constraint(array, pltpu.HBM)


def in_vmem(array):
    return pltpu.with_memory_space_constraint(array, pltpu.VMEM)


def cost(operations):
    return pl.CostEstimate(flops=operations, transcendentals=0, bytes_accessed=0)


def grant(mebibytes):
    return pltpu.CompilerParams(vmem_limit_bytes=mebibytes * 1024 * 1024)


def side_of(place):
    return (place >> SIDE_BIT) & 1


def fetch_kernel(mask, node, place, tokens, cot, target, sem):
    half, rows = target.shape
    start = pl.multiple_of(side_of(place[0]) * half, 16)
    column = pl.multiple_of((node[0] ^ mask) * rows, 128)
    part = (pl.ds(start, half), pl.ds(column, rows))

    @pl.when((place[0] & 1) == 0)
    def _():
        copy = pltpu.make_async_copy(tokens.at[part], target, sem)
        copy.start()
        copy.wait()

    @pl.when((place[0] & 1) == 1)
    def _():
        copy = pltpu.make_async_copy(cot.at[part], target, sem)
        copy.start()
        copy.wait()


def fetch(mask, node, place, tokens, cot, shape):
    return pl.pallas_call(
        functools.partial(fetch_kernel, mask),
        in_specs=[IN_SMEM, IN_SMEM, IN_HBM, IN_HBM],
        out_specs=IN_VMEM,
        out_shape=pltpu.VMEM(shape, tokens.dtype),
        scratch_shapes=[pltpu.SemaphoreType.DMA],
        compiler_params=grant(4),
        cost_estimate=cost(0),
        name="fetch",
    )(node, place, in_hbm(tokens), in_hbm(cot))


def prepare_kernel(
    node, tokens, cot, gate_codes, up_codes, down_codes, gate_scales, up_scales, down_scales,
    own_tokens, own_cot, w_in, w_down, total, short, gate_held, up_held, down_held, sems,
):
    rows, units = gate_codes.shape
    steps, per_step = rows // STEP, STEP // QB
    own = slice(0, tokens.shape[0])

    def copies(step):
        column = pl.multiple_of(node[0] * rows + step * STEP, 128)
        part = pl.ds(pl.multiple_of(step * STEP, 128), STEP)
        pairs = (
            (gate_codes.at[part, :], gate_held.at[part, :]),
            (up_codes.at[part, :], up_held.at[part, :]),
            (tokens.at[:, pl.ds(column, STEP)], own_tokens.at[own, part]),
            (down_codes.at[:, part], down_held.at[:, part]),
            (cot.at[:, pl.ds(column, STEP)], own_cot.at[own, part]),
        )
        return [pltpu.make_async_copy(a, b, sems.at[step, i]) for i, (a, b) in enumerate(pairs)]

    for step in range(steps):
        for copy in copies(step):
            copy.start()
    total[...] = jnp.zeros(total.shape, total.dtype)

    def one(step, carry):
        for copy in copies(step):
            copy.wait()
        first_scale = (node[0] * steps + step) * per_step
        for j in range(per_step):
            part = pl.ds(pl.multiple_of(step * STEP + j * QB, QB), QB)
            scale = pl.ds(first_scale + j, 1)
            w_in[part, :units] = (gate_held[part, :].astype(jnp.float32) * gate_scales[scale, :]).astype(w_in.dtype)
            w_in[part, units:] = (up_held[part, :].astype(jnp.float32) * up_scales[scale, :]).astype(w_in.dtype)
            w_down[:, part] = (
                down_held[:, part].astype(jnp.float32) * down_scales[step, :, j : j + 1]
            ).astype(w_down.dtype)
        part = pl.ds(pl.multiple_of(step * STEP, 128), STEP)
        total[:, : 2 * units] += jnp.dot(own_tokens[own, part], w_in[part, :], preferred_element_type=jnp.float32)
        total[:, 2 * units :] += against(own_cot[own, part], w_down[:, part])
        return carry

    lax.fori_loop(0, steps, one, 0)
    short[...] = total[...].astype(short.dtype)


def prepare(nodes, node, tokens, cot, gate_codes, up_codes, down_codes, gate_scales, up_scales, down_scales):
    rows, units = gate_codes.shape
    count = tokens.shape[0]
    steps, per_step = rows // STEP, STEP // QB
    scales = lax.dynamic_slice_in_dim(down_scales, node[0] * (rows // QB), rows // QB, 1)
    scales = scales.reshape(units, steps, per_step).transpose(1, 0, 2)
    codes = jnp.bfloat16
    return pl.pallas_call(
        prepare_kernel,
        in_specs=[IN_SMEM] + [IN_HBM] * 5 + [IN_VMEM] * 3,
        out_specs=[IN_VMEM] * 6,
        out_shape=[
            pltpu.VMEM((nodes * count, rows), codes),
            pltpu.VMEM((nodes * count, rows), codes),
            pltpu.VMEM((rows, 2 * units), codes),
            pltpu.VMEM((units, rows), codes),
            pltpu.VMEM((count, 3 * units), jnp.float32),
            pltpu.VMEM((count, 3 * units), codes),
        ],
        scratch_shapes=[
            pltpu.VMEM((rows, units), codes),
            pltpu.VMEM((rows, units), codes),
            pltpu.VMEM((units, rows), codes),
            pltpu.SemaphoreType.DMA((steps, 5)),
        ],
        compiler_params=grant(16),
        cost_estimate=cost(0),
        name="prepare",
    )(
        node, *(in_hbm(a) for a in (tokens, cot, gate_codes, up_codes, down_codes)),
        gate_scales, up_scales, scales,
    )


def reorder_kernel(blocks, place, source, target):
    rows = target.shape[0] // blocks
    bits = blocks.bit_length() - 1
    for i in range(blocks):
        block = 0
        for bit in range(bits):
            own = (place[0] >> bit) & 1
            block += (own if (i >> (bits - 1 - bit)) & 1 else 1 - own) << bit
        target[i * rows : (i + 1) * rows, :] = source[pl.ds(pl.multiple_of(block * rows, 16), rows), :]


def reorder(place, weights, blocks):
    return pl.pallas_call(
        functools.partial(reorder_kernel, blocks),
        in_specs=[IN_SMEM, IN_VMEM],
        out_specs=IN_VMEM,
        out_shape=pltpu.VMEM(weights.shape, weights.dtype),
        compiler_params=grant(4),
        cost_estimate=cost(0),
        name="reorder",
    )(place, in_vmem(weights))


def join_kernel(group, far, place, held, given, w_in, w_down, *refs):
    tokens, cot, total, short = refs[-4:]
    half, rows = held.shape
    units = w_down.shape[0]
    side = side_of(place[0])
    natural = (1 - side if far else side) * half
    mine = pl.ds(pl.multiple_of(2 * group * half + natural, 16), half)
    out = pl.ds(pl.multiple_of(natural, 16), half)

    @pl.when((place[0] & 1) == 0)
    def _():
        tokens[mine, :] = held[...]
        cot[mine, :] = given[...]

    @pl.when((place[0] & 1) == 1)
    def _():
        tokens[mine, :] = given[...]
        cot[mine, :] = held[...]

    for step in range(rows // STEP):
        part = slice(step * STEP, (step + 1) * STEP)
        inner = jnp.dot(tokens[mine, part], w_in[part, :], preferred_element_type=jnp.float32)
        outer = against(cot[mine, part], w_down[:, part])
        if step == 0:
            total[out, : 2 * units] = inner
            total[out, 2 * units :] = outer
        else:
            total[out, : 2 * units] += inner
            total[out, 2 * units :] += outer
    short[...] = total[out, :].astype(short.dtype)


def join(group, far, place, held, given, w_in, w_down, before):
    half, rows = held.shape
    units = w_down.shape[0]
    return pl.pallas_call(
        functools.partial(join_kernel, group, far),
        in_specs=[IN_SMEM] + [IN_VMEM] * (4 + len(before)),
        out_specs=[IN_VMEM] * 4,
        out_shape=[
            pltpu.VMEM(before[0].shape, jnp.bfloat16),
            pltpu.VMEM(before[1].shape, jnp.bfloat16),
            pltpu.VMEM((2 * half, 3 * units), jnp.float32),
            pltpu.VMEM((half, 3 * units), jnp.bfloat16),
        ],
        input_output_aliases={5 + i: i for i in range(len(before))},
        compiler_params=grant(8),
        cost_estimate=cost(0),
        name="join",
    )(place, *(in_vmem(a) for a in (held, given, w_in, w_down, *before)))


def activate_kernel(group, turns, count, place, weights, total, arrived, *refs):
    act, d_inner, *targets = refs[-6:]
    units, half, chunk = act.shape[1], count // 2, 32
    side = side_of(place[0])
    width = targets[0].shape[1]

    def rows(first, length):
        return pl.ds(pl.multiple_of(first, 16), length)

    for turn in turns:
        natural = (1 - side if turn else side) * half
        for start in range(0, half, chunk):
            def of(array):
                return rows((natural if array.shape[0] == count else 0) + start, chunk)

            sums = total[of(total), :] + arrived[of(arrived), :].astype(jnp.float32)
            gate, upper, d_act = sums[:, :units], sums[:, units : 2 * units], sums[:, 2 * units :]
            sig = jax.nn.sigmoid(gate)
            silu_val = gate * sig
            kept = rows(group * count + natural + start, chunk)
            act[kept, :] = (silu_val * upper).astype(act.dtype)
            d_inner[kept, :units] = (d_act * upper * sig * (1.0 + gate * (1.0 - sig))).astype(d_inner.dtype)
            d_inner[kept, units:] = (d_act * silu_val).astype(d_inner.dtype)
    if len(turns) == 2:
        mine, out = rows(group * count, count), rows(0, count)
    else:
        mine, out = rows(group * count + natural, half), rows(natural, half)
    for i, target in enumerate(targets):
        product = against(d_inner[mine, :], weights[i * width : (i + 1) * width, :])
        target[out, :] = product.astype(target.dtype)


def activate(group, groups, turns, place, total, arrived, weights, before):
    units = weights.shape[1] // 2
    count = arrived.shape[0] * (3 - len(turns))
    terms = count, weights.shape[0] // 4
    return pl.pallas_call(
        functools.partial(activate_kernel, group, turns, count),
        in_specs=[IN_SMEM] + [IN_VMEM] * (3 + len(before)),
        out_specs=[IN_VMEM] * 6,
        out_shape=[
            pltpu.VMEM((groups * count, units), jnp.bfloat16),
            pltpu.VMEM((groups * count, 2 * units), jnp.bfloat16),
            pltpu.VMEM(terms, jnp.bfloat16),
            pltpu.VMEM(terms, jnp.bfloat16),
            pltpu.VMEM(terms, jnp.float32),
            pltpu.VMEM(terms, jnp.float32),
        ],
        input_output_aliases={4 + i: i for i in range(len(before))},
        compiler_params=grant(12),
        cost_estimate=cost(0),
        name="activate",
    )(place, *(in_vmem(a) for a in (weights, total, arrived, *before)))


def grads_kernel(tokens, cot, act, d_inner, gate_grad, up_grad, down_grad, gate_held, up_held, down_held, sems):
    rows, units = gate_grad.shape
    copies = []

    def send(held, target, part, i):
        copies.append(pltpu.make_async_copy(held.at[part], target.at[part], sems.at[i]))
        copies[-1].start()

    steps = rows // STEP
    for step in range(steps):
        part = slice(step * STEP, (step + 1) * STEP)
        both = contract(tokens[:, part], d_inner[...])
        gate_held[part, :] = both[:, :units].astype(gate_held.dtype)
        send(gate_held, gate_grad, (part, slice(None)), step)
        up_held[part, :] = both[:, units:].astype(up_held.dtype)
        send(up_held, up_grad, (part, slice(None)), steps + step)
    for step in range(steps):
        part = slice(step * STEP, (step + 1) * STEP)
        down_held[:, part] = contract(act[...], cot[:, part]).astype(down_held.dtype)
        send(down_held, down_grad, (slice(None), part), 2 * steps + step)
    for copy in copies:
        copy.wait()


def weight_grads(tokens, cot, act, d_inner):
    rows, units = tokens.shape[1], act.shape[1]
    shapes = [(rows, units), (rows, units), (units, rows)]
    return pl.pallas_call(
        grads_kernel,
        in_specs=[IN_VMEM] * 4,
        out_specs=[IN_HBM] * 3,
        out_shape=[pltpu.HBM(shape, jnp.bfloat16) for shape in shapes],
        scratch_shapes=[pltpu.VMEM(shape, jnp.bfloat16) for shape in shapes]
        + [pltpu.SemaphoreType.DMA((3 * (rows // STEP),))],
        compiler_params=grant(20),
        cost_estimate=cost(6 * tokens.shape[0] * rows * units),
        name="weight_grads",
    )(*(in_vmem(a) for a in (tokens, cot, act, d_inner)))


def after(value, *earlier):
    return lax.optimization_barrier((value, earlier))[0]


def body(tokens, cotangent, gate_codes, up_codes, down_codes, gate_scales, up_scales, down_scales):
    nodes, width = lax.axis_size("node"), lax.axis_size("dp")
    node, place = lax.axis_index("node"), lax.axis_index("dp")
    node_ref, place_ref = node.reshape(1), place.reshape(1)
    rows, units = gate_codes.shape
    count = tokens.shape[0]
    owners = width // nodes
    bits = owners.bit_length() - 1

    side, half = side_of(place), count // 2

    def halves(array):
        return [lax.dynamic_slice_in_dim(array, s * half, half, 0) for s in (side, 1 - side)]

    fetched = [
        swap(fetch(k, node_ref, place_ref, tokens, cotangent, (half, rows)), "node", nodes, k)
        for k in range(1, nodes)
    ]
    all_tokens, all_cots, w_in, w_down, own_sums, own_short = prepare(
        nodes, node_ref, tokens, cotangent, gate_codes, up_codes, down_codes, gate_scales, up_scales, down_scales
    )
    fetched = after(fetched, own_short)
    w_relative = reorder(place_ref, w_in, owners)
    fetched = after(fetched, w_relative)

    sums, shorts = [own_sums], [None]
    for k, mine in enumerate(fetched, 1):
        given = swap(mine, "dp", width, 1)
        beside = swap(mine, "dp", width, 1 << SIDE_BIT)
        before, near_far = [all_tokens, all_cots], []
        for far, held in enumerate((mine, beside)):
            if far:
                given = swap(held, "dp", width, 1)
            *before, short = join(k, far, place_ref, held, given, w_in, w_down, before)
            near_far.append(short)
        all_tokens, all_cots, total = before
        sums.append(total)
        shorts.append(near_far)

    mask = 1
    if nodes > 2:
        while mask < nodes // 2:
            sent = [swap(s.astype(jnp.bfloat16), "node", nodes, mask) for s in sums]
            sums = [s + sent[k ^ mask].astype(jnp.float32) for k, s in enumerate(sums)]
            mask *= 2
        own_short = sums[0].astype(jnp.bfloat16)
        shorts = [halves(s.astype(jnp.bfloat16)) for s in sums]
    near_far = [swap(s, "node", nodes, mask) for s in shorts[mask]]
    arrived = [None]
    for k in range(1, nodes):
        short = own_short if k == mask else sums[k ^ mask].astype(jnp.bfloat16)
        arrived.append(swap(short, "node", nodes, mask))

    def pair(parts):
        got = [swap(part, "dp", width, 1).astype(jnp.float32) for part in parts[:2]]
        return (parts[2] + got[0]).astype(jnp.bfloat16), parts[3] + got[1]

    def cut(terms, got):
        edge = terms.shape[1] // 2
        sending = (terms[:, :edge] + got[:, :edge].astype(jnp.float32)).astype(jnp.bfloat16)
        return sending, terms[:, edge:] + got[:, edge:].astype(jnp.float32)

    blocks, before = [None] * nodes, []
    for k in reversed(range(1, nodes)):
        *before, a, b, c, d = activate(k, nodes, (0, 1), place_ref, sums[k], arrived[k], w_relative, before)
        x_sent, terms = pair((a, b, c, d))
        last = x_sent
        got = swap(x_sent, "dp", width, 2)
        for bit in range(2, bits):
            last, terms = cut(terms, got)
            got = swap(last, "dp", width, 1 << bit)
        blocks[k] = terms, got

    before = activate(0, nodes, (0,), place_ref, sums[0], near_far[0], w_relative, before)
    act, d_inner, *parts = activate(0, nodes, (1,), place_ref, sums[0], after(near_far[1], x_sent), w_relative, before)
    sending, terms = pair(parts)
    got = swap(sending, "dp", width, 2)
    for k in range(1, nodes):
        block = (blocks[k][0] + blocks[k][1].astype(jnp.float32)).astype(jnp.bfloat16)
        act, sending, block = lax.optimization_barrier((act, sending, block))
        blocks[k] = swap(block, "node", nodes, k).astype(jnp.float32)
    act, d_inner = after((act, d_inner), sending)
    gate_grad, up_grad, down_grad = weight_grads(all_tokens, all_cots, act, d_inner)
    got = after(got, gate_grad, up_grad, down_grad)
    for bit in range(2, bits):
        sending, terms = cut(terms, got)
        got = swap(sending, "dp", width, 1 << bit)
    blocks[0] = terms + got.astype(jnp.float32)
    high = place // owners

    def block_for(owner):
        chosen = blocks[0]
        for k in range(1, nodes):
            chosen = jnp.where((owner ^ node) == k, blocks[k], chosen)
        return chosen

    token_grad = block_for(high)
    for j in range(1, nodes):
        token_grad += swap(block_for(high ^ j).astype(jnp.bfloat16), "dp", width, j * owners).astype(jnp.float32)
    return token_grad.astype(jnp.bfloat16), gate_grad, up_grad, down_grad


def solution(mesh):
    return jax.shard_map(
        body,
        mesh=mesh,
        in_specs=(
            P("node", None),
            P("node", None),
            P("node", "dp"),
            P("node", "dp"),
            P("dp", "node"),
            P(None, "dp"),
            P(None, "dp"),
            P("dp", None),
        ),
        out_specs=(P("node", "dp"), P("node", "dp"), P("node", "dp"), P("dp", "node")),
        check_vma=False,
    )
```

time: 438 us -> 75.9 us (0.17)
  waiting for transfers between devices: 327 us -> 30.2 us
  local copies, waits for them, and re-layouts: 28.9 us -> 0.39 us
  other arithmetic: 26.7 us -> 1.46 us
  Pallas kernels: 0 us -> 22.6 us
  matrix products: 21.9 us -> 0 us
  between operations: 13.9 us -> 0.85 us
    all_gather x3 -> x0, waiting for transfers between devices: 198 us -> none  [the longest x1 71.3 us: body(): lax.all_gather(gate_codes, 'node', axis=0, tiled=True)]
    all_to_all x3 -> x0, waiting for transfers between devices: 127 us -> none  [body(): lax.all_to_all(shortened(rounded), 'node', split_axis=0, concat_axis=0, t...]
    ppermute x0 -> x17, waiting for transfers between devices: none -> 30.2 us  [swap(): return lax.ppermute(value, axis, flipped(size, mask))]
    pallas_call x0 -> x9, Pallas kernels: none -> 22.6 us  [the longest x1 6.39 us: prepare(): pl.pallas_call(prepare_kernel, in_specs=[IN_SMEM] + [IN_HBM] * 5 + [IN_VM...]
    dot_general x8 -> x0, matrix products: 21.9 us -> none  [the longest x2 10.6 us: against(): lax.dot_general(left, right, (((1,), (1,)), ((), ())), preferred_element_...]
    ppermute x0 -> x17, starting transfers between devices: none -> 20.2 us  [swap(): return lax.ppermute(value, axis, flipped(size, mask))]
    all_to_all x3 -> x0, starting transfers between devices: 18.2 us -> none  [body(): lax.all_to_all(shortened(rounded), 'node', split_axis=0, concat_axis=0, t...]
    unnamed x20 -> x6, local copies, waits for them, and re-layouts: 17.6 us -> 0.02 us
  transfers between devices with their start and end apart: 7 -> 17, of which waited for: 6 -> 8; matrix products, arithmetic and copies ran while one was open for 15% -> 1% of each run, Pallas kernels for 0% -> 28%
where the time goes in v1:
time: 75.9 us; the launch traced here: 75.7 us
  waiting for transfers between devices  30.2 us (40%)
  Pallas kernels  22.6 us (30%)
  starting transfers between devices  20.2 us (27%)
  other arithmetic  1.46 us (2%)
  between operations  0.85 us (1%)
    ppermute x17, waiting for transfers between devices, swap(): return lax.ppermute(value, axis, flipped(size, mask))  30.2 us
    ppermute x17, starting transfers between devices, swap(): return lax.ppermute(value, axis, flipped(size, mask))  20.2 us
    pallas_call x1, Pallas kernels, prepare(): pl.pallas_call(prepare_kernel, in_specs=[IN_SMEM] + [IN_HBM] * 5 + [IN_VM...  6.39 us
    pallas_call x3, Pallas kernels, activate(): pl.pallas_call(functools.partial(activate_kernel, group, turns, count), i...  5.41 us
    pallas_call x1, Pallas kernels, weight_grads(): pl.pallas_call(grads_kernel, in_specs=[IN_VMEM] * 4, out_specs=[IN_HBM] *...  5.38 us
    pallas_call x2, Pallas kernels, join(): pl.pallas_call(functools.partial(join_kernel, group, far), in_specs=[IN_S...  3.97 us
  transfers between devices with their start and end apart: 17, of which 8 were waited for; matrix products, arithmetic and copies ran while one was open for 1% of the time, Pallas kernels for 28%

profile of v1, /device:TPU:0, one launch (start us, length us, event | category | flops | bytes accessed | tf_op | source)
XLA Modules:
  0.0 75.7 jit_solution(6966883624824516378)
XLA Ops:
  0.6 0.0 copy-start
  0.7 0.0 copy-start.1
  0.7 0.0 copy-start.2
  0.7 1.1 %fetch.1 = bf16[96,2560]{1,0:T(8,128)(2,1)S(1)} custom-call(s32[1]{0:T(128)} %bitcast.1.node, s32[1]{0:T(128)} %bitcast.place, bf16[192,5120]{1,0:T(8,128)(2,1)} %tokens.3, bf16[192,5120]{1,0:T(8,128)(2,1)} %cot.3), custom_call_target="tpu_custom_call" | custom-call | tf_op jit(solution)/shard_map/fetch/pallas_call | solution.py:78
  1.8 3.0 %collective-permute-start = (bf16[96,2560]{1,0:T(8,128)(2,1)S(1)}, bf16[96,2560]{1,0:T(8,128)(2,1)S(1)}, u32[]{:S(2)}, u32[]{:S(2)}) collective-permute-start(bf16[96,2560]{1,0:T(8,128)(2,1)S(1)} %fetch.1), channel_id=1, source_target_pairs={{0,1},{1,0},{2,3},{3,2},{4,5},{5,4},{6,7},{7,6},{8,9},{9,8},{10,11... | collective-permute-start | bytes 1474568 | tf_op jit(solution)/shard_map/ppermute | solution.py:35
  4.8 0.0 copy-done
  4.8 0.4 copy.25
  5.2 0.0 copy-done.1
  5.2 0.0 copy-done.2
  5.2 6.4 %prepare.1 = (bf16[384,2560]{1,0:T(8,128)(2,1)S(1)}, bf16[384,2560]{1,0:T(8,128)(2,1)S(1)}, bf16[2560,1024]{1,0:T(8,128)(2,1)S(1)}, bf16[512,2560]{1,0:T(8,128)(...) custom-call(s32[1]{0:T(128)} %bitcast.1.node, bf16[192,5120]{1,0:T(8,128)(2,1)} %tokens.3, ...), custom_call_target="tpu_custom_call" | custom-call | tf_op jit(solution)/shard_map/prepare/pallas_call | solution.py:143
  11.6 0.3 reorder.1.weights
  12.0 4.1 %collective-permute-done.held = bf16[96,2560]{1,0:T(8,128)(2,1)S(1)} collective-permute-done((bf16[96,2560]{1,0:T(8,128)(2,1)S(1)}, bf16[96,2560]{1,0:T(8,128)(2,1)S(1)}, u32[]{:S(2)}, u32[]{:S(2)}) %collective-permute-start) | collective-permute-done | bytes 491552 | tf_op jit(solution)/shard_map/ppermute | solution.py:35
  16.0 1.8 %collective-permute-start.1 = (bf16[96,2560]{1,0:T(8,128)(2,1)S(1)}, bf16[96,2560]{1,0:T(8,128)(2,1)S(1)}, u32[]{:S(2)}, u32[]{:S(2)}) collective-permute-start(bf16[96,2560]{1,0:T(8,128)(2,1)S(1)} %collective-permute-done.held), channel_id=1, source_target_pairs={{0,8},{2,10},{4,12},{6,14},{8,0},{10,2},{12,4},{14,6},{16,24},{18,... | collective-permute-start | bytes 1474568 | tf_op jit(solution)/shard_map/ppermute | solution.py:35
  17.8 1.5 %collective-permute-start.5 = (bf16[192,1536]{1,0:T(8,128)(2,1)S(1)}, bf16[192,1536]{1,0:T(8,128)(2,1)S(1)}, u32[]{:S(2)}, u32[]{:S(2)}) collective-permute-start(bf16[192,1536]{1,0:T(8,128)(2,1)S(1)} %get-tuple-element.49), channel_id=1, source_target_pairs={{0,1},{1,0},{2,3},{3,2},{4,5},{5,4},{6,7},{7,6},{8,9},{9,8},{10,11... | collective-permute-start | bytes 1769480 | tf_op jit(solution)/shard_map/ppermute | solution.py:35
  19.4 0.0 collective-permute-start.3
  19.4 9.1 %collective-permute-done.1.held = bf16[96,2560]{1,0:T(8,128)(2,1)S(1)} collective-permute-done((bf16[96,2560]{1,0:T(8,128)(2,1)S(1)}, bf16[96,2560]{1,0:T(8,128)(2,1)S(1)}, u32[]{:S(2)}, u32[]{:S(2)}) %collective-permute-start.1) | collective-permute-done | bytes 491552 | tf_op jit(solution)/shard_map/ppermute | solution.py:35
  28.5 0.0 collective-permute-start.2
  28.5 0.0 collective-permute-done.3.given
  28.5 1.9 %join.2 = (bf16[384,2560]{1,0:T(8,128)(2,1)S(1)}, bf16[384,2560]{1,0:T(8,128)(2,1)S(1)}, f32[192,1536]{1,0:T(8,128)S(1)}, bf16[96,1536]{1,0:T(8,128)(2,1)S(1)}) custom-call(s32[1]{0:T(128)} %bitcast.place, bf16[96,2560]{1,0:T(8,128)(2,1)S(1)} %collective-permute-done.held, ...), custom_call_target="tpu_custom_call", output_to_operand_aliasing={{0}: (5, {}), {1}: (6, {})} | custom-call | tf_op jit(solution)/shard_map/join/pallas_call | solution.py:228
  30.4 1.5 %collective-permute-start.7 = (bf16[96,1536]{1,0:T(8,128)(2,1)S(1)}, bf16[96,1536]{1,0:T(8,128)(2,1)S(1)}, u32[]{:S(2)}, u32[]{:S(2)}) collective-permute-start(bf16[96,1536]{1,0:T(8,128)(2,1)S(1)} %get-tuple-element.63), channel_id=1, source_target_pairs={{0,1},{1,0},{2,3},{3,2},{4,5},{5,4},{6,7},{7,6},{8,9},{9,8},{10,11... | collective-permute-start | bytes 884744 | tf_op jit(solution)/shard_map/ppermute | solution.py:35
  31.9 0.0 collective-permute-done.2.given
  31.9 2.1 %join.3 = (bf16[384,2560]{1,0:T(8,128)(2,1)S(1)}, bf16[384,2560]{1,0:T(8,128)(2,1)S(1)}, f32[192,1536]{1,0:T(8,128)S(1)}, bf16[96,1536]{1,0:T(8,128)(2,1)S(1)}) custom-call(s32[1]{0:T(128)} %bitcast.place, bf16[96,2560]{1,0:T(8,128)(2,1)S(1)} %collective-permute-done.1.held, ...), custom_call_target="tpu_custom_call", output_to_operand_aliasing={{0}: (5, {}), {1}: (6, {}), {2}: (7, {})} | custom-call | tf_op jit(solution)/shard_map/join/pallas_call | solution.py:228
  33.9 0.0 collective-permute-done.5.arrived
  34.0 2.0 %activate.3 = (bf16[384,512]{1,0:T(8,128)(2,1)S(1)}, bf16[384,1024]{1,0:T(8,128)(2,1)S(1)}, bf16[192,640]{1,0:T(8,128)(2,1)S(1)}, bf16[192,640]{1,0:T(8,128)(2,1...) custom-call(s32[1]{0:T(128)} %bitcast.place, bf16[2560,1024]{1,0:T(8,128)(2,1)S(1)} %reorder.1.weights, ...), custom_call_target="tpu_custom_call" | custom-call | tf_op jit(solution)/shard_map/activate/pallas_call | solution.py:281
  36.0 0.3 collective-permute-start.6
  36.2 0.6 collective-permute-start.4
  36.8 0.0 collective-permute-start.9
  36.9 3.4 %collective-permute-done.7.arrived = bf16[96,1536]{1,0:T(8,128)(2,1)S(1)} collective-permute-done((bf16[96,1536]{1,0:T(8,128)(2,1)S(1)}, bf16[96,1536]{1,0:T(8,128)(2,1)S(1)}, u32[]{:S(2)}, u32[]{:S(2)}) %collective-permute-start.7) | collective-permute-done | bytes 294944 | tf_op jit(solution)/shard_map/ppermute | solution.py:35
  40.2 1.7 %activate.4 = (bf16[384,512]{1,0:T(8,128)(2,1)S(1)}, bf16[384,1024]{1,0:T(8,128)(2,1)S(1)}, bf16[192,640]{1,0:T(8,128)(2,1)S(1)}, bf16[192,640]{1,0:T(8,128)(2,1...) custom-call(s32[1]{0:T(128)} %bitcast.place, ...), custom_call_target="tpu_custom_call", output_to_operand_aliasing={{0}: (4, {}), {1}: (5, {})} | custom-call | tf_op jit(solution)/shard_map/activate/pallas_call | solution.py:281
  42.0 0.0 collective-permute-done.6
  42.0 1.5 %collective-permute-start.10 = (bf16[192,640]{1,0:T(8,128)(2,1)S(1)}, bf16[192,640]{1,0:T(8,128)(2,1)S(1)}, u32[]{:S(2)}, u32[]{:S(2)}) collective-permute-start(bf16[192,640]{1,0:T(8,128)(2,1)S(1)} %add_convert_fusion.1), channel_id=1, source_target_pairs={{0,4},{2,6},{4,0},{6,2},{8,12},{10,14},{12,8},{14,10},{16,20},{18,... | collective-permute-start | bytes 737288 | tf_op jit(solution)/shard_map/ppermute | solution.py:35
  43.5 2.7 %collective-permute-done.4.arrived = bf16[96,1536]{1,0:T(8,128)(2,1)S(1)} collective-permute-done((bf16[96,1536]{1,0:T(8,128)(2,1)S(1)}, bf16[96,1536]{1,0:T(8,128)(2,1)S(1)}, u32[]{:S(2)}, u32[]{:S(2)}) %collective-permute-start.4) | collective-permute-done | bytes 294944 | tf_op jit(solution)/shard_map/ppermute | solution.py:35
  46.2 1.7 %activate.5 = (bf16[384,512]{1,0:T(8,128)(2,1)S(1)}, bf16[384,1024]{1,0:T(8,128)(2,1)S(1)}, bf16[192,640]{1,0:T(8,128)(2,1)S(1)}, bf16[192,640]{1,0:T(8,128)(2,1...) custom-call(s32[1]{0:T(128)} %bitcast.place, ...), custom_call_target="tpu_custom_call", output_to_operand_aliasing={{0}: (4, {}), {1}: (5, {}), {2}: (6, {}), {3}: (7, {}), {4}... | custom-call | tf_op jit(solution)/shard_map/activate/pallas_call | solution.py:281
  47.9 0.1 collective-permute-start.8
  48.0 0.0 collective-permute-done.9
  48.0 0.5 collective-permute-start.13
  48.6 0.7 collective-permute-done.10
  49.3 1.5 %collective-permute-start.11 = (bf16[192,320]{1,0:T(8,128)(2,1)S(1)}, bf16[192,320]{1,0:T(8,128)(2,1)S(1)}, u32[]{:S(2)}, u32[]{:S(2)}) collective-permute-start(bf16[192,320]{1,0:T(8,128)(2,1)S(1)} %fusion.5), channel_id=1, source_target_pairs={{0,8},{2,10},{4,12},{6,14},{8,0},{10,2},{12,4},{14,6},{16,24},{18,... | collective-permute-start | bytes 368648 | tf_op jit(solution)/shard_map/ppermute | solution.py:35
  50.8 0.0 collective-permute-done.8
  50.9 1.6 %collective-permute-start.14 = (bf16[192,640]{1,0:T(8,128)(2,1)S(1)}, bf16[192,640]{1,0:T(8,128)(2,1)S(1)}, u32[]{:S(2)}, u32[]{:S(2)}) collective-permute-start(bf16[192,640]{1,0:T(8,128)(2,1)S(1)} %add_convert_fusion), channel_id=1, source_target_pairs={{0,4},{2,6},{4,0},{6,2},{8,12},{10,14},{12,8},{14,10},{16,20},{18,... | collective-permute-start | bytes 737288 | tf_op jit(solution)/shard_map/ppermute | solution.py:35
  52.5 0.0 collective-permute-done.13
  52.5 2.0 %collective-permute-done.11 = bf16[192,320]{1,0:T(8,128)(2,1)S(1)} collective-permute-done((bf16[192,320]{1,0:T(8,128)(2,1)S(1)}, bf16[192,320]{1,0:T(8,128)(2,1)S(1)}, u32[]{:S(2)}, u32[]{:S(2)}) %collective-permute-start.11) | collective-permute-done | bytes 122912 | tf_op jit(solution)/shard_map/ppermute | solution.py:35
  54.5 0.2 fusion.7
  54.7 1.5 %collective-permute-start.12 = (bf16[192,320]{1,0:T(8,128)(2,1)S(1)}, bf16[192,320]{1,0:T(8,128)(2,1)S(1)}, u32[]{:S(2)}, u32[]{:S(2)}) collective-permute-start(bf16[192,320]{1,0:T(8,128)(2,1)S(1)} %fusion.7), channel_id=1, source_target_pairs={{0,1},{1,0},{2,3},{3,2},{4,5},{5,4},{6,7},{7,6},{8,9},{9,8},{10,11... | collective-permute-start | bytes 368648 | tf_op jit(solution)/shard_map/ppermute | solution.py:35
  56.2 5.4 %weight_grads.1 = (bf16[2560,512]{1,0:T(8,128)(2,1)}, bf16[2560,512]{1,0:T(8,128)(2,1)}, bf16[512,2560]{1,0:T(8,128)(2,1)}) custom-call(bf16[384,2560]{1,0:T(8,128)(2,1)S(1)} %get-tuple-element.80.tokens, bf16[384,2560]{1,0:T(8,128)(2,1)S(1)} %get-tuple-element.81.cot, bf16[384,512]{1,0:T(8,128)(2,1)S(1)} %get-tuple-element.84.act, ...), custom_call_target="tpu_custom_call" | custom-call | flops 3019898880 | tf_op jit(solution)/shard_map/weight_grads/pallas_call | solution.py:327
  61.6 0.0 collective-permute-done.14
  61.6 1.6 %collective-permute-start.15 = (bf16[192,320]{1,0:T(8,128)(2,1)S(1)}, bf16[192,320]{1,0:T(8,128)(2,1)S(1)}, u32[]{:S(2)}, u32[]{:S(2)}) collective-permute-start(bf16[192,320]{1,0:T(8,128)(2,1)S(1)} %fusion.3), channel_id=1, source_target_pairs={{0,8},{2,10},{4,12},{6,14},{8,0},{10,2},{12,4},{14,6},{16,24},{18,... | collective-permute-start | bytes 368648 | tf_op jit(solution)/shard_map/ppermute | solution.py:35
  63.3 0.0 collective-permute-done.12
  63.3 3.6 %collective-permute-done.15 = bf16[192,320]{1,0:T(8,128)(2,1)S(1)} collective-permute-done((bf16[192,320]{1,0:T(8,128)(2,1)S(1)}, bf16[192,320]{1,0:T(8,128)(2,1)S(1)}, u32[]{:S(2)}, u32[]{:S(2)}) %collective-permute-start.15) | collective-permute-done | bytes 122912 | tf_op jit(solution)/shard_map/ppermute | solution.py:35
  66.8 0.2 fusion.2
  67.0 3.1 %collective-permute-start.16 = (bf16[192,320]{1,0:T(8,128)(2,1)S(1)}, bf16[192,320]{1,0:T(8,128)(2,1)S(1)}, u32[]{:S(2)}, u32[]{:S(2)}) collective-permute-start(bf16[192,320]{1,0:T(8,128)(2,1)S(1)} %fusion.2), channel_id=1, source_target_pairs={{0,16},{2,18},{4,20},{6,22},{8,24},{10,26},{12,28},{14,30},{16,0},... | collective-permute-start | bytes 368648 | tf_op jit(solution)/shard_map/ppermute | solution.py:35
  70.2 4.7 %collective-permute-done.16 = bf16[192,320]{1,0:T(8,128)(2,1)S(1)} collective-permute-done((bf16[192,320]{1,0:T(8,128)(2,1)S(1)}, bf16[192,320]{1,0:T(8,128)(2,1)S(1)}, u32[]{:S(2)}, u32[]{:S(2)}) %collective-permute-start.16) | collective-permute-done | bytes 122912 | tf_op jit(solution)/shard_map/ppermute | solution.py:35
  74.9 0.9 %fusion.1 = bf16[192,320]{1,0:T(8,128)(2,1)} fusion(bf16[192,320]{1,0:T(8,128)(2,1)S(1)} %collective-permute-done.12, bf16[192,320]{1,0:T(8,128)(2,1)S(1)} %collective-permute-done.16, pred[]{:T(512)S(6)} %eq.6, bf16[192,320]{1,0:T(8,128)(2,1)S(1)} %collective-permute-done.15, bf16[192,640]{1,0:T(8,128)(2,1)S(1)} %collective-permute-done.14, ...), kind=kLoop, calls=%fused_computation.7 | loop fusion | flops 552960 | bytes 860161 | tf_op jit(solution)/shard_map/convert_element_type | solution.py:443
  (8 shorter events, 0.3 us)
Async XLA Ops:
  0.6 4.2 %copy-start = (f32[512,40]{0,1:T(8,128)S(1)}, f32[512,40]{0,1:T(8,128)}, u32[]{:S(2)}) copy-start(f32[512,40]{0,1:T(8,128)} %param.15) | copy-start | bytes 245764
  0.7 4.6 %copy-start.1 = (f32[40,512]{1,0:T(8,128)S(1)}, f32[40,512]{1,0:T(8,128)}, u32[]{:S(2)}) copy-start(f32[40,512]{1,0:T(8,128)} %gate_scales.1) | copy-start | bytes 245764
  0.7 4.6 %copy-start.2 = (f32[40,512]{1,0:T(8,128)S(1)}, f32[40,512]{1,0:T(8,128)}, u32[]{:S(2)}) copy-start(f32[40,512]{1,0:T(8,128)} %up_scales.1) | copy-start | bytes 245764
  1.8 14.3 %collective-permute-start = (bf16[96,2560]{1,0:T(8,128)(2,1)S(1)}, bf16[96,2560]{1,0:T(8,128)(2,1)S(1)}, u32[]{:S(2)}, u32[]{:S(2)}) collective-permute-start(bf16[96,2560]{1,0:T(8,128)(2,1)S(1)} %fetch.1), channel_id=1, source_target_pairs={{0,1},{1,0},{2,3},{3,2},{4,5},{5,4},{6,7},{7,6},{8,9},{9,8},{10,11... | collective-permute-start | bytes 1474568 | tf_op jit(solution)/shard_map/ppermute | solution.py:35
  16.0 12.4 %collective-permute-start.1 = (bf16[96,2560]{1,0:T(8,128)(2,1)S(1)}, bf16[96,2560]{1,0:T(8,128)(2,1)S(1)}, u32[]{:S(2)}, u32[]{:S(2)}) collective-permute-start(bf16[96,2560]{1,0:T(8,128)(2,1)S(1)} %collective-permute-done.held), channel_id=1, source_target_pairs={{0,8},{2,10},{4,12},{6,14},{8,0},{10,2},{12,4},{14,6},{16,24},{18,... | collective-permute-start | bytes 1474568 | tf_op jit(solution)/shard_map/ppermute | solution.py:35
  17.8 16.1 %collective-permute-start.5 = (bf16[192,1536]{1,0:T(8,128)(2,1)S(1)}, bf16[192,1536]{1,0:T(8,128)(2,1)S(1)}, u32[]{:S(2)}, u32[]{:S(2)}) collective-permute-start(bf16[192,1536]{1,0:T(8,128)(2,1)S(1)} %get-tuple-element.49), channel_id=1, source_target_pairs={{0,1},{1,0},{2,3},{3,2},{4,5},{5,4},{6,7},{7,6},{8,9},{9,8},{10,11... | collective-permute-start | bytes 1769480 | tf_op jit(solution)/shard_map/ppermute | solution.py:35
  19.4 9.1 %collective-permute-start.3 = (bf16[96,2560]{1,0:T(8,128)(2,1)S(1)}, bf16[96,2560]{1,0:T(8,128)(2,1)S(1)}, u32[]{:S(2)}, u32[]{:S(2)}) collective-permute-start(bf16[96,2560]{1,0:T(8,128)(2,1)S(1)} %collective-permute-done.held), channel_id=1, source_target_pairs={{0,2},{2,0},{4,6},{6,4},{8,10},{10,8},{12,14},{14,12},{16,18},{18,... | collective-permute-start | bytes 1474568 | tf_op jit(solution)/shard_map/ppermute | solution.py:35
  28.5 3.4 %collective-permute-start.2 = (bf16[96,2560]{1,0:T(8,128)(2,1)S(1)}, bf16[96,2560]{1,0:T(8,128)(2,1)S(1)}, u32[]{:S(2)}, u32[]{:S(2)}) collective-permute-start(bf16[96,2560]{1,0:T(8,128)(2,1)S(1)} %collective-permute-done.1.held), channel_id=1, source_target_pairs={{0,2},{2,0},{4,6},{6,4},{8,10},{10,8},{12,14},{14,12},{16,18},{18,... | collective-permute-start | bytes 1474568 | tf_op jit(solution)/shard_map/ppermute | solution.py:35
  30.4 9.9 %collective-permute-start.7 = (bf16[96,1536]{1,0:T(8,128)(2,1)S(1)}, bf16[96,1536]{1,0:T(8,128)(2,1)S(1)}, u32[]{:S(2)}, u32[]{:S(2)}) collective-permute-start(bf16[96,1536]{1,0:T(8,128)(2,1)S(1)} %get-tuple-element.63), channel_id=1, source_target_pairs={{0,1},{1,0},{2,3},{3,2},{4,5},{5,4},{6,7},{7,6},{8,9},{9,8},{10,11... | collective-permute-start | bytes 884744 | tf_op jit(solution)/shard_map/ppermute | solution.py:35
  36.0 6.0 %collective-permute-start.6 = (bf16[192,640]{1,0:T(8,128)(2,1)S(1)}, bf16[192,640]{1,0:T(8,128)(2,1)S(1)}, u32[]{:S(2)}, u32[]{:S(2)}) collective-permute-start(bf16[192,640]{1,0:T(8,128)(2,1)S(1)} %get-tuple-element.61), channel_id=1, source_target_pairs={{0,2},{2,0},{4,6},{6,4},{8,10},{10,8},{12,14},{14,12},{16,18},{18,... | collective-permute-start | bytes 737288 | tf_op jit(solution)/shard_map/ppermute | solution.py:35
  36.2 9.9 %collective-permute-start.4 = (bf16[96,1536]{1,0:T(8,128)(2,1)S(1)}, bf16[96,1536]{1,0:T(8,128)(2,1)S(1)}, u32[]{:S(2)}, u32[]{:S(2)}) collective-permute-start(bf16[96,1536]{1,0:T(8,128)(2,1)S(1)} %get-tuple-element.58), channel_id=1, source_target_pairs={{0,1},{1,0},{2,3},{3,2},{4,5},{5,4},{6,7},{7,6},{8,9},{9,8},{10,11... | collective-permute-start | bytes 884744 | tf_op jit(solution)/shard_map/ppermute | solution.py:35
  36.8 11.1 %collective-permute-start.9 = (bf16[192,640]{1,0:T(8,128)(2,1)S(1)}, bf16[192,640]{1,0:T(8,128)(2,1)S(1)}, u32[]{:S(2)}, u32[]{:S(2)}) collective-permute-start(bf16[192,640]{1,0:T(8,128)(2,1)S(1)} %get-tuple-element.76), channel_id=1, source_target_pairs={{0,2},{2,0},{4,6},{6,4},{8,10},{10,8},{12,14},{14,12},{16,18},{18,... | collective-permute-start | bytes 737288 | tf_op jit(solution)/shard_map/ppermute | solution.py:35
  42.0 7.3 %collective-permute-start.10 = (bf16[192,640]{1,0:T(8,128)(2,1)S(1)}, bf16[192,640]{1,0:T(8,128)(2,1)S(1)}, u32[]{:S(2)}, u32[]{:S(2)}) collective-permute-start(bf16[192,640]{1,0:T(8,128)(2,1)S(1)} %add_convert_fusion.1), channel_id=1, source_target_pairs={{0,4},{2,6},{4,0},{6,2},{8,12},{10,14},{12,8},{14,10},{16,20},{18,... | collective-permute-start | bytes 737288 | tf_op jit(solution)/shard_map/ppermute | solution.py:35
  47.9 3.0 %collective-permute-start.8 = (bf16[192,640]{1,0:T(8,128)(2,1)S(1)}, bf16[192,640]{1,0:T(8,128)(2,1)S(1)}, u32[]{:S(2)}, u32[]{:S(2)}) collective-permute-start(bf16[192,640]{1,0:T(8,128)(2,1)S(1)} %get-tuple-element.74), channel_id=1, source_target_pairs={{0,2},{2,0},{4,6},{6,4},{8,10},{10,8},{12,14},{14,12},{16,18},{18,... | collective-permute-start | bytes 737288 | tf_op jit(solution)/shard_map/ppermute | solution.py:35
  48.0 4.4 %collective-permute-start.13 = (bf16[192,640]{1,0:T(8,128)(2,1)S(1)}, bf16[192,640]{1,0:T(8,128)(2,1)S(1)}, u32[]{:S(2)}, u32[]{:S(2)}) collective-permute-start(bf16[192,640]{1,0:T(8,128)(2,1)S(1)} %get-tuple-element.79), channel_id=1, source_target_pairs={{0,2},{2,0},{4,6},{6,4},{8,10},{10,8},{12,14},{14,12},{16,18},{18,... | collective-permute-start | bytes 737288 | tf_op jit(solution)/shard_map/ppermute | solution.py:35
  49.3 5.2 %collective-permute-start.11 = (bf16[192,320]{1,0:T(8,128)(2,1)S(1)}, bf16[192,320]{1,0:T(8,128)(2,1)S(1)}, u32[]{:S(2)}, u32[]{:S(2)}) collective-permute-start(bf16[192,320]{1,0:T(8,128)(2,1)S(1)} %fusion.5), channel_id=1, source_target_pairs={{0,8},{2,10},{4,12},{6,14},{8,0},{10,2},{12,4},{14,6},{16,24},{18,... | collective-permute-start | bytes 368648 | tf_op jit(solution)/shard_map/ppermute | solution.py:35
  50.9 10.7 %collective-permute-start.14 = (bf16[192,640]{1,0:T(8,128)(2,1)S(1)}, bf16[192,640]{1,0:T(8,128)(2,1)S(1)}, u32[]{:S(2)}, u32[]{:S(2)}) collective-permute-start(bf16[192,640]{1,0:T(8,128)(2,1)S(1)} %add_convert_fusion), channel_id=1, source_target_pairs={{0,4},{2,6},{4,0},{6,2},{8,12},{10,14},{12,8},{14,10},{16,20},{18,... | collective-permute-start | bytes 737288 | tf_op jit(solution)/shard_map/ppermute | solution.py:35
  54.7 8.6 %collective-permute-start.12 = (bf16[192,320]{1,0:T(8,128)(2,1)S(1)}, bf16[192,320]{1,0:T(8,128)(2,1)S(1)}, u32[]{:S(2)}, u32[]{:S(2)}) collective-permute-start(bf16[192,320]{1,0:T(8,128)(2,1)S(1)} %fusion.7), channel_id=1, source_target_pairs={{0,1},{1,0},{2,3},{3,2},{4,5},{5,4},{6,7},{7,6},{8,9},{9,8},{10,11... | collective-permute-start | bytes 368648 | tf_op jit(solution)/shard_map/ppermute | solution.py:35
  61.6 5.2 %collective-permute-start.15 = (bf16[192,320]{1,0:T(8,128)(2,1)S(1)}, bf16[192,320]{1,0:T(8,128)(2,1)S(1)}, u32[]{:S(2)}, u32[]{:S(2)}) collective-permute-start(bf16[192,320]{1,0:T(8,128)(2,1)S(1)} %fusion.3), channel_id=1, source_target_pairs={{0,8},{2,10},{4,12},{6,14},{8,0},{10,2},{12,4},{14,6},{16,24},{18,... | collective-permute-start | bytes 368648 | tf_op jit(solution)/shard_map/ppermute | solution.py:35
  67.0 7.8 %collective-permute-start.16 = (bf16[192,320]{1,0:T(8,128)(2,1)S(1)}, bf16[192,320]{1,0:T(8,128)(2,1)S(1)}, u32[]{:S(2)}, u32[]{:S(2)}) collective-permute-start(bf16[192,320]{1,0:T(8,128)(2,1)S(1)} %fusion.2), channel_id=1, source_target_pairs={{0,16},{2,18},{4,20},{6,22},{8,24},{10,26},{12,28},{14,30},{16,0},... | collective-permute-start | bytes 368648 | tf_op jit(solution)/shard_map/ppermute | solution.py:35

commit v2 on v1

--- a/solution.py
+++ b/solution.py
@@ -242,11 +242,11 @@
     )(place, *(in_vmem(a) for a in (held, given, w_in, w_down, *before)))
 
 
-def activate_kernel(group, turns, count, place, weights, total, arrived, *refs):
-    act, d_inner, *targets = refs[-6:]
+def activate_kernel(group, turns, count, block, place, weights, total, arrived, *refs):
+    pairs = weights.shape[0] // (2 * block)
+    act, d_inner, *targets = refs[-2 - pairs :]
     units, half, chunk = act.shape[1], count // 2, 32
     side = side_of(place[0])
-    width = targets[0].shape[1]
 
     def rows(first, length):
         return pl.ds(pl.multiple_of(first, 16), length)
@@ -266,30 +266,40 @@
             d_inner[kept, :units] = (d_act * upper * sig * (1.0 + gate * (1.0 - sig))).astype(d_inner.dtype)
             d_inner[kept, units:] = (d_act * silu_val).astype(d_inner.dtype)
     if len(turns) == 2:
-        mine, out = rows(group * count, count), rows(0, count)
+        mine = rows(group * count, count)
     else:
-        mine, out = rows(group * count + natural, half), rows(natural, half)
-    for i, target in enumerate(targets):
-        product = against(d_inner[mine, :], weights[i * width : (i + 1) * width, :])
-        target[out, :] = product.astype(target.dtype)
-
-
-def activate(group, groups, turns, place, total, arrived, weights, before):
-    units = weights.shape[1] // 2
+        mine = rows(group * count + natural, half)
+
+    def store(target, product, h):
+        for i in (0, 1):
+            lanes = slice((2 * i + h) * block, (2 * i + h + 1) * block)
+            target[:, lanes] = product[:, i * block : (i + 1) * block].astype(target.dtype)
+
+    for p, target in enumerate(targets):
+        product = against(d_inner[mine, :], weights[2 * p * block : 2 * (p + 1) * block, :])
+        if len(turns) == 2:
+            store(target, product[:half], 0)
+            store(target, product[half:], 1)
+        else:
+            for h in (0, 1):
+                pl.when(natural == h * half)(functools.partial(store, target, product, h))
+
+
+def activate(group, groups, turns, place, total, arrived, weights, blocks, before):
+    units, pairs = weights.shape[1] // 2, blocks // 2
+    block = weights.shape[0] // blocks
     count = arrived.shape[0] * (3 - len(turns))
-    terms = count, weights.shape[0] // 4
-    return pl.pallas_call(
-        functools.partial(activate_kernel, group, turns, count),
+    terms = count // 2, 4 * block
+    return pl.pallas_call(
+        functools.partial(activate_kernel, group, turns, count, block),
         in_specs=[IN_SMEM] + [IN_VMEM] * (3 + len(before)),
-        out_specs=[IN_VMEM] * 6,
+        out_specs=[IN_VMEM] * (2 + pairs),
         out_shape=[
             pltpu.VMEM((groups * count, units), jnp.bfloat16),
             pltpu.VMEM((groups * count, 2 * units), jnp.bfloat16),
-            pltpu.VMEM(terms, jnp.bfloat16),
-            pltpu.VMEM(terms, jnp.bfloat16),
-            pltpu.VMEM(terms, jnp.float32),
-            pltpu.VMEM(terms, jnp.float32),
-        ],
+        ]
+        + [pltpu.VMEM(terms, jnp.bfloat16)] * (pairs // 2)
+        + [pltpu.VMEM(terms, jnp.float32)] * (pairs // 2),
         input_output_aliases={4 + i: i for i in range(len(before))},
         compiler_params=grant(12),
         cost_estimate=cost(0),
@@ -297,44 +307,36 @@
     )(place, *(in_vmem(a) for a in (weights, total, arrived, *before)))
 
 
-def grads_kernel(tokens, cot, act, d_inner, gate_grad, up_grad, down_grad, gate_held, up_held, down_held, sems):
-    rows, units = gate_grad.shape
+def grads_kernel(first, by_rows, left, right, target, held, sems):
+    wide = left if by_rows else right
     copies = []
-
-    def send(held, target, part, i):
-        copies.append(pltpu.make_async_copy(held.at[part], target.at[part], sems.at[i]))
+    for step in range(wide.shape[1] // STEP):
+        part = slice(step * STEP, (step + 1) * STEP)
+        if by_rows:
+            index = (part, slice(None))
+            held[index] = contract(left[:, part], right[:, first : first + target.shape[1]]).astype(held.dtype)
+        else:
+            index = (slice(None), part)
+            held[index] = contract(left[...], right[:, part]).astype(held.dtype)
+        copies.append(pltpu.make_async_copy(held.at[index], target.at[index], sems.at[step]))
         copies[-1].start()
-
-    steps = rows // STEP
-    for step in range(steps):
-        part = slice(step * STEP, (step + 1) * STEP)
-        both = contract(tokens[:, part], d_inner[...])
-        gate_held[part, :] = both[:, :units].astype(gate_held.dtype)
-        send(gate_held, gate_grad, (part, slice(None)), step)
-        up_held[part, :] = both[:, units:].astype(up_held.dtype)
-        send(up_held, up_grad, (part, slice(None)), steps + step)
-    for step in range(steps):
-        part = slice(step * STEP, (step + 1) * STEP)
-        down_held[:, part] = contract(act[...], cot[:, part]).astype(down_held.dtype)
-        send(down_held, down_grad, (slice(None), part), 2 * steps + step)
     for copy in copies:
         copy.wait()
 
 
-def weight_grads(tokens, cot, act, d_inner):
-    rows, units = tokens.shape[1], act.shape[1]
-    shapes = [(rows, units), (rows, units), (units, rows)]
-    return pl.pallas_call(
-        grads_kernel,
-        in_specs=[IN_VMEM] * 4,
-        out_specs=[IN_HBM] * 3,
-        out_shape=[pltpu.HBM(shape, jnp.bfloat16) for shape in shapes],
-        scratch_shapes=[pltpu.VMEM(shape, jnp.bfloat16) for shape in shapes]
-        + [pltpu.SemaphoreType.DMA((3 * (rows // STEP),))],
-        compiler_params=grant(20),
-        cost_estimate=cost(6 * tokens.shape[0] * rows * units),
-        name="weight_grads",
-    )(*(in_vmem(a) for a in (tokens, cot, act, d_inner)))
+def weight_grad(left, right, first, units, by_rows):
+    rows = (left if by_rows else right).shape[1]
+    shape = (rows, units) if by_rows else (units, rows)
+    return pl.pallas_call(
+        functools.partial(grads_kernel, first, by_rows),
+        in_specs=[IN_VMEM] * 2,
+        out_specs=IN_HBM,
+        out_shape=pltpu.HBM(shape, jnp.bfloat16),
+        scratch_shapes=[pltpu.VMEM(shape, jnp.bfloat16), pltpu.SemaphoreType.DMA((rows // STEP,))],
+        compiler_params=grant(10),
+        cost_estimate=cost(2 * left.shape[0] * rows * units),
+        name="weight_grad",
+    )(in_vmem(left), in_vmem(right))
 
 
 def after(value, *earlier):
@@ -349,6 +351,7 @@
     count = tokens.shape[0]
     owners = width // nodes
     bits = owners.bit_length() - 1
+    block = rows // owners
 
     side, half = side_of(place), count // 2
 
@@ -394,41 +397,54 @@
         short = own_short if k == mask else sums[k ^ mask].astype(jnp.bfloat16)
         arrived.append(swap(short, "node", nodes, mask))
 
-    def pair(parts):
-        got = [swap(part, "dp", width, 1).astype(jnp.float32) for part in parts[:2]]
-        return (parts[2] + got[0]).astype(jnp.bfloat16), parts[3] + got[1]
-
-    def cut(terms, got):
-        edge = terms.shape[1] // 2
-        sending = (terms[:, :edge] + got[:, :edge].astype(jnp.float32)).astype(jnp.bfloat16)
-        return sending, terms[:, edge:] + got[:, edge:].astype(jnp.float32)
-
-    blocks, before = [None] * nodes, []
+    peers = owners // 2
+
+    def split(parts, *earlier):
+        size = len(parts) // 2
+        got = [swap(part, "dp", width, 1) for part in parts[:size]]
+        if earlier:
+            got = after(got, *earlier)
+        sending = []
+        for r in range(peers):
+            lanes = slice(r % 2 * 2 * block, (r % 2 + 1) * 2 * block)
+            both = parts[size + r // 2][:, lanes] + got[r // 2][:, lanes].astype(jnp.float32)
+            if r < peers - 1:
+                mask = sum(1 << bit for bit in range(1, bits) if (r >> (bits - 1 - bit)) & 1 == 0)
+                sending.append((mask, both.astype(jnp.bfloat16)))
+        return sending, both
+
+    def exchange(sending):
+        return [swap(value, "dp", width, mask) for mask, value in sending]
+
+    def add(mine, got):
+        for value in got:
+            mine += value.astype(jnp.float32)
+        return mine
+
+    blocks, before, others = [None] * nodes, [], [None] * nodes
     for k in reversed(range(1, nodes)):
-        *before, a, b, c, d = activate(k, nodes, (0, 1), place_ref, sums[k], arrived[k], w_relative, before)
-        x_sent, terms = pair((a, b, c, d))
-        last = x_sent
-        got = swap(x_sent, "dp", width, 2)
-        for bit in range(2, bits):
-            last, terms = cut(terms, got)
-            got = swap(last, "dp", width, 1 << bit)
-        blocks[k] = terms, got
-
-    before = activate(0, nodes, (0,), place_ref, sums[0], near_far[0], w_relative, before)
-    act, d_inner, *parts = activate(0, nodes, (1,), place_ref, sums[0], after(near_far[1], x_sent), w_relative, before)
-    sending, terms = pair(parts)
-    got = swap(sending, "dp", width, 2)
+        act, d_inner, *others[k] = activate(
+            k, nodes, (0, 1), place_ref, sums[k], arrived[k], w_relative, owners, before
+        )
+        before = [act, d_inner]
+    before = activate(0, nodes, (0,), place_ref, sums[0], near_far[0], w_relative, owners, before)
+    last = []
     for k in range(1, nodes):
-        block = (blocks[k][0] + blocks[k][1].astype(jnp.float32)).astype(jnp.bfloat16)
-        act, sending, block = lax.optimization_barrier((act, sending, block))
-        blocks[k] = swap(block, "node", nodes, k).astype(jnp.float32)
-    act, d_inner = after((act, d_inner), sending)
-    gate_grad, up_grad, down_grad = weight_grads(all_tokens, all_cots, act, d_inner)
-    got = after(got, gate_grad, up_grad, down_grad)
-    for bit in range(2, bits):
-        sending, terms = cut(terms, got)
-        got = swap(sending, "dp", width, 1 << bit)
-    blocks[0] = terms + got.astype(jnp.float32)
+        sending, mine = split(others[k], before)
+        last.append([value for _, value in sending])
+        blocks[k] = mine, exchange(sending)
+    act, d_inner, *parts = activate(
+        0, nodes, (1,), place_ref, sums[0], after(near_far[1], last), w_relative, owners, before
+    )
+    sending, mine = split(parts)
+    got = exchange(sending)
+    sent = [value for _, value in sending]
+    for k in range(1, nodes):
+        value = add(*blocks[k]).astype(jnp.bfloat16)
+        act, sent, value = lax.optimization_barrier((act, sent, value))
+        blocks[k] = swap(value, "node", nodes, k).astype(jnp.float32)
+    down_grad = weight_grad(after(act, sent), all_cots, 0, units, False)
+    blocks[0] = add(mine, after(got, down_grad))
     high = place // owners
 
     def block_for(owner):
@@ -437,10 +453,17 @@
             chosen = jnp.where((owner ^ node) == k, blocks[k], chosen)
         return chosen
 
+    sent = [block_for(high ^ j).astype(jnp.bfloat16) for j in range(1, nodes)]
+    d_inner = after(d_inner, sent)
+    gate_grad = weight_grad(all_tokens, d_inner, 0, units, True)
+    up_grad = weight_grad(all_tokens, d_inner, units, units, True)
     token_grad = block_for(high)
     for j in range(1, nodes):
-        token_grad += swap(block_for(high ^ j).astype(jnp.bfloat16), "dp", width, j * owners).astype(jnp.float32)
-    return token_grad.astype(jnp.bfloat16), gate_grad, up_grad, down_grad
+        arrived = after(swap(sent[j - 1], "dp", width, j * owners), gate_grad, up_grad)
+        token_grad += arrived.astype(jnp.float32)
+    token_grad = token_grad.astype(jnp.bfloat16)
+    token_grad = jnp.concatenate([token_grad[:, :block], token_grad[:, block:]])
+    return token_grad, gate_grad, up_grad, down_grad
 
 
 def solution(mesh):

time: 75.9 us -> 76.9 us (1.013)
  waiting for transfers between devices: 30.2 us -> 18.9 us
  Pallas kernels: 22.6 us -> 28.6 us
  other arithmetic: 1.46 us -> 5.3 us
  local copies, waits for them, and re-layouts: 0.39 us -> 2.04 us
    ppermute x17 -> x19, waiting for transfers between devices: 30.2 us -> 18.9 us  [swap(): return lax.ppermute(value, axis, flipped(size, mask))]
    pallas_call x4 -> x6, Pallas kernels: 10.8 us -> 15.2 us  [the longest x3 7.76 us: activate(): pl.pallas_call(functools.partial(activate_kernel, group, turns, count, bl...]
    convert_element_type x7, other arithmetic: 1.37 us -> 4.62 us  [the longest x4 1.49 us: split(): sending.append((mask, both.astype(jnp.bfloat16)))]
    unnamed x6 -> x14, local copies, waits for them, and re-layouts: 0.02 us -> 1.58 us
    pallas_call x2, Pallas kernels: 3.97 us -> 4.81 us  [join(): pl.pallas_call(functools.partial(join_kernel, group, far), in_specs=[IN_S...]
    pallas_call x1, Pallas kernels: 1.1 us -> 1.89 us  [fetch(): pl.pallas_call(functools.partial(fetch_kernel, mask), in_specs=[IN_SMEM,...]
    ppermute x17 -> x19, starting transfers between devices: 20.2 us -> 20.9 us  [swap(): return lax.ppermute(value, axis, flipped(size, mask))]
  transfers between devices with their start and end apart: 17 -> 19, of which waited for: 8 -> 4; matrix products, arithmetic and copies ran while one was open for 1% -> 3% of each run, Pallas kernels for 28% -> 35%
where the time goes in v2:
time: 76.9 us; the launch traced here: 76.6 us
  Pallas kernels  28.6 us (37%)
  starting transfers between devices  20.9 us (27%)
  waiting for transfers between devices  18.9 us (25%)
  other arithmetic  5.3 us (7%)
  local copies, waits for them, and re-layouts  2.04 us (3%)
  between operations  0.92 us (1%)
    ppermute x19, starting transfers between devices, swap(): return lax.ppermute(value, axis, flipped(size, mask))  20.9 us
    ppermute x19, waiting for transfers between devices, swap(): return lax.ppermute(value, axis, flipped(size, mask))  18.9 us
    pallas_call x3, Pallas kernels, activate(): pl.pallas_call(functools.partial(activate_kernel, group, turns, count, bl...  7.76 us
    pallas_call x3, Pallas kernels, weight_grad(): pl.pallas_call(functools.partial(grads_kernel, first, by_rows), in_specs=...  7.41 us
    pallas_call x1, Pallas kernels, prepare(): pl.pallas_call(prepare_kernel, in_specs=[IN_SMEM] + [IN_HBM] * 5 + [IN_VM...  6.4 us
    pallas_call x2, Pallas kernels, join(): pl.pallas_call(functools.partial(join_kernel, group, far), in_specs=[IN_S...  4.81 us
    pallas_call x1, Pallas kernels, fetch(): pl.pallas_call(functools.partial(fetch_kernel, mask), in_specs=[IN_SMEM,...  1.89 us
    unnamed x14, local copies, waits for them, and re-layouts  1.58 us
  transfers between devices with their start and end apart: 19, of which 4 were waited for; matrix products, arithmetic and copies ran while one was open for 3% of the time, Pallas kernels for 35%

profile of v2, /device:TPU:0, one launch (start us, length us, event | category | flops | bytes accessed | tf_op | source)
XLA Modules:
  0.0 76.6 jit_solution(9918156046509112913)
XLA Ops:
  0.6 0.0 copy-start
  0.7 0.0 copy-start.5
  0.7 0.0 copy-start.6
  0.7 1.9 %fetch.1 = bf16[96,2560]{1,0:T(8,128)(2,1)} custom-call(s32[1]{0:T(128)} %bitcast.1.node, s32[1]{0:T(128)} %bitcast.place, bf16[192,5120]{1,0:T(8,128)(2,1)} %tokens.3, bf16[192,5120]{1,0:T(8,128)(2,1)} %cot.3), custom_call_target="tpu_custom_call" | custom-call | tf_op jit(solution)/shard_map/fetch/pallas_call | solution.py:78
  2.6 3.0 %collective-permute-start = (bf16[96,2560]{1,0:T(8,128)(2,1)}, bf16[96,2560]{1,0:T(8,128)(2,1)}, u32[]{:S(2)}, u32[]{:S(2)}) collective-permute-start(bf16[96,2560]{1,0:T(8,128)(2,1)} %fetch.1), channel_id=1, source_target_pairs={{0,1},{1,0},{2,3},{3,2},{4,5},{5,4},{6,7},{7,6},{8,9},{9,8},{10,11... | collective-permute-start | bytes 1474568 | tf_op jit(solution)/shard_map/ppermute | solution.py:35
  5.6 0.0 copy-done
  5.6 0.4 copy.25
  6.0 6.4 %prepare.1 = (bf16[384,2560]{1,0:T(8,128)(2,1)S(1)}, bf16[384,2560]{1,0:T(8,128)(2,1)S(1)}, bf16[2560,1024]{1,0:T(8,128)(2,1)S(1)}, bf16[512,2560]{1,0:T(8,128)(...) custom-call(s32[1]{0:T(128)} %bitcast.1.node, bf16[192,5120]{1,0:T(8,128)(2,1)} %tokens.3, ...), custom_call_target="tpu_custom_call" | custom-call | tf_op jit(solution)/shard_map/prepare/pallas_call | solution.py:143
  12.4 0.3 reorder.1.weights
  12.8 4.4 %collective-permute-done.held = bf16[96,2560]{1,0:T(8,128)(2,1)} collective-permute-done((bf16[96,2560]{1,0:T(8,128)(2,1)}, bf16[96,2560]{1,0:T(8,128)(2,1)}, u32[]{:S(2)}, u32[]{:S(2)}) %collective-permute-start) | collective-permute-done | bytes 491552 | tf_op jit(solution)/shard_map/ppermute | solution.py:35
  17.1 1.8 %collective-permute-start.1 = (bf16[96,2560]{1,0:T(8,128)(2,1)}, bf16[96,2560]{1,0:T(8,128)(2,1)S(1)}, u32[]{:S(2)}, u32[]{:S(2)}) collective-permute-start(bf16[96,2560]{1,0:T(8,128)(2,1)} %collective-permute-done.held), channel_id=1, source_target_pairs={{0,8},{2,10},{4,12},{6,14},{8,0},{10,2},{12,4},{14,6},{16,24},{18,... | collective-permute-start | bytes 1474568 | tf_op jit(solution)/shard_map/ppermute | solution.py:35
  18.9 1.5 %collective-permute-start.5 = (bf16[192,1536]{1,0:T(8,128)(2,1)S(1)}, bf16[192,1536]{1,0:T(8,128)(2,1)S(1)}, u32[]{:S(2)}, u32[]{:S(2)}) collective-permute-start(bf16[192,1536]{1,0:T(8,128)(2,1)S(1)} %get-tuple-element.50), channel_id=1, source_target_pairs={{0,1},{1,0},{2,3},{3,2},{4,5},{5,4},{6,7},{7,6},{8,9},{9,8},{10,11... | collective-permute-start | bytes 1769480 | tf_op jit(solution)/shard_map/ppermute | solution.py:35
  20.5 0.0 collective-permute-start.3
  20.5 9.3 %collective-permute-done.1.held = bf16[96,2560]{1,0:T(8,128)(2,1)S(1)} collective-permute-done((bf16[96,2560]{1,0:T(8,128)(2,1)}, bf16[96,2560]{1,0:T(8,128)(2,1)S(1)}, u32[]{:S(2)}, u32[]{:S(2)}) %collective-permute-start.1) | collective-permute-done | bytes 491552 | tf_op jit(solution)/shard_map/ppermute | solution.py:35
  29.8 0.0 collective-permute-start.2
  29.8 0.0 collective-permute-done.3.given
  29.8 2.9 %join.2 = (bf16[384,2560]{1,0:T(8,128)(2,1)S(1)}, bf16[384,2560]{1,0:T(8,128)(2,1)S(1)}, f32[192,1536]{1,0:T(8,128)S(1)}, bf16[96,1536]{1,0:T(8,128)(2,1)S(1)}) custom-call(s32[1]{0:T(128)} %bitcast.place, bf16[96,2560]{1,0:T(8,128)(2,1)} %collective-permute-done.held, ...), custom_call_target="tpu_custom_call", output_to_operand_aliasing={{0}: (5, {}), {1}: (6, {})} | custom-call | tf_op jit(solution)/shard_map/join/pallas_call | solution.py:228
  32.7 1.5 %collective-permute-start.8 = (bf16[96,1536]{1,0:T(8,128)(2,1)S(1)}, bf16[96,1536]{1,0:T(8,128)(2,1)S(1)}, u32[]{:S(2)}, u32[]{:S(2)}) collective-permute-start(bf16[96,1536]{1,0:T(8,128)(2,1)S(1)} %get-tuple-element.64), channel_id=1, source_target_pairs={{0,1},{1,0},{2,3},{3,2},{4,5},{5,4},{6,7},{7,6},{8,9},{9,8},{10,11... | collective-permute-start | bytes 884744 | tf_op jit(solution)/shard_map/ppermute | solution.py:35
  34.2 0.0 collective-permute-done.2.given
  34.2 1.9 %join.3 = (bf16[384,2560]{1,0:T(8,128)(2,1)S(1)}, bf16[384,2560]{1,0:T(8,128)(2,1)S(1)}, f32[192,1536]{1,0:T(8,128)S(1)}, bf16[96,1536]{1,0:T(8,128)(2,1)S(1)}) custom-call(s32[1]{0:T(128)} %bitcast.place, bf16[96,2560]{1,0:T(8,128)(2,1)S(1)} %collective-permute-done.1.held, ...), custom_call_target="tpu_custom_call", output_to_operand_aliasing={{0}: (5, {}), {1}: (6, {}), {2}: (7, {})} | custom-call | tf_op jit(solution)/shard_map/join/pallas_call | solution.py:228
  36.1 0.0 copy-start.1
  36.1 0.0 collective-permute-done.5.arrived
  36.1 2.1 %activate.3 = (bf16[384,512]{1,0:T(8,128)(2,1)S(1)}, bf16[384,1024]{1,0:T(8,128)(2,1)S(1)}, bf16[96,1280]{1,0:T(8,128)(2,1)S(1)}, bf16[96,1280]{1,0:T(8,128)(2,1...) custom-call(s32[1]{0:T(128)} %bitcast.place, bf16[2560,1024]{1,0:T(8,128)(2,1)S(1)} %reorder.1.weights, ...), custom_call_target="tpu_custom_call" | custom-call | tf_op jit(solution)/shard_map/activate/pallas_call | solution.py:293
  38.2 0.3 collective-permute-start.6
  38.5 0.3 collective-permute-start.7
  38.8 0.6 collective-permute-start.4
  39.4 3.2 %collective-permute-done.8.arrived = bf16[96,1536]{1,0:T(8,128)(2,1)S(1)} collective-permute-done((bf16[96,1536]{1,0:T(8,128)(2,1)S(1)}, bf16[96,1536]{1,0:T(8,128)(2,1)S(1)}, u32[]{:S(2)}, u32[]{:S(2)}) %collective-permute-start.8) | collective-permute-done | bytes 294944 | tf_op jit(solution)/shard_map/ppermute | solution.py:35
  42.6 2.7 %activate.4 = (bf16[384,512]{1,0:T(8,128)(2,1)S(1)}, bf16[384,1024]{1,0:T(8,128)(2,1)S(1)}, bf16[96,1280]{1,0:T(8,128)(2,1)S(1)}, bf16[96,1280]{1,0:T(8,128)(2,1...) custom-call(s32[1]{0:T(128)} %bitcast.place, ...), custom_call_target="tpu_custom_call", output_to_operand_aliasing={{0}: (4, {}), {1}: (5, {})} | custom-call | tf_op jit(solution)/shard_map/activate/pallas_call | solution.py:293
  45.3 0.0 collective-permute-done.6
  45.3 0.0 collective-permute-done.7
  45.4 1.6 %collective-permute-start.13 = (bf16[96,640]{1,0:T(8,128)(2,1)S(1)}, bf16[96,640]{1,0:T(8,128)(2,1)S(1)}, u32[]{:S(2)}, u32[]{:S(2)}) collective-permute-start(bf16[96,640]{1,0:T(8,128)(2,1)S(1)} %add_convert_fusion.4), channel_id=1, source_target_pairs={{0,8},{2,10},{4,12},{6,14},{8,0},{10,2},{12,4},{14,6},{16,24},{18,... | collective-permute-start | bytes 368648 | tf_op jit(solution)/shard_map/ppermute | solution.py:35
  47.0 1.6 %collective-permute-start.12 = (bf16[96,640]{1,0:T(8,128)(2,1)S(1)}, bf16[96,640]{1,0:T(8,128)(2,1)S(1)}, u32[]{:S(2)}, u32[]{:S(2)}) collective-permute-start(bf16[96,640]{1,0:T(8,128)(2,1)S(1)} %get-tuple-element.94), channel_id=1, source_target_pairs={{0,4},{2,6},{4,0},{6,2},{8,12},{10,14},{12,8},{14,10},{16,20},{18,... | collective-permute-start | bytes 368648 | tf_op jit(solution)/shard_map/ppermute | solution.py:35
  48.6 0.5 collective-permute-start.11
  49.0 0.0 collective-permute-done.4.arrived
  49.0 3.0 %activate.5 = (bf16[384,512]{1,0:T(8,128)(2,1)S(1)}, bf16[384,1024]{1,0:T(8,128)(2,1)S(1)}, bf16[96,1280]{1,0:T(8,128)(2,1)S(1)}, bf16[96,1280]{1,0:T(8,128)(2,1...) custom-call(s32[1]{0:T(128)} %bitcast.place, ...), custom_call_target="tpu_custom_call", output_to_operand_aliasing={{0}: (4, {}), {1}: (5, {}), {2}: (6, {}), {3}: (7, {}), {4}... | custom-call | tf_op jit(solution)/shard_map/activate/pallas_call | solution.py:293
  52.0 0.0 copy-start.3
  52.0 0.1 collective-permute-start.9
  52.1 0.5 collective-permute-start.10
  52.6 0.0 collective-permute-done.13
  52.6 2.0 %collective-permute-done.12 = bf16[96,640]{1,0:T(8,128)(2,1)S(1)} collective-permute-done((bf16[96,640]{1,0:T(8,128)(2,1)S(1)}, bf16[96,640]{1,0:T(8,128)(2,1)S(1)}, u32[]{:S(2)}, u32[]{:S(2)}) %collective-permute-start.12) | collective-permute-done | bytes 122912 | tf_op jit(solution)/shard_map/ppermute | solution.py:35
  54.6 0.0 collective-permute-done.11
  54.6 0.7 add_convert_fusion
  55.3 0.0 collective-permute-done.9
  55.3 0.7 add_convert_fusion.2
  56.1 0.9 %collective-permute-start.15 = (bf16[96,640]{1,0:T(8,128)(2,1)}, bf16[96,640]{1,0:T(8,128)(2,1)}, u32[]{:S(2)}, u32[]{:S(2)}) collective-permute-start(bf16[96,640]{1,0:T(8,128)(2,1)} %get-tuple-element.93), channel_id=1, source_target_pairs={{0,12},{2,14},{4,8},{6,10},{8,4},{10,6},{12,0},{14,2},{16,28},{18,... | collective-permute-start | bytes 368648 | tf_op jit(solution)/shard_map/ppermute | solution.py:35
  57.0 1.1 %collective-permute-start.16 = (bf16[96,640]{1,0:T(8,128)(2,1)}, bf16[96,640]{1,0:T(8,128)(2,1)}, u32[]{:S(2)}, u32[]{:S(2)}) collective-permute-start(bf16[96,640]{1,0:T(8,128)(2,1)} %get-tuple-element.92), channel_id=1, source_target_pairs={{0,4},{2,6},{4,0},{6,2},{8,12},{10,14},{12,8},{14,10},{16,20},{18,... | collective-permute-start | bytes 368648 | tf_op jit(solution)/shard_map/ppermute | solution.py:35
  58.1 0.0 collective-permute-done.10
  58.1 0.7 add_convert_fusion.1
  58.8 1.4 %collective-permute-start.17 = (bf16[96,640]{1,0:T(8,128)(2,1)}, bf16[96,640]{1,0:T(8,128)(2,1)}, u32[]{:S(2)}, u32[]{:S(2)}) collective-permute-start(bf16[96,640]{1,0:T(8,128)(2,1)} %add_convert_fusion.1), channel_id=1, source_target_pairs={{0,8},{2,10},{4,12},{6,14},{8,0},{10,2},{12,4},{14,6},{16,24},{18,... | collective-permute-start | bytes 368648 | tf_op jit(solution)/shard_map/ppermute | solution.py:35
  60.2 1.5 %collective-permute-start.14 = (bf16[96,640]{1,0:T(8,128)(2,1)}, bf16[96,640]{1,0:T(8,128)(2,1)}, u32[]{:S(2)}, u32[]{:S(2)}) collective-permute-start(bf16[96,640]{1,0:T(8,128)(2,1)} %add_convert_fusion), channel_id=1, source_target_pairs={{0,1},{1,0},{2,3},{3,2},{4,5},{5,4},{6,7},{7,6},{8,9},{9,8},{10,11... | collective-permute-start | bytes 368648 | tf_op jit(solution)/shard_map/ppermute | solution.py:35
  61.8 1.5 %copy-done.2 = bf16[384,2560]{1,0:T(8,128)(2,1)S(1)} copy-done((bf16[384,2560]{1,0:T(8,128)(2,1)S(1)}, bf16[384,2560]{1,0:T(8,128)(2,1)}, u32[]{:S(2)}) %copy-start.2) | copy-done | bytes 1966104
  63.3 2.6 %weight_grad.3 = bf16[512,2560]{1,0:T(8,128)(2,1)} custom-call(bf16[384,512]{1,0:T(8,128)(2,1)S(1)} %get-tuple-element.83.left, bf16[384,2560]{1,0:T(8,128)(2,1)S(1)} %copy-done.2), custom_call_target="tpu_custom_call" | custom-call | flops 1006632960 | tf_op jit(solution)/shard_map/weight_grad/pallas_call | solution.py:330
  65.9 0.0 collective-permute-done.15
  65.9 0.0 collective-permute-done.16
  65.9 0.0 collective-permute-done.17
  65.9 0.0 collective-permute-done.14
  65.9 1.2 %fusion.2 = bf16[96,640]{1,0:T(8,128)(2,1)S(1)} fusion(bf16[96,640]{1,0:T(8,128)(2,1)} %collective-permute-done.14, pred[]{:T(512)S(6)} %eq.7, bf16[96,640]{1,0:T(8,128)(2,1)} %collective-permute-done.17, bf16[96,640]{1,0:T(8,128)(2,1)} %collective-permute-done.16, bf16[96,640]{1,0:T(8,128)(2,1)} %collective-permute-done.15, ...), kind=kLoop, calls=%fused_computation.4 | loop fusion | flops 675840 | bytes 983041 | tf_op jit(solution)/shard_map/convert_element_type | solution.py:456
  67.1 2.6 %collective-permute-start.18 = (bf16[96,640]{1,0:T(8,128)(2,1)S(1)}, bf16[96,640]{1,0:T(8,128)(2,1)S(1)}, u32[]{:S(2)}, u32[]{:S(2)}) collective-permute-start(bf16[96,640]{1,0:T(8,128)(2,1)S(1)} %fusion.2), channel_id=1, source_target_pairs={{0,16},{2,18},{4,20},{6,22},{8,24},{10,26},{12,28},{14,30},{16,0},... | collective-permute-start | bytes 368648 | tf_op jit(solution)/shard_map/ppermute | solution.py:35
  69.8 2.4 %weight_grad.4 = bf16[2560,512]{1,0:T(8,128)(2,1)} custom-call(bf16[384,2560]{1,0:T(8,128)(2,1)S(1)} %get-tuple-element.88.left, bf16[384,1024]{1,0:T(8,128)(2,1)S(1)} %get-tuple-element.90.right), custom_call_target="tpu_custom_call" | custom-call | flops 1006632960 | tf_op jit(solution)/shard_map/weight_grad/pallas_call | solution.py:330
  72.2 2.4 %weight_grad.5 = bf16[2560,512]{1,0:T(8,128)(2,1)} custom-call(bf16[384,2560]{1,0:T(8,128)(2,1)S(1)} %get-tuple-element.88.left, bf16[384,1024]{1,0:T(8,128)(2,1)S(1)} %get-tuple-element.90.right), custom_call_target="tpu_custom_call" | custom-call | flops 1006632960 | tf_op jit(solution)/shard_map/weight_grad/pallas_call | solution.py:330
  74.6 0.0 collective-permute-done.18
  74.6 1.2 %fusion.1 = bf16[96,640]{1,0:T(8,128)(2,1)S(1)} fusion(bf16[96,640]{1,0:T(8,128)(2,1)} %collective-permute-done.14, bf16[96,640]{1,0:T(8,128)(2,1)S(1)} %collective-permute-done.18, pred[]{:T(512)S(6)} %eq.6, bf16[96,640]{1,0:T(8,128)(2,1)} %collective-permute-done.17, bf16[96,640]{1,0:T(8,128)(2,1)} %collective-permute-done.16, ...), kind=kLoop, calls=%fused_computation.3 | loop fusion | flops 798720 | bytes 1105921 | tf_op jit(solution)/shard_map/convert_element_type | solution.py:464
  75.8 0.1 fusion.3
  75.9 0.7 pad_maximum_fusion
  (11 shorter events, 0.1 us)
Async XLA Ops:
  0.6 5.0 %copy-start = (f32[512,40]{0,1:T(8,128)S(1)}, f32[512,40]{0,1:T(8,128)}, u32[]{:S(2)}) copy-start(f32[512,40]{0,1:T(8,128)} %param.15) | copy-start | bytes 245764
  0.7 5.3 %copy-start.5 = (f32[40,512]{1,0:T(8,128)S(1)}, f32[40,512]{1,0:T(8,128)}, u32[]{:S(2)}) copy-start(f32[40,512]{1,0:T(8,128)} %gate_scales.1) | copy-start | bytes 245764
  0.7 5.3 %copy-start.6 = (f32[40,512]{1,0:T(8,128)S(1)}, f32[40,512]{1,0:T(8,128)}, u32[]{:S(2)}) copy-start(f32[40,512]{1,0:T(8,128)} %up_scales.1) | copy-start | bytes 245764
  2.6 14.6 %collective-permute-start = (bf16[96,2560]{1,0:T(8,128)(2,1)}, bf16[96,2560]{1,0:T(8,128)(2,1)}, u32[]{:S(2)}, u32[]{:S(2)}) collective-permute-start(bf16[96,2560]{1,0:T(8,128)(2,1)} %fetch.1), channel_id=1, source_target_pairs={{0,1},{1,0},{2,3},{3,2},{4,5},{5,4},{6,7},{7,6},{8,9},{9,8},{10,11... | collective-permute-start | bytes 1474568 | tf_op jit(solution)/shard_map/ppermute | solution.py:35
  17.1 12.6 %collective-permute-start.1 = (bf16[96,2560]{1,0:T(8,128)(2,1)}, bf16[96,2560]{1,0:T(8,128)(2,1)S(1)}, u32[]{:S(2)}, u32[]{:S(2)}) collective-permute-start(bf16[96,2560]{1,0:T(8,128)(2,1)} %collective-permute-done.held), channel_id=1, source_target_pairs={{0,8},{2,10},{4,12},{6,14},{8,0},{10,2},{12,4},{14,6},{16,24},{18,... | collective-permute-start | bytes 1474568 | tf_op jit(solution)/shard_map/ppermute | solution.py:35
  18.9 17.2 %collective-permute-start.5 = (bf16[192,1536]{1,0:T(8,128)(2,1)S(1)}, bf16[192,1536]{1,0:T(8,128)(2,1)S(1)}, u32[]{:S(2)}, u32[]{:S(2)}) collective-permute-start(bf16[192,1536]{1,0:T(8,128)(2,1)S(1)} %get-tuple-element.50), channel_id=1, source_target_pairs={{0,1},{1,0},{2,3},{3,2},{4,5},{5,4},{6,7},{7,6},{8,9},{9,8},{10,11... | collective-permute-start | bytes 1769480 | tf_op jit(solution)/shard_map/ppermute | solution.py:35
  20.5 9.3 %collective-permute-start.3 = (bf16[96,2560]{1,0:T(8,128)(2,1)}, bf16[96,2560]{1,0:T(8,128)(2,1)S(1)}, u32[]{:S(2)}, u32[]{:S(2)}) collective-permute-start(bf16[96,2560]{1,0:T(8,128)(2,1)} %collective-permute-done.held), channel_id=1, source_target_pairs={{0,2},{2,0},{4,6},{6,4},{8,10},{10,8},{12,14},{14,12},{16,18},{18,... | collective-permute-start | bytes 1474568 | tf_op jit(solution)/shard_map/ppermute | solution.py:35
  29.8 4.4 %collective-permute-start.2 = (bf16[96,2560]{1,0:T(8,128)(2,1)S(1)}, bf16[96,2560]{1,0:T(8,128)(2,1)S(1)}, u32[]{:S(2)}, u32[]{:S(2)}) collective-permute-start(bf16[96,2560]{1,0:T(8,128)(2,1)S(1)} %collective-permute-done.1.held), channel_id=1, source_target_pairs={{0,2},{2,0},{4,6},{6,4},{8,10},{10,8},{12,14},{14,12},{16,18},{18,... | collective-permute-start | bytes 1474568 | tf_op jit(solution)/shard_map/ppermute | solution.py:35
  32.7 9.9 %collective-permute-start.8 = (bf16[96,1536]{1,0:T(8,128)(2,1)S(1)}, bf16[96,1536]{1,0:T(8,128)(2,1)S(1)}, u32[]{:S(2)}, u32[]{:S(2)}) collective-permute-start(bf16[96,1536]{1,0:T(8,128)(2,1)S(1)} %get-tuple-element.64), channel_id=1, source_target_pairs={{0,1},{1,0},{2,3},{3,2},{4,5},{5,4},{6,7},{7,6},{8,9},{9,8},{10,11... | collective-permute-start | bytes 884744 | tf_op jit(solution)/shard_map/ppermute | solution.py:35
  36.1 2.1 %copy-start.1 = (bf16[384,2560]{1,0:T(8,128)(2,1)}, bf16[384,2560]{1,0:T(8,128)(2,1)S(1)}, u32[]{:S(2)}) copy-start(bf16[384,2560]{1,0:T(8,128)(2,1)S(1)} %get-tuple-element.84.right) | copy-start | bytes 5898244
  38.2 7.1 %collective-permute-start.6 = (bf16[96,1280]{1,0:T(8,128)(2,1)S(1)}, bf16[96,1280]{1,0:T(8,128)(2,1)S(1)}, u32[]{:S(2)}, u32[]{:S(2)}) collective-permute-start(bf16[96,1280]{1,0:T(8,128)(2,1)S(1)} %get-tuple-element.62), channel_id=1, source_target_pairs={{0,2},{2,0},{4,6},{6,4},{8,10},{10,8},{12,14},{14,12},{16,18},{18,... | collective-permute-start | bytes 737288 | tf_op jit(solution)/shard_map/ppermute | solution.py:35
  38.5 6.8 %collective-permute-start.7 = (bf16[96,1280]{1,0:T(8,128)(2,1)S(1)}, bf16[96,1280]{1,0:T(8,128)(2,1)S(1)}, u32[]{:S(2)}, u32[]{:S(2)}) collective-permute-start(bf16[96,1280]{1,0:T(8,128)(2,1)S(1)} %get-tuple-element.63), channel_id=1, source_target_pairs={{0,2},{2,0},{4,6},{6,4},{8,10},{10,8},{12,14},{14,12},{16,18},{18,... | collective-permute-start | bytes 737288 | tf_op jit(solution)/shard_map/ppermute | solution.py:35
  38.8 10.3 %collective-permute-start.4 = (bf16[96,1536]{1,0:T(8,128)(2,1)S(1)}, bf16[96,1536]{1,0:T(8,128)(2,1)S(1)}, u32[]{:S(2)}, u32[]{:S(2)}) collective-permute-start(bf16[96,1536]{1,0:T(8,128)(2,1)S(1)} %get-tuple-element.59), channel_id=1, source_target_pairs={{0,1},{1,0},{2,3},{3,2},{4,5},{5,4},{6,7},{7,6},{8,9},{9,8},{10,11... | collective-permute-start | bytes 884744 | tf_op jit(solution)/shard_map/ppermute | solution.py:35
  45.4 7.2 %collective-permute-start.13 = (bf16[96,640]{1,0:T(8,128)(2,1)S(1)}, bf16[96,640]{1,0:T(8,128)(2,1)S(1)}, u32[]{:S(2)}, u32[]{:S(2)}) collective-permute-start(bf16[96,640]{1,0:T(8,128)(2,1)S(1)} %add_convert_fusion.4), channel_id=1, source_target_pairs={{0,8},{2,10},{4,12},{6,14},{8,0},{10,2},{12,4},{14,6},{16,24},{18,... | collective-permute-start | bytes 368648 | tf_op jit(solution)/shard_map/ppermute | solution.py:35
  47.0 7.6 %collective-permute-start.12 = (bf16[96,640]{1,0:T(8,128)(2,1)S(1)}, bf16[96,640]{1,0:T(8,128)(2,1)S(1)}, u32[]{:S(2)}, u32[]{:S(2)}) collective-permute-start(bf16[96,640]{1,0:T(8,128)(2,1)S(1)} %get-tuple-element.94), channel_id=1, source_target_pairs={{0,4},{2,6},{4,0},{6,2},{8,12},{10,14},{12,8},{14,10},{16,20},{18,... | collective-permute-start | bytes 368648 | tf_op jit(solution)/shard_map/ppermute | solution.py:35
  48.6 6.0 %collective-permute-start.11 = (bf16[96,640]{1,0:T(8,128)(2,1)S(1)}, bf16[96,640]{1,0:T(8,128)(2,1)S(1)}, u32[]{:S(2)}, u32[]{:S(2)}) collective-permute-start(bf16[96,640]{1,0:T(8,128)(2,1)S(1)} %get-tuple-element.95), channel_id=1, source_target_pairs={{0,12},{2,14},{4,8},{6,10},{8,4},{10,6},{12,0},{14,2},{16,28},{18,... | collective-permute-start | bytes 368648 | tf_op jit(solution)/shard_map/ppermute | solution.py:35
  52.0 6.1 %copy-start.3 = (f32[96,1280]{1,0:T(8,128)}, f32[96,1280]{1,0:T(8,128)S(1)}, u32[]{:S(2)}) copy-start(f32[96,1280]{1,0:T(8,128)S(1)} %get-tuple-element.80) | copy-start | bytes 1474564
  52.0 3.3 %collective-permute-start.9 = (bf16[96,1280]{1,0:T(8,128)(2,1)S(1)}, bf16[96,1280]{1,0:T(8,128)(2,1)S(1)}, u32[]{:S(2)}, u32[]{:S(2)}) collective-permute-start(bf16[96,1280]{1,0:T(8,128)(2,1)S(1)} %get-tuple-element.79), channel_id=1, source_target_pairs={{0,2},{2,0},{4,6},{6,4},{8,10},{10,8},{12,14},{14,12},{16,18},{18,... | collective-permute-start | bytes 737288 | tf_op jit(solution)/shard_map/ppermute | solution.py:35
  52.1 6.0 %collective-permute-start.10 = (bf16[96,1280]{1,0:T(8,128)(2,1)S(1)}, bf16[96,1280]{1,0:T(8,128)(2,1)S(1)}, u32[]{:S(2)}, u32[]{:S(2)}) collective-permute-start(bf16[96,1280]{1,0:T(8,128)(2,1)S(1)} %get-tuple-element.81), channel_id=1, source_target_pairs={{0,2},{2,0},{4,6},{6,4},{8,10},{10,8},{12,14},{14,12},{16,18},{18,... | collective-permute-start | bytes 737288 | tf_op jit(solution)/shard_map/ppermute | solution.py:35
  56.1 9.8 %collective-permute-start.15 = (bf16[96,640]{1,0:T(8,128)(2,1)}, bf16[96,640]{1,0:T(8,128)(2,1)}, u32[]{:S(2)}, u32[]{:S(2)}) collective-permute-start(bf16[96,640]{1,0:T(8,128)(2,1)} %get-tuple-element.93), channel_id=1, source_target_pairs={{0,12},{2,14},{4,8},{6,10},{8,4},{10,6},{12,0},{14,2},{16,28},{18,... | collective-permute-start | bytes 368648 | tf_op jit(solution)/shard_map/ppermute | solution.py:35
  57.0 8.9 %collective-permute-start.16 = (bf16[96,640]{1,0:T(8,128)(2,1)}, bf16[96,640]{1,0:T(8,128)(2,1)}, u32[]{:S(2)}, u32[]{:S(2)}) collective-permute-start(bf16[96,640]{1,0:T(8,128)(2,1)} %get-tuple-element.92), channel_id=1, source_target_pairs={{0,4},{2,6},{4,0},{6,2},{8,12},{10,14},{12,8},{14,10},{16,20},{18,... | collective-permute-start | bytes 368648 | tf_op jit(solution)/shard_map/ppermute | solution.py:35
  58.8 7.1 %collective-permute-start.17 = (bf16[96,640]{1,0:T(8,128)(2,1)}, bf16[96,640]{1,0:T(8,128)(2,1)}, u32[]{:S(2)}, u32[]{:S(2)}) collective-permute-start(bf16[96,640]{1,0:T(8,128)(2,1)} %add_convert_fusion.1), channel_id=1, source_target_pairs={{0,8},{2,10},{4,12},{6,14},{8,0},{10,2},{12,4},{14,6},{16,24},{18,... | collective-permute-start | bytes 368648 | tf_op jit(solution)/shard_map/ppermute | solution.py:35
  60.2 5.7 %collective-permute-start.14 = (bf16[96,640]{1,0:T(8,128)(2,1)}, bf16[96,640]{1,0:T(8,128)(2,1)}, u32[]{:S(2)}, u32[]{:S(2)}) collective-permute-start(bf16[96,640]{1,0:T(8,128)(2,1)} %add_convert_fusion), channel_id=1, source_target_pairs={{0,1},{1,0},{2,3},{3,2},{4,5},{5,4},{6,7},{7,6},{8,9},{9,8},{10,11... | collective-permute-start | bytes 368648 | tf_op jit(solution)/shard_map/ppermute | solution.py:35
  61.8 1.5 %copy-start.2 = (bf16[384,2560]{1,0:T(8,128)(2,1)S(1)}, bf16[384,2560]{1,0:T(8,128)(2,1)}, u32[]{:S(2)}) copy-start(bf16[384,2560]{1,0:T(8,128)(2,1)} %copy-done.1) | copy-start | bytes 5898244
  63.3 2.6 %copy-start.4 = (f32[96,1280]{1,0:T(8,128)S(1)}, f32[96,1280]{1,0:T(8,128)}, u32[]{:S(2)}) copy-start(f32[96,1280]{1,0:T(8,128)} %copy-done.3) | copy-start | bytes 1474564
  67.1 7.5 %collective-permute-start.18 = (bf16[96,640]{1,0:T(8,128)(2,1)S(1)}, bf16[96,640]{1,0:T(8,128)(2,1)S(1)}, u32[]{:S(2)}, u32[]{:S(2)}) collective-permute-start(bf16[96,640]{1,0:T(8,128)(2,1)S(1)} %fusion.2), channel_id=1, source_target_pairs={{0,16},{2,18},{4,20},{6,22},{8,24},{10,26},{12,28},{14,30},{16,0},... | collective-permute-start | bytes 368648 | tf_op jit(solution)/shard_map/ppermute | solution.py:35

commit v3 on v2

--- a/solution.py
+++ b/solution.py
@@ -81,7 +81,7 @@
         out_specs=IN_VMEM,
         out_shape=pltpu.VMEM(shape, tokens.dtype),
         scratch_shapes=[pltpu.SemaphoreType.DMA],
-        compiler_params=grant(4),
+        compiler_params=grant(2),
         cost_estimate=cost(0),
         name="fetch",
     )(node, place, in_hbm(tokens), in_hbm(cot))
@@ -89,21 +89,22 @@
 
 def prepare_kernel(
     node, tokens, cot, gate_codes, up_codes, down_codes, gate_scales, up_scales, down_scales,
-    own_tokens, own_cot, w_in, w_down, total, short, gate_held, up_held, down_held, sems,
+    all_tokens, all_cots, w_in, w_down, total, short, sems,
 ):
     rows, units = gate_codes.shape
     steps, per_step = rows // STEP, STEP // QB
     own = slice(0, tokens.shape[0])
+    gate, up = slice(0, units), slice(units, 2 * units)
 
     def copies(step):
         column = pl.multiple_of(node[0] * rows + step * STEP, 128)
         part = pl.ds(pl.multiple_of(step * STEP, 128), STEP)
         pairs = (
-            (gate_codes.at[part, :], gate_held.at[part, :]),
-            (up_codes.at[part, :], up_held.at[part, :]),
-            (tokens.at[:, pl.ds(column, STEP)], own_tokens.at[own, part]),
-            (down_codes.at[:, part], down_held.at[:, part]),
-            (cot.at[:, pl.ds(column, STEP)], own_cot.at[own, part]),
+            (gate_codes.at[part, :], w_in.at[part, gate]),
+            (up_codes.at[part, :], w_in.at[part, up]),
+            (tokens.at[:, pl.ds(column, STEP)], all_tokens.at[own, part]),
+            (down_codes.at[:, part], w_down.at[:, part]),
+            (cot.at[:, pl.ds(column, STEP)], all_cots.at[own, part]),
         )
         return [pltpu.make_async_copy(a, b, sems.at[step, i]) for i, (a, b) in enumerate(pairs)]
 
@@ -111,6 +112,9 @@
         for copy in copies(step):
             copy.start()
     total[...] = jnp.zeros(total.shape, total.dtype)
+
+    def scale(weights, index, factor):
+        weights[index] = (weights[index].astype(jnp.float32) * factor).astype(weights.dtype)
 
     def one(step, carry):
         for copy in copies(step):
@@ -118,15 +122,13 @@
         first_scale = (node[0] * steps + step) * per_step
         for j in range(per_step):
             part = pl.ds(pl.multiple_of(step * STEP + j * QB, QB), QB)
-            scale = pl.ds(first_scale + j, 1)
-            w_in[part, :units] = (gate_held[part, :].astype(jnp.float32) * gate_scales[scale, :]).astype(w_in.dtype)
-            w_in[part, units:] = (up_held[part, :].astype(jnp.float32) * up_scales[scale, :]).astype(w_in.dtype)
-            w_down[:, part] = (
-                down_held[:, part].astype(jnp.float32) * down_scales[step, :, j : j + 1]
-            ).astype(w_down.dtype)
+            row = pl.ds(first_scale + j, 1)
+            scale(w_in, (part, gate), gate_scales[row, :])
+            scale(w_in, (part, up), up_scales[row, :])
+            scale(w_down, (slice(None), part), down_scales[step, :, j : j + 1])
         part = pl.ds(pl.multiple_of(step * STEP, 128), STEP)
-        total[:, : 2 * units] += jnp.dot(own_tokens[own, part], w_in[part, :], preferred_element_type=jnp.float32)
-        total[:, 2 * units :] += against(own_cot[own, part], w_down[:, part])
+        total[:, : 2 * units] += jnp.dot(all_tokens[own, part], w_in[part, :], preferred_element_type=jnp.float32)
+        total[:, 2 * units :] += against(all_cots[own, part], w_down[:, part])
         return carry
 
     lax.fori_loop(0, steps, one, 0)
@@ -152,42 +154,14 @@
             pltpu.VMEM((count, 3 * units), jnp.float32),
             pltpu.VMEM((count, 3 * units), codes),
         ],
-        scratch_shapes=[
-            pltpu.VMEM((rows, units), codes),
-            pltpu.VMEM((rows, units), codes),
-            pltpu.VMEM((units, rows), codes),
-            pltpu.SemaphoreType.DMA((steps, 5)),
-        ],
-        compiler_params=grant(16),
+        scratch_shapes=[pltpu.SemaphoreType.DMA((steps, 5))],
+        compiler_params=grant(4),
         cost_estimate=cost(0),
         name="prepare",
     )(
         node, *(in_hbm(a) for a in (tokens, cot, gate_codes, up_codes, down_codes)),
         gate_scales, up_scales, scales,
     )
-
-
-def reorder_kernel(blocks, place, source, target):
-    rows = target.shape[0] // blocks
-    bits = blocks.bit_length() - 1
-    for i in range(blocks):
-        block = 0
-        for bit in range(bits):
-            own = (place[0] >> bit) & 1
-            block += (own if (i >> (bits - 1 - bit)) & 1 else 1 - own) << bit
-        target[i * rows : (i + 1) * rows, :] = source[pl.ds(pl.multiple_of(block * rows, 16), rows), :]
-
-
-def reorder(place, weights, blocks):
-    return pl.pallas_call(
-        functools.partial(reorder_kernel, blocks),
-        in_specs=[IN_SMEM, IN_VMEM],
-        out_specs=IN_VMEM,
-        out_shape=pltpu.VMEM(weights.shape, weights.dtype),
-        compiler_params=grant(4),
-        cost_estimate=cost(0),
-        name="reorder",
-    )(place, in_vmem(weights))
 
 
 def join_kernel(group, far, place, held, given, w_in, w_down, *refs):
@@ -236,15 +210,15 @@
             pltpu.VMEM((half, 3 * units), jnp.bfloat16),
         ],
         input_output_aliases={5 + i: i for i in range(len(before))},
-        compiler_params=grant(8),
+        compiler_params=grant(6),
         cost_estimate=cost(0),
         name="join",
     )(place, *(in_vmem(a) for a in (held, given, w_in, w_down, *before)))
 
 
-def activate_kernel(group, turns, count, block, place, weights, total, arrived, *refs):
-    pairs = weights.shape[0] // (2 * block)
-    act, d_inner, *targets = refs[-2 - pairs :]
+def activate_kernel(group, turns, count, blocks, place, weights, total, arrived, *refs):
+    block = weights.shape[0] // blocks
+    act, d_inner, *targets = refs[-2 - blocks // 2 :]
     units, half, chunk = act.shape[1], count // 2, 32
     side = side_of(place[0])
 
@@ -265,24 +239,34 @@
             act[kept, :] = (silu_val * upper).astype(act.dtype)
             d_inner[kept, :units] = (d_act * upper * sig * (1.0 + gate * (1.0 - sig))).astype(d_inner.dtype)
             d_inner[kept, units:] = (d_act * silu_val).astype(d_inner.dtype)
-    if len(turns) == 2:
-        mine = rows(group * count, count)
-    else:
-        mine = rows(group * count + natural, half)
-
-    def store(target, product, h):
-        for i in (0, 1):
-            lanes = slice((2 * i + h) * block, (2 * i + h + 1) * block)
-            target[:, lanes] = product[:, i * block : (i + 1) * block].astype(target.dtype)
-
-    for p, target in enumerate(targets):
-        product = against(d_inner[mine, :], weights[2 * p * block : 2 * (p + 1) * block, :])
+    def block_rows(relative):
+        bits = blocks.bit_length() - 1
+        owner = 0
+        for bit in range(bits):
+            own = (place[0] >> bit) & 1
+            owner += (own if (relative >> (bits - 1 - bit)) & 1 else 1 - own) << bit
+        return weights[rows(owner * block, block), :]
+
+    def store(h, mine):
+        for p, target in enumerate(targets):
+            pieces, places, width = [], [], 0
+            for i in (0, 1):
+                pad = ((2 * i + h) * block - width) % 128
+                if pad:
+                    pieces.append(weights[:pad, :])
+                pieces.append(block_rows(2 * p + i))
+                places.append(width + pad)
+                width += pad + block
+            product = against(mine, jnp.concatenate(pieces))
+            for i in (0, 1):
+                lanes = slice((2 * i + h) * block, (2 * i + h + 1) * block)
+                target[:, lanes] = product[:, places[i] : places[i] + block].astype(target.dtype)
+
+    for h in (0, 1):
         if len(turns) == 2:
-            store(target, product[:half], 0)
-            store(target, product[half:], 1)
+            store(h, d_inner[rows(group * count + h * half, half), :])
         else:
-            for h in (0, 1):
-                pl.when(natural == h * half)(functools.partial(store, target, product, h))
+            pl.when(natural == h * half)(lambda: store(h, d_inner[rows(group * count + h * half, half), :]))
 
 
 def activate(group, groups, turns, place, total, arrived, weights, blocks, before):
@@ -291,7 +275,7 @@
     count = arrived.shape[0] * (3 - len(turns))
     terms = count // 2, 4 * block
     return pl.pallas_call(
-        functools.partial(activate_kernel, group, turns, count, block),
+        functools.partial(activate_kernel, group, turns, count, blocks),
         in_specs=[IN_SMEM] + [IN_VMEM] * (3 + len(before)),
         out_specs=[IN_VMEM] * (2 + pairs),
         out_shape=[
@@ -301,7 +285,7 @@
         + [pltpu.VMEM(terms, jnp.bfloat16)] * (pairs // 2)
         + [pltpu.VMEM(terms, jnp.float32)] * (pairs // 2),
         input_output_aliases={4 + i: i for i in range(len(before))},
-        compiler_params=grant(12),
+        compiler_params=grant(8),
         cost_estimate=cost(0),
         name="activate",
     )(place, *(in_vmem(a) for a in (weights, total, arrived, *before)))
@@ -333,7 +317,7 @@
         out_specs=IN_HBM,
         out_shape=pltpu.HBM(shape, jnp.bfloat16),
         scratch_shapes=[pltpu.VMEM(shape, jnp.bfloat16), pltpu.SemaphoreType.DMA((rows // STEP,))],
-        compiler_params=grant(10),
+        compiler_params=grant(6),
         cost_estimate=cost(2 * left.shape[0] * rows * units),
         name="weight_grad",
     )(in_vmem(left), in_vmem(right))
@@ -366,8 +350,6 @@
         nodes, node_ref, tokens, cotangent, gate_codes, up_codes, down_codes, gate_scales, up_scales, down_scales
     )
     fetched = after(fetched, own_short)
-    w_relative = reorder(place_ref, w_in, owners)
-    fetched = after(fetched, w_relative)
 
     sums, shorts = [own_sums], [None]
     for k, mine in enumerate(fetched, 1):
@@ -424,17 +406,17 @@
     blocks, before, others = [None] * nodes, [], [None] * nodes
     for k in reversed(range(1, nodes)):
         act, d_inner, *others[k] = activate(
-            k, nodes, (0, 1), place_ref, sums[k], arrived[k], w_relative, owners, before
+            k, nodes, (0, 1), place_ref, sums[k], arrived[k], w_in, owners, before
         )
         before = [act, d_inner]
-    before = activate(0, nodes, (0,), place_ref, sums[0], near_far[0], w_relative, owners, before)
+    before = activate(0, nodes, (0,), place_ref, sums[0], near_far[0], w_in, owners, before)
     last = []
     for k in range(1, nodes):
         sending, mine = split(others[k], before)
         last.append([value for _, value in sending])
         blocks[k] = mine, exchange(sending)
     act, d_inner, *parts = activate(
-        0, nodes, (1,), place_ref, sums[0], after(near_far[1], last), w_relative, owners, before
+        0, nodes, (1,), place_ref, sums[0], after(near_far[1], last), w_in, owners, before
     )
     sending, mine = split(parts)
     got = exchange(sending)

time: 76.9 us -> 77.1 us (level)
  local copies, waits for them, and re-layouts: 2.04 us -> 3.3 us
  waiting for transfers between devices: 18.9 us -> 18 us
    unnamed x14, local copies, waits for them, and re-layouts: 1.58 us -> 2.84 us
    ppermute x19, waiting for transfers between devices: 18.9 us -> 18 us  [swap(): return lax.ppermute(value, axis, flipped(size, mask))]
  transfers between devices with their start and end apart: 19 -> 19, of which waited for: 4 -> 5; matrix products, arithmetic and copies ran while one was open for 3% -> 3% of each run, Pallas kernels for 35% -> 35%
where the time goes in v3:
time: 77.1 us; the launch traced here: 76.8 us
  Pallas kernels  28.8 us (37%)
  starting transfers between devices  20.6 us (27%)
  waiting for transfers between devices  18 us (23%)
  other arithmetic  5.3 us (7%)
  local copies, waits for them, and re-layouts  3.3 us (4%)
  between operations  0.89 us (1%)
    ppermute x19, starting transfers between devices, swap(): return lax.ppermute(value, axis, flipped(size, mask))  20.6 us
    ppermute x19, waiting for transfers between devices, swap(): return lax.ppermute(value, axis, flipped(size, mask))  18 us
    pallas_call x3, Pallas kernels, activate(): pl.pallas_call(functools.partial(activate_kernel, group, turns, count, bl...  8.1 us
    pallas_call x3, Pallas kernels, weight_grad(): pl.pallas_call(functools.partial(grads_kernel, first, by_rows), in_specs=...  7.42 us
    pallas_call x1, Pallas kernels, prepare(): pl.pallas_call(prepare_kernel, in_specs=[IN_SMEM] + [IN_HBM] * 5 + [IN_VM...  6.54 us
    pallas_call x2, Pallas kernels, join(): pl.pallas_call(functools.partial(join_kernel, group, far), in_specs=[IN_S...  4.82 us
    unnamed x14, local copies, waits for them, and re-layouts  2.84 us
    pallas_call x1, Pallas kernels, fetch(): pl.pallas_call(functools.partial(fetch_kernel, mask), in_specs=[IN_SMEM,...  1.89 us
  transfers between devices with their start and end apart: 19, of which 5 were waited for; matrix products, arithmetic and copies ran while one was open for 3% of the time, Pallas kernels for 35%

profile of v3, /device:TPU:0, one launch (start us, length us, event | category | flops | bytes accessed | tf_op | source)
XLA Modules:
  0.0 76.8 jit_solution(2983358445367799763)
XLA Ops:
  0.6 0.0 copy-start
  0.7 1.9 %fetch.1 = bf16[96,2560]{1,0:T(8,128)(2,1)} custom-call(s32[1]{0:T(128)} %bitcast.1.node, s32[1]{0:T(128)} %bitcast.place, bf16[192,5120]{1,0:T(8,128)(2,1)} %tokens.3, bf16[192,5120]{1,0:T(8,128)(2,1)} %cot.3), custom_call_target="tpu_custom_call" | custom-call | tf_op jit(solution)/shard_map/fetch/pallas_call | solution.py:78
  2.6 3.0 %collective-permute-start = (bf16[96,2560]{1,0:T(8,128)(2,1)}, bf16[96,2560]{1,0:T(8,128)(2,1)}, u32[]{:S(2)}, u32[]{:S(2)}) collective-permute-start(bf16[96,2560]{1,0:T(8,128)(2,1)} %fetch.1), channel_id=1, source_target_pairs={{0,1},{1,0},{2,3},{3,2},{4,5},{5,4},{6,7},{7,6},{8,9},{9,8},{10,11... | collective-permute-start | bytes 1474568 | tf_op jit(solution)/shard_map/ppermute | solution.py:35
  5.6 0.0 copy-done
  5.6 0.4 copy.25
  6.0 0.0 copy-done.5
  6.0 6.5 %prepare.1 = (bf16[384,2560]{1,0:T(8,128)(2,1)S(1)}, bf16[384,2560]{1,0:T(8,128)(2,1)S(1)}, bf16[2560,1024]{1,0:T(8,128)(2,1)S(1)}, bf16[512,2560]{1,0:T(8,128)(...) custom-call(s32[1]{0:T(128)} %bitcast.1.node, bf16[192,5120]{1,0:T(8,128)(2,1)} %tokens.3, ...), custom_call_target="tpu_custom_call" | custom-call | tf_op jit(solution)/shard_map/prepare/pallas_call | solution.py:145
  12.6 4.6 %collective-permute-done.held = bf16[96,2560]{1,0:T(8,128)(2,1)} collective-permute-done((bf16[96,2560]{1,0:T(8,128)(2,1)}, bf16[96,2560]{1,0:T(8,128)(2,1)}, u32[]{:S(2)}, u32[]{:S(2)}) %collective-permute-start) | collective-permute-done | bytes 491552 | tf_op jit(solution)/shard_map/ppermute | solution.py:35
  17.1 1.8 %collective-permute-start.1 = (bf16[96,2560]{1,0:T(8,128)(2,1)}, bf16[96,2560]{1,0:T(8,128)(2,1)S(1)}, u32[]{:S(2)}, u32[]{:S(2)}) collective-permute-start(bf16[96,2560]{1,0:T(8,128)(2,1)} %collective-permute-done.held), channel_id=1, source_target_pairs={{0,8},{2,10},{4,12},{6,14},{8,0},{10,2},{12,4},{14,6},{16,24},{18,... | collective-permute-start | bytes 1474568 | tf_op jit(solution)/shard_map/ppermute | solution.py:35
  18.9 1.5 %collective-permute-start.5 = (bf16[192,1536]{1,0:T(8,128)(2,1)S(1)}, bf16[192,1536]{1,0:T(8,128)(2,1)S(1)}, u32[]{:S(2)}, u32[]{:S(2)}) collective-permute-start(bf16[192,1536]{1,0:T(8,128)(2,1)S(1)} %get-tuple-element.49), channel_id=1, source_target_pairs={{0,1},{1,0},{2,3},{3,2},{4,5},{5,4},{6,7},{7,6},{8,9},{9,8},{10,11... | collective-permute-start | bytes 1769480 | tf_op jit(solution)/shard_map/ppermute | solution.py:35
  20.5 0.0 collective-permute-start.3
  20.5 9.3 %collective-permute-done.1.held = bf16[96,2560]{1,0:T(8,128)(2,1)S(1)} collective-permute-done((bf16[96,2560]{1,0:T(8,128)(2,1)}, bf16[96,2560]{1,0:T(8,128)(2,1)S(1)}, u32[]{:S(2)}, u32[]{:S(2)}) %collective-permute-start.1) | collective-permute-done | bytes 491552 | tf_op jit(solution)/shard_map/ppermute | solution.py:35
  29.8 0.0 collective-permute-start.2
  29.8 0.0 collective-permute-done.3.given
  29.8 2.9 %join.2 = (bf16[384,2560]{1,0:T(8,128)(2,1)S(1)}, bf16[384,2560]{1,0:T(8,128)(2,1)S(1)}, f32[192,1536]{1,0:T(8,128)S(1)}, bf16[96,1536]{1,0:T(8,128)(2,1)S(1)}) custom-call(s32[1]{0:T(128)} %bitcast.place, bf16[96,2560]{1,0:T(8,128)(2,1)} %collective-permute-done.held, ...), custom_call_target="tpu_custom_call", output_to_operand_aliasing={{0}: (5, {}), {1}: (6, {})} | custom-call | tf_op jit(solution)/shard_map/join/pallas_call | solution.py:202
  32.7 1.5 %collective-permute-start.8 = (bf16[96,1536]{1,0:T(8,128)(2,1)S(1)}, bf16[96,1536]{1,0:T(8,128)(2,1)S(1)}, u32[]{:S(2)}, u32[]{:S(2)}) collective-permute-start(bf16[96,1536]{1,0:T(8,128)(2,1)S(1)} %get-tuple-element.62), channel_id=1, source_target_pairs={{0,1},{1,0},{2,3},{3,2},{4,5},{5,4},{6,7},{7,6},{8,9},{9,8},{10,11... | collective-permute-start | bytes 884744 | tf_op jit(solution)/shard_map/ppermute | solution.py:35
  34.2 0.0 collective-permute-done.2.given
  34.2 1.9 %join.3 = (bf16[384,2560]{1,0:T(8,128)(2,1)S(1)}, bf16[384,2560]{1,0:T(8,128)(2,1)S(1)}, f32[192,1536]{1,0:T(8,128)S(1)}, bf16[96,1536]{1,0:T(8,128)(2,1)S(1)}) custom-call(s32[1]{0:T(128)} %bitcast.place, bf16[96,2560]{1,0:T(8,128)(2,1)S(1)} %collective-permute-done.1.held, ...), custom_call_target="tpu_custom_call", output_to_operand_aliasing={{0}: (5, {}), {1}: (6, {}), {2}: (7, {})} | custom-call | tf_op jit(solution)/shard_map/join/pallas_call | solution.py:202
  36.1 0.0 copy-start.1
  36.1 1.3 %copy-done.1 = bf16[384,2560]{1,0:T(8,128)(2,1)} copy-done((bf16[384,2560]{1,0:T(8,128)(2,1)}, bf16[384,2560]{1,0:T(8,128)(2,1)S(1)}, u32[]{:S(2)}) %copy-start.1) | copy-done | bytes 1966104
  37.4 0.0 collective-permute-done.5.arrived
  37.4 3.8 %activate.3 = (bf16[384,512]{1,0:T(8,128)(2,1)S(1)}, bf16[384,1024]{1,0:T(8,128)(2,1)S(1)}, bf16[96,1280]{1,0:T(8,128)(2,1)S(1)}, bf16[96,1280]{1,0:T(8,128)(2,1...) custom-call(s32[1]{0:T(128)} %bitcast.place, bf16[2560,1024]{1,0:T(8,128)(2,1)S(1)} %get-tuple-element.47.w_in.weights, ...), custom_call_target="tpu_custom_call" | custom-call | tf_op jit(solution)/shard_map/activate/pallas_call | solution.py:277
  41.2 0.3 collective-permute-start.6
  41.5 0.3 collective-permute-start.7
  41.8 0.6 collective-permute-start.4
  42.4 0.0 collective-permute-done.8.arrived
  42.4 2.0 %activate.4 = (bf16[384,512]{1,0:T(8,128)(2,1)S(1)}, bf16[384,1024]{1,0:T(8,128)(2,1)S(1)}, bf16[96,1280]{1,0:T(8,128)(2,1)S(1)}, bf16[96,1280]{1,0:T(8,128)(2,1...) custom-call(s32[1]{0:T(128)} %bitcast.place, ...), custom_call_target="tpu_custom_call", output_to_operand_aliasing={{0}: (4, {}), {1}: (5, {})} | custom-call | tf_op jit(solution)/shard_map/activate/pallas_call | solution.py:277
  44.4 0.0 collective-permute-done.6
  44.4 0.0 collective-permute-done.7
  44.4 1.7 %collective-permute-start.13 = (bf16[96,640]{1,0:T(8,128)(2,1)S(1)}, bf16[96,640]{1,0:T(8,128)(2,1)S(1)}, u32[]{:S(2)}, u32[]{:S(2)}) collective-permute-start(bf16[96,640]{1,0:T(8,128)(2,1)S(1)} %add_convert_fusion.4), channel_id=1, source_target_pairs={{0,8},{2,10},{4,12},{6,14},{8,0},{10,2},{12,4},{14,6},{16,24},{18,... | collective-permute-start | bytes 368648 | tf_op jit(solution)/shard_map/ppermute | solution.py:35
  46.1 0.1 add_convert_fusion.5
  46.2 1.6 %collective-permute-start.12 = (bf16[96,640]{1,0:T(8,128)(2,1)S(1)}, bf16[96,640]{1,0:T(8,128)(2,1)S(1)}, u32[]{:S(2)}, u32[]{:S(2)}) collective-permute-start(bf16[96,640]{1,0:T(8,128)(2,1)S(1)} %get-tuple-element.92), channel_id=1, source_target_pairs={{0,4},{2,6},{4,0},{6,2},{8,12},{10,14},{12,8},{14,10},{16,20},{18,... | collective-permute-start | bytes 368648 | tf_op jit(solution)/shard_map/ppermute | solution.py:35
  47.8 0.3 collective-permute-start.11
  48.1 2.8 %collective-permute-done.4.arrived = bf16[96,1536]{1,0:T(8,128)(2,1)S(1)} collective-permute-done((bf16[96,1536]{1,0:T(8,128)(2,1)S(1)}, bf16[96,1536]{1,0:T(8,128)(2,1)S(1)}, u32[]{:S(2)}, u32[]{:S(2)}) %collective-permute-start.4) | collective-permute-done | bytes 294944 | tf_op jit(solution)/shard_map/ppermute | solution.py:35
  50.9 2.3 %activate.5 = (bf16[384,512]{1,0:T(8,128)(2,1)S(1)}, bf16[384,1024]{1,0:T(8,128)(2,1)S(1)}, bf16[96,1280]{1,0:T(8,128)(2,1)S(1)}, bf16[96,1280]{1,0:T(8,128)(2,1...) custom-call(s32[1]{0:T(128)} %bitcast.place, ...), custom_call_target="tpu_custom_call", output_to_operand_aliasing={{0}: (4, {}), {1}: (5, {}), {2}: (6, {}), {3}: (7, {}), {4}... | custom-call | tf_op jit(solution)/shard_map/activate/pallas_call | solution.py:277
  53.2 0.0 copy-start.3
  53.3 0.1 collective-permute-start.9
  53.3 0.5 collective-permute-start.10
  53.8 0.0 collective-permute-done.13
  53.8 0.0 collective-permute-done.12
  53.8 0.0 collective-permute-done.11
  53.8 0.7 add_convert_fusion
  54.6 0.3 collective-permute-done.9
  54.8 0.7 add_convert_fusion.2
  55.6 2.3 %collective-permute-start.15 = (bf16[96,640]{1,0:T(8,128)(2,1)}, bf16[96,640]{1,0:T(8,128)(2,1)}, u32[]{:S(2)}, u32[]{:S(2)}) collective-permute-start(bf16[96,640]{1,0:T(8,128)(2,1)} %get-tuple-element.91), channel_id=1, source_target_pairs={{0,12},{2,14},{4,8},{6,10},{8,4},{10,6},{12,0},{14,2},{16,28},{18,... | collective-permute-start | bytes 368648 | tf_op jit(solution)/shard_map/ppermute | solution.py:35
  57.9 0.5 collective-permute-start.16
  58.5 0.0 collective-permute-done.10
  58.5 0.7 add_convert_fusion.1
  59.1 0.6 collective-permute-start.17
  59.8 1.2 %collective-permute-start.14 = (bf16[96,640]{1,0:T(8,128)(2,1)}, bf16[96,640]{1,0:T(8,128)(2,1)}, u32[]{:S(2)}, u32[]{:S(2)}) collective-permute-start(bf16[96,640]{1,0:T(8,128)(2,1)} %add_convert_fusion), channel_id=1, source_target_pairs={{0,1},{1,0},{2,3},{3,2},{4,5},{5,4},{6,7},{7,6},{8,9},{9,8},{10,11... | collective-permute-start | bytes 368648 | tf_op jit(solution)/shard_map/ppermute | solution.py:35
  61.0 1.5 %copy-done.2 = bf16[384,2560]{1,0:T(8,128)(2,1)S(1)} copy-done((bf16[384,2560]{1,0:T(8,128)(2,1)S(1)}, bf16[384,2560]{1,0:T(8,128)(2,1)}, u32[]{:S(2)}) %copy-start.2) | copy-done | bytes 1966104
  62.5 2.6 %weight_grad.3 = bf16[512,2560]{1,0:T(8,128)(2,1)} custom-call(bf16[384,512]{1,0:T(8,128)(2,1)S(1)} %get-tuple-element.81.left, bf16[384,2560]{1,0:T(8,128)(2,1)S(1)} %copy-done.2), custom_call_target="tpu_custom_call" | custom-call | flops 1006632960 | tf_op jit(solution)/shard_map/weight_grad/pallas_call | solution.py:314
  65.1 0.0 collective-permute-done.15
  65.1 0.0 collective-permute-done.16
  65.1 0.0 collective-permute-done.17
  65.1 0.0 collective-permute-done.14
  65.1 1.2 %fusion.2 = bf16[96,640]{1,0:T(8,128)(2,1)S(1)} fusion(bf16[96,640]{1,0:T(8,128)(2,1)} %collective-permute-done.14, pred[]{:T(512)S(6)} %eq.7, bf16[96,640]{1,0:T(8,128)(2,1)} %collective-permute-done.17, bf16[96,640]{1,0:T(8,128)(2,1)} %collective-permute-done.16, bf16[96,640]{1,0:T(8,128)(2,1)} %collective-permute-done.15, ...), kind=kLoop, calls=%fused_computation.4 | loop fusion | flops 675840 | bytes 983041 | tf_op jit(solution)/shard_map/convert_element_type | solution.py:438
  66.3 2.7 %collective-permute-start.18 = (bf16[96,640]{1,0:T(8,128)(2,1)S(1)}, bf16[96,640]{1,0:T(8,128)(2,1)S(1)}, u32[]{:S(2)}, u32[]{:S(2)}) collective-permute-start(bf16[96,640]{1,0:T(8,128)(2,1)S(1)} %fusion.2), channel_id=1, source_target_pairs={{0,16},{2,18},{4,20},{6,22},{8,24},{10,26},{12,28},{14,30},{16,0},... | collective-permute-start | bytes 368648 | tf_op jit(solution)/shard_map/ppermute | solution.py:35
  69.0 2.4 %weight_grad.4 = bf16[2560,512]{1,0:T(8,128)(2,1)} custom-call(bf16[384,2560]{1,0:T(8,128)(2,1)S(1)} %get-tuple-element.86.left, bf16[384,1024]{1,0:T(8,128)(2,1)S(1)} %get-tuple-element.88.right), custom_call_target="tpu_custom_call" | custom-call | flops 1006632960 | tf_op jit(solution)/shard_map/weight_grad/pallas_call | solution.py:314
  71.4 2.4 %weight_grad.5 = bf16[2560,512]{1,0:T(8,128)(2,1)} custom-call(bf16[384,2560]{1,0:T(8,128)(2,1)S(1)} %get-tuple-element.86.left, bf16[384,1024]{1,0:T(8,128)(2,1)S(1)} %get-tuple-element.88.right), custom_call_target="tpu_custom_call" | custom-call | flops 1006632960 | tf_op jit(solution)/shard_map/weight_grad/pallas_call | solution.py:314
  73.9 1.0 %collective-permute-done.18 = bf16[96,640]{1,0:T(8,128)(2,1)S(1)} collective-permute-done((bf16[96,640]{1,0:T(8,128)(2,1)S(1)}, bf16[96,640]{1,0:T(8,128)(2,1)S(1)}, u32[]{:S(2)}, u32[]{:S(2)}) %collective-permute-start.18) | collective-permute-done | bytes 122912 | tf_op jit(solution)/shard_map/ppermute | solution.py:35
  74.8 1.2 %fusion.1 = bf16[96,640]{1,0:T(8,128)(2,1)S(1)} fusion(bf16[96,640]{1,0:T(8,128)(2,1)} %collective-permute-done.14, bf16[96,640]{1,0:T(8,128)(2,1)S(1)} %collective-permute-done.18, pred[]{:T(512)S(6)} %eq.6, bf16[96,640]{1,0:T(8,128)(2,1)} %collective-permute-done.17, bf16[96,640]{1,0:T(8,128)(2,1)} %collective-permute-done.16, ...), kind=kLoop, calls=%fused_computation.3 | loop fusion | flops 798720 | bytes 1105921 | tf_op jit(solution)/shard_map/convert_element_type | solution.py:446
  76.0 0.1 fusion.3
  76.1 0.7 pad_maximum_fusion
  (10 shorter events, 0.1 us)
Async XLA Ops:
  0.6 5.0 %copy-start = (f32[512,40]{0,1:T(8,128)S(1)}, f32[512,40]{0,1:T(8,128)}, u32[]{:S(2)}) copy-start(f32[512,40]{0,1:T(8,128)} %param.15) | copy-start | bytes 245764
  0.7 5.3 %copy-start.5 = (f32[40,512]{1,0:T(8,128)S(1)}, f32[40,512]{1,0:T(8,128)}, u32[]{:S(2)}) copy-start(f32[40,512]{1,0:T(8,128)} %gate_scales.1) | copy-start | bytes 245764
  0.7 5.3 %copy-start.6 = (f32[40,512]{1,0:T(8,128)S(1)}, f32[40,512]{1,0:T(8,128)}, u32[]{:S(2)}) copy-start(f32[40,512]{1,0:T(8,128)} %up_scales.1) | copy-start | bytes 245764
  2.6 14.6 %collective-permute-start = (bf16[96,2560]{1,0:T(8,128)(2,1)}, bf16[96,2560]{1,0:T(8,128)(2,1)}, u32[]{:S(2)}, u32[]{:S(2)}) collective-permute-start(bf16[96,2560]{1,0:T(8,128)(2,1)} %fetch.1), channel_id=1, source_target_pairs={{0,1},{1,0},{2,3},{3,2},{4,5},{5,4},{6,7},{7,6},{8,9},{9,8},{10,11... | collective-permute-start | bytes 1474568 | tf_op jit(solution)/shard_map/ppermute | solution.py:35
  17.1 12.6 %collective-permute-start.1 = (bf16[96,2560]{1,0:T(8,128)(2,1)}, bf16[96,2560]{1,0:T(8,128)(2,1)S(1)}, u32[]{:S(2)}, u32[]{:S(2)}) collective-permute-start(bf16[96,2560]{1,0:T(8,128)(2,1)} %collective-permute-done.held), channel_id=1, source_target_pairs={{0,8},{2,10},{4,12},{6,14},{8,0},{10,2},{12,4},{14,6},{16,24},{18,... | collective-permute-start | bytes 1474568 | tf_op jit(solution)/shard_map/ppermute | solution.py:35
  18.9 18.4 %collective-permute-start.5 = (bf16[192,1536]{1,0:T(8,128)(2,1)S(1)}, bf16[192,1536]{1,0:T(8,128)(2,1)S(1)}, u32[]{:S(2)}, u32[]{:S(2)}) collective-permute-start(bf16[192,1536]{1,0:T(8,128)(2,1)S(1)} %get-tuple-element.49), channel_id=1, source_target_pairs={{0,1},{1,0},{2,3},{3,2},{4,5},{5,4},{6,7},{7,6},{8,9},{9,8},{10,11... | collective-permute-start | bytes 1769480 | tf_op jit(solution)/shard_map/ppermute | solution.py:35
  20.5 9.3 %collective-permute-start.3 = (bf16[96,2560]{1,0:T(8,128)(2,1)}, bf16[96,2560]{1,0:T(8,128)(2,1)S(1)}, u32[]{:S(2)}, u32[]{:S(2)}) collective-permute-start(bf16[96,2560]{1,0:T(8,128)(2,1)} %collective-permute-done.held), channel_id=1, source_target_pairs={{0,2},{2,0},{4,6},{6,4},{8,10},{10,8},{12,14},{14,12},{16,18},{18,... | collective-permute-start | bytes 1474568 | tf_op jit(solution)/shard_map/ppermute | solution.py:35
  29.8 4.4 %collective-permute-start.2 = (bf16[96,2560]{1,0:T(8,128)(2,1)S(1)}, bf16[96,2560]{1,0:T(8,128)(2,1)S(1)}, u32[]{:S(2)}, u32[]{:S(2)}) collective-permute-start(bf16[96,2560]{1,0:T(8,128)(2,1)S(1)} %collective-permute-done.1.held), channel_id=1, source_target_pairs={{0,2},{2,0},{4,6},{6,4},{8,10},{10,8},{12,14},{14,12},{16,18},{18,... | collective-permute-start | bytes 1474568 | tf_op jit(solution)/shard_map/ppermute | solution.py:35
  32.7 9.7 %collective-permute-start.8 = (bf16[96,1536]{1,0:T(8,128)(2,1)S(1)}, bf16[96,1536]{1,0:T(8,128)(2,1)S(1)}, u32[]{:S(2)}, u32[]{:S(2)}) collective-permute-start(bf16[96,1536]{1,0:T(8,128)(2,1)S(1)} %get-tuple-element.62), channel_id=1, source_target_pairs={{0,1},{1,0},{2,3},{3,2},{4,5},{5,4},{6,7},{7,6},{8,9},{9,8},{10,11... | collective-permute-start | bytes 884744 | tf_op jit(solution)/shard_map/ppermute | solution.py:35
  36.1 1.3 %copy-start.1 = (bf16[384,2560]{1,0:T(8,128)(2,1)}, bf16[384,2560]{1,0:T(8,128)(2,1)S(1)}, u32[]{:S(2)}) copy-start(bf16[384,2560]{1,0:T(8,128)(2,1)S(1)} %get-tuple-element.82.right) | copy-start | bytes 5898244
  41.2 3.2 %collective-permute-start.6 = (bf16[96,1280]{1,0:T(8,128)(2,1)S(1)}, bf16[96,1280]{1,0:T(8,128)(2,1)S(1)}, u32[]{:S(2)}, u32[]{:S(2)}) collective-permute-start(bf16[96,1280]{1,0:T(8,128)(2,1)S(1)} %get-tuple-element.60), channel_id=1, source_target_pairs={{0,2},{2,0},{4,6},{6,4},{8,10},{10,8},{12,14},{14,12},{16,18},{18,... | collective-permute-start | bytes 737288 | tf_op jit(solution)/shard_map/ppermute | solution.py:35
  41.5 2.9 %collective-permute-start.7 = (bf16[96,1280]{1,0:T(8,128)(2,1)S(1)}, bf16[96,1280]{1,0:T(8,128)(2,1)S(1)}, u32[]{:S(2)}, u32[]{:S(2)}) collective-permute-start(bf16[96,1280]{1,0:T(8,128)(2,1)S(1)} %get-tuple-element.61), channel_id=1, source_target_pairs={{0,2},{2,0},{4,6},{6,4},{8,10},{10,8},{12,14},{14,12},{16,18},{18,... | collective-permute-start | bytes 737288 | tf_op jit(solution)/shard_map/ppermute | solution.py:35
  41.8 9.1 %collective-permute-start.4 = (bf16[96,1536]{1,0:T(8,128)(2,1)S(1)}, bf16[96,1536]{1,0:T(8,128)(2,1)S(1)}, u32[]{:S(2)}, u32[]{:S(2)}) collective-permute-start(bf16[96,1536]{1,0:T(8,128)(2,1)S(1)} %get-tuple-element.57), channel_id=1, source_target_pairs={{0,1},{1,0},{2,3},{3,2},{4,5},{5,4},{6,7},{7,6},{8,9},{9,8},{10,11... | collective-permute-start | bytes 884744 | tf_op jit(solution)/shard_map/ppermute | solution.py:35
  44.4 9.4 %collective-permute-start.13 = (bf16[96,640]{1,0:T(8,128)(2,1)S(1)}, bf16[96,640]{1,0:T(8,128)(2,1)S(1)}, u32[]{:S(2)}, u32[]{:S(2)}) collective-permute-start(bf16[96,640]{1,0:T(8,128)(2,1)S(1)} %add_convert_fusion.4), channel_id=1, source_target_pairs={{0,8},{2,10},{4,12},{6,14},{8,0},{10,2},{12,4},{14,6},{16,24},{18,... | collective-permute-start | bytes 368648 | tf_op jit(solution)/shard_map/ppermute | solution.py:35
  46.2 7.6 %collective-permute-start.12 = (bf16[96,640]{1,0:T(8,128)(2,1)S(1)}, bf16[96,640]{1,0:T(8,128)(2,1)S(1)}, u32[]{:S(2)}, u32[]{:S(2)}) collective-permute-start(bf16[96,640]{1,0:T(8,128)(2,1)S(1)} %get-tuple-element.92), channel_id=1, source_target_pairs={{0,4},{2,6},{4,0},{6,2},{8,12},{10,14},{12,8},{14,10},{16,20},{18,... | collective-permute-start | bytes 368648 | tf_op jit(solution)/shard_map/ppermute | solution.py:35
  47.8 6.1 %collective-permute-start.11 = (bf16[96,640]{1,0:T(8,128)(2,1)S(1)}, bf16[96,640]{1,0:T(8,128)(2,1)S(1)}, u32[]{:S(2)}, u32[]{:S(2)}) collective-permute-start(bf16[96,640]{1,0:T(8,128)(2,1)S(1)} %get-tuple-element.93), channel_id=1, source_target_pairs={{0,12},{2,14},{4,8},{6,10},{8,4},{10,6},{12,0},{14,2},{16,28},{18,... | collective-permute-start | bytes 368648 | tf_op jit(solution)/shard_map/ppermute | solution.py:35
  53.2 5.2 %copy-start.3 = (f32[96,1280]{1,0:T(8,128)}, f32[96,1280]{1,0:T(8,128)S(1)}, u32[]{:S(2)}) copy-start(f32[96,1280]{1,0:T(8,128)S(1)} %get-tuple-element.78) | copy-start | bytes 1474564
  53.3 1.6 %collective-permute-start.9 = (bf16[96,1280]{1,0:T(8,128)(2,1)S(1)}, bf16[96,1280]{1,0:T(8,128)(2,1)S(1)}, u32[]{:S(2)}, u32[]{:S(2)}) collective-permute-start(bf16[96,1280]{1,0:T(8,128)(2,1)S(1)} %get-tuple-element.77), channel_id=1, source_target_pairs={{0,2},{2,0},{4,6},{6,4},{8,10},{10,8},{12,14},{14,12},{16,18},{18,... | collective-permute-start | bytes 737288 | tf_op jit(solution)/shard_map/ppermute | solution.py:35
  53.3 5.1 %collective-permute-start.10 = (bf16[96,1280]{1,0:T(8,128)(2,1)S(1)}, bf16[96,1280]{1,0:T(8,128)(2,1)S(1)}, u32[]{:S(2)}, u32[]{:S(2)}) collective-permute-start(bf16[96,1280]{1,0:T(8,128)(2,1)S(1)} %get-tuple-element.79), channel_id=1, source_target_pairs={{0,2},{2,0},{4,6},{6,4},{8,10},{10,8},{12,14},{14,12},{16,18},{18,... | collective-permute-start | bytes 737288 | tf_op jit(solution)/shard_map/ppermute | solution.py:35
  55.6 9.5 %collective-permute-start.15 = (bf16[96,640]{1,0:T(8,128)(2,1)}, bf16[96,640]{1,0:T(8,128)(2,1)}, u32[]{:S(2)}, u32[]{:S(2)}) collective-permute-start(bf16[96,640]{1,0:T(8,128)(2,1)} %get-tuple-element.91), channel_id=1, source_target_pairs={{0,12},{2,14},{4,8},{6,10},{8,4},{10,6},{12,0},{14,2},{16,28},{18,... | collective-permute-start | bytes 368648 | tf_op jit(solution)/shard_map/ppermute | solution.py:35
  57.9 7.2 %collective-permute-start.16 = (bf16[96,640]{1,0:T(8,128)(2,1)}, bf16[96,640]{1,0:T(8,128)(2,1)}, u32[]{:S(2)}, u32[]{:S(2)}) collective-permute-start(bf16[96,640]{1,0:T(8,128)(2,1)} %get-tuple-element.90), channel_id=1, source_target_pairs={{0,4},{2,6},{4,0},{6,2},{8,12},{10,14},{12,8},{14,10},{16,20},{18,... | collective-permute-start | bytes 368648 | tf_op jit(solution)/shard_map/ppermute | solution.py:35
  59.1 6.0 %collective-permute-start.17 = (bf16[96,640]{1,0:T(8,128)(2,1)}, bf16[96,640]{1,0:T(8,128)(2,1)}, u32[]{:S(2)}, u32[]{:S(2)}) collective-permute-start(bf16[96,640]{1,0:T(8,128)(2,1)} %add_convert_fusion.1), channel_id=1, source_target_pairs={{0,8},{2,10},{4,12},{6,14},{8,0},{10,2},{12,4},{14,6},{16,24},{18,... | collective-permute-start | bytes 368648 | tf_op jit(solution)/shard_map/ppermute | solution.py:35
  59.8 5.4 %collective-permute-start.14 = (bf16[96,640]{1,0:T(8,128)(2,1)}, bf16[96,640]{1,0:T(8,128)(2,1)}, u32[]{:S(2)}, u32[]{:S(2)}) collective-permute-start(bf16[96,640]{1,0:T(8,128)(2,1)} %add_convert_fusion), channel_id=1, source_target_pairs={{0,1},{1,0},{2,3},{3,2},{4,5},{5,4},{6,7},{7,6},{8,9},{9,8},{10,11... | collective-permute-start | bytes 368648 | tf_op jit(solution)/shard_map/ppermute | solution.py:35
  61.0 1.5 %copy-start.2 = (bf16[384,2560]{1,0:T(8,128)(2,1)S(1)}, bf16[384,2560]{1,0:T(8,128)(2,1)}, u32[]{:S(2)}) copy-start(bf16[384,2560]{1,0:T(8,128)(2,1)} %copy-done.1) | copy-start | bytes 5898244
  62.5 2.6 %copy-start.4 = (f32[96,1280]{1,0:T(8,128)S(1)}, f32[96,1280]{1,0:T(8,128)}, u32[]{:S(2)}) copy-start(f32[96,1280]{1,0:T(8,128)} %copy-done.3) | copy-start | bytes 1474564
  66.3 8.5 %collective-permute-start.18 = (bf16[96,640]{1,0:T(8,128)(2,1)S(1)}, bf16[96,640]{1,0:T(8,128)(2,1)S(1)}, u32[]{:S(2)}, u32[]{:S(2)}) collective-permute-start(bf16[96,640]{1,0:T(8,128)(2,1)S(1)} %fusion.2), channel_id=1, source_target_pairs={{0,16},{2,18},{4,20},{6,22},{8,24},{10,26},{12,28},{14,30},{16,0},... | collective-permute-start | bytes 368648 | tf_op jit(solution)/shard_map/ppermute | solution.py:35

commit v4 on v3

--- a/solution.py
+++ b/solution.py
@@ -291,36 +291,44 @@
     )(place, *(in_vmem(a) for a in (weights, total, arrived, *before)))
 
 
-def grads_kernel(first, by_rows, left, right, target, held, sems):
-    wide = left if by_rows else right
+def grads_kernel(tokens, cot, act, d_inner, gate_grad, up_grad, down_grad, gate_held, up_held, down_held, sems):
+    rows, units = gate_grad.shape
     copies = []
-    for step in range(wide.shape[1] // STEP):
+
+    def send(held, target, part, i):
+        copies.append(pltpu.make_async_copy(held.at[part], target.at[part], sems.at[i]))
+        copies[-1].start()
+
+    steps = rows // STEP
+    for step in range(steps):
         part = slice(step * STEP, (step + 1) * STEP)
-        if by_rows:
-            index = (part, slice(None))
-            held[index] = contract(left[:, part], right[:, first : first + target.shape[1]]).astype(held.dtype)
-        else:
-            index = (slice(None), part)
-            held[index] = contract(left[...], right[:, part]).astype(held.dtype)
-        copies.append(pltpu.make_async_copy(held.at[index], target.at[index], sems.at[step]))
-        copies[-1].start()
+        both = contract(tokens[:, part], d_inner[...])
+        gate_held[part, :] = both[:, :units].astype(gate_held.dtype)
+        send(gate_held, gate_grad, (part, slice(None)), step)
+        up_held[part, :] = both[:, units:].astype(up_held.dtype)
+        send(up_held, up_grad, (part, slice(None)), steps + step)
+    for step in range(steps):
+        part = slice(step * STEP, (step + 1) * STEP)
+        down_held[:, part] = contract(act[...], cot[:, part]).astype(down_held.dtype)
+        send(down_held, down_grad, (slice(None), part), 2 * steps + step)
     for copy in copies:
         copy.wait()
 
 
-def weight_grad(left, right, first, units, by_rows):
-    rows = (left if by_rows else right).shape[1]
-    shape = (rows, units) if by_rows else (units, rows)
+def weight_grads(tokens, cot, act, d_inner):
+    rows, units = tokens.shape[1], act.shape[1]
+    shapes = [(rows, units), (rows, units), (units, rows)]
     return pl.pallas_call(
-        functools.partial(grads_kernel, first, by_rows),
-        in_specs=[IN_VMEM] * 2,
-        out_specs=IN_HBM,
-        out_shape=pltpu.HBM(shape, jnp.bfloat16),
-        scratch_shapes=[pltpu.VMEM(shape, jnp.bfloat16), pltpu.SemaphoreType.DMA((rows // STEP,))],
-        compiler_params=grant(6),
-        cost_estimate=cost(2 * left.shape[0] * rows * units),
-        name="weight_grad",
-    )(in_vmem(left), in_vmem(right))
+        grads_kernel,
+        in_specs=[IN_VMEM] * 4,
+        out_specs=[IN_HBM] * 3,
+        out_shape=[pltpu.HBM(shape, jnp.bfloat16) for shape in shapes],
+        scratch_shapes=[pltpu.VMEM(shape, jnp.bfloat16) for shape in shapes]
+        + [pltpu.SemaphoreType.DMA((3 * (rows // STEP),))],
+        compiler_params=grant(20),
+        cost_estimate=cost(6 * tokens.shape[0] * rows * units),
+        name="weight_grads",
+    )(*(in_vmem(a) for a in (tokens, cot, act, d_inner)))
 
 
 def after(value, *earlier):
@@ -425,8 +433,7 @@
         value = add(*blocks[k]).astype(jnp.bfloat16)
         act, sent, value = lax.optimization_barrier((act, sent, value))
         blocks[k] = swap(value, "node", nodes, k).astype(jnp.float32)
-    down_grad = weight_grad(after(act, sent), all_cots, 0, units, False)
-    blocks[0] = add(mine, after(got, down_grad))
+    blocks[0] = add(mine, after(got, sent))
     high = place // owners
 
     def block_for(owner):
@@ -436,12 +443,11 @@
         return chosen
 
     sent = [block_for(high ^ j).astype(jnp.bfloat16) for j in range(1, nodes)]
-    d_inner = after(d_inner, sent)
-    gate_grad = weight_grad(all_tokens, d_inner, 0, units, True)
-    up_grad = weight_grad(all_tokens, d_inner, units, units, True)
+    act, d_inner = after((act, d_inner), sent)
+    gate_grad, up_grad, down_grad = weight_grads(all_tokens, all_cots, act, d_inner)
     token_grad = block_for(high)
     for j in range(1, nodes):
-        arrived = after(swap(sent[j - 1], "dp", width, j * owners), gate_grad, up_grad)
+        arrived = after(swap(sent[j - 1], "dp", width, j * owners), gate_grad)
         token_grad += arrived.astype(jnp.float32)
     token_grad = token_grad.astype(jnp.bfloat16)
     token_grad = jnp.concatenate([token_grad[:, :block], token_grad[:, block:]])

time: 77.1 us -> 79.9 us (1.036)
  waiting for transfers between devices: 18 us -> 21 us
  Pallas kernels: 28.8 us -> 26.7 us
  local copies, waits for them, and re-layouts: 3.3 us -> 4.3 us
  other arithmetic: 5.3 us -> 6.17 us
    ppermute x19, waiting for transfers between devices: 18 us -> 21 us  [swap(): return lax.ppermute(value, axis, flipped(size, mask))]
    pallas_call x3 -> x1, Pallas kernels: 7.42 us -> 5.36 us  [weight_grads(): pl.pallas_call(grads_kernel, in_specs=[IN_VMEM] * 4, out_specs=[IN_HBM] *...]
    unnamed x14, local copies, waits for them, and re-layouts: 2.84 us -> 3.83 us
    convert_element_type x4, other arithmetic: 1.51 us -> 2.4 us  [split(): sending.append((mask, both.astype(jnp.bfloat16)))]
  transfers between devices with their start and end apart: 19 -> 19, of which waited for: 5 -> 8; matrix products, arithmetic and copies ran while one was open for 3% -> 4% of each run, Pallas kernels for 35% -> 31%
where the time goes in v4:
time: 79.9 us; the launch traced here: 79.6 us
  Pallas kernels  26.7 us (33%)
  waiting for transfers between devices  21 us (26%)
  starting transfers between devices  20.6 us (26%)
  other arithmetic  6.17 us (8%)
  local copies, waits for them, and re-layouts  4.3 us (5%)
  between operations  0.85 us (1%)
    ppermute x19, waiting for transfers between devices, swap(): return lax.ppermute(value, axis, flipped(size, mask))  21 us
    ppermute x19, starting transfers between devices, swap(): return lax.ppermute(value, axis, flipped(size, mask))  20.6 us
    pallas_call x3, Pallas kernels, activate(): pl.pallas_call(functools.partial(activate_kernel, group, turns, count, bl...  8.09 us
    pallas_call x1, Pallas kernels, prepare(): pl.pallas_call(prepare_kernel, in_specs=[IN_SMEM] + [IN_HBM] * 5 + [IN_VM...  6.54 us
    pallas_call x1, Pallas kernels, weight_grads(): pl.pallas_call(grads_kernel, in_specs=[IN_VMEM] * 4, out_specs=[IN_HBM] *...  5.36 us
    pallas_call x2, Pallas kernels, join(): pl.pallas_call(functools.partial(join_kernel, group, far), in_specs=[IN_S...  4.82 us
    unnamed x14, local copies, waits for them, and re-layouts  3.83 us
    convert_element_type x4, other arithmetic, split(): sending.append((mask, both.astype(jnp.bfloat16)))  2.4 us
  transfers between devices with their start and end apart: 19, of which 8 were waited for; matrix products, arithmetic and copies ran while one was open for 4% of the time, Pallas kernels for 31%

profile of v4, /device:TPU:0, one launch (start us, length us, event | category | flops | bytes accessed | tf_op | source)
XLA Modules:
  0.0 79.6 jit_solution(16189972035215163780)
XLA Ops:
  0.6 0.0 copy-start
  0.7 0.0 copy-start.5
  0.7 0.0 copy-start.6
  0.7 1.9 %fetch.1 = bf16[96,2560]{1,0:T(8,128)(2,1)} custom-call(s32[1]{0:T(128)} %bitcast.1.node, s32[1]{0:T(128)} %bitcast.place, bf16[192,5120]{1,0:T(8,128)(2,1)} %tokens.3, bf16[192,5120]{1,0:T(8,128)(2,1)} %cot.3), custom_call_target="tpu_custom_call" | custom-call | tf_op jit(solution)/shard_map/fetch/pallas_call | solution.py:78
  2.6 3.0 %collective-permute-start = (bf16[96,2560]{1,0:T(8,128)(2,1)}, bf16[96,2560]{1,0:T(8,128)(2,1)}, u32[]{:S(2)}, u32[]{:S(2)}) collective-permute-start(bf16[96,2560]{1,0:T(8,128)(2,1)} %fetch.1), channel_id=1, source_target_pairs={{0,1},{1,0},{2,3},{3,2},{4,5},{5,4},{6,7},{7,6},{8,9},{9,8},{10,11... | collective-permute-start | bytes 1474568 | tf_op jit(solution)/shard_map/ppermute | solution.py:35
  5.6 0.0 copy-done
  5.6 0.4 copy.25
  6.0 0.0 copy-done.5
  6.0 6.5 %prepare.1 = (bf16[384,2560]{1,0:T(8,128)(2,1)S(1)}, bf16[384,2560]{1,0:T(8,128)(2,1)S(1)}, bf16[2560,1024]{1,0:T(8,128)(2,1)S(1)}, bf16[512,2560]{1,0:T(8,128)(...) custom-call(s32[1]{0:T(128)} %bitcast.1.node, bf16[192,5120]{1,0:T(8,128)(2,1)} %tokens.3, ...), custom_call_target="tpu_custom_call" | custom-call | tf_op jit(solution)/shard_map/prepare/pallas_call | solution.py:145
  12.6 4.6 %collective-permute-done.held = bf16[96,2560]{1,0:T(8,128)(2,1)} collective-permute-done((bf16[96,2560]{1,0:T(8,128)(2,1)}, bf16[96,2560]{1,0:T(8,128)(2,1)}, u32[]{:S(2)}, u32[]{:S(2)}) %collective-permute-start) | collective-permute-done | bytes 491552 | tf_op jit(solution)/shard_map/ppermute | solution.py:35
  17.1 1.8 %collective-permute-start.1 = (bf16[96,2560]{1,0:T(8,128)(2,1)}, bf16[96,2560]{1,0:T(8,128)(2,1)S(1)}, u32[]{:S(2)}, u32[]{:S(2)}) collective-permute-start(bf16[96,2560]{1,0:T(8,128)(2,1)} %collective-permute-done.held), channel_id=1, source_target_pairs={{0,8},{2,10},{4,12},{6,14},{8,0},{10,2},{12,4},{14,6},{16,24},{18,... | collective-permute-start | bytes 1474568 | tf_op jit(solution)/shard_map/ppermute | solution.py:35
  18.9 1.5 %collective-permute-start.5 = (bf16[192,1536]{1,0:T(8,128)(2,1)S(1)}, bf16[192,1536]{1,0:T(8,128)(2,1)S(1)}, u32[]{:S(2)}, u32[]{:S(2)}) collective-permute-start(bf16[192,1536]{1,0:T(8,128)(2,1)S(1)} %get-tuple-element.53), channel_id=1, source_target_pairs={{0,1},{1,0},{2,3},{3,2},{4,5},{5,4},{6,7},{7,6},{8,9},{9,8},{10,11... | collective-permute-start | bytes 1769480 | tf_op jit(solution)/shard_map/ppermute | solution.py:35
  20.5 0.0 collective-permute-start.3
  20.5 9.3 %collective-permute-done.1.held = bf16[96,2560]{1,0:T(8,128)(2,1)S(1)} collective-permute-done((bf16[96,2560]{1,0:T(8,128)(2,1)}, bf16[96,2560]{1,0:T(8,128)(2,1)S(1)}, u32[]{:S(2)}, u32[]{:S(2)}) %collective-permute-start.1) | collective-permute-done | bytes 491552 | tf_op jit(solution)/shard_map/ppermute | solution.py:35
  29.8 0.0 collective-permute-start.2
  29.8 0.0 collective-permute-done.3.given
  29.8 2.9 %join.2 = (bf16[384,2560]{1,0:T(8,128)(2,1)S(1)}, bf16[384,2560]{1,0:T(8,128)(2,1)S(1)}, f32[192,1536]{1,0:T(8,128)S(1)}, bf16[96,1536]{1,0:T(8,128)(2,1)S(1)}) custom-call(s32[1]{0:T(128)} %bitcast.place, bf16[96,2560]{1,0:T(8,128)(2,1)} %collective-permute-done.held, ...), custom_call_target="tpu_custom_call", output_to_operand_aliasing={{0}: (5, {}), {1}: (6, {})} | custom-call | tf_op jit(solution)/shard_map/join/pallas_call | solution.py:202
  32.7 1.5 %collective-permute-start.8 = (bf16[96,1536]{1,0:T(8,128)(2,1)S(1)}, bf16[96,1536]{1,0:T(8,128)(2,1)S(1)}, u32[]{:S(2)}, u32[]{:S(2)}) collective-permute-start(bf16[96,1536]{1,0:T(8,128)(2,1)S(1)} %get-tuple-element.66), channel_id=1, source_target_pairs={{0,1},{1,0},{2,3},{3,2},{4,5},{5,4},{6,7},{7,6},{8,9},{9,8},{10,11... | collective-permute-start | bytes 884744 | tf_op jit(solution)/shard_map/ppermute | solution.py:35
  34.2 0.0 collective-permute-done.2.given
  34.2 1.9 %join.3 = (bf16[384,2560]{1,0:T(8,128)(2,1)S(1)}, bf16[384,2560]{1,0:T(8,128)(2,1)S(1)}, f32[192,1536]{1,0:T(8,128)S(1)}, bf16[96,1536]{1,0:T(8,128)(2,1)S(1)}) custom-call(s32[1]{0:T(128)} %bitcast.place, bf16[96,2560]{1,0:T(8,128)(2,1)S(1)} %collective-permute-done.1.held, ...), custom_call_target="tpu_custom_call", output_to_operand_aliasing={{0}: (5, {}), {1}: (6, {}), {2}: (7, {})} | custom-call | tf_op jit(solution)/shard_map/join/pallas_call | solution.py:202
  36.1 0.0 copy-start.1
  36.1 1.3 %copy-done.1 = bf16[384,2560]{1,0:T(8,128)(2,1)} copy-done((bf16[384,2560]{1,0:T(8,128)(2,1)}, bf16[384,2560]{1,0:T(8,128)(2,1)S(1)}, u32[]{:S(2)}) %copy-start.1) | copy-done | bytes 1966104
  37.4 0.0 collective-permute-done.5.arrived
  37.4 3.8 %activate.3 = (bf16[384,512]{1,0:T(8,128)(2,1)S(1)}, bf16[384,1024]{1,0:T(8,128)(2,1)S(1)}, bf16[96,1280]{1,0:T(8,128)(2,1)S(1)}, bf16[96,1280]{1,0:T(8,128)(2,1...) custom-call(s32[1]{0:T(128)} %bitcast.place, bf16[2560,1024]{1,0:T(8,128)(2,1)S(1)} %get-tuple-element.51.w_in.weights, ...), custom_call_target="tpu_custom_call" | custom-call | tf_op jit(solution)/shard_map/activate/pallas_call | solution.py:277
  41.2 0.3 collective-permute-start.6
  41.5 0.3 collective-permute-start.7
  41.8 0.6 collective-permute-start.4
  42.4 0.0 collective-permute-done.8.arrived
  42.4 2.0 %activate.4 = (bf16[384,512]{1,0:T(8,128)(2,1)S(1)}, bf16[384,1024]{1,0:T(8,128)(2,1)S(1)}, bf16[96,1280]{1,0:T(8,128)(2,1)S(1)}, bf16[96,1280]{1,0:T(8,128)(2,1...) custom-call(s32[1]{0:T(128)} %bitcast.place, ...), custom_call_target="tpu_custom_call", output_to_operand_aliasing={{0}: (4, {}), {1}: (5, {})} | custom-call | tf_op jit(solution)/shard_map/activate/pallas_call | solution.py:277
  44.3 0.0 collective-permute-done.6
  44.4 0.0 collective-permute-done.7
  44.4 1.7 %collective-permute-start.13 = (bf16[96,640]{1,0:T(8,128)(2,1)S(1)}, bf16[96,640]{1,0:T(8,128)(2,1)S(1)}, u32[]{:S(2)}, u32[]{:S(2)}) collective-permute-start(bf16[96,640]{1,0:T(8,128)(2,1)S(1)} %add_convert_fusion.4), channel_id=1, source_target_pairs={{0,8},{2,10},{4,12},{6,14},{8,0},{10,2},{12,4},{14,6},{16,24},{18,... | collective-permute-start | bytes 368648 | tf_op jit(solution)/shard_map/ppermute | solution.py:35
  46.2 1.6 %collective-permute-start.12 = (bf16[96,640]{1,0:T(8,128)(2,1)S(1)}, bf16[96,640]{1,0:T(8,128)(2,1)S(1)}, u32[]{:S(2)}, u32[]{:S(2)}) collective-permute-start(bf16[96,640]{1,0:T(8,128)(2,1)S(1)} %get-tuple-element.100), channel_id=1, source_target_pairs={{0,4},{2,6},{4,0},{6,2},{8,12},{10,14},{12,8},{14,10},{16,20},{18,... | collective-permute-start | bytes 368648 | tf_op jit(solution)/shard_map/ppermute | solution.py:35
  47.7 0.3 collective-permute-start.11
  48.1 2.8 %collective-permute-done.4.arrived = bf16[96,1536]{1,0:T(8,128)(2,1)S(1)} collective-permute-done((bf16[96,1536]{1,0:T(8,128)(2,1)S(1)}, bf16[96,1536]{1,0:T(8,128)(2,1)S(1)}, u32[]{:S(2)}, u32[]{:S(2)}) %collective-permute-start.4) | collective-permute-done | bytes 294944 | tf_op jit(solution)/shard_map/ppermute | solution.py:35
  50.9 2.3 %activate.5 = (bf16[384,512]{1,0:T(8,128)(2,1)S(1)}, bf16[384,1024]{1,0:T(8,128)(2,1)S(1)}, bf16[96,1280]{1,0:T(8,128)(2,1)S(1)}, bf16[96,1280]{1,0:T(8,128)(2,1...) custom-call(s32[1]{0:T(128)} %bitcast.place, ...), custom_call_target="tpu_custom_call", output_to_operand_aliasing={{0}: (4, {}), {1}: (5, {}), {2}: (6, {}), {3}: (7, {}), {4}... | custom-call | tf_op jit(solution)/shard_map/activate/pallas_call | solution.py:277
  53.2 0.0 copy-start.3
  53.2 0.1 collective-permute-start.9
  53.3 0.5 collective-permute-start.10
  53.8 0.0 collective-permute-done.13
  53.8 0.0 collective-permute-done.12
  53.8 0.0 collective-permute-done.11
  53.8 0.7 add_convert_fusion
  54.6 0.3 collective-permute-done.9
  54.8 0.8 add_convert_fusion.2
  55.6 2.3 %collective-permute-start.15 = (bf16[96,640]{1,0:T(8,128)(2,1)}, bf16[96,640]{1,0:T(8,128)(2,1)S(1)}, u32[]{:S(2)}, u32[]{:S(2)}) collective-permute-start(bf16[96,640]{1,0:T(8,128)(2,1)} %get-tuple-element.99), channel_id=1, source_target_pairs={{0,12},{2,14},{4,8},{6,10},{8,4},{10,6},{12,0},{14,2},{16,28},{18,... | collective-permute-start | bytes 368648 | tf_op jit(solution)/shard_map/ppermute | solution.py:35
  57.9 0.5 collective-permute-start.16
  58.5 0.0 collective-permute-done.10
  58.5 1.6 %add_convert_fusion.1 = bf16[96,640]{1,0:T(8,128)(2,1)} fusion(f32[96,1280]{1,0:T(8,128)S(1)} %get-tuple-element.82, bf16[96,1280]{1,0:T(8,128)(2,1)} %collective-permute-done.10), kind=kLoop, calls=%fused_computation.7 | loop fusion | flops 184320 | bytes 491520 | tf_op jit(solution)/shard_map/convert_element_type | solution.py:403
  60.0 0.6 collective-permute-start.17
  60.6 1.2 %collective-permute-start.14 = (bf16[96,640]{1,0:T(8,128)(2,1)}, bf16[96,640]{1,0:T(8,128)(2,1)}, u32[]{:S(2)}, u32[]{:S(2)}) collective-permute-start(bf16[96,640]{1,0:T(8,128)(2,1)} %add_convert_fusion), channel_id=1, source_target_pairs={{0,1},{1,0},{2,3},{3,2},{4,5},{5,4},{6,7},{7,6},{8,9},{9,8},{10,11... | collective-permute-start | bytes 368648 | tf_op jit(solution)/shard_map/ppermute | solution.py:35
  61.8 0.3 collective-permute-done.15
  62.1 2.6 %collective-permute-done.16 = bf16[96,640]{1,0:T(8,128)(2,1)} collective-permute-done((bf16[96,640]{1,0:T(8,128)(2,1)}, bf16[96,640]{1,0:T(8,128)(2,1)}, u32[]{:S(2)}, u32[]{:S(2)}) %collective-permute-start.16) | collective-permute-done | bytes 122912 | tf_op jit(solution)/shard_map/ppermute | solution.py:35
  64.8 0.4 collective-permute-done.17
  65.2 0.6 collective-permute-done.14
  65.8 1.2 %fusion.2 = bf16[96,640]{1,0:T(8,128)(2,1)S(1)} fusion(bf16[96,640]{1,0:T(8,128)(2,1)} %collective-permute-done.14, pred[]{:T(512)S(6)} %eq.7, bf16[96,640]{1,0:T(8,128)(2,1)} %collective-permute-done.17, bf16[96,640]{1,0:T(8,128)(2,1)} %collective-permute-done.16, bf16[96,640]{1,0:T(8,128)(2,1)S(1)} %collective-permute-done.15, ...), kind=kLoop, calls=%fused_computation.4 | loop fusion | flops 675840 | bytes 983041 | tf_op jit(solution)/shard_map/convert_element_type | solution.py:445
  67.0 2.7 %collective-permute-start.18 = (bf16[96,640]{1,0:T(8,128)(2,1)S(1)}, bf16[96,640]{1,0:T(8,128)(2,1)S(1)}, u32[]{:S(2)}, u32[]{:S(2)}) collective-permute-start(bf16[96,640]{1,0:T(8,128)(2,1)S(1)} %fusion.2), channel_id=1, source_target_pairs={{0,16},{2,18},{4,20},{6,22},{8,24},{10,26},{12,28},{14,30},{16,0},... | collective-permute-start | bytes 368648 | tf_op jit(solution)/shard_map/ppermute | solution.py:35
  69.7 1.5 %copy-done.2 = bf16[384,2560]{1,0:T(8,128)(2,1)S(1)} copy-done((bf16[384,2560]{1,0:T(8,128)(2,1)S(1)}, bf16[384,2560]{1,0:T(8,128)(2,1)}, u32[]{:S(2)}) %copy-start.2) | copy-done | bytes 1966104
  71.2 1.0 %copy-done.4 = bf16[384,512]{1,0:T(8,128)(2,1)S(1)} copy-done((bf16[384,512]{1,0:T(8,128)(2,1)S(1)}, bf16[384,512]{1,0:T(8,128)(2,1)}, u32[]{:S(2)}) %copy-start.4) | copy-done | bytes 393240
  72.2 5.4 %weight_grads.1 = (bf16[2560,512]{1,0:T(8,128)(2,1)}, bf16[2560,512]{1,0:T(8,128)(2,1)}, bf16[512,2560]{1,0:T(8,128)(2,1)}) custom-call(bf16[384,2560]{1,0:T(8,128)(2,1)S(1)} %get-tuple-element.88.tokens, bf16[384,2560]{1,0:T(8,128)(2,1)S(1)} %copy-done.2, bf16[384,512]{1,0:T(8,128)(2,1)S(1)} %copy-done.4, bf16[384,1024]{1,0:T(8,128)(2,1)S(1)} %get-tuple-element.93.d_inner), custom_call_target="tpu_custom_call" | custom-call | flops 3019898880 | tf_op jit(solution)/shard_map/weight_grads/pallas_call | solution.py:321
  77.6 0.0 collective-permute-done.18
  77.6 1.2 %fusion.1 = bf16[96,640]{1,0:T(8,128)(2,1)S(1)} fusion(bf16[96,640]{1,0:T(8,128)(2,1)} %collective-permute-done.14, bf16[96,640]{1,0:T(8,128)(2,1)S(1)} %collective-permute-done.18, pred[]{:T(512)S(6)} %eq.6, bf16[96,640]{1,0:T(8,128)(2,1)} %collective-permute-done.17, bf16[96,640]{1,0:T(8,128)(2,1)} %collective-permute-done.16, ...), kind=kLoop, calls=%fused_computation.3 | loop fusion | flops 798720 | bytes 1105921 | tf_op jit(solution)/shard_map/convert_element_type | solution.py:452
  78.8 0.1 fusion.3
  78.9 0.7 pad_maximum_fusion
  (8 shorter events, 0.1 us)
Async XLA Ops:
  0.6 5.0 %copy-start = (f32[512,40]{0,1:T(8,128)S(1)}, f32[512,40]{0,1:T(8,128)}, u32[]{:S(2)}) copy-start(f32[512,40]{0,1:T(8,128)} %param.15) | copy-start | bytes 245764
  0.7 5.3 %copy-start.5 = (f32[40,512]{1,0:T(8,128)S(1)}, f32[40,512]{1,0:T(8,128)}, u32[]{:S(2)}) copy-start(f32[40,512]{1,0:T(8,128)} %gate_scales.1) | copy-start | bytes 245764
  0.7 5.3 %copy-start.6 = (f32[40,512]{1,0:T(8,128)S(1)}, f32[40,512]{1,0:T(8,128)}, u32[]{:S(2)}) copy-start(f32[40,512]{1,0:T(8,128)} %up_scales.1) | copy-start | bytes 245764
  2.6 14.6 %collective-permute-start = (bf16[96,2560]{1,0:T(8,128)(2,1)}, bf16[96,2560]{1,0:T(8,128)(2,1)}, u32[]{:S(2)}, u32[]{:S(2)}) collective-permute-start(bf16[96,2560]{1,0:T(8,128)(2,1)} %fetch.1), channel_id=1, source_target_pairs={{0,1},{1,0},{2,3},{3,2},{4,5},{5,4},{6,7},{7,6},{8,9},{9,8},{10,11... | collective-permute-start | bytes 1474568 | tf_op jit(solution)/shard_map/ppermute | solution.py:35
  17.1 12.6 %collective-permute-start.1 = (bf16[96,2560]{1,0:T(8,128)(2,1)}, bf16[96,2560]{1,0:T(8,128)(2,1)S(1)}, u32[]{:S(2)}, u32[]{:S(2)}) collective-permute-start(bf16[96,2560]{1,0:T(8,128)(2,1)} %collective-permute-done.held), channel_id=1, source_target_pairs={{0,8},{2,10},{4,12},{6,14},{8,0},{10,2},{12,4},{14,6},{16,24},{18,... | collective-permute-start | bytes 1474568 | tf_op jit(solution)/shard_map/ppermute | solution.py:35
  18.9 18.4 %collective-permute-start.5 = (bf16[192,1536]{1,0:T(8,128)(2,1)S(1)}, bf16[192,1536]{1,0:T(8,128)(2,1)S(1)}, u32[]{:S(2)}, u32[]{:S(2)}) collective-permute-start(bf16[192,1536]{1,0:T(8,128)(2,1)S(1)} %get-tuple-element.53), channel_id=1, source_target_pairs={{0,1},{1,0},{2,3},{3,2},{4,5},{5,4},{6,7},{7,6},{8,9},{9,8},{10,11... | collective-permute-start | bytes 1769480 | tf_op jit(solution)/shard_map/ppermute | solution.py:35
  20.5 9.3 %collective-permute-start.3 = (bf16[96,2560]{1,0:T(8,128)(2,1)}, bf16[96,2560]{1,0:T(8,128)(2,1)S(1)}, u32[]{:S(2)}, u32[]{:S(2)}) collective-permute-start(bf16[96,2560]{1,0:T(8,128)(2,1)} %collective-permute-done.held), channel_id=1, source_target_pairs={{0,2},{2,0},{4,6},{6,4},{8,10},{10,8},{12,14},{14,12},{16,18},{18,... | collective-permute-start | bytes 1474568 | tf_op jit(solution)/shard_map/ppermute | solution.py:35
  29.8 4.4 %collective-permute-start.2 = (bf16[96,2560]{1,0:T(8,128)(2,1)S(1)}, bf16[96,2560]{1,0:T(8,128)(2,1)S(1)}, u32[]{:S(2)}, u32[]{:S(2)}) collective-permute-start(bf16[96,2560]{1,0:T(8,128)(2,1)S(1)} %collective-permute-done.1.held), channel_id=1, source_target_pairs={{0,2},{2,0},{4,6},{6,4},{8,10},{10,8},{12,14},{14,12},{16,18},{18,... | collective-permute-start | bytes 1474568 | tf_op jit(solution)/shard_map/ppermute | solution.py:35
  32.7 9.7 %collective-permute-start.8 = (bf16[96,1536]{1,0:T(8,128)(2,1)S(1)}, bf16[96,1536]{1,0:T(8,128)(2,1)S(1)}, u32[]{:S(2)}, u32[]{:S(2)}) collective-permute-start(bf16[96,1536]{1,0:T(8,128)(2,1)S(1)} %get-tuple-element.66), channel_id=1, source_target_pairs={{0,1},{1,0},{2,3},{3,2},{4,5},{5,4},{6,7},{7,6},{8,9},{9,8},{10,11... | collective-permute-start | bytes 884744 | tf_op jit(solution)/shard_map/ppermute | solution.py:35
  36.1 1.3 %copy-start.1 = (bf16[384,2560]{1,0:T(8,128)(2,1)}, bf16[384,2560]{1,0:T(8,128)(2,1)S(1)}, u32[]{:S(2)}) copy-start(bf16[384,2560]{1,0:T(8,128)(2,1)S(1)} %get-tuple-element.89.cot) | copy-start | bytes 5898244
  41.2 3.2 %collective-permute-start.6 = (bf16[96,1280]{1,0:T(8,128)(2,1)S(1)}, bf16[96,1280]{1,0:T(8,128)(2,1)S(1)}, u32[]{:S(2)}, u32[]{:S(2)}) collective-permute-start(bf16[96,1280]{1,0:T(8,128)(2,1)S(1)} %get-tuple-element.64), channel_id=1, source_target_pairs={{0,2},{2,0},{4,6},{6,4},{8,10},{10,8},{12,14},{14,12},{16,18},{18,... | collective-permute-start | bytes 737288 | tf_op jit(solution)/shard_map/ppermute | solution.py:35
  41.5 2.9 %collective-permute-start.7 = (bf16[96,1280]{1,0:T(8,128)(2,1)S(1)}, bf16[96,1280]{1,0:T(8,128)(2,1)S(1)}, u32[]{:S(2)}, u32[]{:S(2)}) collective-permute-start(bf16[96,1280]{1,0:T(8,128)(2,1)S(1)} %get-tuple-element.65), channel_id=1, source_target_pairs={{0,2},{2,0},{4,6},{6,4},{8,10},{10,8},{12,14},{14,12},{16,18},{18,... | collective-permute-start | bytes 737288 | tf_op jit(solution)/shard_map/ppermute | solution.py:35
  41.8 9.1 %collective-permute-start.4 = (bf16[96,1536]{1,0:T(8,128)(2,1)S(1)}, bf16[96,1536]{1,0:T(8,128)(2,1)S(1)}, u32[]{:S(2)}, u32[]{:S(2)}) collective-permute-start(bf16[96,1536]{1,0:T(8,128)(2,1)S(1)} %get-tuple-element.61), channel_id=1, source_target_pairs={{0,1},{1,0},{2,3},{3,2},{4,5},{5,4},{6,7},{7,6},{8,9},{9,8},{10,11... | collective-permute-start | bytes 884744 | tf_op jit(solution)/shard_map/ppermute | solution.py:35
  44.4 9.4 %collective-permute-start.13 = (bf16[96,640]{1,0:T(8,128)(2,1)S(1)}, bf16[96,640]{1,0:T(8,128)(2,1)S(1)}, u32[]{:S(2)}, u32[]{:S(2)}) collective-permute-start(bf16[96,640]{1,0:T(8,128)(2,1)S(1)} %add_convert_fusion.4), channel_id=1, source_target_pairs={{0,8},{2,10},{4,12},{6,14},{8,0},{10,2},{12,4},{14,6},{16,24},{18,... | collective-permute-start | bytes 368648 | tf_op jit(solution)/shard_map/ppermute | solution.py:35
  46.2 7.6 %collective-permute-start.12 = (bf16[96,640]{1,0:T(8,128)(2,1)S(1)}, bf16[96,640]{1,0:T(8,128)(2,1)S(1)}, u32[]{:S(2)}, u32[]{:S(2)}) collective-permute-start(bf16[96,640]{1,0:T(8,128)(2,1)S(1)} %get-tuple-element.100), channel_id=1, source_target_pairs={{0,4},{2,6},{4,0},{6,2},{8,12},{10,14},{12,8},{14,10},{16,20},{18,... | collective-permute-start | bytes 368648 | tf_op jit(solution)/shard_map/ppermute | solution.py:35
  47.7 6.1 %collective-permute-start.11 = (bf16[96,640]{1,0:T(8,128)(2,1)S(1)}, bf16[96,640]{1,0:T(8,128)(2,1)S(1)}, u32[]{:S(2)}, u32[]{:S(2)}) collective-permute-start(bf16[96,640]{1,0:T(8,128)(2,1)S(1)} %get-tuple-element.101), channel_id=1, source_target_pairs={{0,12},{2,14},{4,8},{6,10},{8,4},{10,6},{12,0},{14,2},{16,28},{18,... | collective-permute-start | bytes 368648 | tf_op jit(solution)/shard_map/ppermute | solution.py:35
  53.2 2.3 %copy-start.3 = (bf16[384,512]{1,0:T(8,128)(2,1)}, bf16[384,512]{1,0:T(8,128)(2,1)S(1)}, u32[]{:S(2)}) copy-start(bf16[384,512]{1,0:T(8,128)(2,1)S(1)} %get-tuple-element.92.act) | copy-start | bytes 1179652
  53.2 1.6 %collective-permute-start.9 = (bf16[96,1280]{1,0:T(8,128)(2,1)S(1)}, bf16[96,1280]{1,0:T(8,128)(2,1)S(1)}, u32[]{:S(2)}, u32[]{:S(2)}) collective-permute-start(bf16[96,1280]{1,0:T(8,128)(2,1)S(1)} %get-tuple-element.81), channel_id=1, source_target_pairs={{0,2},{2,0},{4,6},{6,4},{8,10},{10,8},{12,14},{14,12},{16,18},{18,... | collective-permute-start | bytes 737288 | tf_op jit(solution)/shard_map/ppermute | solution.py:35
  53.3 5.1 %collective-permute-start.10 = (bf16[96,1280]{1,0:T(8,128)(2,1)S(1)}, bf16[96,1280]{1,0:T(8,128)(2,1)}, u32[]{:S(2)}, u32[]{:S(2)}) collective-permute-start(bf16[96,1280]{1,0:T(8,128)(2,1)S(1)} %get-tuple-element.83), channel_id=1, source_target_pairs={{0,2},{2,0},{4,6},{6,4},{8,10},{10,8},{12,14},{14,12},{16,18},{18,... | collective-permute-start | bytes 737288 | tf_op jit(solution)/shard_map/ppermute | solution.py:35
  55.6 6.6 %collective-permute-start.15 = (bf16[96,640]{1,0:T(8,128)(2,1)}, bf16[96,640]{1,0:T(8,128)(2,1)S(1)}, u32[]{:S(2)}, u32[]{:S(2)}) collective-permute-start(bf16[96,640]{1,0:T(8,128)(2,1)} %get-tuple-element.99), channel_id=1, source_target_pairs={{0,12},{2,14},{4,8},{6,10},{8,4},{10,6},{12,0},{14,2},{16,28},{18,... | collective-permute-start | bytes 368648 | tf_op jit(solution)/shard_map/ppermute | solution.py:35
  57.9 6.9 %collective-permute-start.16 = (bf16[96,640]{1,0:T(8,128)(2,1)}, bf16[96,640]{1,0:T(8,128)(2,1)}, u32[]{:S(2)}, u32[]{:S(2)}) collective-permute-start(bf16[96,640]{1,0:T(8,128)(2,1)} %get-tuple-element.98), channel_id=1, source_target_pairs={{0,4},{2,6},{4,0},{6,2},{8,12},{10,14},{12,8},{14,10},{16,20},{18,... | collective-permute-start | bytes 368648 | tf_op jit(solution)/shard_map/ppermute | solution.py:35
  60.0 5.2 %collective-permute-start.17 = (bf16[96,640]{1,0:T(8,128)(2,1)}, bf16[96,640]{1,0:T(8,128)(2,1)}, u32[]{:S(2)}, u32[]{:S(2)}) collective-permute-start(bf16[96,640]{1,0:T(8,128)(2,1)} %add_convert_fusion.1), channel_id=1, source_target_pairs={{0,8},{2,10},{4,12},{6,14},{8,0},{10,2},{12,4},{14,6},{16,24},{18,... | collective-permute-start | bytes 368648 | tf_op jit(solution)/shard_map/ppermute | solution.py:35
  60.6 5.2 %collective-permute-start.14 = (bf16[96,640]{1,0:T(8,128)(2,1)}, bf16[96,640]{1,0:T(8,128)(2,1)}, u32[]{:S(2)}, u32[]{:S(2)}) collective-permute-start(bf16[96,640]{1,0:T(8,128)(2,1)} %add_convert_fusion), channel_id=1, source_target_pairs={{0,1},{1,0},{2,3},{3,2},{4,5},{5,4},{6,7},{7,6},{8,9},{9,8},{10,11... | collective-permute-start | bytes 368648 | tf_op jit(solution)/shard_map/ppermute | solution.py:35
  67.0 10.6 %collective-permute-start.18 = (bf16[96,640]{1,0:T(8,128)(2,1)S(1)}, bf16[96,640]{1,0:T(8,128)(2,1)S(1)}, u32[]{:S(2)}, u32[]{:S(2)}) collective-permute-start(bf16[96,640]{1,0:T(8,128)(2,1)S(1)} %fusion.2), channel_id=1, source_target_pairs={{0,16},{2,18},{4,20},{6,22},{8,24},{10,26},{12,28},{14,30},{16,0},... | collective-permute-start | bytes 368648 | tf_op jit(solution)/shard_map/ppermute | solution.py:35
  69.7 1.5 %copy-start.2 = (bf16[384,2560]{1,0:T(8,128)(2,1)S(1)}, bf16[384,2560]{1,0:T(8,128)(2,1)}, u32[]{:S(2)}) copy-start(bf16[384,2560]{1,0:T(8,128)(2,1)} %copy-done.1) | copy-start | bytes 5898244
  71.2 1.0 %copy-start.4 = (bf16[384,512]{1,0:T(8,128)(2,1)S(1)}, bf16[384,512]{1,0:T(8,128)(2,1)}, u32[]{:S(2)}) copy-start(bf16[384,512]{1,0:T(8,128)(2,1)} %copy-done.3) | copy-start | bytes 1179652

commit v5 on v4

--- a/solution.py
+++ b/solution.py
@@ -81,7 +81,7 @@
         out_specs=IN_VMEM,
         out_shape=pltpu.VMEM(shape, tokens.dtype),
         scratch_shapes=[pltpu.SemaphoreType.DMA],
-        compiler_params=grant(2),
+        compiler_params=grant(10),
         cost_estimate=cost(0),
         name="fetch",
     )(node, place, in_hbm(tokens), in_hbm(cot))
@@ -155,7 +155,7 @@
             pltpu.VMEM((count, 3 * units), codes),
         ],
         scratch_shapes=[pltpu.SemaphoreType.DMA((steps, 5))],
-        compiler_params=grant(4),
+        compiler_params=grant(10),
         cost_estimate=cost(0),
         name="prepare",
     )(
@@ -210,7 +210,7 @@
             pltpu.VMEM((half, 3 * units), jnp.bfloat16),
         ],
         input_output_aliases={5 + i: i for i in range(len(before))},
-        compiler_params=grant(6),
+        compiler_params=grant(10),
         cost_estimate=cost(0),
         name="join",
     )(place, *(in_vmem(a) for a in (held, given, w_in, w_down, *before)))
@@ -285,7 +285,7 @@
         + [pltpu.VMEM(terms, jnp.bfloat16)] * (pairs // 2)
         + [pltpu.VMEM(terms, jnp.float32)] * (pairs // 2),
         input_output_aliases={4 + i: i for i in range(len(before))},
-        compiler_params=grant(8),
+        compiler_params=grant(10),
         cost_estimate=cost(0),
         name="activate",
     )(place, *(in_vmem(a) for a in (weights, total, arrived, *before)))
@@ -325,7 +325,7 @@
         out_shape=[pltpu.HBM(shape, jnp.bfloat16) for shape in shapes],
         scratch_shapes=[pltpu.VMEM(shape, jnp.bfloat16) for shape in shapes]
         + [pltpu.SemaphoreType.DMA((3 * (rows // STEP),))],
-        compiler_params=grant(20),
+        compiler_params=grant(10),
         cost_estimate=cost(6 * tokens.shape[0] * rows * units),
         name="weight_grads",
     )(*(in_vmem(a) for a in (tokens, cot, act, d_inner)))

time: 79.9 us -> 79.9 us (level)
  no operation moved by 1% of the time
where the time goes in v5:
time: 79.9 us; the launch traced here: 79.6 us
  Pallas kernels  26.7 us (33%)
  waiting for transfers between devices  21 us (26%)
  starting transfers between devices  20.6 us (26%)
  other arithmetic  6.17 us (8%)
  local copies, waits for them, and re-layouts  4.3 us (5%)
  between operations  0.84 us (1%)
    ppermute x19, waiting for transfers between devices, swap(): return lax.ppermute(value, axis, flipped(size, mask))  21 us
    ppermute x19, starting transfers between devices, swap(): return lax.ppermute(value, axis, flipped(size, mask))  20.6 us
    pallas_call x3, Pallas kernels, activate(): pl.pallas_call(functools.partial(activate_kernel, group, turns, count, bl...  8.1 us
    pallas_call x1, Pallas kernels, prepare(): pl.pallas_call(prepare_kernel, in_specs=[IN_SMEM] + [IN_HBM] * 5 + [IN_VM...  6.54 us
    pallas_call x1, Pallas kernels, weight_grads(): pl.pallas_call(grads_kernel, in_specs=[IN_VMEM] * 4, out_specs=[IN_HBM] *...  5.36 us
    pallas_call x2, Pallas kernels, join(): pl.pallas_call(functools.partial(join_kernel, group, far), in_specs=[IN_S...  4.81 us
    unnamed x14, local copies, waits for them, and re-layouts  3.83 us
    convert_element_type x4, other arithmetic, split(): sending.append((mask, both.astype(jnp.bfloat16)))  2.4 us
  transfers between devices with their start and end apart: 19, of which 8 were waited for; matrix products, arithmetic and copies ran while one was open for 4% of the time, Pallas kernels for 31%

profile of v5, /device:TPU:0, one launch (start us, length us, event | category | flops | bytes accessed | tf_op | source)
XLA Modules:
  0.0 79.6 jit_solution(557396917533348222)
XLA Ops:
  0.6 0.0 copy-start
  0.7 0.0 copy-start.5
  0.7 0.0 copy-start.6
  0.7 1.9 %fetch.1 = bf16[96,2560]{1,0:T(8,128)(2,1)} custom-call(s32[1]{0:T(128)} %bitcast.1.node, s32[1]{0:T(128)} %bitcast.place, bf16[192,5120]{1,0:T(8,128)(2,1)} %tokens.3, bf16[192,5120]{1,0:T(8,128)(2,1)} %cot.3), custom_call_target="tpu_custom_call" | custom-call | tf_op jit(solution)/shard_map/fetch/pallas_call | solution.py:78
  2.6 3.0 %collective-permute-start = (bf16[96,2560]{1,0:T(8,128)(2,1)}, bf16[96,2560]{1,0:T(8,128)(2,1)}, u32[]{:S(2)}, u32[]{:S(2)}) collective-permute-start(bf16[96,2560]{1,0:T(8,128)(2,1)} %fetch.1), channel_id=1, source_target_pairs={{0,1},{1,0},{2,3},{3,2},{4,5},{5,4},{6,7},{7,6},{8,9},{9,8},{10,11... | collective-permute-start | bytes 1474568 | tf_op jit(solution)/shard_map/ppermute | solution.py:35
  5.6 0.0 copy-done
  5.6 0.4 copy.25
  6.0 0.0 copy-done.5
  6.0 6.5 %prepare.1 = (bf16[384,2560]{1,0:T(8,128)(2,1)S(1)}, bf16[384,2560]{1,0:T(8,128)(2,1)S(1)}, bf16[2560,1024]{1,0:T(8,128)(2,1)S(1)}, bf16[512,2560]{1,0:T(8,128)(...) custom-call(s32[1]{0:T(128)} %bitcast.1.node, bf16[192,5120]{1,0:T(8,128)(2,1)} %tokens.3, ...), custom_call_target="tpu_custom_call" | custom-call | tf_op jit(solution)/shard_map/prepare/pallas_call | solution.py:145
  12.6 4.6 %collective-permute-done.held = bf16[96,2560]{1,0:T(8,128)(2,1)} collective-permute-done((bf16[96,2560]{1,0:T(8,128)(2,1)}, bf16[96,2560]{1,0:T(8,128)(2,1)}, u32[]{:S(2)}, u32[]{:S(2)}) %collective-permute-start) | collective-permute-done | bytes 491552 | tf_op jit(solution)/shard_map/ppermute | solution.py:35
  17.1 1.8 %collective-permute-start.1 = (bf16[96,2560]{1,0:T(8,128)(2,1)}, bf16[96,2560]{1,0:T(8,128)(2,1)S(1)}, u32[]{:S(2)}, u32[]{:S(2)}) collective-permute-start(bf16[96,2560]{1,0:T(8,128)(2,1)} %collective-permute-done.held), channel_id=1, source_target_pairs={{0,8},{2,10},{4,12},{6,14},{8,0},{10,2},{12,4},{14,6},{16,24},{18,... | collective-permute-start | bytes 1474568 | tf_op jit(solution)/shard_map/ppermute | solution.py:35
  18.9 1.5 %collective-permute-start.5 = (bf16[192,1536]{1,0:T(8,128)(2,1)S(1)}, bf16[192,1536]{1,0:T(8,128)(2,1)S(1)}, u32[]{:S(2)}, u32[]{:S(2)}) collective-permute-start(bf16[192,1536]{1,0:T(8,128)(2,1)S(1)} %get-tuple-element.53), channel_id=1, source_target_pairs={{0,1},{1,0},{2,3},{3,2},{4,5},{5,4},{6,7},{7,6},{8,9},{9,8},{10,11... | collective-permute-start | bytes 1769480 | tf_op jit(solution)/shard_map/ppermute | solution.py:35
  20.5 0.0 collective-permute-start.3
  20.5 9.3 %collective-permute-done.1.held = bf16[96,2560]{1,0:T(8,128)(2,1)S(1)} collective-permute-done((bf16[96,2560]{1,0:T(8,128)(2,1)}, bf16[96,2560]{1,0:T(8,128)(2,1)S(1)}, u32[]{:S(2)}, u32[]{:S(2)}) %collective-permute-start.1) | collective-permute-done | bytes 491552 | tf_op jit(solution)/shard_map/ppermute | solution.py:35
  29.8 0.0 collective-permute-start.2
  29.8 0.0 collective-permute-done.3.given
  29.8 2.9 %join.2 = (bf16[384,2560]{1,0:T(8,128)(2,1)S(1)}, bf16[384,2560]{1,0:T(8,128)(2,1)S(1)}, f32[192,1536]{1,0:T(8,128)S(1)}, bf16[96,1536]{1,0:T(8,128)(2,1)S(1)}) custom-call(s32[1]{0:T(128)} %bitcast.place, bf16[96,2560]{1,0:T(8,128)(2,1)} %collective-permute-done.held, ...), custom_call_target="tpu_custom_call", output_to_operand_aliasing={{0}: (5, {}), {1}: (6, {})} | custom-call | tf_op jit(solution)/shard_map/join/pallas_call | solution.py:202
  32.7 1.5 %collective-permute-start.8 = (bf16[96,1536]{1,0:T(8,128)(2,1)S(1)}, bf16[96,1536]{1,0:T(8,128)(2,1)S(1)}, u32[]{:S(2)}, u32[]{:S(2)}) collective-permute-start(bf16[96,1536]{1,0:T(8,128)(2,1)S(1)} %get-tuple-element.66), channel_id=1, source_target_pairs={{0,1},{1,0},{2,3},{3,2},{4,5},{5,4},{6,7},{7,6},{8,9},{9,8},{10,11... | collective-permute-start | bytes 884744 | tf_op jit(solution)/shard_map/ppermute | solution.py:35
  34.2 0.0 collective-permute-done.2.given
  34.2 1.9 %join.3 = (bf16[384,2560]{1,0:T(8,128)(2,1)S(1)}, bf16[384,2560]{1,0:T(8,128)(2,1)S(1)}, f32[192,1536]{1,0:T(8,128)S(1)}, bf16[96,1536]{1,0:T(8,128)(2,1)S(1)}) custom-call(s32[1]{0:T(128)} %bitcast.place, bf16[96,2560]{1,0:T(8,128)(2,1)S(1)} %collective-permute-done.1.held, ...), custom_call_target="tpu_custom_call", output_to_operand_aliasing={{0}: (5, {}), {1}: (6, {}), {2}: (7, {})} | custom-call | tf_op jit(solution)/shard_map/join/pallas_call | solution.py:202
  36.1 0.0 copy-start.1
  36.1 1.3 %copy-done.1 = bf16[384,2560]{1,0:T(8,128)(2,1)} copy-done((bf16[384,2560]{1,0:T(8,128)(2,1)}, bf16[384,2560]{1,0:T(8,128)(2,1)S(1)}, u32[]{:S(2)}) %copy-start.1) | copy-done | bytes 1966104
  37.4 0.0 collective-permute-done.5.arrived
  37.4 3.8 %activate.3 = (bf16[384,512]{1,0:T(8,128)(2,1)S(1)}, bf16[384,1024]{1,0:T(8,128)(2,1)S(1)}, bf16[96,1280]{1,0:T(8,128)(2,1)S(1)}, bf16[96,1280]{1,0:T(8,128)(2,1...) custom-call(s32[1]{0:T(128)} %bitcast.place, bf16[2560,1024]{1,0:T(8,128)(2,1)S(1)} %get-tuple-element.51.w_in.weights, ...), custom_call_target="tpu_custom_call" | custom-call | tf_op jit(solution)/shard_map/activate/pallas_call | solution.py:277
  41.2 0.3 collective-permute-start.6
  41.5 0.3 collective-permute-start.7
  41.8 0.6 collective-permute-start.4
  42.4 0.0 collective-permute-done.8.arrived
  42.4 2.0 %activate.4 = (bf16[384,512]{1,0:T(8,128)(2,1)S(1)}, bf16[384,1024]{1,0:T(8,128)(2,1)S(1)}, bf16[96,1280]{1,0:T(8,128)(2,1)S(1)}, bf16[96,1280]{1,0:T(8,128)(2,1...) custom-call(s32[1]{0:T(128)} %bitcast.place, ...), custom_call_target="tpu_custom_call", output_to_operand_aliasing={{0}: (4, {}), {1}: (5, {})} | custom-call | tf_op jit(solution)/shard_map/activate/pallas_call | solution.py:277
  44.3 0.0 collective-permute-done.6
  44.4 0.0 collective-permute-done.7
  44.4 1.7 %collective-permute-start.13 = (bf16[96,640]{1,0:T(8,128)(2,1)S(1)}, bf16[96,640]{1,0:T(8,128)(2,1)S(1)}, u32[]{:S(2)}, u32[]{:S(2)}) collective-permute-start(bf16[96,640]{1,0:T(8,128)(2,1)S(1)} %add_convert_fusion.4), channel_id=1, source_target_pairs={{0,8},{2,10},{4,12},{6,14},{8,0},{10,2},{12,4},{14,6},{16,24},{18,... | collective-permute-start | bytes 368648 | tf_op jit(solution)/shard_map/ppermute | solution.py:35
  46.2 1.6 %collective-permute-start.12 = (bf16[96,640]{1,0:T(8,128)(2,1)S(1)}, bf16[96,640]{1,0:T(8,128)(2,1)S(1)}, u32[]{:S(2)}, u32[]{:S(2)}) collective-permute-start(bf16[96,640]{1,0:T(8,128)(2,1)S(1)} %get-tuple-element.100), channel_id=1, source_target_pairs={{0,4},{2,6},{4,0},{6,2},{8,12},{10,14},{12,8},{14,10},{16,20},{18,... | collective-permute-start | bytes 368648 | tf_op jit(solution)/shard_map/ppermute | solution.py:35
  47.7 0.3 collective-permute-start.11
  48.1 2.8 %collective-permute-done.4.arrived = bf16[96,1536]{1,0:T(8,128)(2,1)S(1)} collective-permute-done((bf16[96,1536]{1,0:T(8,128)(2,1)S(1)}, bf16[96,1536]{1,0:T(8,128)(2,1)S(1)}, u32[]{:S(2)}, u32[]{:S(2)}) %collective-permute-start.4) | collective-permute-done | bytes 294944 | tf_op jit(solution)/shard_map/ppermute | solution.py:35
  50.9 2.3 %activate.5 = (bf16[384,512]{1,0:T(8,128)(2,1)S(1)}, bf16[384,1024]{1,0:T(8,128)(2,1)S(1)}, bf16[96,1280]{1,0:T(8,128)(2,1)S(1)}, bf16[96,1280]{1,0:T(8,128)(2,1...) custom-call(s32[1]{0:T(128)} %bitcast.place, ...), custom_call_target="tpu_custom_call", output_to_operand_aliasing={{0}: (4, {}), {1}: (5, {}), {2}: (6, {}), {3}: (7, {}), {4}... | custom-call | tf_op jit(solution)/shard_map/activate/pallas_call | solution.py:277
  53.2 0.0 copy-start.3
  53.2 0.1 collective-permute-start.9
  53.3 0.5 collective-permute-start.10
  53.8 0.0 collective-permute-done.13
  53.8 0.0 collective-permute-done.12
  53.8 0.0 collective-permute-done.11
  53.8 0.7 add_convert_fusion
  54.6 0.3 collective-permute-done.9
  54.8 0.8 add_convert_fusion.2
  55.6 2.3 %collective-permute-start.15 = (bf16[96,640]{1,0:T(8,128)(2,1)}, bf16[96,640]{1,0:T(8,128)(2,1)S(1)}, u32[]{:S(2)}, u32[]{:S(2)}) collective-permute-start(bf16[96,640]{1,0:T(8,128)(2,1)} %get-tuple-element.99), channel_id=1, source_target_pairs={{0,12},{2,14},{4,8},{6,10},{8,4},{10,6},{12,0},{14,2},{16,28},{18,... | collective-permute-start | bytes 368648 | tf_op jit(solution)/shard_map/ppermute | solution.py:35
  57.9 0.5 collective-permute-start.16
  58.5 0.0 collective-permute-done.10
  58.5 1.6 %add_convert_fusion.1 = bf16[96,640]{1,0:T(8,128)(2,1)} fusion(f32[96,1280]{1,0:T(8,128)S(1)} %get-tuple-element.82, bf16[96,1280]{1,0:T(8,128)(2,1)} %collective-permute-done.10), kind=kLoop, calls=%fused_computation.7 | loop fusion | flops 184320 | bytes 491520 | tf_op jit(solution)/shard_map/convert_element_type | solution.py:403
  60.0 0.6 collective-permute-start.17
  60.6 1.2 %collective-permute-start.14 = (bf16[96,640]{1,0:T(8,128)(2,1)}, bf16[96,640]{1,0:T(8,128)(2,1)}, u32[]{:S(2)}, u32[]{:S(2)}) collective-permute-start(bf16[96,640]{1,0:T(8,128)(2,1)} %add_convert_fusion), channel_id=1, source_target_pairs={{0,1},{1,0},{2,3},{3,2},{4,5},{5,4},{6,7},{7,6},{8,9},{9,8},{10,11... | collective-permute-start | bytes 368648 | tf_op jit(solution)/shard_map/ppermute | solution.py:35
  61.8 0.3 collective-permute-done.15
  62.1 2.6 %collective-permute-done.16 = bf16[96,640]{1,0:T(8,128)(2,1)} collective-permute-done((bf16[96,640]{1,0:T(8,128)(2,1)}, bf16[96,640]{1,0:T(8,128)(2,1)}, u32[]{:S(2)}, u32[]{:S(2)}) %collective-permute-start.16) | collective-permute-done | bytes 122912 | tf_op jit(solution)/shard_map/ppermute | solution.py:35
  64.8 0.4 collective-permute-done.17
  65.2 0.6 collective-permute-done.14
  65.8 1.2 %fusion.2 = bf16[96,640]{1,0:T(8,128)(2,1)S(1)} fusion(bf16[96,640]{1,0:T(8,128)(2,1)} %collective-permute-done.14, pred[]{:T(512)S(6)} %eq.7, bf16[96,640]{1,0:T(8,128)(2,1)} %collective-permute-done.17, bf16[96,640]{1,0:T(8,128)(2,1)} %collective-permute-done.16, bf16[96,640]{1,0:T(8,128)(2,1)S(1)} %collective-permute-done.15, ...), kind=kLoop, calls=%fused_computation.4 | loop fusion | flops 675840 | bytes 983041 | tf_op jit(solution)/shard_map/convert_element_type | solution.py:445
  67.0 2.7 %collective-permute-start.18 = (bf16[96,640]{1,0:T(8,128)(2,1)S(1)}, bf16[96,640]{1,0:T(8,128)(2,1)S(1)}, u32[]{:S(2)}, u32[]{:S(2)}) collective-permute-start(bf16[96,640]{1,0:T(8,128)(2,1)S(1)} %fusion.2), channel_id=1, source_target_pairs={{0,16},{2,18},{4,20},{6,22},{8,24},{10,26},{12,28},{14,30},{16,0},... | collective-permute-start | bytes 368648 | tf_op jit(solution)/shard_map/ppermute | solution.py:35
  69.7 1.5 %copy-done.2 = bf16[384,2560]{1,0:T(8,128)(2,1)S(1)} copy-done((bf16[384,2560]{1,0:T(8,128)(2,1)S(1)}, bf16[384,2560]{1,0:T(8,128)(2,1)}, u32[]{:S(2)}) %copy-start.2) | copy-done | bytes 1966104
  71.2 1.0 %copy-done.4 = bf16[384,512]{1,0:T(8,128)(2,1)S(1)} copy-done((bf16[384,512]{1,0:T(8,128)(2,1)S(1)}, bf16[384,512]{1,0:T(8,128)(2,1)}, u32[]{:S(2)}) %copy-start.4) | copy-done | bytes 393240
  72.2 5.4 %weight_grads.1 = (bf16[2560,512]{1,0:T(8,128)(2,1)}, bf16[2560,512]{1,0:T(8,128)(2,1)}, bf16[512,2560]{1,0:T(8,128)(2,1)}) custom-call(bf16[384,2560]{1,0:T(8,128)(2,1)S(1)} %get-tuple-element.88.tokens, bf16[384,2560]{1,0:T(8,128)(2,1)S(1)} %copy-done.2, bf16[384,512]{1,0:T(8,128)(2,1)S(1)} %copy-done.4, bf16[384,1024]{1,0:T(8,128)(2,1)S(1)} %get-tuple-element.93.d_inner), custom_call_target="tpu_custom_call" | custom-call | flops 3019898880 | tf_op jit(solution)/shard_map/weight_grads/pallas_call | solution.py:321
  77.6 0.0 collective-permute-done.18
  77.6 1.2 %fusion.1 = bf16[96,640]{1,0:T(8,128)(2,1)S(1)} fusion(bf16[96,640]{1,0:T(8,128)(2,1)} %collective-permute-done.14, bf16[96,640]{1,0:T(8,128)(2,1)S(1)} %collective-permute-done.18, pred[]{:T(512)S(6)} %eq.6, bf16[96,640]{1,0:T(8,128)(2,1)} %collective-permute-done.17, bf16[96,640]{1,0:T(8,128)(2,1)} %collective-permute-done.16, ...), kind=kLoop, calls=%fused_computation.3 | loop fusion | flops 798720 | bytes 1105921 | tf_op jit(solution)/shard_map/convert_element_type | solution.py:452
  78.8 0.1 fusion.3
  78.9 0.7 pad_maximum_fusion
  (8 shorter events, 0.1 us)
Async XLA Ops:
  0.6 5.0 %copy-start = (f32[512,40]{0,1:T(8,128)S(1)}, f32[512,40]{0,1:T(8,128)}, u32[]{:S(2)}) copy-start(f32[512,40]{0,1:T(8,128)} %param.15) | copy-start | bytes 245764
  0.7 5.3 %copy-start.5 = (f32[40,512]{1,0:T(8,128)S(1)}, f32[40,512]{1,0:T(8,128)}, u32[]{:S(2)}) copy-start(f32[40,512]{1,0:T(8,128)} %gate_scales.1) | copy-start | bytes 245764
  0.7 5.3 %copy-start.6 = (f32[40,512]{1,0:T(8,128)S(1)}, f32[40,512]{1,0:T(8,128)}, u32[]{:S(2)}) copy-start(f32[40,512]{1,0:T(8,128)} %up_scales.1) | copy-start | bytes 245764
  2.6 14.6 %collective-permute-start = (bf16[96,2560]{1,0:T(8,128)(2,1)}, bf16[96,2560]{1,0:T(8,128)(2,1)}, u32[]{:S(2)}, u32[]{:S(2)}) collective-permute-start(bf16[96,2560]{1,0:T(8,128)(2,1)} %fetch.1), channel_id=1, source_target_pairs={{0,1},{1,0},{2,3},{3,2},{4,5},{5,4},{6,7},{7,6},{8,9},{9,8},{10,11... | collective-permute-start | bytes 1474568 | tf_op jit(solution)/shard_map/ppermute | solution.py:35
  17.1 12.6 %collective-permute-start.1 = (bf16[96,2560]{1,0:T(8,128)(2,1)}, bf16[96,2560]{1,0:T(8,128)(2,1)S(1)}, u32[]{:S(2)}, u32[]{:S(2)}) collective-permute-start(bf16[96,2560]{1,0:T(8,128)(2,1)} %collective-permute-done.held), channel_id=1, source_target_pairs={{0,8},{2,10},{4,12},{6,14},{8,0},{10,2},{12,4},{14,6},{16,24},{18,... | collective-permute-start | bytes 1474568 | tf_op jit(solution)/shard_map/ppermute | solution.py:35
  18.9 18.4 %collective-permute-start.5 = (bf16[192,1536]{1,0:T(8,128)(2,1)S(1)}, bf16[192,1536]{1,0:T(8,128)(2,1)S(1)}, u32[]{:S(2)}, u32[]{:S(2)}) collective-permute-start(bf16[192,1536]{1,0:T(8,128)(2,1)S(1)} %get-tuple-element.53), channel_id=1, source_target_pairs={{0,1},{1,0},{2,3},{3,2},{4,5},{5,4},{6,7},{7,6},{8,9},{9,8},{10,11... | collective-permute-start | bytes 1769480 | tf_op jit(solution)/shard_map/ppermute | solution.py:35
  20.5 9.3 %collective-permute-start.3 = (bf16[96,2560]{1,0:T(8,128)(2,1)}, bf16[96,2560]{1,0:T(8,128)(2,1)S(1)}, u32[]{:S(2)}, u32[]{:S(2)}) collective-permute-start(bf16[96,2560]{1,0:T(8,128)(2,1)} %collective-permute-done.held), channel_id=1, source_target_pairs={{0,2},{2,0},{4,6},{6,4},{8,10},{10,8},{12,14},{14,12},{16,18},{18,... | collective-permute-start | bytes 1474568 | tf_op jit(solution)/shard_map/ppermute | solution.py:35
  29.8 4.4 %collective-permute-start.2 = (bf16[96,2560]{1,0:T(8,128)(2,1)S(1)}, bf16[96,2560]{1,0:T(8,128)(2,1)S(1)}, u32[]{:S(2)}, u32[]{:S(2)}) collective-permute-start(bf16[96,2560]{1,0:T(8,128)(2,1)S(1)} %collective-permute-done.1.held), channel_id=1, source_target_pairs={{0,2},{2,0},{4,6},{6,4},{8,10},{10,8},{12,14},{14,12},{16,18},{18,... | collective-permute-start | bytes 1474568 | tf_op jit(solution)/shard_map/ppermute | solution.py:35
  32.7 9.7 %collective-permute-start.8 = (bf16[96,1536]{1,0:T(8,128)(2,1)S(1)}, bf16[96,1536]{1,0:T(8,128)(2,1)S(1)}, u32[]{:S(2)}, u32[]{:S(2)}) collective-permute-start(bf16[96,1536]{1,0:T(8,128)(2,1)S(1)} %get-tuple-element.66), channel_id=1, source_target_pairs={{0,1},{1,0},{2,3},{3,2},{4,5},{5,4},{6,7},{7,6},{8,9},{9,8},{10,11... | collective-permute-start | bytes 884744 | tf_op jit(solution)/shard_map/ppermute | solution.py:35
  36.1 1.3 %copy-start.1 = (bf16[384,2560]{1,0:T(8,128)(2,1)}, bf16[384,2560]{1,0:T(8,128)(2,1)S(1)}, u32[]{:S(2)}) copy-start(bf16[384,2560]{1,0:T(8,128)(2,1)S(1)} %get-tuple-element.89.cot) | copy-start | bytes 5898244
  41.2 3.2 %collective-permute-start.6 = (bf16[96,1280]{1,0:T(8,128)(2,1)S(1)}, bf16[96,1280]{1,0:T(8,128)(2,1)S(1)}, u32[]{:S(2)}, u32[]{:S(2)}) collective-permute-start(bf16[96,1280]{1,0:T(8,128)(2,1)S(1)} %get-tuple-element.64), channel_id=1, source_target_pairs={{0,2},{2,0},{4,6},{6,4},{8,10},{10,8},{12,14},{14,12},{16,18},{18,... | collective-permute-start | bytes 737288 | tf_op jit(solution)/shard_map/ppermute | solution.py:35
  41.5 2.9 %collective-permute-start.7 = (bf16[96,1280]{1,0:T(8,128)(2,1)S(1)}, bf16[96,1280]{1,0:T(8,128)(2,1)S(1)}, u32[]{:S(2)}, u32[]{:S(2)}) collective-permute-start(bf16[96,1280]{1,0:T(8,128)(2,1)S(1)} %get-tuple-element.65), channel_id=1, source_target_pairs={{0,2},{2,0},{4,6},{6,4},{8,10},{10,8},{12,14},{14,12},{16,18},{18,... | collective-permute-start | bytes 737288 | tf_op jit(solution)/shard_map/ppermute | solution.py:35
  41.8 9.1 %collective-permute-start.4 = (bf16[96,1536]{1,0:T(8,128)(2,1)S(1)}, bf16[96,1536]{1,0:T(8,128)(2,1)S(1)}, u32[]{:S(2)}, u32[]{:S(2)}) collective-permute-start(bf16[96,1536]{1,0:T(8,128)(2,1)S(1)} %get-tuple-element.61), channel_id=1, source_target_pairs={{0,1},{1,0},{2,3},{3,2},{4,5},{5,4},{6,7},{7,6},{8,9},{9,8},{10,11... | collective-permute-start | bytes 884744 | tf_op jit(solution)/shard_map/ppermute | solution.py:35
  44.4 9.4 %collective-permute-start.13 = (bf16[96,640]{1,0:T(8,128)(2,1)S(1)}, bf16[96,640]{1,0:T(8,128)(2,1)S(1)}, u32[]{:S(2)}, u32[]{:S(2)}) collective-permute-start(bf16[96,640]{1,0:T(8,128)(2,1)S(1)} %add_convert_fusion.4), channel_id=1, source_target_pairs={{0,8},{2,10},{4,12},{6,14},{8,0},{10,2},{12,4},{14,6},{16,24},{18,... | collective-permute-start | bytes 368648 | tf_op jit(solution)/shard_map/ppermute | solution.py:35
  46.2 7.7 %collective-permute-start.12 = (bf16[96,640]{1,0:T(8,128)(2,1)S(1)}, bf16[96,640]{1,0:T(8,128)(2,1)S(1)}, u32[]{:S(2)}, u32[]{:S(2)}) collective-permute-start(bf16[96,640]{1,0:T(8,128)(2,1)S(1)} %get-tuple-element.100), channel_id=1, source_target_pairs={{0,4},{2,6},{4,0},{6,2},{8,12},{10,14},{12,8},{14,10},{16,20},{18,... | collective-permute-start | bytes 368648 | tf_op jit(solution)/shard_map/ppermute | solution.py:35
  47.7 6.1 %collective-permute-start.11 = (bf16[96,640]{1,0:T(8,128)(2,1)S(1)}, bf16[96,640]{1,0:T(8,128)(2,1)S(1)}, u32[]{:S(2)}, u32[]{:S(2)}) collective-permute-start(bf16[96,640]{1,0:T(8,128)(2,1)S(1)} %get-tuple-element.101), channel_id=1, source_target_pairs={{0,12},{2,14},{4,8},{6,10},{8,4},{10,6},{12,0},{14,2},{16,28},{18,... | collective-permute-start | bytes 368648 | tf_op jit(solution)/shard_map/ppermute | solution.py:35
  53.2 2.3 %copy-start.3 = (bf16[384,512]{1,0:T(8,128)(2,1)}, bf16[384,512]{1,0:T(8,128)(2,1)S(1)}, u32[]{:S(2)}) copy-start(bf16[384,512]{1,0:T(8,128)(2,1)S(1)} %get-tuple-element.92.act) | copy-start | bytes 1179652
  53.2 1.6 %collective-permute-start.9 = (bf16[96,1280]{1,0:T(8,128)(2,1)S(1)}, bf16[96,1280]{1,0:T(8,128)(2,1)S(1)}, u32[]{:S(2)}, u32[]{:S(2)}) collective-permute-start(bf16[96,1280]{1,0:T(8,128)(2,1)S(1)} %get-tuple-element.81), channel_id=1, source_target_pairs={{0,2},{2,0},{4,6},{6,4},{8,10},{10,8},{12,14},{14,12},{16,18},{18,... | collective-permute-start | bytes 737288 | tf_op jit(solution)/shard_map/ppermute | solution.py:35
  53.3 5.1 %collective-permute-start.10 = (bf16[96,1280]{1,0:T(8,128)(2,1)S(1)}, bf16[96,1280]{1,0:T(8,128)(2,1)}, u32[]{:S(2)}, u32[]{:S(2)}) collective-permute-start(bf16[96,1280]{1,0:T(8,128)(2,1)S(1)} %get-tuple-element.83), channel_id=1, source_target_pairs={{0,2},{2,0},{4,6},{6,4},{8,10},{10,8},{12,14},{14,12},{16,18},{18,... | collective-permute-start | bytes 737288 | tf_op jit(solution)/shard_map/ppermute | solution.py:35
  55.6 6.6 %collective-permute-start.15 = (bf16[96,640]{1,0:T(8,128)(2,1)}, bf16[96,640]{1,0:T(8,128)(2,1)S(1)}, u32[]{:S(2)}, u32[]{:S(2)}) collective-permute-start(bf16[96,640]{1,0:T(8,128)(2,1)} %get-tuple-element.99), channel_id=1, source_target_pairs={{0,12},{2,14},{4,8},{6,10},{8,4},{10,6},{12,0},{14,2},{16,28},{18,... | collective-permute-start | bytes 368648 | tf_op jit(solution)/shard_map/ppermute | solution.py:35
  57.9 6.9 %collective-permute-start.16 = (bf16[96,640]{1,0:T(8,128)(2,1)}, bf16[96,640]{1,0:T(8,128)(2,1)}, u32[]{:S(2)}, u32[]{:S(2)}) collective-permute-start(bf16[96,640]{1,0:T(8,128)(2,1)} %get-tuple-element.98), channel_id=1, source_target_pairs={{0,4},{2,6},{4,0},{6,2},{8,12},{10,14},{12,8},{14,10},{16,20},{18,... | collective-permute-start | bytes 368648 | tf_op jit(solution)/shard_map/ppermute | solution.py:35
  60.0 5.2 %collective-permute-start.17 = (bf16[96,640]{1,0:T(8,128)(2,1)}, bf16[96,640]{1,0:T(8,128)(2,1)}, u32[]{:S(2)}, u32[]{:S(2)}) collective-permute-start(bf16[96,640]{1,0:T(8,128)(2,1)} %add_convert_fusion.1), channel_id=1, source_target_pairs={{0,8},{2,10},{4,12},{6,14},{8,0},{10,2},{12,4},{14,6},{16,24},{18,... | collective-permute-start | bytes 368648 | tf_op jit(solution)/shard_map/ppermute | solution.py:35
  60.6 5.2 %collective-permute-start.14 = (bf16[96,640]{1,0:T(8,128)(2,1)}, bf16[96,640]{1,0:T(8,128)(2,1)}, u32[]{:S(2)}, u32[]{:S(2)}) collective-permute-start(bf16[96,640]{1,0:T(8,128)(2,1)} %add_convert_fusion), channel_id=1, source_target_pairs={{0,1},{1,0},{2,3},{3,2},{4,5},{5,4},{6,7},{7,6},{8,9},{9,8},{10,11... | collective-permute-start | bytes 368648 | tf_op jit(solution)/shard_map/ppermute | solution.py:35
  67.0 10.6 %collective-permute-start.18 = (bf16[96,640]{1,0:T(8,128)(2,1)S(1)}, bf16[96,640]{1,0:T(8,128)(2,1)S(1)}, u32[]{:S(2)}, u32[]{:S(2)}) collective-permute-start(bf16[96,640]{1,0:T(8,128)(2,1)S(1)} %fusion.2), channel_id=1, source_target_pairs={{0,16},{2,18},{4,20},{6,22},{8,24},{10,26},{12,28},{14,30},{16,0},... | collective-permute-start | bytes 368648 | tf_op jit(solution)/shard_map/ppermute | solution.py:35
  69.7 1.5 %copy-start.2 = (bf16[384,2560]{1,0:T(8,128)(2,1)S(1)}, bf16[384,2560]{1,0:T(8,128)(2,1)}, u32[]{:S(2)}) copy-start(bf16[384,2560]{1,0:T(8,128)(2,1)} %copy-done.1) | copy-start | bytes 5898244
  71.2 1.0 %copy-start.4 = (bf16[384,512]{1,0:T(8,128)(2,1)S(1)}, bf16[384,512]{1,0:T(8,128)(2,1)}, u32[]{:S(2)}) copy-start(bf16[384,512]{1,0:T(8,128)(2,1)} %copy-done.3) | copy-start | bytes 1179652

commit v6 on v5

--- a/solution.py
+++ b/solution.py
@@ -433,7 +433,9 @@
         value = add(*blocks[k]).astype(jnp.bfloat16)
         act, sent, value = lax.optimization_barrier((act, sent, value))
         blocks[k] = swap(value, "node", nodes, k).astype(jnp.float32)
-    blocks[0] = add(mine, after(got, sent))
+    act, d_inner = after((act, d_inner), sent, value)
+    gate_grad, up_grad, down_grad = weight_grads(all_tokens, all_cots, act, d_inner)
+    blocks[0] = add(mine, after(got, gate_grad))
     high = place // owners
 
     def block_for(owner):
@@ -442,13 +444,9 @@
             chosen = jnp.where((owner ^ node) == k, blocks[k], chosen)
         return chosen
 
-    sent = [block_for(high ^ j).astype(jnp.bfloat16) for j in range(1, nodes)]
-    act, d_inner = after((act, d_inner), sent)
-    gate_grad, up_grad, down_grad = weight_grads(all_tokens, all_cots, act, d_inner)
     token_grad = block_for(high)
     for j in range(1, nodes):
-        arrived = after(swap(sent[j - 1], "dp", width, j * owners), gate_grad)
-        token_grad += arrived.astype(jnp.float32)
+        token_grad += swap(block_for(high ^ j).astype(jnp.bfloat16), "dp", width, j * owners).astype(jnp.float32)
     token_grad = token_grad.astype(jnp.bfloat16)
     token_grad = jnp.concatenate([token_grad[:, :block], token_grad[:, block:]])
     return token_grad, gate_grad, up_grad, down_grad

time: 79.9 us -> 90.6 us (1.13)
  local copies, waits for them, and re-layouts: 4.3 us -> 19.5 us
  waiting for transfers between devices: 21 us -> 16.6 us
  other arithmetic: 6.17 us -> 4.8 us
    unnamed x14 -> x58, local copies, waits for them, and re-layouts: 3.83 us -> 18.1 us
    ppermute x19, waiting for transfers between devices: 21 us -> 16.6 us  [swap(): return lax.ppermute(value, axis, flipped(size, mask))]
    convert_element_type x1, other arithmetic: 1.17 us -> 0.11 us  [body(): block_for(high ^ j).astype(jnp.bfloat16)]
    reshape x2, local copies, waits for them, and re-layouts: 0.37 us -> 1.35 us  [prepare(): scales = scales.reshape(units, steps, per_step).transpose(1, 0, 2)]
  transfers between devices with their start and end apart: 19 -> 19, of which waited for: 8 -> 3; matrix products, arithmetic and copies ran while one was open for 4% -> 5% of each run, Pallas kernels for 31% -> 28%
where the time goes in v6:
time: 90.6 us; the launch traced here: 89.9 us
  Pallas kernels  27.4 us (30%)
  starting transfers between devices  20.7 us (23%)
  local copies, waits for them, and re-layouts  19.5 us (22%)
  waiting for transfers between devices  16.6 us (18%)
  other arithmetic  4.8 us (5%)
    ppermute x19, starting transfers between devices, swap(): return lax.ppermute(value, axis, flipped(size, mask))  20.7 us
    unnamed x58, local copies, waits for them, and re-layouts  18.1 us
    ppermute x19, waiting for transfers between devices, swap(): return lax.ppermute(value, axis, flipped(size, mask))  16.6 us
    pallas_call x3, Pallas kernels, activate(): pl.pallas_call(functools.partial(activate_kernel, group, turns, count, bl...  8.1 us
    pallas_call x1, Pallas kernels, prepare(): pl.pallas_call(prepare_kernel, in_specs=[IN_SMEM] + [IN_HBM] * 5 + [IN_VM...  6.49 us
    pallas_call x2, Pallas kernels, join(): pl.pallas_call(functools.partial(join_kernel, group, far), in_specs=[IN_S...  5.54 us
    pallas_call x1, Pallas kernels, weight_grads(): pl.pallas_call(grads_kernel, in_specs=[IN_VMEM] * 4, out_specs=[IN_HBM] *...  5.36 us
    pallas_call x1, Pallas kernels, fetch(): pl.pallas_call(functools.partial(fetch_kernel, mask), in_specs=[IN_SMEM,...  1.89 us
  transfers between devices with their start and end apart: 19, of which 3 were waited for; matrix products, arithmetic and copies ran while one was open for 5% of the time, Pallas kernels for 28%

profile of v6, /device:TPU:0, one launch (start us, length us, event | category | flops | bytes accessed | tf_op | source)
XLA Modules:
  0.0 89.9 jit_solution(12237119208172335547)
XLA Ops:
  0.6 0.0 copy-start
  0.7 1.9 %fetch.1 = bf16[96,2560]{1,0:T(8,128)(2,1)} custom-call(s32[1]{0:T(128)} %bitcast.1.node, s32[1]{0:T(128)} %bitcast.place, bf16[192,5120]{1,0:T(8,128)(2,1)} %tokens.3, bf16[192,5120]{1,0:T(8,128)(2,1)} %cot.3), custom_call_target="tpu_custom_call" | custom-call | tf_op jit(solution)/shard_map/fetch/pallas_call | solution.py:78
  2.6 3.0 %collective-permute-start = (bf16[96,2560]{1,0:T(8,128)(2,1)}, bf16[96,2560]{1,0:T(8,128)(2,1)}, u32[]{:S(2)}, u32[]{:S(2)}) collective-permute-start(bf16[96,2560]{1,0:T(8,128)(2,1)} %fetch.1), channel_id=1, source_target_pairs={{0,1},{1,0},{2,3},{3,2},{4,5},{5,4},{6,7},{7,6},{8,9},{9,8},{10,11... | collective-permute-start | bytes 1474568 | tf_op jit(solution)/shard_map/ppermute | solution.py:35
  5.6 1.3 %copy.25 = f32[512,4,5]{2,0,1:T(8,128)} copy(f32[512,4,5]{0,2,1:T(8,128)S(1)} %reshape.19) | data formatting | bytes 81920 | tf_op jit(solution)/shard_map/reshape | solution.py:143
  7.0 1.2 %copy-done.5 = f32[512,4,5]{2,0,1:T(8,128)S(1)} copy-done((f32[512,4,5]{2,0,1:T(8,128)S(1)}, f32[512,4,5]{2,0,1:T(8,128)}, u32[]{:S(2)}) %copy-start.5) | copy-done | bytes 40984
  8.2 6.5 %prepare.1 = (bf16[384,2560]{1,0:T(8,128)(2,1)S(1)}, bf16[384,2560]{1,0:T(8,128)(2,1)S(1)}, bf16[2560,1024]{1,0:T(8,128)(2,1)S(1)}, bf16[512,2560]{1,0:T(8,128)(...) custom-call(s32[1]{0:T(128)} %bitcast.1.node, bf16[192,5120]{1,0:T(8,128)(2,1)} %tokens.3, ...), custom_call_target="tpu_custom_call" | custom-call | tf_op jit(solution)/shard_map/prepare/pallas_call | solution.py:145
  14.7 2.4 %collective-permute-done.held = bf16[96,2560]{1,0:T(8,128)(2,1)} collective-permute-done((bf16[96,2560]{1,0:T(8,128)(2,1)}, bf16[96,2560]{1,0:T(8,128)(2,1)}, u32[]{:S(2)}, u32[]{:S(2)}) %collective-permute-start) | collective-permute-done | bytes 491552 | tf_op jit(solution)/shard_map/ppermute | solution.py:35
  17.1 1.8 %collective-permute-start.1 = (bf16[96,2560]{1,0:T(8,128)(2,1)}, bf16[96,2560]{1,0:T(8,128)(2,1)S(1)}, u32[]{:S(2)}, u32[]{:S(2)}) collective-permute-start(bf16[96,2560]{1,0:T(8,128)(2,1)} %collective-permute-done.held), channel_id=1, source_target_pairs={{0,8},{2,10},{4,12},{6,14},{8,0},{10,2},{12,4},{14,6},{16,24},{18,... | collective-permute-start | bytes 1474568 | tf_op jit(solution)/shard_map/ppermute | solution.py:35
  18.9 1.5 %collective-permute-start.5 = (bf16[192,1536]{1,0:T(8,128)(2,1)S(1)}, bf16[192,1536]{1,0:T(8,128)(2,1)S(1)}, u32[]{:S(2)}, u32[]{:S(2)}) collective-permute-start(bf16[192,1536]{1,0:T(8,128)(2,1)S(1)} %get-tuple-element.52), channel_id=1, source_target_pairs={{0,1},{1,0},{2,3},{3,2},{4,5},{5,4},{6,7},{7,6},{8,9},{9,8},{10,11... | collective-permute-start | bytes 1769480 | tf_op jit(solution)/shard_map/ppermute | solution.py:35
  20.5 9.3 %collective-permute-done.1.held = bf16[96,2560]{1,0:T(8,128)(2,1)S(1)} collective-permute-done((bf16[96,2560]{1,0:T(8,128)(2,1)}, bf16[96,2560]{1,0:T(8,128)(2,1)S(1)}, u32[]{:S(2)}, u32[]{:S(2)}) %collective-permute-start.1) | collective-permute-done | bytes 491552 | tf_op jit(solution)/shard_map/ppermute | solution.py:35
  29.8 2.9 %join.2 = (bf16[384,2560]{1,0:T(8,128)(2,1)S(1)}, bf16[384,2560]{1,0:T(8,128)(2,1)S(1)}, f32[192,1536]{1,0:T(8,128)S(1)}, bf16[96,1536]{1,0:T(8,128)(2,1)S(1)}) custom-call(s32[1]{0:T(128)} %bitcast.place, bf16[96,2560]{1,0:T(8,128)(2,1)} %collective-permute-done.held, ...), custom_call_target="tpu_custom_call", output_to_operand_aliasing={{0}: (5, {}), {1}: (6, {})} | custom-call | tf_op jit(solution)/shard_map/join/pallas_call | solution.py:202
  32.7 1.5 %collective-permute-start.8 = (bf16[96,1536]{1,0:T(8,128)(2,1)S(1)}, bf16[96,1536]{1,0:T(8,128)(2,1)S(1)}, u32[]{:S(2)}, u32[]{:S(2)}) collective-permute-start(bf16[96,1536]{1,0:T(8,128)(2,1)S(1)} %get-tuple-element.65), channel_id=1, source_target_pairs={{0,1},{1,0},{2,3},{3,2},{4,5},{5,4},{6,7},{7,6},{8,9},{9,8},{10,11... | collective-permute-start | bytes 884744 | tf_op jit(solution)/shard_map/ppermute | solution.py:35
  34.2 0.0 collective-permute-done.2.given
  34.2 2.6 %join.3 = (bf16[384,2560]{1,0:T(8,128)(2,1)S(1)}, bf16[384,2560]{1,0:T(8,128)(2,1)S(1)}, f32[192,1536]{1,0:T(8,128)S(1)}, bf16[96,1536]{1,0:T(8,128)(2,1)}) custom-call(s32[1]{0:T(128)} %bitcast.place, bf16[96,2560]{1,0:T(8,128)(2,1)S(1)} %collective-permute-done.1.held, ...), custom_call_target="tpu_custom_call", output_to_operand_aliasing={{0}: (5, {}), {1}: (6, {}), {2}: (7, {})} | custom-call | tf_op jit(solution)/shard_map/join/pallas_call | solution.py:202
  36.8 1.3 %copy-done.3 = bf16[384,2560]{1,0:T(8,128)(2,1)} copy-done((bf16[384,2560]{1,0:T(8,128)(2,1)}, bf16[384,2560]{1,0:T(8,128)(2,1)S(1)}, u32[]{:S(2)}) %copy-start.3) | copy-done | bytes 1966104
  38.1 0.0 collective-permute-done.5.arrived
  38.1 3.8 %activate.3 = (bf16[384,512]{1,0:T(8,128)(2,1)S(1)}, bf16[384,1024]{1,0:T(8,128)(2,1)S(1)}, bf16[96,1280]{1,0:T(8,128)(2,1)S(1)}, bf16[96,1280]{1,0:T(8,128)(2,1...) custom-call(s32[1]{0:T(128)} %bitcast.place, bf16[2560,1024]{1,0:T(8,128)(2,1)S(1)} %get-tuple-element.50.w_in.weights, ...), custom_call_target="tpu_custom_call" | custom-call | tf_op jit(solution)/shard_map/activate/pallas_call | solution.py:277
  41.9 0.0 copy-start.19
  41.9 0.3 collective-permute-start.6
  42.2 0.3 collective-permute-start.7
  42.5 0.6 collective-permute-start.4
  43.1 0.0 collective-permute-done.8.arrived
  43.1 2.0 %activate.4 = (bf16[384,512]{1,0:T(8,128)(2,1)S(1)}, bf16[384,1024]{1,0:T(8,128)(2,1)S(1)}, bf16[96,1280]{1,0:T(8,128)(2,1)S(1)}, bf16[96,1280]{1,0:T(8,128)(2,1...) custom-call(s32[1]{0:T(128)} %bitcast.place, ...), custom_call_target="tpu_custom_call", output_to_operand_aliasing={{0}: (4, {}), {1}: (5, {})} | custom-call | tf_op jit(solution)/shard_map/activate/pallas_call | solution.py:277
  45.1 0.0 copy-start.6
  45.1 0.9 copy-done.6
  46.0 0.8 copy-done.10
  46.7 0.8 copy-done.13
  47.6 0.7 copy-done.15
  48.3 0.0 collective-permute-done.6
  48.3 0.0 collective-permute-done.7
  48.3 0.8 add_convert_fusion.4
  49.1 1.7 %collective-permute-start.13 = (bf16[96,640]{1,0:T(8,128)(2,1)}, bf16[96,640]{1,0:T(8,128)(2,1)}, u32[]{:S(2)}, u32[]{:S(2)}) collective-permute-start(bf16[96,640]{1,0:T(8,128)(2,1)} %add_convert_fusion.4), channel_id=1, source_target_pairs={{0,8},{2,10},{4,12},{6,14},{8,0},{10,2},{12,4},{14,6},{16,24},{18,... | collective-permute-start | bytes 368648 | tf_op jit(solution)/shard_map/ppermute | solution.py:35
  50.8 0.8 add_convert_fusion.5
  51.5 1.5 %collective-permute-start.12 = (bf16[96,640]{1,0:T(8,128)(2,1)}, bf16[96,640]{1,0:T(8,128)(2,1)}, u32[]{:S(2)}, u32[]{:S(2)}) collective-permute-start(bf16[96,640]{1,0:T(8,128)(2,1)} %get-tuple-element.98), channel_id=1, source_target_pairs={{0,4},{2,6},{4,0},{6,2},{8,12},{10,14},{12,8},{14,10},{16,20},{18,... | collective-permute-start | bytes 368648 | tf_op jit(solution)/shard_map/ppermute | solution.py:35
  53.0 0.3 collective-permute-start.11
  53.4 0.0 collective-permute-done.4.arrived
  53.4 2.5 %copy-done.2 = bf16[2560,1024]{1,0:T(8,128)(2,1)S(1)} copy-done((bf16[2560,1024]{1,0:T(8,128)(2,1)S(1)}, bf16[2560,1024]{1,0:T(8,128)(2,1)}, u32[]{:S(2)}) %copy-start.2) | copy-done | bytes 5242904
  55.9 1.1 %copy-done.7 = bf16[384,1024]{1,0:T(8,128)(2,1)S(1)} copy-done((bf16[384,1024]{1,0:T(8,128)(2,1)S(1)}, bf16[384,1024]{1,0:T(8,128)(2,1)}, u32[]{:S(2)}) %copy-start.7) | copy-done | bytes 786456
  57.0 1.0 %copy-done.11 = f32[96,1280]{1,0:T(8,128)S(1)} copy-done((f32[96,1280]{1,0:T(8,128)S(1)}, f32[96,1280]{1,0:T(8,128)}, u32[]{:S(2)}) %copy-start.11) | copy-done | bytes 491544
  58.0 1.0 %copy-done.14 = f32[96,1280]{1,0:T(8,128)S(1)} copy-done((f32[96,1280]{1,0:T(8,128)S(1)}, f32[96,1280]{1,0:T(8,128)}, u32[]{:S(2)}) %copy-start.14) | copy-done | bytes 491544
  59.0 1.0 %copy-done.16 = bf16[384,512]{1,0:T(8,128)(2,1)S(1)} copy-done((bf16[384,512]{1,0:T(8,128)(2,1)S(1)}, bf16[384,512]{1,0:T(8,128)(2,1)}, u32[]{:S(2)}) %copy-start.16) | copy-done | bytes 393240
  60.0 0.9 %copy-done.22 = bf16[96,1280]{1,0:T(8,128)(2,1)S(1)} copy-done((bf16[96,1280]{1,0:T(8,128)(2,1)S(1)}, bf16[96,1280]{1,0:T(8,128)(2,1)}, u32[]{:S(2)}) %copy-start.22) | copy-done | bytes 245784
  61.0 0.9 %copy-done.24 = bf16[96,1280]{1,0:T(8,128)(2,1)S(1)} copy-done((bf16[96,1280]{1,0:T(8,128)(2,1)S(1)}, bf16[96,1280]{1,0:T(8,128)(2,1)}, u32[]{:S(2)}) %copy-start.24) | copy-done | bytes 245784
  61.9 2.3 %activate.5 = (bf16[384,512]{1,0:T(8,128)(2,1)S(1)}, bf16[384,1024]{1,0:T(8,128)(2,1)S(1)}, bf16[96,1280]{1,0:T(8,128)(2,1)S(1)}, bf16[96,1280]{1,0:T(8,128)(2,1...) custom-call(s32[1]{0:T(128)} %bitcast.place, ...), custom_call_target="tpu_custom_call", output_to_operand_aliasing={{0}: (4, {}), {1}: (5, {}), {2}: (6, {}), {3}: (7, {}), {4}... | custom-call | tf_op jit(solution)/shard_map/activate/pallas_call | solution.py:277
  64.3 0.0 copy-start.8
  64.3 0.9 copy-done.8
  65.1 0.8 copy-done.17
  65.9 0.0 collective-permute-start.9
  65.9 0.5 collective-permute-start.10
  66.4 1.3 %add_convert_fusion = bf16[96,640]{1,0:T(8,128)(2,1)S(1)} fusion(bf16[96,640]{1,0:T(8,128)(2,1)} %collective-permute-done.13, bf16[96,640]{1,0:T(8,128)(2,1)} %collective-permute-done.12, bf16[96,640]{1,0:T(8,128)(2,1)} %collective-permute-done.11, f32[96,1280]{1,0:T(8,128)S(1)} %copy-done.20, bf16[96,1280]{1,0:T(8,128)(2,1)S(1)} %copy-done.28), kind=kLoop, calls=%fused_computation.6 | loop fusion | flops 552960 | bytes 860160 | tf_op jit(solution)/shard_map/convert_element_type | solution.py:433
  67.8 0.1 add_convert_fusion.2
  67.8 2.5 %collective-permute-start.15 = (bf16[96,640]{1,0:T(8,128)(2,1)S(1)}, bf16[96,640]{1,0:T(8,128)(2,1)S(1)}, u32[]{:S(2)}, u32[]{:S(2)}) collective-permute-start(bf16[96,640]{1,0:T(8,128)(2,1)S(1)} %get-tuple-element.97), channel_id=1, source_target_pairs={{0,12},{2,14},{4,8},{6,10},{8,4},{10,6},{12,0},{14,2},{16,28},{18,... | collective-permute-start | bytes 368648 | tf_op jit(solution)/shard_map/ppermute | solution.py:35
  70.3 0.5 collective-permute-start.16
  70.9 0.6 collective-permute-start.17
  71.5 1.4 %collective-permute-start.14 = (bf16[96,640]{1,0:T(8,128)(2,1)S(1)}, bf16[96,640]{1,0:T(8,128)(2,1)S(1)}, u32[]{:S(2)}, u32[]{:S(2)}) collective-permute-start(bf16[96,640]{1,0:T(8,128)(2,1)S(1)} %add_convert_fusion), channel_id=1, source_target_pairs={{0,1},{1,0},{2,3},{3,2},{4,5},{5,4},{6,7},{7,6},{8,9},{9,8},{10,11... | collective-permute-start | bytes 368648 | tf_op jit(solution)/shard_map/ppermute | solution.py:35
  72.9 1.1 %copy-done.9 = bf16[384,1024]{1,0:T(8,128)(2,1)S(1)} copy-done((bf16[384,1024]{1,0:T(8,128)(2,1)S(1)}, bf16[384,1024]{1,0:T(8,128)(2,1)}, u32[]{:S(2)}) %copy-start.9) | copy-done | bytes 786456
  74.1 1.0 %copy-done.18 = bf16[384,512]{1,0:T(8,128)(2,1)S(1)} copy-done((bf16[384,512]{1,0:T(8,128)(2,1)S(1)}, bf16[384,512]{1,0:T(8,128)(2,1)}, u32[]{:S(2)}) %copy-start.18) | copy-done | bytes 393240
  75.1 5.4 %weight_grads.1 = (bf16[2560,512]{1,0:T(8,128)(2,1)}, bf16[2560,512]{1,0:T(8,128)(2,1)}, bf16[512,2560]{1,0:T(8,128)(2,1)}) custom-call(bf16[384,2560]{1,0:T(8,128)(2,1)S(1)} %get-tuple-element.84.tokens, bf16[384,2560]{1,0:T(8,128)(2,1)S(1)} %copy-done.4, bf16[384,512]{1,0:T(8,128)(2,1)S(1)} %copy-done.18, bf16[384,1024]{1,0:T(8,128)(2,1)S(1)} %copy-done.9), custom_call_target="tpu_custom_call" | custom-call | flops 3019898880 | tf_op jit(solution)/shard_map/weight_grads/pallas_call | solution.py:321
  80.5 0.1 fusion.2
  80.6 2.6 %collective-permute-start.18 = (bf16[96,640]{1,0:T(8,128)(2,1)S(1)}, bf16[96,640]{1,0:T(8,128)(2,1)S(1)}, u32[]{:S(2)}, u32[]{:S(2)}) collective-permute-start(bf16[96,640]{1,0:T(8,128)(2,1)S(1)} %fusion.2), channel_id=1, source_target_pairs={{0,16},{2,18},{4,20},{6,22},{8,24},{10,26},{12,28},{14,30},{16,0},... | collective-permute-start | bytes 368648 | tf_op jit(solution)/shard_map/ppermute | solution.py:35
  83.2 4.8 %collective-permute-done.18 = bf16[96,640]{1,0:T(8,128)(2,1)S(1)} collective-permute-done((bf16[96,640]{1,0:T(8,128)(2,1)S(1)}, bf16[96,640]{1,0:T(8,128)(2,1)S(1)}, u32[]{:S(2)}, u32[]{:S(2)}) %collective-permute-start.18) | collective-permute-done | bytes 122912 | tf_op jit(solution)/shard_map/ppermute | solution.py:35
  88.1 1.1 %fusion.1 = bf16[96,640]{1,0:T(8,128)(2,1)S(1)} fusion(bf16[96,640]{1,0:T(8,128)(2,1)S(1)} %collective-permute-done.14, bf16[96,640]{1,0:T(8,128)(2,1)S(1)} %collective-permute-done.18, pred[]{:T(512)S(6)} %eq.6, bf16[96,640]{1,0:T(8,128)(2,1)S(1)} %collective-permute-done.17, bf16[96,640]{1,0:T(8,128)(2,1)S(1)} %collective-permute-done.16, ...), kind=kLoop, calls=%fused_computation.3 | loop fusion | flops 798720 | bytes 1105921 | tf_op jit(solution)/shard_map/convert_element_type | solution.py:450
  89.2 0.1 fusion.3
  89.2 0.7 pad_maximum_fusion
  (52 shorter events, 0.1 us)
Async XLA Ops:
  0.6 5.0 %copy-start = (f32[512,40]{0,1:T(8,128)S(1)}, f32[512,40]{0,1:T(8,128)}, u32[]{:S(2)}) copy-start(f32[512,40]{0,1:T(8,128)} %param.15) | copy-start | bytes 245764
  0.7 6.3 %copy-start.25 = (f32[40,512]{1,0:T(8,128)S(1)}, f32[40,512]{1,0:T(8,128)}, u32[]{:S(2)}) copy-start(f32[40,512]{1,0:T(8,128)} %gate_scales.1) | copy-start | bytes 245764
  0.7 6.3 %copy-start.26 = (f32[40,512]{1,0:T(8,128)S(1)}, f32[40,512]{1,0:T(8,128)}, u32[]{:S(2)}) copy-start(f32[40,512]{1,0:T(8,128)} %up_scales.1) | copy-start | bytes 245764
  2.6 14.6 %collective-permute-start = (bf16[96,2560]{1,0:T(8,128)(2,1)}, bf16[96,2560]{1,0:T(8,128)(2,1)}, u32[]{:S(2)}, u32[]{:S(2)}) collective-permute-start(bf16[96,2560]{1,0:T(8,128)(2,1)} %fetch.1), channel_id=1, source_target_pairs={{0,1},{1,0},{2,3},{3,2},{4,5},{5,4},{6,7},{7,6},{8,9},{9,8},{10,11... | collective-permute-start | bytes 1474568 | tf_op jit(solution)/shard_map/ppermute | solution.py:35
  7.0 1.2 %copy-start.5 = (f32[512,4,5]{2,0,1:T(8,128)S(1)}, f32[512,4,5]{2,0,1:T(8,128)}, u32[]{:S(2)}) copy-start(f32[512,4,5]{2,0,1:T(8,128)} %copy.25) | copy-start | bytes 122884
  14.7 28.4 %copy-start.1 = (bf16[2560,1024]{1,0:T(8,128)(2,1)}, bf16[2560,1024]{1,0:T(8,128)(2,1)S(1)}, u32[]{:S(2)}) copy-start(bf16[2560,1024]{1,0:T(8,128)(2,1)S(1)} %get-tuple-element.50.w_in.weights) | copy-start | bytes 15728644
  17.1 12.6 %collective-permute-start.1 = (bf16[96,2560]{1,0:T(8,128)(2,1)}, bf16[96,2560]{1,0:T(8,128)(2,1)S(1)}, u32[]{:S(2)}, u32[]{:S(2)}) collective-permute-start(bf16[96,2560]{1,0:T(8,128)(2,1)} %collective-permute-done.held), channel_id=1, source_target_pairs={{0,8},{2,10},{4,12},{6,14},{8,0},{10,2},{12,4},{14,6},{16,24},{18,... | collective-permute-start | bytes 1474568 | tf_op jit(solution)/shard_map/ppermute | solution.py:35
  18.9 19.1 %collective-permute-start.5 = (bf16[192,1536]{1,0:T(8,128)(2,1)S(1)}, bf16[192,1536]{1,0:T(8,128)(2,1)S(1)}, u32[]{:S(2)}, u32[]{:S(2)}) collective-permute-start(bf16[192,1536]{1,0:T(8,128)(2,1)S(1)} %get-tuple-element.52), channel_id=1, source_target_pairs={{0,1},{1,0},{2,3},{3,2},{4,5},{5,4},{6,7},{7,6},{8,9},{9,8},{10,11... | collective-permute-start | bytes 1769480 | tf_op jit(solution)/shard_map/ppermute | solution.py:35
  20.5 9.3 %collective-permute-start.3 = (bf16[96,2560]{1,0:T(8,128)(2,1)}, bf16[96,2560]{1,0:T(8,128)(2,1)S(1)}, u32[]{:S(2)}, u32[]{:S(2)}) collective-permute-start(bf16[96,2560]{1,0:T(8,128)(2,1)} %collective-permute-done.held), channel_id=1, source_target_pairs={{0,2},{2,0},{4,6},{6,4},{8,10},{10,8},{12,14},{14,12},{16,18},{18,... | collective-permute-start | bytes 1474568 | tf_op jit(solution)/shard_map/ppermute | solution.py:35
  29.8 4.4 %collective-permute-start.2 = (bf16[96,2560]{1,0:T(8,128)(2,1)S(1)}, bf16[96,2560]{1,0:T(8,128)(2,1)S(1)}, u32[]{:S(2)}, u32[]{:S(2)}) collective-permute-start(bf16[96,2560]{1,0:T(8,128)(2,1)S(1)} %collective-permute-done.1.held), channel_id=1, source_target_pairs={{0,2},{2,0},{4,6},{6,4},{8,10},{10,8},{12,14},{14,12},{16,18},{18,... | collective-permute-start | bytes 1474568 | tf_op jit(solution)/shard_map/ppermute | solution.py:35
  32.7 10.4 %collective-permute-start.8 = (bf16[96,1536]{1,0:T(8,128)(2,1)S(1)}, bf16[96,1536]{1,0:T(8,128)(2,1)S(1)}, u32[]{:S(2)}, u32[]{:S(2)}) collective-permute-start(bf16[96,1536]{1,0:T(8,128)(2,1)S(1)} %get-tuple-element.65), channel_id=1, source_target_pairs={{0,1},{1,0},{2,3},{3,2},{4,5},{5,4},{6,7},{7,6},{8,9},{9,8},{10,11... | collective-permute-start | bytes 884744 | tf_op jit(solution)/shard_map/ppermute | solution.py:35
  36.8 1.3 %copy-start.3 = (bf16[384,2560]{1,0:T(8,128)(2,1)}, bf16[384,2560]{1,0:T(8,128)(2,1)S(1)}, u32[]{:S(2)}) copy-start(bf16[384,2560]{1,0:T(8,128)(2,1)S(1)} %get-tuple-element.85.cot) | copy-start | bytes 5898244
  41.9 6.4 %copy-start.19 = (f32[96,1280]{1,0:T(8,128)}, f32[96,1280]{1,0:T(8,128)S(1)}, u32[]{:S(2)}) copy-start(f32[96,1280]{1,0:T(8,128)S(1)} %get-tuple-element.75) | copy-start | bytes 1474564
  41.9 6.4 %collective-permute-start.6 = (bf16[96,1280]{1,0:T(8,128)(2,1)S(1)}, bf16[96,1280]{1,0:T(8,128)(2,1)S(1)}, u32[]{:S(2)}, u32[]{:S(2)}) collective-permute-start(bf16[96,1280]{1,0:T(8,128)(2,1)S(1)} %get-tuple-element.63), channel_id=1, source_target_pairs={{0,2},{2,0},{4,6},{6,4},{8,10},{10,8},{12,14},{14,12},{16,18},{18,... | collective-permute-start | bytes 737288 | tf_op jit(solution)/shard_map/ppermute | solution.py:35
  42.2 6.1 %collective-permute-start.7 = (bf16[96,1280]{1,0:T(8,128)(2,1)S(1)}, bf16[96,1280]{1,0:T(8,128)(2,1)S(1)}, u32[]{:S(2)}, u32[]{:S(2)}) collective-permute-start(bf16[96,1280]{1,0:T(8,128)(2,1)S(1)} %get-tuple-element.64), channel_id=1, source_target_pairs={{0,2},{2,0},{4,6},{6,4},{8,10},{10,8},{12,14},{14,12},{16,18},{18,... | collective-permute-start | bytes 737288 | tf_op jit(solution)/shard_map/ppermute | solution.py:35
  42.5 10.9 %collective-permute-start.4 = (bf16[96,1536]{1,0:T(8,128)(2,1)}, bf16[96,1536]{1,0:T(8,128)(2,1)S(1)}, u32[]{:S(2)}, u32[]{:S(2)}) collective-permute-start(bf16[96,1536]{1,0:T(8,128)(2,1)} %get-tuple-element.60), channel_id=1, source_target_pairs={{0,1},{1,0},{2,3},{3,2},{4,5},{5,4},{6,7},{7,6},{8,9},{9,8},{10,11... | collective-permute-start | bytes 884744 | tf_op jit(solution)/shard_map/ppermute | solution.py:35
  45.1 0.9 copy-start.6
  46.0 0.8 copy-start.10
  46.7 0.8 copy-start.13
  47.6 0.7 copy-start.15
  48.3 3.2 %copy-start.21 = (bf16[96,1280]{1,0:T(8,128)(2,1)}, bf16[96,1280]{1,0:T(8,128)(2,1)S(1)}, u32[]{:S(2)}) copy-start(bf16[96,1280]{1,0:T(8,128)(2,1)S(1)} %get-tuple-element.70.refs_2_) | copy-start | bytes 737284
  48.3 3.2 %copy-start.23 = (bf16[96,1280]{1,0:T(8,128)(2,1)}, bf16[96,1280]{1,0:T(8,128)(2,1)S(1)}, u32[]{:S(2)}) copy-start(bf16[96,1280]{1,0:T(8,128)(2,1)S(1)} %get-tuple-element.71.refs_3_) | copy-start | bytes 737284
  48.3 4.7 %copy-start.27 = (bf16[96,1280]{1,0:T(8,128)(2,1)}, bf16[96,1280]{1,0:T(8,128)(2,1)S(1)}, u32[]{:S(2)}) copy-start(bf16[96,1280]{1,0:T(8,128)(2,1)S(1)} %collective-permute-done.7) | copy-start | bytes 737284
  49.1 17.3 %collective-permute-start.13 = (bf16[96,640]{1,0:T(8,128)(2,1)}, bf16[96,640]{1,0:T(8,128)(2,1)}, u32[]{:S(2)}, u32[]{:S(2)}) collective-permute-start(bf16[96,640]{1,0:T(8,128)(2,1)} %add_convert_fusion.4), channel_id=1, source_target_pairs={{0,8},{2,10},{4,12},{6,14},{8,0},{10,2},{12,4},{14,6},{16,24},{18,... | collective-permute-start | bytes 368648 | tf_op jit(solution)/shard_map/ppermute | solution.py:35
  51.5 14.9 %collective-permute-start.12 = (bf16[96,640]{1,0:T(8,128)(2,1)}, bf16[96,640]{1,0:T(8,128)(2,1)}, u32[]{:S(2)}, u32[]{:S(2)}) collective-permute-start(bf16[96,640]{1,0:T(8,128)(2,1)} %get-tuple-element.98), channel_id=1, source_target_pairs={{0,4},{2,6},{4,0},{6,2},{8,12},{10,14},{12,8},{14,10},{16,20},{18,... | collective-permute-start | bytes 368648 | tf_op jit(solution)/shard_map/ppermute | solution.py:35
  53.0 13.4 %collective-permute-start.11 = (bf16[96,640]{1,0:T(8,128)(2,1)}, bf16[96,640]{1,0:T(8,128)(2,1)}, u32[]{:S(2)}, u32[]{:S(2)}) collective-permute-start(bf16[96,640]{1,0:T(8,128)(2,1)} %get-tuple-element.99), channel_id=1, source_target_pairs={{0,12},{2,14},{4,8},{6,10},{8,4},{10,6},{12,0},{14,2},{16,28},{18,... | collective-permute-start | bytes 368648 | tf_op jit(solution)/shard_map/ppermute | solution.py:35
  53.4 2.5 %copy-start.2 = (bf16[2560,1024]{1,0:T(8,128)(2,1)S(1)}, bf16[2560,1024]{1,0:T(8,128)(2,1)}, u32[]{:S(2)}) copy-start(bf16[2560,1024]{1,0:T(8,128)(2,1)} %copy-done.1) | copy-start | bytes 15728644
  55.8 1.1 %copy-start.7 = (bf16[384,1024]{1,0:T(8,128)(2,1)S(1)}, bf16[384,1024]{1,0:T(8,128)(2,1)}, u32[]{:S(2)}) copy-start(bf16[384,1024]{1,0:T(8,128)(2,1)} %copy-done.6) | copy-start | bytes 2359300
  57.0 1.0 %copy-start.11 = (f32[96,1280]{1,0:T(8,128)S(1)}, f32[96,1280]{1,0:T(8,128)}, u32[]{:S(2)}) copy-start(f32[96,1280]{1,0:T(8,128)} %copy-done.10) | copy-start | bytes 1474564
  58.0 1.0 %copy-start.14 = (f32[96,1280]{1,0:T(8,128)S(1)}, f32[96,1280]{1,0:T(8,128)}, u32[]{:S(2)}) copy-start(f32[96,1280]{1,0:T(8,128)} %copy-done.13) | copy-start | bytes 1474564
  59.0 1.0 %copy-start.16 = (bf16[384,512]{1,0:T(8,128)(2,1)S(1)}, bf16[384,512]{1,0:T(8,128)(2,1)}, u32[]{:S(2)}) copy-start(bf16[384,512]{1,0:T(8,128)(2,1)} %copy-done.15) | copy-start | bytes 1179652
  60.0 0.9 %copy-start.22 = (bf16[96,1280]{1,0:T(8,128)(2,1)S(1)}, bf16[96,1280]{1,0:T(8,128)(2,1)}, u32[]{:S(2)}) copy-start(bf16[96,1280]{1,0:T(8,128)(2,1)} %copy-done.21) | copy-start | bytes 737284
  61.0 0.9 %copy-start.24 = (bf16[96,1280]{1,0:T(8,128)(2,1)S(1)}, bf16[96,1280]{1,0:T(8,128)(2,1)}, u32[]{:S(2)}) copy-start(bf16[96,1280]{1,0:T(8,128)(2,1)} %copy-done.23) | copy-start | bytes 737284
  61.9 4.5 %copy-start.20 = (f32[96,1280]{1,0:T(8,128)S(1)}, f32[96,1280]{1,0:T(8,128)}, u32[]{:S(2)}) copy-start(f32[96,1280]{1,0:T(8,128)} %copy-done.19) | copy-start | bytes 1474564
  61.9 4.5 %copy-start.28 = (bf16[96,1280]{1,0:T(8,128)(2,1)S(1)}, bf16[96,1280]{1,0:T(8,128)(2,1)}, u32[]{:S(2)}) copy-start(bf16[96,1280]{1,0:T(8,128)(2,1)} %copy-done.27) | copy-start | bytes 737284
  64.3 0.9 copy-start.8
  65.1 0.8 copy-start.17
  65.9 14.6 %copy-start.12 = (f32[96,1280]{1,0:T(8,128)}, f32[96,1280]{1,0:T(8,128)S(1)}, u32[]{:S(2)}) copy-start(f32[96,1280]{1,0:T(8,128)S(1)} %get-tuple-element.81) | copy-start | bytes 1474564
  65.9 7.0 %copy-start.4 = (bf16[384,2560]{1,0:T(8,128)(2,1)S(1)}, bf16[384,2560]{1,0:T(8,128)(2,1)}, u32[]{:S(2)}) copy-start(bf16[384,2560]{1,0:T(8,128)(2,1)} %copy-done.3) | copy-start | bytes 5898244
  65.9 1.9 %collective-permute-start.9 = (bf16[96,1280]{1,0:T(8,128)(2,1)S(1)}, bf16[96,1280]{1,0:T(8,128)(2,1)S(1)}, u32[]{:S(2)}, u32[]{:S(2)}) collective-permute-start(bf16[96,1280]{1,0:T(8,128)(2,1)S(1)} %get-tuple-element.80), channel_id=1, source_target_pairs={{0,2},{2,0},{4,6},{6,4},{8,10},{10,8},{12,14},{14,12},{16,18},{18,... | collective-permute-start | bytes 737288 | tf_op jit(solution)/shard_map/ppermute | solution.py:35
  65.9 5.0 %collective-permute-start.10 = (bf16[96,1280]{1,0:T(8,128)(2,1)S(1)}, bf16[96,1280]{1,0:T(8,128)(2,1)S(1)}, u32[]{:S(2)}, u32[]{:S(2)}) collective-permute-start(bf16[96,1280]{1,0:T(8,128)(2,1)S(1)} %get-tuple-element.82), channel_id=1, source_target_pairs={{0,2},{2,0},{4,6},{6,4},{8,10},{10,8},{12,14},{14,12},{16,18},{18,... | collective-permute-start | bytes 737288 | tf_op jit(solution)/shard_map/ppermute | solution.py:35
  67.8 12.6 %collective-permute-start.15 = (bf16[96,640]{1,0:T(8,128)(2,1)S(1)}, bf16[96,640]{1,0:T(8,128)(2,1)S(1)}, u32[]{:S(2)}, u32[]{:S(2)}) collective-permute-start(bf16[96,640]{1,0:T(8,128)(2,1)S(1)} %get-tuple-element.97), channel_id=1, source_target_pairs={{0,12},{2,14},{4,8},{6,10},{8,4},{10,6},{12,0},{14,2},{16,28},{18,... | collective-permute-start | bytes 368648 | tf_op jit(solution)/shard_map/ppermute | solution.py:35
  70.3 10.1 %collective-permute-start.16 = (bf16[96,640]{1,0:T(8,128)(2,1)S(1)}, bf16[96,640]{1,0:T(8,128)(2,1)S(1)}, u32[]{:S(2)}, u32[]{:S(2)}) collective-permute-start(bf16[96,640]{1,0:T(8,128)(2,1)S(1)} %get-tuple-element.96), channel_id=1, source_target_pairs={{0,4},{2,6},{4,0},{6,2},{8,12},{10,14},{12,8},{14,10},{16,20},{18,... | collective-permute-start | bytes 368648 | tf_op jit(solution)/shard_map/ppermute | solution.py:35
  70.9 9.5 %collective-permute-start.17 = (bf16[96,640]{1,0:T(8,128)(2,1)S(1)}, bf16[96,640]{1,0:T(8,128)(2,1)S(1)}, u32[]{:S(2)}, u32[]{:S(2)}) collective-permute-start(bf16[96,640]{1,0:T(8,128)(2,1)S(1)} %add_convert_fusion.1), channel_id=1, source_target_pairs={{0,8},{2,10},{4,12},{6,14},{8,0},{10,2},{12,4},{14,6},{16,24},{18,... | collective-permute-start | bytes 368648 | tf_op jit(solution)/shard_map/ppermute | solution.py:35
  71.5 8.9 %collective-permute-start.14 = (bf16[96,640]{1,0:T(8,128)(2,1)S(1)}, bf16[96,640]{1,0:T(8,128)(2,1)S(1)}, u32[]{:S(2)}, u32[]{:S(2)}) collective-permute-start(bf16[96,640]{1,0:T(8,128)(2,1)S(1)} %add_convert_fusion), channel_id=1, source_target_pairs={{0,1},{1,0},{2,3},{3,2},{4,5},{5,4},{6,7},{7,6},{8,9},{9,8},{10,11... | collective-permute-start | bytes 368648 | tf_op jit(solution)/shard_map/ppermute | solution.py:35
  72.9 1.1 %copy-start.9 = (bf16[384,1024]{1,0:T(8,128)(2,1)S(1)}, bf16[384,1024]{1,0:T(8,128)(2,1)}, u32[]{:S(2)}) copy-start(bf16[384,1024]{1,0:T(8,128)(2,1)} %copy-done.8) | copy-start | bytes 2359300
  74.1 1.0 %copy-start.18 = (bf16[384,512]{1,0:T(8,128)(2,1)S(1)}, bf16[384,512]{1,0:T(8,128)(2,1)}, u32[]{:S(2)}) copy-start(bf16[384,512]{1,0:T(8,128)(2,1)} %copy-done.17) | copy-start | bytes 1179652
  80.6 7.5 %collective-permute-start.18 = (bf16[96,640]{1,0:T(8,128)(2,1)S(1)}, bf16[96,640]{1,0:T(8,128)(2,1)S(1)}, u32[]{:S(2)}, u32[]{:S(2)}) collective-permute-start(bf16[96,640]{1,0:T(8,128)(2,1)S(1)} %fusion.2), channel_id=1, source_target_pairs={{0,16},{2,18},{4,20},{6,22},{8,24},{10,26},{12,28},{14,30},{16,0},... | collective-permute-start | bytes 368648 | tf_op jit(solution)/shard_map/ppermute | solution.py:35

commit v7 on v5

--- a/solution.py
+++ b/solution.py
@@ -218,7 +218,7 @@
 
 def activate_kernel(group, turns, count, blocks, place, weights, total, arrived, *refs):
     block = weights.shape[0] // blocks
-    act, d_inner, *targets = refs[-2 - blocks // 2 :]
+    act, d_inner, _, _, *targets = refs[-4 - blocks // 2 :]
     units, half, chunk = act.shape[1], count // 2, 32
     side = side_of(place[0])
 
@@ -277,14 +277,15 @@
     return pl.pallas_call(
         functools.partial(activate_kernel, group, turns, count, blocks),
         in_specs=[IN_SMEM] + [IN_VMEM] * (3 + len(before)),
-        out_specs=[IN_VMEM] * (2 + pairs),
+        out_specs=[IN_VMEM] * (4 + pairs),
         out_shape=[
             pltpu.VMEM((groups * count, units), jnp.bfloat16),
             pltpu.VMEM((groups * count, 2 * units), jnp.bfloat16),
         ]
+        + [pltpu.VMEM(array.shape, array.dtype) for array in before[:4][-2:]]
         + [pltpu.VMEM(terms, jnp.bfloat16)] * (pairs // 2)
         + [pltpu.VMEM(terms, jnp.float32)] * (pairs // 2),
-        input_output_aliases={4 + i: i for i in range(len(before))},
+        input_output_aliases={4 + i: max(4 - len(before), 0) + i for i in range(len(before))},
         compiler_params=grant(10),
         cost_estimate=cost(0),
         name="activate",
@@ -326,7 +327,7 @@
         scratch_shapes=[pltpu.VMEM(shape, jnp.bfloat16) for shape in shapes]
         + [pltpu.SemaphoreType.DMA((3 * (rows // STEP),))],
         compiler_params=grant(10),
-        cost_estimate=cost(6 * tokens.shape[0] * rows * units),
+        cost_estimate=cost(0),
         name="weight_grads",
     )(*(in_vmem(a) for a in (tokens, cot, act, d_inner)))
 
@@ -389,6 +390,9 @@
 
     peers = owners // 2
 
+    def passed(results):
+        return *results[:4], results[4:]
+
     def split(parts, *earlier):
         size = len(parts) // 2
         got = [swap(part, "dp", width, 1) for part in parts[:size]]
@@ -411,24 +415,23 @@
             mine += value.astype(jnp.float32)
         return mine
 
-    blocks, before, others = [None] * nodes, [], [None] * nodes
+    blocks, before, others = [None] * nodes, [all_tokens, all_cots], [None] * nodes
     for k in reversed(range(1, nodes)):
-        act, d_inner, *others[k] = activate(
-            k, nodes, (0, 1), place_ref, sums[k], arrived[k], w_in, owners, before
+        *before, others[k] = passed(
+            activate(k, nodes, (0, 1), place_ref, sums[k], arrived[k], w_in, owners, before)
         )
-        before = [act, d_inner]
-    before = activate(0, nodes, (0,), place_ref, sums[0], near_far[0], w_in, owners, before)
+    *before, parts = passed(activate(0, nodes, (0,), place_ref, sums[0], near_far[0], w_in, owners, before))
     last = []
     for k in range(1, nodes):
-        sending, mine = split(others[k], before)
+        sending, mine = split(others[k], before[:2])
         last.append([value for _, value in sending])
         blocks[k] = mine, exchange(sending)
-    act, d_inner, *parts = activate(
-        0, nodes, (1,), place_ref, sums[0], after(near_far[1], last), w_in, owners, before
+    act, d_inner, all_tokens, all_cots, parts = passed(
+        activate(0, nodes, (1,), place_ref, sums[0], after(near_far[1], last), w_in, owners, [*before, *parts])
     )
     sending, mine = split(parts)
-    got = exchange(sending)
-    sent = [value for _, value in sending]
+    sent, mine = lax.optimization_barrier(([value for _, value in sending], mine))
+    got = exchange([(mask, value) for (mask, _), value in zip(sending, sent)])
     for k in range(1, nodes):
         value = add(*blocks[k]).astype(jnp.bfloat16)
         act, sent, value = lax.optimization_barrier((act, sent, value))
@@ -442,10 +445,11 @@
             chosen = jnp.where((owner ^ node) == k, blocks[k], chosen)
         return chosen
 
+    token_grad = block_for(high)
     sent = [block_for(high ^ j).astype(jnp.bfloat16) for j in range(1, nodes)]
+    token_grad, sent = lax.optimization_barrier((token_grad, sent))
     act, d_inner = after((act, d_inner), sent)
     gate_grad, up_grad, down_grad = weight_grads(all_tokens, all_cots, act, d_inner)
-    token_grad = block_for(high)
     for j in range(1, nodes):
         arrived = after(swap(sent[j - 1], "dp", width, j * owners), gate_grad)
         token_grad += arrived.astype(jnp.float32)

time: 79.9 us -> 77.3 us (0.967)
  other arithmetic: 6.17 us -> 4.09 us
  local copies, waits for them, and re-layouts: 4.3 us -> 3.29 us
    convert_element_type x4 -> x3, other arithmetic: 2.4 us -> 0.8 us  [split(): sending.append((mask, both.astype(jnp.bfloat16)))]
    convert_element_type x1, other arithmetic: 1.2 us -> 0.03 us  [body(): token_grad = token_grad.astype(jnp.bfloat16)]
    unnamed x14 -> x10, local copies, waits for them, and re-layouts: 3.83 us -> 2.83 us
  transfers between devices with their start and end apart: 19 -> 19, of which waited for: 8 -> 7; matrix products, arithmetic and copies ran while one was open for 4% -> 2% of each run, Pallas kernels for 31% -> 32%
where the time goes in v7:
time: 77.3 us; the launch traced here: 77 us
  Pallas kernels  26.8 us (35%)
  waiting for transfers between devices  21.7 us (28%)
  starting transfers between devices  20.3 us (26%)
  other arithmetic  4.09 us (5%)
  local copies, waits for them, and re-layouts  3.29 us (4%)
  between operations  0.83 us (1%)
    ppermute x19, waiting for transfers between devices, swap(): return lax.ppermute(value, axis, flipped(size, mask))  21.7 us
    ppermute x19, starting transfers between devices, swap(): return lax.ppermute(value, axis, flipped(size, mask))  20.3 us
    pallas_call x3, Pallas kernels, activate(): pl.pallas_call(functools.partial(activate_kernel, group, turns, count, bl...  8.16 us
    pallas_call x1, Pallas kernels, prepare(): pl.pallas_call(prepare_kernel, in_specs=[IN_SMEM] + [IN_HBM] * 5 + [IN_VM...  6.58 us
    pallas_call x1, Pallas kernels, weight_grads(): pl.pallas_call(grads_kernel, in_specs=[IN_VMEM] * 4, out_specs=[IN_HBM] *...  5.35 us
    pallas_call x2, Pallas kernels, join(): pl.pallas_call(functools.partial(join_kernel, group, far), in_specs=[IN_S...  4.82 us
    unnamed x10, local copies, waits for them, and re-layouts  2.83 us
    pallas_call x1, Pallas kernels, fetch(): pl.pallas_call(functools.partial(fetch_kernel, mask), in_specs=[IN_SMEM,...  1.89 us
  transfers between devices with their start and end apart: 19, of which 7 were waited for; matrix products, arithmetic and copies ran while one was open for 2% of the time, Pallas kernels for 32%

profile of v7, /device:TPU:0, one launch (start us, length us, event | category | flops | bytes accessed | tf_op | source)
XLA Modules:
  0.0 77.0 jit_solution(2721735158627139742)
XLA Ops:
  0.6 0.0 copy-start
  0.7 0.0 copy-start.3
  0.7 0.0 copy-start.4
  0.7 1.9 %fetch.1 = bf16[96,2560]{1,0:T(8,128)(2,1)} custom-call(s32[1]{0:T(128)} %bitcast.1.node, s32[1]{0:T(128)} %bitcast.place, bf16[192,5120]{1,0:T(8,128)(2,1)} %tokens.3, bf16[192,5120]{1,0:T(8,128)(2,1)} %cot.3), custom_call_target="tpu_custom_call" | custom-call | tf_op jit(solution)/shard_map/fetch/pallas_call | solution.py:78
  2.6 3.0 %collective-permute-start = (bf16[96,2560]{1,0:T(8,128)(2,1)}, bf16[96,2560]{1,0:T(8,128)(2,1)}, u32[]{:S(2)}, u32[]{:S(2)}) collective-permute-start(bf16[96,2560]{1,0:T(8,128)(2,1)} %fetch.1), channel_id=1, source_target_pairs={{0,1},{1,0},{2,3},{3,2},{4,5},{5,4},{6,7},{7,6},{8,9},{9,8},{10,11... | collective-permute-start | bytes 1474568 | tf_op jit(solution)/shard_map/ppermute | solution.py:35
  5.6 0.0 copy-done
  5.6 0.4 copy.31
  6.0 0.0 copy-done.3
  6.0 0.0 copy-done.4
  6.0 6.6 %prepare.1 = (bf16[384,2560]{1,0:T(8,128)(2,1)S(1)}, bf16[384,2560]{1,0:T(8,128)(2,1)S(1)}, bf16[2560,1024]{1,0:T(8,128)(2,1)S(1)}, bf16[512,2560]{1,0:T(8,128)(...) custom-call(s32[1]{0:T(128)} %bitcast.1.node, bf16[192,5120]{1,0:T(8,128)(2,1)} %tokens.3, ...), custom_call_target="tpu_custom_call" | custom-call | tf_op jit(solution)/shard_map/prepare/pallas_call | solution.py:145
  12.6 4.5 %collective-permute-done.held = bf16[96,2560]{1,0:T(8,128)(2,1)} collective-permute-done((bf16[96,2560]{1,0:T(8,128)(2,1)}, bf16[96,2560]{1,0:T(8,128)(2,1)}, u32[]{:S(2)}, u32[]{:S(2)}) %collective-permute-start) | collective-permute-done | bytes 491552 | tf_op jit(solution)/shard_map/ppermute | solution.py:35
  17.1 1.8 %collective-permute-start.1 = (bf16[96,2560]{1,0:T(8,128)(2,1)}, bf16[96,2560]{1,0:T(8,128)(2,1)S(1)}, u32[]{:S(2)}, u32[]{:S(2)}) collective-permute-start(bf16[96,2560]{1,0:T(8,128)(2,1)} %collective-permute-done.held), channel_id=1, source_target_pairs={{0,8},{2,10},{4,12},{6,14},{8,0},{10,2},{12,4},{14,6},{16,24},{18,... | collective-permute-start | bytes 1474568 | tf_op jit(solution)/shard_map/ppermute | solution.py:35
  18.9 1.5 %collective-permute-start.5 = (bf16[192,1536]{1,0:T(8,128)(2,1)S(1)}, bf16[192,1536]{1,0:T(8,128)(2,1)S(1)}, u32[]{:S(2)}, u32[]{:S(2)}) collective-permute-start(bf16[192,1536]{1,0:T(8,128)(2,1)S(1)} %get-tuple-element.65), channel_id=1, source_target_pairs={{0,1},{1,0},{2,3},{3,2},{4,5},{5,4},{6,7},{7,6},{8,9},{9,8},{10,11... | collective-permute-start | bytes 1769480 | tf_op jit(solution)/shard_map/ppermute | solution.py:35
  20.5 0.0 collective-permute-start.3
  20.5 9.3 %collective-permute-done.1.held = bf16[96,2560]{1,0:T(8,128)(2,1)S(1)} collective-permute-done((bf16[96,2560]{1,0:T(8,128)(2,1)}, bf16[96,2560]{1,0:T(8,128)(2,1)S(1)}, u32[]{:S(2)}, u32[]{:S(2)}) %collective-permute-start.1) | collective-permute-done | bytes 491552 | tf_op jit(solution)/shard_map/ppermute | solution.py:35
  29.8 0.0 collective-permute-start.2
  29.8 0.0 collective-permute-done.3.given
  29.8 2.9 %join.2 = (bf16[384,2560]{1,0:T(8,128)(2,1)S(1)}, bf16[384,2560]{1,0:T(8,128)(2,1)S(1)}, f32[192,1536]{1,0:T(8,128)S(1)}, bf16[96,1536]{1,0:T(8,128)(2,1)S(1)}) custom-call(s32[1]{0:T(128)} %bitcast.place, bf16[96,2560]{1,0:T(8,128)(2,1)} %collective-permute-done.held, ...), custom_call_target="tpu_custom_call", output_to_operand_aliasing={{0}: (5, {}), {1}: (6, {})} | custom-call | tf_op jit(solution)/shard_map/join/pallas_call | solution.py:202
  32.7 1.5 %collective-permute-start.8 = (bf16[96,1536]{1,0:T(8,128)(2,1)S(1)}, bf16[96,1536]{1,0:T(8,128)(2,1)S(1)}, u32[]{:S(2)}, u32[]{:S(2)}) collective-permute-start(bf16[96,1536]{1,0:T(8,128)(2,1)S(1)} %get-tuple-element.80), channel_id=1, source_target_pairs={{0,1},{1,0},{2,3},{3,2},{4,5},{5,4},{6,7},{7,6},{8,9},{9,8},{10,11... | collective-permute-start | bytes 884744 | tf_op jit(solution)/shard_map/ppermute | solution.py:35
  34.2 0.0 collective-permute-done.2.given
  34.2 1.9 %join.3 = (bf16[384,2560]{1,0:T(8,128)(2,1)S(1)}, bf16[384,2560]{1,0:T(8,128)(2,1)S(1)}, f32[192,1536]{1,0:T(8,128)S(1)}, bf16[96,1536]{1,0:T(8,128)(2,1)S(1)}) custom-call(s32[1]{0:T(128)} %bitcast.place, bf16[96,2560]{1,0:T(8,128)(2,1)S(1)} %collective-permute-done.1.held, ...), custom_call_target="tpu_custom_call", output_to_operand_aliasing={{0}: (5, {}), {1}: (6, {}), {2}: (7, {})} | custom-call | tf_op jit(solution)/shard_map/join/pallas_call | solution.py:202
  36.1 0.0 collective-permute-done.5.arrived
  36.1 3.8 %activate.3 = (bf16[384,512]{1,0:T(8,128)(2,1)S(1)}, bf16[384,1024]{1,0:T(8,128)(2,1)S(1)}, bf16[384,2560]{1,0:T(8,128)(2,1)S(1)}, bf16[384,2560]{1,0:T(8,128)(2...) custom-call(s32[1]{0:T(128)} %bitcast.place, ...), custom_call_target="tpu_custom_call", output_to_operand_aliasing={{2}: (4, {}), {3}: (5, {})} | custom-call | tf_op jit(solution)/shard_map/activate/pallas_call | solution.py:277
  39.9 0.3 collective-permute-start.6
  40.2 0.3 collective-permute-start.7
  40.5 0.6 collective-permute-start.4
  41.1 1.1 %collective-permute-done.8.arrived = bf16[96,1536]{1,0:T(8,128)(2,1)S(1)} collective-permute-done((bf16[96,1536]{1,0:T(8,128)(2,1)S(1)}, bf16[96,1536]{1,0:T(8,128)(2,1)S(1)}, u32[]{:S(2)}, u32[]{:S(2)}) %collective-permute-start.8) | collective-permute-done | bytes 294944 | tf_op jit(solution)/shard_map/ppermute | solution.py:35
  42.2 2.0 %activate.4 = (bf16[384,512]{1,0:T(8,128)(2,1)S(1)}, bf16[384,1024]{1,0:T(8,128)(2,1)S(1)}, bf16[384,2560]{1,0:T(8,128)(2,1)S(1)}, bf16[384,2560]{1,0:T(8,128)(2...) custom-call(s32[1]{0:T(128)} %bitcast.place, ...), custom_call_target="tpu_custom_call", output_to_operand_aliasing={{0}: (4, {}), {1}: (5, {}), {2}: (6, {}), {3}: (7, {})} | custom-call | tf_op jit(solution)/shard_map/activate/pallas_call | solution.py:277
  44.2 0.0 collective-permute-done.6
  44.2 0.0 collective-permute-done.7
  44.2 1.7 %collective-permute-start.13 = (bf16[96,640]{1,0:T(8,128)(2,1)S(1)}, bf16[96,640]{1,0:T(8,128)(2,1)S(1)}, u32[]{:S(2)}, u32[]{:S(2)}) collective-permute-start(bf16[96,640]{1,0:T(8,128)(2,1)S(1)} %add_convert_fusion.5), channel_id=1, source_target_pairs={{0,8},{2,10},{4,12},{6,14},{8,0},{10,2},{12,4},{14,6},{16,24},{18,... | collective-permute-start | bytes 368648 | tf_op jit(solution)/shard_map/ppermute | solution.py:35
  46.0 1.5 %collective-permute-start.12 = (bf16[96,640]{1,0:T(8,128)(2,1)S(1)}, bf16[96,640]{1,0:T(8,128)(2,1)S(1)}, u32[]{:S(2)}, u32[]{:S(2)}) collective-permute-start(bf16[96,640]{1,0:T(8,128)(2,1)S(1)} %get-tuple-element.128), channel_id=1, source_target_pairs={{0,4},{2,6},{4,0},{6,2},{8,12},{10,14},{12,8},{14,10},{16,20},{18,... | collective-permute-start | bytes 368648 | tf_op jit(solution)/shard_map/ppermute | solution.py:35
  47.5 0.3 collective-permute-start.11
  47.9 1.8 %collective-permute-done.4.arrived = bf16[96,1536]{1,0:T(8,128)(2,1)S(1)} collective-permute-done((bf16[96,1536]{1,0:T(8,128)(2,1)S(1)}, bf16[96,1536]{1,0:T(8,128)(2,1)S(1)}, u32[]{:S(2)}, u32[]{:S(2)}) %collective-permute-start.4) | collective-permute-done | bytes 294944 | tf_op jit(solution)/shard_map/ppermute | solution.py:35
  49.6 2.4 %activate.5 = (bf16[384,512]{1,0:T(8,128)(2,1)S(1)}, bf16[384,1024]{1,0:T(8,128)(2,1)S(1)}, bf16[384,2560]{1,0:T(8,128)(2,1)S(1)}, bf16[384,2560]{1,0:T(8,128)(2...) custom-call(s32[1]{0:T(128)} %bitcast.place, ...), custom_call_target="tpu_custom_call", output_to_operand_aliasing={{0}: (4, {}), {1}: (5, {}), {2}: (6, {}), {3}: (7, {}), {4}... | custom-call | tf_op jit(solution)/shard_map/activate/pallas_call | solution.py:277
  52.0 0.0 copy-start.1
  52.0 1.3 %copy-done.1 = bf16[384,2560]{1,0:T(8,128)(2,1)} copy-done((bf16[384,2560]{1,0:T(8,128)(2,1)}, bf16[384,2560]{1,0:T(8,128)(2,1)S(1)}, u32[]{:S(2)}) %copy-start.1) | copy-done | bytes 1966104
  53.3 0.0 collective-permute-start.9
  53.3 0.5 collective-permute-start.10
  53.8 0.0 collective-permute-done.13
  53.8 0.0 collective-permute-done.12
  53.8 0.0 collective-permute-done.11
  53.8 0.7 add_convert_fusion.1
  54.5 0.3 collective-permute-done.9
  54.8 0.7 add_convert_fusion.3
  55.5 0.0 collective-permute-done.10
  55.5 0.7 convert_add_fusion.1
  56.2 2.3 %collective-permute-start.15 = (bf16[96,640]{1,0:T(8,128)(2,1)}, bf16[96,640]{1,0:T(8,128)(2,1)}, u32[]{:S(2)}, u32[]{:S(2)}) collective-permute-start(bf16[96,640]{1,0:T(8,128)(2,1)} %get-tuple-element.102), channel_id=1, source_target_pairs={{0,12},{2,14},{4,8},{6,10},{8,4},{10,6},{12,0},{14,2},{16,28},{18,... | collective-permute-start | bytes 368648 | tf_op jit(solution)/shard_map/ppermute | solution.py:35
  58.5 0.5 collective-permute-start.16
  59.0 0.7 collective-permute-start.17
  59.7 1.0 %collective-permute-start.14 = (bf16[96,640]{1,0:T(8,128)(2,1)}, bf16[96,640]{1,0:T(8,128)(2,1)}, u32[]{:S(2)}, u32[]{:S(2)}) collective-permute-start(bf16[96,640]{1,0:T(8,128)(2,1)} %add_convert_fusion.1), channel_id=1, source_target_pairs={{0,1},{1,0},{2,3},{3,2},{4,5},{5,4},{6,7},{7,6},{8,9},{9,8},{10,11... | collective-permute-start | bytes 368648 | tf_op jit(solution)/shard_map/ppermute | solution.py:35
  60.7 2.3 %collective-permute-done.15 = bf16[96,640]{1,0:T(8,128)(2,1)} collective-permute-done((bf16[96,640]{1,0:T(8,128)(2,1)}, bf16[96,640]{1,0:T(8,128)(2,1)}, u32[]{:S(2)}, u32[]{:S(2)}) %collective-permute-start.15) | collective-permute-done | bytes 122912 | tf_op jit(solution)/shard_map/ppermute | solution.py:35
  63.0 2.4 %collective-permute-done.16 = bf16[96,640]{1,0:T(8,128)(2,1)} collective-permute-done((bf16[96,640]{1,0:T(8,128)(2,1)}, bf16[96,640]{1,0:T(8,128)(2,1)}, u32[]{:S(2)}, u32[]{:S(2)}) %collective-permute-start.16) | collective-permute-done | bytes 122912 | tf_op jit(solution)/shard_map/ppermute | solution.py:35
  65.4 0.0 collective-permute-done.17
  65.5 0.0 collective-permute-done.14
  65.5 1.2 %fusion = (bf16[96,640]{1,0:T(8,128)(2,1)S(1)}, f32[96,640]{1,0:T(8,128)S(1)}) fusion(bf16[96,640]{1,0:T(8,128)(2,1)} %collective-permute-done.14, pred[]{:T(512)S(6)} %eq.7, bf16[96,640]{1,0:T(8,128)(2,1)} %collective-permute-done.17, bf16[96,640]{1,0:T(8,128)(2,1)} %collective-permute-done.16, f32[96,640]{1,0:T(8,128)S(1)} %get-tuple-element.106, ...), kind=kLoop, calls=%fused_computation.2 | loop fusion | flops 614400 | bytes 1105922 | tf_op jit(solution)/shard_map/convert_element_type | solution.py:449
  66.6 2.7 %collective-permute-start.18 = (bf16[96,640]{1,0:T(8,128)(2,1)S(1)}, bf16[96,640]{1,0:T(8,128)(2,1)S(1)}, u32[]{:S(2)}, u32[]{:S(2)}) collective-permute-start(bf16[96,640]{1,0:T(8,128)(2,1)S(1)} %get-tuple-element.111), channel_id=1, source_target_pairs={{0,16},{2,18},{4,20},{6,22},{8,24},{10,26},{12,28},{14,30},{16,0},... | collective-permute-start | bytes 368648 | tf_op jit(solution)/shard_map/ppermute | solution.py:35
  69.3 0.0 copy-start.2
  69.3 1.5 %copy-done.2 = bf16[384,2560]{1,0:T(8,128)(2,1)S(1)} copy-done((bf16[384,2560]{1,0:T(8,128)(2,1)S(1)}, bf16[384,2560]{1,0:T(8,128)(2,1)}, u32[]{:S(2)}) %copy-start.2) | copy-done | bytes 1966104
  70.8 5.4 %weight_grads.1 = (bf16[2560,512]{1,0:T(8,128)(2,1)}, bf16[2560,512]{1,0:T(8,128)(2,1)}, bf16[512,2560]{1,0:T(8,128)(2,1)}) custom-call(bf16[384,2560]{1,0:T(8,128)(2,1)S(1)} %get-tuple-element.112.tokens, bf16[384,2560]{1,0:T(8,128)(2,1)S(1)} %copy-done.2, bf16[384,512]{1,0:T(8,128)(2,1)S(1)} %get-tuple-element.116.act, ...), custom_call_target="tpu_custom_call" | custom-call | tf_op jit(solution)/shard_map/weight_grads/pallas_call | solution.py:322
  76.2 0.0 collective-permute-done.18
  76.2 0.1 fusion.1
  76.3 0.7 pad_maximum_fusion
  (5 shorter events, 0.1 us)
Async XLA Ops:
  0.6 5.0 %copy-start = (f32[512,40]{0,1:T(8,128)S(1)}, f32[512,40]{0,1:T(8,128)}, u32[]{:S(2)}) copy-start(f32[512,40]{0,1:T(8,128)} %param.15) | copy-start | bytes 245764
  0.7 5.3 %copy-start.3 = (f32[40,512]{1,0:T(8,128)S(1)}, f32[40,512]{1,0:T(8,128)}, u32[]{:S(2)}) copy-start(f32[40,512]{1,0:T(8,128)} %gate_scales.1) | copy-start | bytes 245764
  0.7 5.3 %copy-start.4 = (f32[40,512]{1,0:T(8,128)S(1)}, f32[40,512]{1,0:T(8,128)}, u32[]{:S(2)}) copy-start(f32[40,512]{1,0:T(8,128)} %up_scales.1) | copy-start | bytes 245764
  2.6 14.6 %collective-permute-start = (bf16[96,2560]{1,0:T(8,128)(2,1)}, bf16[96,2560]{1,0:T(8,128)(2,1)}, u32[]{:S(2)}, u32[]{:S(2)}) collective-permute-start(bf16[96,2560]{1,0:T(8,128)(2,1)} %fetch.1), channel_id=1, source_target_pairs={{0,1},{1,0},{2,3},{3,2},{4,5},{5,4},{6,7},{7,6},{8,9},{9,8},{10,11... | collective-permute-start | bytes 1474568 | tf_op jit(solution)/shard_map/ppermute | solution.py:35
  17.1 12.6 %collective-permute-start.1 = (bf16[96,2560]{1,0:T(8,128)(2,1)}, bf16[96,2560]{1,0:T(8,128)(2,1)S(1)}, u32[]{:S(2)}, u32[]{:S(2)}) collective-permute-start(bf16[96,2560]{1,0:T(8,128)(2,1)} %collective-permute-done.held), channel_id=1, source_target_pairs={{0,8},{2,10},{4,12},{6,14},{8,0},{10,2},{12,4},{14,6},{16,24},{18,... | collective-permute-start | bytes 1474568 | tf_op jit(solution)/shard_map/ppermute | solution.py:35
  18.9 17.1 %collective-permute-start.5 = (bf16[192,1536]{1,0:T(8,128)(2,1)S(1)}, bf16[192,1536]{1,0:T(8,128)(2,1)S(1)}, u32[]{:S(2)}, u32[]{:S(2)}) collective-permute-start(bf16[192,1536]{1,0:T(8,128)(2,1)S(1)} %get-tuple-element.65), channel_id=1, source_target_pairs={{0,1},{1,0},{2,3},{3,2},{4,5},{5,4},{6,7},{7,6},{8,9},{9,8},{10,11... | collective-permute-start | bytes 1769480 | tf_op jit(solution)/shard_map/ppermute | solution.py:35
  20.5 9.3 %collective-permute-start.3 = (bf16[96,2560]{1,0:T(8,128)(2,1)}, bf16[96,2560]{1,0:T(8,128)(2,1)S(1)}, u32[]{:S(2)}, u32[]{:S(2)}) collective-permute-start(bf16[96,2560]{1,0:T(8,128)(2,1)} %collective-permute-done.held), channel_id=1, source_target_pairs={{0,2},{2,0},{4,6},{6,4},{8,10},{10,8},{12,14},{14,12},{16,18},{18,... | collective-permute-start | bytes 1474568 | tf_op jit(solution)/shard_map/ppermute | solution.py:35
  29.8 4.4 %collective-permute-start.2 = (bf16[96,2560]{1,0:T(8,128)(2,1)S(1)}, bf16[96,2560]{1,0:T(8,128)(2,1)S(1)}, u32[]{:S(2)}, u32[]{:S(2)}) collective-permute-start(bf16[96,2560]{1,0:T(8,128)(2,1)S(1)} %collective-permute-done.1.held), channel_id=1, source_target_pairs={{0,2},{2,0},{4,6},{6,4},{8,10},{10,8},{12,14},{14,12},{16,18},{18,... | collective-permute-start | bytes 1474568 | tf_op jit(solution)/shard_map/ppermute | solution.py:35
  32.7 9.5 %collective-permute-start.8 = (bf16[96,1536]{1,0:T(8,128)(2,1)S(1)}, bf16[96,1536]{1,0:T(8,128)(2,1)S(1)}, u32[]{:S(2)}, u32[]{:S(2)}) collective-permute-start(bf16[96,1536]{1,0:T(8,128)(2,1)S(1)} %get-tuple-element.80), channel_id=1, source_target_pairs={{0,1},{1,0},{2,3},{3,2},{4,5},{5,4},{6,7},{7,6},{8,9},{9,8},{10,11... | collective-permute-start | bytes 884744 | tf_op jit(solution)/shard_map/ppermute | solution.py:35
  39.9 4.2 %collective-permute-start.6 = (bf16[96,1280]{1,0:T(8,128)(2,1)S(1)}, bf16[96,1280]{1,0:T(8,128)(2,1)S(1)}, u32[]{:S(2)}, u32[]{:S(2)}) collective-permute-start(bf16[96,1280]{1,0:T(8,128)(2,1)S(1)} %get-tuple-element.78), channel_id=1, source_target_pairs={{0,2},{2,0},{4,6},{6,4},{8,10},{10,8},{12,14},{14,12},{16,18},{18,... | collective-permute-start | bytes 737288 | tf_op jit(solution)/shard_map/ppermute | solution.py:35
  40.2 4.0 %collective-permute-start.7 = (bf16[96,1280]{1,0:T(8,128)(2,1)S(1)}, bf16[96,1280]{1,0:T(8,128)(2,1)S(1)}, u32[]{:S(2)}, u32[]{:S(2)}) collective-permute-start(bf16[96,1280]{1,0:T(8,128)(2,1)S(1)} %get-tuple-element.79), channel_id=1, source_target_pairs={{0,2},{2,0},{4,6},{6,4},{8,10},{10,8},{12,14},{14,12},{16,18},{18,... | collective-permute-start | bytes 737288 | tf_op jit(solution)/shard_map/ppermute | solution.py:35
  40.5 9.1 %collective-permute-start.4 = (bf16[96,1536]{1,0:T(8,128)(2,1)S(1)}, bf16[96,1536]{1,0:T(8,128)(2,1)S(1)}, u32[]{:S(2)}, u32[]{:S(2)}) collective-permute-start(bf16[96,1536]{1,0:T(8,128)(2,1)S(1)} %get-tuple-element.73), channel_id=1, source_target_pairs={{0,1},{1,0},{2,3},{3,2},{4,5},{5,4},{6,7},{7,6},{8,9},{9,8},{10,11... | collective-permute-start | bytes 884744 | tf_op jit(solution)/shard_map/ppermute | solution.py:35
  44.2 9.6 %collective-permute-start.13 = (bf16[96,640]{1,0:T(8,128)(2,1)S(1)}, bf16[96,640]{1,0:T(8,128)(2,1)S(1)}, u32[]{:S(2)}, u32[]{:S(2)}) collective-permute-start(bf16[96,640]{1,0:T(8,128)(2,1)S(1)} %add_convert_fusion.5), channel_id=1, source_target_pairs={{0,8},{2,10},{4,12},{6,14},{8,0},{10,2},{12,4},{14,6},{16,24},{18,... | collective-permute-start | bytes 368648 | tf_op jit(solution)/shard_map/ppermute | solution.py:35
  46.0 7.8 %collective-permute-start.12 = (bf16[96,640]{1,0:T(8,128)(2,1)S(1)}, bf16[96,640]{1,0:T(8,128)(2,1)S(1)}, u32[]{:S(2)}, u32[]{:S(2)}) collective-permute-start(bf16[96,640]{1,0:T(8,128)(2,1)S(1)} %get-tuple-element.128), channel_id=1, source_target_pairs={{0,4},{2,6},{4,0},{6,2},{8,12},{10,14},{12,8},{14,10},{16,20},{18,... | collective-permute-start | bytes 368648 | tf_op jit(solution)/shard_map/ppermute | solution.py:35
  47.5 6.3 %collective-permute-start.11 = (bf16[96,640]{1,0:T(8,128)(2,1)S(1)}, bf16[96,640]{1,0:T(8,128)(2,1)S(1)}, u32[]{:S(2)}, u32[]{:S(2)}) collective-permute-start(bf16[96,640]{1,0:T(8,128)(2,1)S(1)} %get-tuple-element.129), channel_id=1, source_target_pairs={{0,12},{2,14},{4,8},{6,10},{8,4},{10,6},{12,0},{14,2},{16,28},{18,... | collective-permute-start | bytes 368648 | tf_op jit(solution)/shard_map/ppermute | solution.py:35
  52.0 1.3 %copy-start.1 = (bf16[384,2560]{1,0:T(8,128)(2,1)}, bf16[384,2560]{1,0:T(8,128)(2,1)S(1)}, u32[]{:S(2)}) copy-start(bf16[384,2560]{1,0:T(8,128)(2,1)S(1)} %get-tuple-element.113.cot) | copy-start | bytes 5898244
  53.3 1.5 %collective-permute-start.9 = (bf16[96,1280]{1,0:T(8,128)(2,1)S(1)}, bf16[96,1280]{1,0:T(8,128)(2,1)S(1)}, u32[]{:S(2)}, u32[]{:S(2)}) collective-permute-start(bf16[96,1280]{1,0:T(8,128)(2,1)S(1)} %get-tuple-element.99), channel_id=1, source_target_pairs={{0,2},{2,0},{4,6},{6,4},{8,10},{10,8},{12,14},{14,12},{16,18},{18,... | collective-permute-start | bytes 737288 | tf_op jit(solution)/shard_map/ppermute | solution.py:35
  53.3 2.2 %collective-permute-start.10 = (bf16[96,1280]{1,0:T(8,128)(2,1)S(1)}, bf16[96,1280]{1,0:T(8,128)(2,1)S(1)}, u32[]{:S(2)}, u32[]{:S(2)}) collective-permute-start(bf16[96,1280]{1,0:T(8,128)(2,1)S(1)} %get-tuple-element.101), channel_id=1, source_target_pairs={{0,2},{2,0},{4,6},{6,4},{8,10},{10,8},{12,14},{14,12},{16,18},{18,... | collective-permute-start | bytes 737288 | tf_op jit(solution)/shard_map/ppermute | solution.py:35
  56.2 6.8 %collective-permute-start.15 = (bf16[96,640]{1,0:T(8,128)(2,1)}, bf16[96,640]{1,0:T(8,128)(2,1)}, u32[]{:S(2)}, u32[]{:S(2)}) collective-permute-start(bf16[96,640]{1,0:T(8,128)(2,1)} %get-tuple-element.102), channel_id=1, source_target_pairs={{0,12},{2,14},{4,8},{6,10},{8,4},{10,6},{12,0},{14,2},{16,28},{18,... | collective-permute-start | bytes 368648 | tf_op jit(solution)/shard_map/ppermute | solution.py:35
  58.5 6.9 %collective-permute-start.16 = (bf16[96,640]{1,0:T(8,128)(2,1)}, bf16[96,640]{1,0:T(8,128)(2,1)}, u32[]{:S(2)}, u32[]{:S(2)}) collective-permute-start(bf16[96,640]{1,0:T(8,128)(2,1)} %get-tuple-element.103), channel_id=1, source_target_pairs={{0,4},{2,6},{4,0},{6,2},{8,12},{10,14},{12,8},{14,10},{16,20},{18,... | collective-permute-start | bytes 368648 | tf_op jit(solution)/shard_map/ppermute | solution.py:35
  59.0 6.4 %collective-permute-start.17 = (bf16[96,640]{1,0:T(8,128)(2,1)}, bf16[96,640]{1,0:T(8,128)(2,1)}, u32[]{:S(2)}, u32[]{:S(2)}) collective-permute-start(bf16[96,640]{1,0:T(8,128)(2,1)} %get-tuple-element.104), channel_id=1, source_target_pairs={{0,8},{2,10},{4,12},{6,14},{8,0},{10,2},{12,4},{14,6},{16,24},{18,... | collective-permute-start | bytes 368648 | tf_op jit(solution)/shard_map/ppermute | solution.py:35
  59.7 5.8 %collective-permute-start.14 = (bf16[96,640]{1,0:T(8,128)(2,1)}, bf16[96,640]{1,0:T(8,128)(2,1)}, u32[]{:S(2)}, u32[]{:S(2)}) collective-permute-start(bf16[96,640]{1,0:T(8,128)(2,1)} %add_convert_fusion.1), channel_id=1, source_target_pairs={{0,1},{1,0},{2,3},{3,2},{4,5},{5,4},{6,7},{7,6},{8,9},{9,8},{10,11... | collective-permute-start | bytes 368648 | tf_op jit(solution)/shard_map/ppermute | solution.py:35
  66.6 9.6 %collective-permute-start.18 = (bf16[96,640]{1,0:T(8,128)(2,1)S(1)}, bf16[96,640]{1,0:T(8,128)(2,1)S(1)}, u32[]{:S(2)}, u32[]{:S(2)}) collective-permute-start(bf16[96,640]{1,0:T(8,128)(2,1)S(1)} %get-tuple-element.111), channel_id=1, source_target_pairs={{0,16},{2,18},{4,20},{6,22},{8,24},{10,26},{12,28},{14,30},{16,0},... | collective-permute-start | bytes 368648 | tf_op jit(solution)/shard_map/ppermute | solution.py:35
  69.3 1.5 %copy-start.2 = (bf16[384,2560]{1,0:T(8,128)(2,1)S(1)}, bf16[384,2560]{1,0:T(8,128)(2,1)}, u32[]{:S(2)}) copy-start(bf16[384,2560]{1,0:T(8,128)(2,1)} %copy-done.1) | copy-start | bytes 5898244

commit v8 on v7

--- a/solution.py
+++ b/solution.py
@@ -81,7 +81,7 @@
         out_specs=IN_VMEM,
         out_shape=pltpu.VMEM(shape, tokens.dtype),
         scratch_shapes=[pltpu.SemaphoreType.DMA],
-        compiler_params=grant(10),
+        compiler_params=grant(12),
         cost_estimate=cost(0),
         name="fetch",
     )(node, place, in_hbm(tokens), in_hbm(cot))
@@ -155,7 +155,7 @@
             pltpu.VMEM((count, 3 * units), codes),
         ],
         scratch_shapes=[pltpu.SemaphoreType.DMA((steps, 5))],
-        compiler_params=grant(10),
+        compiler_params=grant(12),
         cost_estimate=cost(0),
         name="prepare",
     )(
@@ -210,15 +210,20 @@
             pltpu.VMEM((half, 3 * units), jnp.bfloat16),
         ],
         input_output_aliases={5 + i: i for i in range(len(before))},
-        compiler_params=grant(10),
+        compiler_params=grant(12),
         cost_estimate=cost(0),
         name="join",
     )(place, *(in_vmem(a) for a in (held, given, w_in, w_down, *before)))
 
 
-def activate_kernel(group, turns, count, blocks, place, weights, total, arrived, *refs):
+def activate_kernel(group, turns, count, blocks, parked, place, weights, total, arrived, *refs):
     block = weights.shape[0] // blocks
-    act, d_inner, _, _, *targets = refs[-4 - blocks // 2 :]
+    if parked:
+        cots, sem = refs[-6 - blocks // 2], refs[-1]
+        copy = pltpu.make_async_copy(cots, refs[-2], sem)
+        copy.start()
+        refs = refs[:-2]
+    act, d_inner, _, *targets = refs[-3 - blocks // 2 :]
     units, half, chunk = act.shape[1], count // 2, 32
     side = side_of(place[0])
 
@@ -262,37 +267,51 @@
                 lanes = slice((2 * i + h) * block, (2 * i + h + 1) * block)
                 target[:, lanes] = product[:, places[i] : places[i] + block].astype(target.dtype)
 
-    for h in (0, 1):
-        if len(turns) == 2:
-            store(h, d_inner[rows(group * count + h * half, half), :])
-        else:
+    if len(turns) == 2:
+        for p, target in enumerate(targets):
+            both = jnp.concatenate([block_rows(2 * p), block_rows(2 * p + 1)])
+            product = against(d_inner[rows(group * count, count), :], both)
+            for n in range(4):
+                i, h = n // 2, n % 2
+                value = product[h * half : (h + 1) * half, i * block : (i + 1) * block]
+                target[:, n * block : (n + 1) * block] = value.astype(target.dtype)
+    else:
+        for h in (0, 1):
             pl.when(natural == h * half)(lambda: store(h, d_inner[rows(group * count + h * half, half), :]))
-
-
-def activate(group, groups, turns, place, total, arrived, weights, blocks, before):
+    if parked:
+        copy.wait()
+
+
+def activate(group, groups, turns, place, total, arrived, weights, blocks, before, park=()):
     units, pairs = weights.shape[1] // 2, blocks // 2
     block = weights.shape[0] // blocks
     count = arrived.shape[0] * (3 - len(turns))
     terms = count // 2, 4 * block
     return pl.pallas_call(
-        functools.partial(activate_kernel, group, turns, count, blocks),
-        in_specs=[IN_SMEM] + [IN_VMEM] * (3 + len(before)),
-        out_specs=[IN_VMEM] * (4 + pairs),
+        functools.partial(activate_kernel, group, turns, count, blocks, len(park)),
+        in_specs=[IN_SMEM] + [IN_VMEM] * (3 + len(before) + len(park)),
+        out_specs=[IN_VMEM] * (3 + pairs) + [IN_HBM] * len(park),
         out_shape=[
             pltpu.VMEM((groups * count, units), jnp.bfloat16),
             pltpu.VMEM((groups * count, 2 * units), jnp.bfloat16),
+            pltpu.VMEM((groups * count, weights.shape[0]), jnp.bfloat16),
         ]
-        + [pltpu.VMEM(array.shape, array.dtype) for array in before[:4][-2:]]
         + [pltpu.VMEM(terms, jnp.bfloat16)] * (pairs // 2)
-        + [pltpu.VMEM(terms, jnp.float32)] * (pairs // 2),
-        input_output_aliases={4 + i: max(4 - len(before), 0) + i for i in range(len(before))},
-        compiler_params=grant(10),
+        + [pltpu.VMEM(terms, jnp.float32)] * (pairs // 2)
+        + [pltpu.HBM(array.shape, array.dtype) for array in park],
+        scratch_shapes=[pltpu.SemaphoreType.DMA] * len(park),
+        input_output_aliases={4 + i: max(3 - len(before), 0) + i for i in range(len(before))},
+        compiler_params=grant(12),
         cost_estimate=cost(0),
         name="activate",
-    )(place, *(in_vmem(a) for a in (weights, total, arrived, *before)))
-
-
-def grads_kernel(tokens, cot, act, d_inner, gate_grad, up_grad, down_grad, gate_held, up_held, down_held, sems):
+    )(place, *(in_vmem(a) for a in (weights, total, arrived, *before, *park)))
+
+
+def grads_kernel(
+    tokens, cots, act, d_inner, gate_grad, up_grad, down_grad, gate_held, up_held, down_held, cot, sems, cot_sem
+):
+    arriving = pltpu.make_async_copy(cots, cot, cot_sem)
+    arriving.start()
     rows, units = gate_grad.shape
     copies = []
 
@@ -308,6 +327,7 @@
         send(gate_held, gate_grad, (part, slice(None)), step)
         up_held[part, :] = both[:, units:].astype(up_held.dtype)
         send(up_held, up_grad, (part, slice(None)), steps + step)
+    arriving.wait()
     for step in range(steps):
         part = slice(step * STEP, (step + 1) * STEP)
         down_held[:, part] = contract(act[...], cot[:, part]).astype(down_held.dtype)
@@ -321,15 +341,19 @@
     shapes = [(rows, units), (rows, units), (units, rows)]
     return pl.pallas_call(
         grads_kernel,
-        in_specs=[IN_VMEM] * 4,
+        in_specs=[IN_VMEM, IN_HBM, IN_VMEM, IN_VMEM],
         out_specs=[IN_HBM] * 3,
         out_shape=[pltpu.HBM(shape, jnp.bfloat16) for shape in shapes],
         scratch_shapes=[pltpu.VMEM(shape, jnp.bfloat16) for shape in shapes]
-        + [pltpu.SemaphoreType.DMA((3 * (rows // STEP),))],
-        compiler_params=grant(10),
+        + [
+            pltpu.VMEM(cot.shape, cot.dtype),
+            pltpu.SemaphoreType.DMA((3 * (rows // STEP),)),
+            pltpu.SemaphoreType.DMA,
+        ],
+        compiler_params=grant(12),
         cost_estimate=cost(0),
         name="weight_grads",
-    )(*(in_vmem(a) for a in (tokens, cot, act, d_inner)))
+    )(in_vmem(tokens), in_hbm(cot), in_vmem(act), in_vmem(d_inner))
 
 
 def after(value, *earlier):
@@ -391,7 +415,7 @@
     peers = owners // 2
 
     def passed(results):
-        return *results[:4], results[4:]
+        return *results[:3], results[3:]
 
     def split(parts, *earlier):
         size = len(parts) // 2
@@ -415,18 +439,20 @@
             mine += value.astype(jnp.float32)
         return mine
 
-    blocks, before, others = [None] * nodes, [all_tokens, all_cots], [None] * nodes
+    blocks, before, others = [None] * nodes, [all_tokens], [None] * nodes
     for k in reversed(range(1, nodes)):
+        park = [all_cots] if k == 1 else []
         *before, others[k] = passed(
-            activate(k, nodes, (0, 1), place_ref, sums[k], arrived[k], w_in, owners, before)
+            activate(k, nodes, (0, 1), place_ref, sums[k], arrived[k], w_in, owners, before, park)
         )
+    *others[1], all_cots = others[1]
     *before, parts = passed(activate(0, nodes, (0,), place_ref, sums[0], near_far[0], w_in, owners, before))
     last = []
     for k in range(1, nodes):
         sending, mine = split(others[k], before[:2])
         last.append([value for _, value in sending])
         blocks[k] = mine, exchange(sending)
-    act, d_inner, all_tokens, all_cots, parts = passed(
+    act, d_inner, all_tokens, parts = passed(
         activate(0, nodes, (1,), place_ref, sums[0], after(near_far[1], last), w_in, owners, [*before, *parts])
     )
     sending, mine = split(parts)
@@ -436,7 +462,9 @@
         value = add(*blocks[k]).astype(jnp.bfloat16)
         act, sent, value = lax.optimization_barrier((act, sent, value))
         blocks[k] = swap(value, "node", nodes, k).astype(jnp.float32)
-    blocks[0] = add(mine, after(got, sent))
+    act, d_inner = after((act, d_inner), sent, value)
+    gate_grad, up_grad, down_grad = weight_grads(all_tokens, all_cots, act, d_inner)
+    blocks[0] = add(mine, after(got, gate_grad))
     high = place // owners
 
     def block_for(owner):
@@ -448,10 +476,8 @@
     token_grad = block_for(high)
     sent = [block_for(high ^ j).astype(jnp.bfloat16) for j in range(1, nodes)]
     token_grad, sent = lax.optimization_barrier((token_grad, sent))
-    act, d_inner = after((act, d_inner), sent)
-    gate_grad, up_grad, down_grad = weight_grads(all_tokens, all_cots, act, d_inner)
     for j in range(1, nodes):
-        arrived = after(swap(sent[j - 1], "dp", width, j * owners), gate_grad)
+        arrived = swap(sent[j - 1], "dp", width, j * owners)
         token_grad += arrived.astype(jnp.float32)
     token_grad = token_grad.astype(jnp.bfloat16)
     token_grad = jnp.concatenate([token_grad[:, :block], token_grad[:, block:]])

time: 77.3 us -> 77.3 us (level)
  local copies, waits for them, and re-layouts: 3.29 us -> 0.48 us
  waiting for transfers between devices: 21.7 us -> 23.3 us
  starting transfers between devices: 20.3 us -> 21.3 us
    unnamed x10 -> x6, local copies, waits for them, and re-layouts: 2.83 us -> 0.02 us
    ppermute x19, waiting for transfers between devices: 21.7 us -> 23.3 us  [swap(): return lax.ppermute(value, axis, flipped(size, mask))]
    pallas_call x1, Pallas kernels: 5.35 us -> 6.72 us  [weight_grads(): pl.pallas_call(grads_kernel, in_specs=[IN_VMEM, IN_HBM, IN_VMEM, IN_VMEM]...]
    pallas_call x3, Pallas kernels: 8.16 us -> 6.94 us  [activate(): pl.pallas_call(functools.partial(activate_kernel, group, turns, count, bl...]
    ppermute x19, starting transfers between devices: 20.3 us -> 21.3 us  [swap(): return lax.ppermute(value, axis, flipped(size, mask))]
  transfers between devices with their start and end apart: 19 -> 19, of which waited for: 7 -> 6; matrix products, arithmetic and copies ran while one was open for 2% -> 3% of each run, Pallas kernels for 32% -> 33%
where the time goes in v8:
time: 77.3 us; the launch traced here: 77 us
  Pallas kernels  26.9 us (35%)
  waiting for transfers between devices  23.3 us (30%)
  starting transfers between devices  21.3 us (28%)
  other arithmetic  4.15 us (5%)
  between operations  0.85 us (1%)
    ppermute x19, waiting for transfers between devices, swap(): return lax.ppermute(value, axis, flipped(size, mask))  23.3 us
    ppermute x19, starting transfers between devices, swap(): return lax.ppermute(value, axis, flipped(size, mask))  21.3 us
    pallas_call x3, Pallas kernels, activate(): pl.pallas_call(functools.partial(activate_kernel, group, turns, count, bl...  6.94 us
    pallas_call x1, Pallas kernels, weight_grads(): pl.pallas_call(grads_kernel, in_specs=[IN_VMEM, IN_HBM, IN_VMEM, IN_VMEM]...  6.72 us
    pallas_call x1, Pallas kernels, prepare(): pl.pallas_call(prepare_kernel, in_specs=[IN_SMEM] + [IN_HBM] * 5 + [IN_VM...  6.58 us
    pallas_call x2, Pallas kernels, join(): pl.pallas_call(functools.partial(join_kernel, group, far), in_specs=[IN_S...  4.82 us
    pallas_call x1, Pallas kernels, fetch(): pl.pallas_call(functools.partial(fetch_kernel, mask), in_specs=[IN_SMEM,...  1.89 us
  transfers between devices with their start and end apart: 19, of which 6 were waited for; matrix products, arithmetic and copies ran while one was open for 3% of the time, Pallas kernels for 33%

profile of v8, /device:TPU:0, one launch (start us, length us, event | category | flops | bytes accessed | tf_op | source)
XLA Modules:
  0.0 77.0 jit_solution(2991791383503773257)
XLA Ops:
  0.6 0.0 copy-start
  0.7 0.0 copy-start.1
  0.7 0.0 copy-start.2
  0.7 1.9 %fetch.1 = bf16[96,2560]{1,0:T(8,128)(2,1)} custom-call(s32[1]{0:T(128)} %bitcast.1.node, s32[1]{0:T(128)} %bitcast.place, bf16[192,5120]{1,0:T(8,128)(2,1)} %tokens.3, bf16[192,5120]{1,0:T(8,128)(2,1)} %cot.3), custom_call_target="tpu_custom_call" | custom-call | tf_op jit(solution)/shard_map/fetch/pallas_call | solution.py:78
  2.6 3.0 %collective-permute-start = (bf16[96,2560]{1,0:T(8,128)(2,1)}, bf16[96,2560]{1,0:T(8,128)(2,1)}, u32[]{:S(2)}, u32[]{:S(2)}) collective-permute-start(bf16[96,2560]{1,0:T(8,128)(2,1)} %fetch.1), channel_id=1, source_target_pairs={{0,1},{1,0},{2,3},{3,2},{4,5},{5,4},{6,7},{7,6},{8,9},{9,8},{10,11... | collective-permute-start | bytes 1474568 | tf_op jit(solution)/shard_map/ppermute | solution.py:35
  5.6 0.0 copy-done
  5.6 0.4 copy.28
  6.0 0.0 copy-done.1
  6.0 0.0 copy-done.2
  6.0 6.6 %prepare.1 = (bf16[384,2560]{1,0:T(8,128)(2,1)S(1)}, bf16[384,2560]{1,0:T(8,128)(2,1)S(1)}, bf16[2560,1024]{1,0:T(8,128)(2,1)S(1)}, bf16[512,2560]{1,0:T(8,128)(...) custom-call(s32[1]{0:T(128)} %bitcast.1.node, bf16[192,5120]{1,0:T(8,128)(2,1)} %tokens.3, ...), custom_call_target="tpu_custom_call" | custom-call | tf_op jit(solution)/shard_map/prepare/pallas_call | solution.py:145
  12.6 4.5 %collective-permute-done.held = bf16[96,2560]{1,0:T(8,128)(2,1)} collective-permute-done((bf16[96,2560]{1,0:T(8,128)(2,1)}, bf16[96,2560]{1,0:T(8,128)(2,1)}, u32[]{:S(2)}, u32[]{:S(2)}) %collective-permute-start) | collective-permute-done | bytes 491552 | tf_op jit(solution)/shard_map/ppermute | solution.py:35
  17.1 1.8 %collective-permute-start.1 = (bf16[96,2560]{1,0:T(8,128)(2,1)}, bf16[96,2560]{1,0:T(8,128)(2,1)S(1)}, u32[]{:S(2)}, u32[]{:S(2)}) collective-permute-start(bf16[96,2560]{1,0:T(8,128)(2,1)} %collective-permute-done.held), channel_id=1, source_target_pairs={{0,8},{2,10},{4,12},{6,14},{8,0},{10,2},{12,4},{14,6},{16,24},{18,... | collective-permute-start | bytes 1474568 | tf_op jit(solution)/shard_map/ppermute | solution.py:35
  18.9 1.5 %collective-permute-start.5 = (bf16[192,1536]{1,0:T(8,128)(2,1)S(1)}, bf16[192,1536]{1,0:T(8,128)(2,1)S(1)}, u32[]{:S(2)}, u32[]{:S(2)}) collective-permute-start(bf16[192,1536]{1,0:T(8,128)(2,1)S(1)} %get-tuple-element.62), channel_id=1, source_target_pairs={{0,1},{1,0},{2,3},{3,2},{4,5},{5,4},{6,7},{7,6},{8,9},{9,8},{10,11... | collective-permute-start | bytes 1769480 | tf_op jit(solution)/shard_map/ppermute | solution.py:35
  20.5 0.0 collective-permute-start.3
  20.5 9.3 %collective-permute-done.1.held = bf16[96,2560]{1,0:T(8,128)(2,1)S(1)} collective-permute-done((bf16[96,2560]{1,0:T(8,128)(2,1)}, bf16[96,2560]{1,0:T(8,128)(2,1)S(1)}, u32[]{:S(2)}, u32[]{:S(2)}) %collective-permute-start.1) | collective-permute-done | bytes 491552 | tf_op jit(solution)/shard_map/ppermute | solution.py:35
  29.8 0.0 collective-permute-start.2
  29.8 0.0 collective-permute-done.3.given
  29.8 2.9 %join.2 = (bf16[384,2560]{1,0:T(8,128)(2,1)S(1)}, bf16[384,2560]{1,0:T(8,128)(2,1)S(1)}, f32[192,1536]{1,0:T(8,128)S(1)}, bf16[96,1536]{1,0:T(8,128)(2,1)S(1)}) custom-call(s32[1]{0:T(128)} %bitcast.place, bf16[96,2560]{1,0:T(8,128)(2,1)} %collective-permute-done.held, ...), custom_call_target="tpu_custom_call", output_to_operand_aliasing={{0}: (5, {}), {1}: (6, {})} | custom-call | tf_op jit(solution)/shard_map/join/pallas_call | solution.py:202
  32.7 1.5 %collective-permute-start.8 = (bf16[96,1536]{1,0:T(8,128)(2,1)S(1)}, bf16[96,1536]{1,0:T(8,128)(2,1)S(1)}, u32[]{:S(2)}, u32[]{:S(2)}) collective-permute-start(bf16[96,1536]{1,0:T(8,128)(2,1)S(1)} %get-tuple-element.77), channel_id=1, source_target_pairs={{0,1},{1,0},{2,3},{3,2},{4,5},{5,4},{6,7},{7,6},{8,9},{9,8},{10,11... | collective-permute-start | bytes 884744 | tf_op jit(solution)/shard_map/ppermute | solution.py:35
  34.2 0.0 collective-permute-done.2.given
  34.2 1.9 %join.3 = (bf16[384,2560]{1,0:T(8,128)(2,1)S(1)}, bf16[384,2560]{1,0:T(8,128)(2,1)S(1)}, f32[192,1536]{1,0:T(8,128)S(1)}, bf16[96,1536]{1,0:T(8,128)(2,1)S(1)}) custom-call(s32[1]{0:T(128)} %bitcast.place, bf16[96,2560]{1,0:T(8,128)(2,1)S(1)} %collective-permute-done.1.held, ...), custom_call_target="tpu_custom_call", output_to_operand_aliasing={{0}: (5, {}), {1}: (6, {}), {2}: (7, {})} | custom-call | tf_op jit(solution)/shard_map/join/pallas_call | solution.py:202
  36.1 0.0 collective-permute-done.5.arrived
  36.1 2.6 %activate.3 = (bf16[384,512]{1,0:T(8,128)(2,1)S(1)}, bf16[384,1024]{1,0:T(8,128)(2,1)S(1)}, bf16[384,2560]{1,0:T(8,128)(2,1)S(1)}, bf16[96,1280]{1,0:T(8,128)(2,...) custom-call(s32[1]{0:T(128)} %bitcast.place, ...), custom_call_target="tpu_custom_call", output_to_operand_aliasing={{2}: (4, {})} | custom-call | tf_op jit(solution)/shard_map/activate/pallas_call | solution.py:290
  38.7 0.3 collective-permute-start.6
  39.0 0.3 collective-permute-start.7
  39.3 0.6 collective-permute-start.4
  39.9 2.3 %collective-permute-done.8.arrived = bf16[96,1536]{1,0:T(8,128)(2,1)S(1)} collective-permute-done((bf16[96,1536]{1,0:T(8,128)(2,1)S(1)}, bf16[96,1536]{1,0:T(8,128)(2,1)S(1)}, u32[]{:S(2)}, u32[]{:S(2)}) %collective-permute-start.8) | collective-permute-done | bytes 294944 | tf_op jit(solution)/shard_map/ppermute | solution.py:35
  42.2 2.0 %activate.4 = (bf16[384,512]{1,0:T(8,128)(2,1)S(1)}, bf16[384,1024]{1,0:T(8,128)(2,1)S(1)}, bf16[384,2560]{1,0:T(8,128)(2,1)S(1)}, bf16[96,1280]{1,0:T(8,128)(2,...) custom-call(s32[1]{0:T(128)} %bitcast.place, ...), custom_call_target="tpu_custom_call", output_to_operand_aliasing={{0}: (4, {}), {1}: (5, {}), {2}: (6, {})} | custom-call | tf_op jit(solution)/shard_map/activate/pallas_call | solution.py:290
  44.2 0.0 collective-permute-done.6
  44.2 0.0 collective-permute-done.7
  44.2 1.7 %collective-permute-start.13 = (bf16[96,640]{1,0:T(8,128)(2,1)S(1)}, bf16[96,640]{1,0:T(8,128)(2,1)S(1)}, u32[]{:S(2)}, u32[]{:S(2)}) collective-permute-start(bf16[96,640]{1,0:T(8,128)(2,1)S(1)} %add_convert_fusion.5), channel_id=1, source_target_pairs={{0,8},{2,10},{4,12},{6,14},{8,0},{10,2},{12,4},{14,6},{16,24},{18,... | collective-permute-start | bytes 368648 | tf_op jit(solution)/shard_map/ppermute | solution.py:35
  45.9 0.1 add_convert_fusion.6
  46.0 1.5 %collective-permute-start.12 = (bf16[96,640]{1,0:T(8,128)(2,1)S(1)}, bf16[96,640]{1,0:T(8,128)(2,1)S(1)}, u32[]{:S(2)}, u32[]{:S(2)}) collective-permute-start(bf16[96,640]{1,0:T(8,128)(2,1)S(1)} %get-tuple-element.122), channel_id=1, source_target_pairs={{0,4},{2,6},{4,0},{6,2},{8,12},{10,14},{12,8},{14,10},{16,20},{18,... | collective-permute-start | bytes 368648 | tf_op jit(solution)/shard_map/ppermute | solution.py:35
  47.5 0.4 collective-permute-start.11
  47.9 0.6 collective-permute-done.4.arrived
  48.5 2.4 %activate.5 = (bf16[384,512]{1,0:T(8,128)(2,1)S(1)}, bf16[384,1024]{1,0:T(8,128)(2,1)S(1)}, bf16[384,2560]{1,0:T(8,128)(2,1)S(1)}, bf16[96,1280]{1,0:T(8,128)(2,...) custom-call(s32[1]{0:T(128)} %bitcast.place, ...), custom_call_target="tpu_custom_call", output_to_operand_aliasing={{0}: (4, {}), {1}: (5, {}), {2}: (6, {}), {3}: (7, {}), {4}... | custom-call | tf_op jit(solution)/shard_map/activate/pallas_call | solution.py:290
  50.9 0.1 collective-permute-start.9
  50.9 0.5 collective-permute-start.10
  51.4 0.0 collective-permute-done.13
  51.4 2.1 %collective-permute-done.12 = bf16[96,640]{1,0:T(8,128)(2,1)S(1)} collective-permute-done((bf16[96,640]{1,0:T(8,128)(2,1)S(1)}, bf16[96,640]{1,0:T(8,128)(2,1)S(1)}, u32[]{:S(2)}, u32[]{:S(2)}) %collective-permute-start.12) | collective-permute-done | bytes 122912 | tf_op jit(solution)/shard_map/ppermute | solution.py:35
  53.6 0.0 collective-permute-done.11
  53.6 0.7 add_convert_fusion.1
  54.3 0.0 collective-permute-done.9
  54.3 0.8 %add_convert_fusion.3 = (bf16[96,640]{1,0:T(8,128)(2,1)}, bf16[96,640]{1,0:T(8,128)(2,1)}) fusion(f32[96,1280]{1,0:T(8,128)S(1)} %get-tuple-element.93, bf16[96,1280]{1,0:T(8,128)(2,1)S(1)} %collective-permute-done.9), kind=kLoop, calls=%fused_computation.8 | loop fusion | flops 368640 | bytes 983040 | tf_op jit(solution)/shard_map/convert_element_type | solution.py:431
  55.1 0.0 collective-permute-done.10
  55.1 0.7 convert_add_fusion.1
  55.8 1.0 %collective-permute-start.15 = (bf16[96,640]{1,0:T(8,128)(2,1)}, bf16[96,640]{1,0:T(8,128)(2,1)}, u32[]{:S(2)}, u32[]{:S(2)}) collective-permute-start(bf16[96,640]{1,0:T(8,128)(2,1)} %get-tuple-element.97), channel_id=1, source_target_pairs={{0,12},{2,14},{4,8},{6,10},{8,4},{10,6},{12,0},{14,2},{16,28},{18,... | collective-permute-start | bytes 368648 | tf_op jit(solution)/shard_map/ppermute | solution.py:35
  56.8 1.3 %collective-permute-start.16 = (bf16[96,640]{1,0:T(8,128)(2,1)}, bf16[96,640]{1,0:T(8,128)(2,1)}, u32[]{:S(2)}, u32[]{:S(2)}) collective-permute-start(bf16[96,640]{1,0:T(8,128)(2,1)} %get-tuple-element.98), channel_id=1, source_target_pairs={{0,4},{2,6},{4,0},{6,2},{8,12},{10,14},{12,8},{14,10},{16,20},{18,... | collective-permute-start | bytes 368648 | tf_op jit(solution)/shard_map/ppermute | solution.py:35
  58.1 1.2 %collective-permute-start.17 = (bf16[96,640]{1,0:T(8,128)(2,1)}, bf16[96,640]{1,0:T(8,128)(2,1)}, u32[]{:S(2)}, u32[]{:S(2)}) collective-permute-start(bf16[96,640]{1,0:T(8,128)(2,1)} %get-tuple-element.99), channel_id=1, source_target_pairs={{0,8},{2,10},{4,12},{6,14},{8,0},{10,2},{12,4},{14,6},{16,24},{18,... | collective-permute-start | bytes 368648 | tf_op jit(solution)/shard_map/ppermute | solution.py:35
  59.3 1.9 %collective-permute-start.14 = (bf16[96,640]{1,0:T(8,128)(2,1)}, bf16[96,640]{1,0:T(8,128)(2,1)}, u32[]{:S(2)}, u32[]{:S(2)}) collective-permute-start(bf16[96,640]{1,0:T(8,128)(2,1)} %add_convert_fusion.1), channel_id=1, source_target_pairs={{0,1},{1,0},{2,3},{3,2},{4,5},{5,4},{6,7},{7,6},{8,9},{9,8},{10,11... | collective-permute-start | bytes 368648 | tf_op jit(solution)/shard_map/ppermute | solution.py:35
  61.2 6.7 %weight_grads.1 = (bf16[2560,512]{1,0:T(8,128)(2,1)}, bf16[2560,512]{1,0:T(8,128)(2,1)}, bf16[512,2560]{1,0:T(8,128)(2,1)}) custom-call(bf16[384,2560]{1,0:T(8,128)(2,1)S(1)} %get-tuple-element.102.tokens, bf16[384,2560]{1,0:T(8,128)(2,1)} %get-tuple-element.103.cots, bf16[384,512]{1,0:T(8,128)(2,1)S(1)} %get-tuple-element.106.act, ...), custom_call_target="tpu_custom_call" | custom-call | tf_op jit(solution)/shard_map/weight_grads/pallas_call | solution.py:342
  67.9 0.0 collective-permute-done.15
  67.9 0.0 collective-permute-done.16
  67.9 0.0 collective-permute-done.17
  67.9 0.0 collective-permute-done.14
  67.9 1.2 %fusion = (bf16[96,640]{1,0:T(8,128)(2,1)S(1)}, f32[96,640]{1,0:T(8,128)S(1)}) fusion(bf16[96,640]{1,0:T(8,128)(2,1)} %collective-permute-done.14, pred[]{:T(512)S(6)} %eq.7, bf16[96,640]{1,0:T(8,128)(2,1)} %collective-permute-done.17, bf16[96,640]{1,0:T(8,128)(2,1)} %collective-permute-done.16, f32[96,640]{1,0:T(8,128)S(1)} %get-tuple-element.101, ...), kind=kLoop, calls=%fused_computation.2 | loop fusion | flops 614400 | bytes 1105922 | tf_op jit(solution)/shard_map/convert_element_type | solution.py:477
  69.1 2.7 %collective-permute-start.18 = (bf16[96,640]{1,0:T(8,128)(2,1)S(1)}, bf16[96,640]{1,0:T(8,128)(2,1)S(1)}, u32[]{:S(2)}, u32[]{:S(2)}) collective-permute-start(bf16[96,640]{1,0:T(8,128)(2,1)S(1)} %get-tuple-element.113), channel_id=1, source_target_pairs={{0,16},{2,18},{4,20},{6,22},{8,24},{10,26},{12,28},{14,30},{16,0},... | collective-permute-start | bytes 368648 | tf_op jit(solution)/shard_map/ppermute | solution.py:35
  71.8 4.4 %collective-permute-done.18 = bf16[96,640]{1,0:T(8,128)(2,1)S(1)} collective-permute-done((bf16[96,640]{1,0:T(8,128)(2,1)S(1)}, bf16[96,640]{1,0:T(8,128)(2,1)S(1)}, u32[]{:S(2)}, u32[]{:S(2)}) %collective-permute-start.18) | collective-permute-done | bytes 122912 | tf_op jit(solution)/shard_map/ppermute | solution.py:35
  76.2 0.1 fusion.1
  76.3 0.7 pad_maximum_fusion
  (4 shorter events, 0.1 us)
Async XLA Ops:
  0.6 5.0 %copy-start = (f32[512,40]{0,1:T(8,128)S(1)}, f32[512,40]{0,1:T(8,128)}, u32[]{:S(2)}) copy-start(f32[512,40]{0,1:T(8,128)} %param.15) | copy-start | bytes 245764
  0.7 5.3 %copy-start.1 = (f32[40,512]{1,0:T(8,128)S(1)}, f32[40,512]{1,0:T(8,128)}, u32[]{:S(2)}) copy-start(f32[40,512]{1,0:T(8,128)} %gate_scales.1) | copy-start | bytes 245764
  0.7 5.3 %copy-start.2 = (f32[40,512]{1,0:T(8,128)S(1)}, f32[40,512]{1,0:T(8,128)}, u32[]{:S(2)}) copy-start(f32[40,512]{1,0:T(8,128)} %up_scales.1) | copy-start | bytes 245764
  2.6 14.6 %collective-permute-start = (bf16[96,2560]{1,0:T(8,128)(2,1)}, bf16[96,2560]{1,0:T(8,128)(2,1)}, u32[]{:S(2)}, u32[]{:S(2)}) collective-permute-start(bf16[96,2560]{1,0:T(8,128)(2,1)} %fetch.1), channel_id=1, source_target_pairs={{0,1},{1,0},{2,3},{3,2},{4,5},{5,4},{6,7},{7,6},{8,9},{9,8},{10,11... | collective-permute-start | bytes 1474568 | tf_op jit(solution)/shard_map/ppermute | solution.py:35
  17.1 12.6 %collective-permute-start.1 = (bf16[96,2560]{1,0:T(8,128)(2,1)}, bf16[96,2560]{1,0:T(8,128)(2,1)S(1)}, u32[]{:S(2)}, u32[]{:S(2)}) collective-permute-start(bf16[96,2560]{1,0:T(8,128)(2,1)} %collective-permute-done.held), channel_id=1, source_target_pairs={{0,8},{2,10},{4,12},{6,14},{8,0},{10,2},{12,4},{14,6},{16,24},{18,... | collective-permute-start | bytes 1474568 | tf_op jit(solution)/shard_map/ppermute | solution.py:35
  18.9 17.1 %collective-permute-start.5 = (bf16[192,1536]{1,0:T(8,128)(2,1)S(1)}, bf16[192,1536]{1,0:T(8,128)(2,1)S(1)}, u32[]{:S(2)}, u32[]{:S(2)}) collective-permute-start(bf16[192,1536]{1,0:T(8,128)(2,1)S(1)} %get-tuple-element.62), channel_id=1, source_target_pairs={{0,1},{1,0},{2,3},{3,2},{4,5},{5,4},{6,7},{7,6},{8,9},{9,8},{10,11... | collective-permute-start | bytes 1769480 | tf_op jit(solution)/shard_map/ppermute | solution.py:35
  20.5 9.3 %collective-permute-start.3 = (bf16[96,2560]{1,0:T(8,128)(2,1)}, bf16[96,2560]{1,0:T(8,128)(2,1)S(1)}, u32[]{:S(2)}, u32[]{:S(2)}) collective-permute-start(bf16[96,2560]{1,0:T(8,128)(2,1)} %collective-permute-done.held), channel_id=1, source_target_pairs={{0,2},{2,0},{4,6},{6,4},{8,10},{10,8},{12,14},{14,12},{16,18},{18,... | collective-permute-start | bytes 1474568 | tf_op jit(solution)/shard_map/ppermute | solution.py:35
  29.8 4.4 %collective-permute-start.2 = (bf16[96,2560]{1,0:T(8,128)(2,1)S(1)}, bf16[96,2560]{1,0:T(8,128)(2,1)S(1)}, u32[]{:S(2)}, u32[]{:S(2)}) collective-permute-start(bf16[96,2560]{1,0:T(8,128)(2,1)S(1)} %collective-permute-done.1.held), channel_id=1, source_target_pairs={{0,2},{2,0},{4,6},{6,4},{8,10},{10,8},{12,14},{14,12},{16,18},{18,... | collective-permute-start | bytes 1474568 | tf_op jit(solution)/shard_map/ppermute | solution.py:35
  32.7 9.5 %collective-permute-start.8 = (bf16[96,1536]{1,0:T(8,128)(2,1)S(1)}, bf16[96,1536]{1,0:T(8,128)(2,1)S(1)}, u32[]{:S(2)}, u32[]{:S(2)}) collective-permute-start(bf16[96,1536]{1,0:T(8,128)(2,1)S(1)} %get-tuple-element.77), channel_id=1, source_target_pairs={{0,1},{1,0},{2,3},{3,2},{4,5},{5,4},{6,7},{7,6},{8,9},{9,8},{10,11... | collective-permute-start | bytes 884744 | tf_op jit(solution)/shard_map/ppermute | solution.py:35
  38.7 5.5 %collective-permute-start.6 = (bf16[96,1280]{1,0:T(8,128)(2,1)S(1)}, bf16[96,1280]{1,0:T(8,128)(2,1)S(1)}, u32[]{:S(2)}, u32[]{:S(2)}) collective-permute-start(bf16[96,1280]{1,0:T(8,128)(2,1)S(1)} %get-tuple-element.75), channel_id=1, source_target_pairs={{0,2},{2,0},{4,6},{6,4},{8,10},{10,8},{12,14},{14,12},{16,18},{18,... | collective-permute-start | bytes 737288 | tf_op jit(solution)/shard_map/ppermute | solution.py:35
  39.0 5.2 %collective-permute-start.7 = (bf16[96,1280]{1,0:T(8,128)(2,1)S(1)}, bf16[96,1280]{1,0:T(8,128)(2,1)S(1)}, u32[]{:S(2)}, u32[]{:S(2)}) collective-permute-start(bf16[96,1280]{1,0:T(8,128)(2,1)S(1)} %get-tuple-element.76), channel_id=1, source_target_pairs={{0,2},{2,0},{4,6},{6,4},{8,10},{10,8},{12,14},{14,12},{16,18},{18,... | collective-permute-start | bytes 737288 | tf_op jit(solution)/shard_map/ppermute | solution.py:35
  39.3 9.2 %collective-permute-start.4 = (bf16[96,1536]{1,0:T(8,128)(2,1)S(1)}, bf16[96,1536]{1,0:T(8,128)(2,1)S(1)}, u32[]{:S(2)}, u32[]{:S(2)}) collective-permute-start(bf16[96,1536]{1,0:T(8,128)(2,1)S(1)} %get-tuple-element.70), channel_id=1, source_target_pairs={{0,1},{1,0},{2,3},{3,2},{4,5},{5,4},{6,7},{7,6},{8,9},{9,8},{10,11... | collective-permute-start | bytes 884744 | tf_op jit(solution)/shard_map/ppermute | solution.py:35
  44.2 7.2 %collective-permute-start.13 = (bf16[96,640]{1,0:T(8,128)(2,1)S(1)}, bf16[96,640]{1,0:T(8,128)(2,1)S(1)}, u32[]{:S(2)}, u32[]{:S(2)}) collective-permute-start(bf16[96,640]{1,0:T(8,128)(2,1)S(1)} %add_convert_fusion.5), channel_id=1, source_target_pairs={{0,8},{2,10},{4,12},{6,14},{8,0},{10,2},{12,4},{14,6},{16,24},{18,... | collective-permute-start | bytes 368648 | tf_op jit(solution)/shard_map/ppermute | solution.py:35
  46.0 7.6 %collective-permute-start.12 = (bf16[96,640]{1,0:T(8,128)(2,1)S(1)}, bf16[96,640]{1,0:T(8,128)(2,1)S(1)}, u32[]{:S(2)}, u32[]{:S(2)}) collective-permute-start(bf16[96,640]{1,0:T(8,128)(2,1)S(1)} %get-tuple-element.122), channel_id=1, source_target_pairs={{0,4},{2,6},{4,0},{6,2},{8,12},{10,14},{12,8},{14,10},{16,20},{18,... | collective-permute-start | bytes 368648 | tf_op jit(solution)/shard_map/ppermute | solution.py:35
  47.5 6.0 %collective-permute-start.11 = (bf16[96,640]{1,0:T(8,128)(2,1)S(1)}, bf16[96,640]{1,0:T(8,128)(2,1)S(1)}, u32[]{:S(2)}, u32[]{:S(2)}) collective-permute-start(bf16[96,640]{1,0:T(8,128)(2,1)S(1)} %get-tuple-element.123), channel_id=1, source_target_pairs={{0,12},{2,14},{4,8},{6,10},{8,4},{10,6},{12,0},{14,2},{16,28},{18,... | collective-permute-start | bytes 368648 | tf_op jit(solution)/shard_map/ppermute | solution.py:35
  50.9 3.5 %collective-permute-start.9 = (bf16[96,1280]{1,0:T(8,128)(2,1)S(1)}, bf16[96,1280]{1,0:T(8,128)(2,1)S(1)}, u32[]{:S(2)}, u32[]{:S(2)}) collective-permute-start(bf16[96,1280]{1,0:T(8,128)(2,1)S(1)} %get-tuple-element.94), channel_id=1, source_target_pairs={{0,2},{2,0},{4,6},{6,4},{8,10},{10,8},{12,14},{14,12},{16,18},{18,... | collective-permute-start | bytes 737288 | tf_op jit(solution)/shard_map/ppermute | solution.py:35
  50.9 4.1 %collective-permute-start.10 = (bf16[96,1280]{1,0:T(8,128)(2,1)S(1)}, bf16[96,1280]{1,0:T(8,128)(2,1)S(1)}, u32[]{:S(2)}, u32[]{:S(2)}) collective-permute-start(bf16[96,1280]{1,0:T(8,128)(2,1)S(1)} %get-tuple-element.96), channel_id=1, source_target_pairs={{0,2},{2,0},{4,6},{6,4},{8,10},{10,8},{12,14},{14,12},{16,18},{18,... | collective-permute-start | bytes 737288 | tf_op jit(solution)/shard_map/ppermute | solution.py:35
  55.8 12.1 %collective-permute-start.15 = (bf16[96,640]{1,0:T(8,128)(2,1)}, bf16[96,640]{1,0:T(8,128)(2,1)}, u32[]{:S(2)}, u32[]{:S(2)}) collective-permute-start(bf16[96,640]{1,0:T(8,128)(2,1)} %get-tuple-element.97), channel_id=1, source_target_pairs={{0,12},{2,14},{4,8},{6,10},{8,4},{10,6},{12,0},{14,2},{16,28},{18,... | collective-permute-start | bytes 368648 | tf_op jit(solution)/shard_map/ppermute | solution.py:35
  56.8 11.1 %collective-permute-start.16 = (bf16[96,640]{1,0:T(8,128)(2,1)}, bf16[96,640]{1,0:T(8,128)(2,1)}, u32[]{:S(2)}, u32[]{:S(2)}) collective-permute-start(bf16[96,640]{1,0:T(8,128)(2,1)} %get-tuple-element.98), channel_id=1, source_target_pairs={{0,4},{2,6},{4,0},{6,2},{8,12},{10,14},{12,8},{14,10},{16,20},{18,... | collective-permute-start | bytes 368648 | tf_op jit(solution)/shard_map/ppermute | solution.py:35
  58.1 9.8 %collective-permute-start.17 = (bf16[96,640]{1,0:T(8,128)(2,1)}, bf16[96,640]{1,0:T(8,128)(2,1)}, u32[]{:S(2)}, u32[]{:S(2)}) collective-permute-start(bf16[96,640]{1,0:T(8,128)(2,1)} %get-tuple-element.99), channel_id=1, source_target_pairs={{0,8},{2,10},{4,12},{6,14},{8,0},{10,2},{12,4},{14,6},{16,24},{18,... | collective-permute-start | bytes 368648 | tf_op jit(solution)/shard_map/ppermute | solution.py:35
  59.3 8.7 %collective-permute-start.14 = (bf16[96,640]{1,0:T(8,128)(2,1)}, bf16[96,640]{1,0:T(8,128)(2,1)}, u32[]{:S(2)}, u32[]{:S(2)}) collective-permute-start(bf16[96,640]{1,0:T(8,128)(2,1)} %add_convert_fusion.1), channel_id=1, source_target_pairs={{0,1},{1,0},{2,3},{3,2},{4,5},{5,4},{6,7},{7,6},{8,9},{9,8},{10,11... | collective-permute-start | bytes 368648 | tf_op jit(solution)/shard_map/ppermute | solution.py:35
  69.1 7.1 %collective-permute-start.18 = (bf16[96,640]{1,0:T(8,128)(2,1)S(1)}, bf16[96,640]{1,0:T(8,128)(2,1)S(1)}, u32[]{:S(2)}, u32[]{:S(2)}) collective-permute-start(bf16[96,640]{1,0:T(8,128)(2,1)S(1)} %get-tuple-element.113), channel_id=1, source_target_pairs={{0,16},{2,18},{4,20},{6,22},{8,24},{10,26},{12,28},{14,30},{16,0},... | collective-permute-start | bytes 368648 | tf_op jit(solution)/shard_map/ppermute | solution.py:35

commit v9 on v8

--- a/solution.py
+++ b/solution.py
@@ -307,53 +307,70 @@
     )(place, *(in_vmem(a) for a in (weights, total, arrived, *before, *park)))
 
 
-def grads_kernel(
-    tokens, cots, act, d_inner, gate_grad, up_grad, down_grad, gate_held, up_held, down_held, cot, sems, cot_sem
-):
-    arriving = pltpu.make_async_copy(cots, cot, cot_sem)
-    arriving.start()
+def inner_grads_kernel(tokens, d_inner, gate_grad, up_grad, gate_held, up_held, sems):
     rows, units = gate_grad.shape
+    steps = rows // STEP
     copies = []
-
-    def send(held, target, part, i):
-        copies.append(pltpu.make_async_copy(held.at[part], target.at[part], sems.at[i]))
-        copies[-1].start()
-
-    steps = rows // STEP
     for step in range(steps):
         part = slice(step * STEP, (step + 1) * STEP)
         both = contract(tokens[:, part], d_inner[...])
         gate_held[part, :] = both[:, :units].astype(gate_held.dtype)
-        send(gate_held, gate_grad, (part, slice(None)), step)
         up_held[part, :] = both[:, units:].astype(up_held.dtype)
-        send(up_held, up_grad, (part, slice(None)), steps + step)
-    arriving.wait()
-    for step in range(steps):
-        part = slice(step * STEP, (step + 1) * STEP)
-        down_held[:, part] = contract(act[...], cot[:, part]).astype(down_held.dtype)
-        send(down_held, down_grad, (slice(None), part), 2 * steps + step)
+        for i, (held, target) in enumerate(((gate_held, gate_grad), (up_held, up_grad))):
+            copies.append(pltpu.make_async_copy(held.at[part, :], target.at[part, :], sems.at[2 * step + i]))
+            copies[-1].start()
     for copy in copies:
         copy.wait()
 
 
-def weight_grads(tokens, cot, act, d_inner):
-    rows, units = tokens.shape[1], act.shape[1]
-    shapes = [(rows, units), (rows, units), (units, rows)]
+def inner_grads(tokens, d_inner):
+    rows, units = tokens.shape[1], d_inner.shape[1] // 2
     return pl.pallas_call(
-        grads_kernel,
-        in_specs=[IN_VMEM, IN_HBM, IN_VMEM, IN_VMEM],
-        out_specs=[IN_HBM] * 3,
-        out_shape=[pltpu.HBM(shape, jnp.bfloat16) for shape in shapes],
-        scratch_shapes=[pltpu.VMEM(shape, jnp.bfloat16) for shape in shapes]
-        + [
-            pltpu.VMEM(cot.shape, cot.dtype),
-            pltpu.SemaphoreType.DMA((3 * (rows // STEP),)),
-            pltpu.SemaphoreType.DMA,
-        ],
+        inner_grads_kernel,
+        in_specs=[IN_VMEM] * 2,
+        out_specs=[IN_HBM] * 2,
+        out_shape=[pltpu.HBM((rows, units), jnp.bfloat16)] * 2,
+        scratch_shapes=[pltpu.VMEM((rows, units), jnp.bfloat16)] * 2
+        + [pltpu.SemaphoreType.DMA((2 * (rows // STEP),))],
         compiler_params=grant(12),
         cost_estimate=cost(0),
-        name="weight_grads",
-    )(in_vmem(tokens), in_hbm(cot), in_vmem(act), in_vmem(d_inner))
+        name="inner_grads",
+    )(in_vmem(tokens), in_vmem(d_inner))
+
+
+def down_grads_kernel(cots, act, down_grad, cot, held, in_sems, out_sems):
+    steps = cots.shape[1] // STEP
+    parts = [slice(step * STEP, (step + 1) * STEP) for step in range(steps)]
+    arriving = [
+        pltpu.make_async_copy(cots.at[:, part], cot.at[:, part], in_sems.at[step]) for step, part in enumerate(parts)
+    ]
+    leaving = [
+        pltpu.make_async_copy(held.at[:, part], down_grad.at[:, part], out_sems.at[step])
+        for step, part in enumerate(parts)
+    ]
+    for copy in arriving:
+        copy.start()
+    for step, part in enumerate(parts):
+        arriving[step].wait()
+        held[:, part] = contract(act[...], cot[:, part]).astype(held.dtype)
+        leaving[step].start()
+    for copy in leaving:
+        copy.wait()
+
+
+def down_grads(cots, act):
+    shape = act.shape[1], cots.shape[1]
+    sems = pltpu.SemaphoreType.DMA((shape[1] // STEP,))
+    return pl.pallas_call(
+        down_grads_kernel,
+        in_specs=[IN_HBM, IN_VMEM],
+        out_specs=IN_HBM,
+        out_shape=pltpu.HBM(shape, jnp.bfloat16),
+        scratch_shapes=[pltpu.VMEM(cots.shape, cots.dtype), pltpu.VMEM(shape, jnp.bfloat16), sems, sems],
+        compiler_params=grant(12),
+        cost_estimate=cost(0),
+        name="down_grads",
+    )(in_hbm(cots), in_vmem(act))
 
 
 def after(value, *earlier):
@@ -462,8 +479,7 @@
         value = add(*blocks[k]).astype(jnp.bfloat16)
         act, sent, value = lax.optimization_barrier((act, sent, value))
         blocks[k] = swap(value, "node", nodes, k).astype(jnp.float32)
-    act, d_inner = after((act, d_inner), sent, value)
-    gate_grad, up_grad, down_grad = weight_grads(all_tokens, all_cots, act, d_inner)
+    gate_grad, up_grad = inner_grads(all_tokens, after(d_inner, sent, value))
     blocks[0] = add(mine, after(got, gate_grad))
     high = place // owners
 
@@ -476,8 +492,9 @@
     token_grad = block_for(high)
     sent = [block_for(high ^ j).astype(jnp.bfloat16) for j in range(1, nodes)]
     token_grad, sent = lax.optimization_barrier((token_grad, sent))
+    down_grad = down_grads(all_cots, after(act, sent))
     for j in range(1, nodes):
-        arrived = swap(sent[j - 1], "dp", width, j * owners)
+        arrived = after(swap(sent[j - 1], "dp", width, j * owners), down_grad)
         token_grad += arrived.astype(jnp.float32)
     token_grad = token_grad.astype(jnp.bfloat16)
     token_grad = jnp.concatenate([token_grad[:, :block], token_grad[:, block:]])

time: 77.3 us -> 74.3 us (0.961)
  waiting for transfers between devices: 23.3 us -> 19 us
  Pallas kernels: 26.9 us -> 28.4 us
    ppermute x19, waiting for transfers between devices: 23.3 us -> 19 us  [swap(): return lax.ppermute(value, axis, flipped(size, mask))]
    pallas_call x1 -> x2, Pallas kernels: 6.72 us -> 8.16 us  [the longest x1 4.34 us: down_grads(): pl.pallas_call(down_grads_kernel, in_specs=[IN_HBM, IN_VMEM], out_specs=I...]
  transfers between devices with their start and end apart: 19 -> 19, of which waited for: 6 -> 6; matrix products, arithmetic and copies ran while one was open for 3% -> 3% of each run, Pallas kernels for 33% -> 36%
where the time goes in v9:
time: 74.3 us; the launch traced here: 74.1 us
  Pallas kernels  28.4 us (38%)
  starting transfers between devices  21.3 us (29%)
  waiting for transfers between devices  19 us (26%)
  other arithmetic  4.14 us (6%)
  between operations  0.86 us (1%)
    ppermute x19, starting transfers between devices, swap(): return lax.ppermute(value, axis, flipped(size, mask))  21.3 us
    ppermute x19, waiting for transfers between devices, swap(): return lax.ppermute(value, axis, flipped(size, mask))  19 us
    pallas_call x3, Pallas kernels, activate(): pl.pallas_call(functools.partial(activate_kernel, group, turns, count, bl...  6.94 us
    pallas_call x1, Pallas kernels, prepare(): pl.pallas_call(prepare_kernel, in_specs=[IN_SMEM] + [IN_HBM] * 5 + [IN_VM...  6.58 us
    pallas_call x2, Pallas kernels, join(): pl.pallas_call(functools.partial(join_kernel, group, far), in_specs=[IN_S...  4.82 us
    pallas_call x1, Pallas kernels, down_grads(): pl.pallas_call(down_grads_kernel, in_specs=[IN_HBM, IN_VMEM], out_specs=I...  4.34 us
    pallas_call x1, Pallas kernels, inner_grads(): pl.pallas_call(inner_grads_kernel, in_specs=[IN_VMEM] * 2, out_specs=[IN_...  3.82 us
    pallas_call x1, Pallas kernels, fetch(): pl.pallas_call(functools.partial(fetch_kernel, mask), in_specs=[IN_SMEM,...  1.89 us
  transfers between devices with their start and end apart: 19, of which 6 were waited for; matrix products, arithmetic and copies ran while one was open for 3% of the time, Pallas kernels for 36%

profile of v9, /device:TPU:0, one launch (start us, length us, event | category | flops | bytes accessed | tf_op | source)
XLA Modules:
  0.0 74.1 jit_solution(6632298206544055084)
XLA Ops:
  0.6 0.0 copy-start
  0.7 0.0 copy-start.1
  0.7 0.0 copy-start.2
  0.7 1.9 %fetch.1 = bf16[96,2560]{1,0:T(8,128)(2,1)} custom-call(s32[1]{0:T(128)} %bitcast.1.node, s32[1]{0:T(128)} %bitcast.place, bf16[192,5120]{1,0:T(8,128)(2,1)} %tokens.3, bf16[192,5120]{1,0:T(8,128)(2,1)} %cot.3), custom_call_target="tpu_custom_call" | custom-call | tf_op jit(solution)/shard_map/fetch/pallas_call | solution.py:78
  2.6 3.0 %collective-permute-start = (bf16[96,2560]{1,0:T(8,128)(2,1)}, bf16[96,2560]{1,0:T(8,128)(2,1)}, u32[]{:S(2)}, u32[]{:S(2)}) collective-permute-start(bf16[96,2560]{1,0:T(8,128)(2,1)} %fetch.1), channel_id=1, source_target_pairs={{0,1},{1,0},{2,3},{3,2},{4,5},{5,4},{6,7},{7,6},{8,9},{9,8},{10,11... | collective-permute-start | bytes 1474568 | tf_op jit(solution)/shard_map/ppermute | solution.py:35
  5.6 0.0 copy-done
  5.6 0.4 copy.28
  6.0 0.0 copy-done.1
  6.0 0.0 copy-done.2
  6.0 6.6 %prepare.1 = (bf16[384,2560]{1,0:T(8,128)(2,1)S(1)}, bf16[384,2560]{1,0:T(8,128)(2,1)S(1)}, bf16[2560,1024]{1,0:T(8,128)(2,1)S(1)}, bf16[512,2560]{1,0:T(8,128)(...) custom-call(s32[1]{0:T(128)} %bitcast.1.node, bf16[192,5120]{1,0:T(8,128)(2,1)} %tokens.3, ...), custom_call_target="tpu_custom_call" | custom-call | tf_op jit(solution)/shard_map/prepare/pallas_call | solution.py:145
  12.6 4.5 %collective-permute-done.held = bf16[96,2560]{1,0:T(8,128)(2,1)} collective-permute-done((bf16[96,2560]{1,0:T(8,128)(2,1)}, bf16[96,2560]{1,0:T(8,128)(2,1)}, u32[]{:S(2)}, u32[]{:S(2)}) %collective-permute-start) | collective-permute-done | bytes 491552 | tf_op jit(solution)/shard_map/ppermute | solution.py:35
  17.1 1.8 %collective-permute-start.1 = (bf16[96,2560]{1,0:T(8,128)(2,1)}, bf16[96,2560]{1,0:T(8,128)(2,1)S(1)}, u32[]{:S(2)}, u32[]{:S(2)}) collective-permute-start(bf16[96,2560]{1,0:T(8,128)(2,1)} %collective-permute-done.held), channel_id=1, source_target_pairs={{0,8},{2,10},{4,12},{6,14},{8,0},{10,2},{12,4},{14,6},{16,24},{18,... | collective-permute-start | bytes 1474568 | tf_op jit(solution)/shard_map/ppermute | solution.py:35
  18.9 1.5 %collective-permute-start.5 = (bf16[192,1536]{1,0:T(8,128)(2,1)S(1)}, bf16[192,1536]{1,0:T(8,128)(2,1)S(1)}, u32[]{:S(2)}, u32[]{:S(2)}) collective-permute-start(bf16[192,1536]{1,0:T(8,128)(2,1)S(1)} %get-tuple-element.62), channel_id=1, source_target_pairs={{0,1},{1,0},{2,3},{3,2},{4,5},{5,4},{6,7},{7,6},{8,9},{9,8},{10,11... | collective-permute-start | bytes 1769480 | tf_op jit(solution)/shard_map/ppermute | solution.py:35
  20.5 0.0 collective-permute-start.3
  20.5 9.3 %collective-permute-done.1.held = bf16[96,2560]{1,0:T(8,128)(2,1)S(1)} collective-permute-done((bf16[96,2560]{1,0:T(8,128)(2,1)}, bf16[96,2560]{1,0:T(8,128)(2,1)S(1)}, u32[]{:S(2)}, u32[]{:S(2)}) %collective-permute-start.1) | collective-permute-done | bytes 491552 | tf_op jit(solution)/shard_map/ppermute | solution.py:35
  29.8 0.0 collective-permute-start.2
  29.8 0.0 collective-permute-done.3.given
  29.8 2.9 %join.2 = (bf16[384,2560]{1,0:T(8,128)(2,1)S(1)}, bf16[384,2560]{1,0:T(8,128)(2,1)S(1)}, f32[192,1536]{1,0:T(8,128)S(1)}, bf16[96,1536]{1,0:T(8,128)(2,1)S(1)}) custom-call(s32[1]{0:T(128)} %bitcast.place, bf16[96,2560]{1,0:T(8,128)(2,1)} %collective-permute-done.held, ...), custom_call_target="tpu_custom_call", output_to_operand_aliasing={{0}: (5, {}), {1}: (6, {})} | custom-call | tf_op jit(solution)/shard_map/join/pallas_call | solution.py:202
  32.7 1.5 %collective-permute-start.8 = (bf16[96,1536]{1,0:T(8,128)(2,1)S(1)}, bf16[96,1536]{1,0:T(8,128)(2,1)S(1)}, u32[]{:S(2)}, u32[]{:S(2)}) collective-permute-start(bf16[96,1536]{1,0:T(8,128)(2,1)S(1)} %get-tuple-element.77), channel_id=1, source_target_pairs={{0,1},{1,0},{2,3},{3,2},{4,5},{5,4},{6,7},{7,6},{8,9},{9,8},{10,11... | collective-permute-start | bytes 884744 | tf_op jit(solution)/shard_map/ppermute | solution.py:35
  34.2 0.0 collective-permute-done.2.given
  34.2 1.9 %join.3 = (bf16[384,2560]{1,0:T(8,128)(2,1)S(1)}, bf16[384,2560]{1,0:T(8,128)(2,1)S(1)}, f32[192,1536]{1,0:T(8,128)S(1)}, bf16[96,1536]{1,0:T(8,128)(2,1)S(1)}) custom-call(s32[1]{0:T(128)} %bitcast.place, bf16[96,2560]{1,0:T(8,128)(2,1)S(1)} %collective-permute-done.1.held, ...), custom_call_target="tpu_custom_call", output_to_operand_aliasing={{0}: (5, {}), {1}: (6, {}), {2}: (7, {})} | custom-call | tf_op jit(solution)/shard_map/join/pallas_call | solution.py:202
  36.1 0.0 collective-permute-done.5.arrived
  36.1 2.6 %activate.3 = (bf16[384,512]{1,0:T(8,128)(2,1)S(1)}, bf16[384,1024]{1,0:T(8,128)(2,1)S(1)}, bf16[384,2560]{1,0:T(8,128)(2,1)S(1)}, bf16[96,1280]{1,0:T(8,128)(2,...) custom-call(s32[1]{0:T(128)} %bitcast.place, ...), custom_call_target="tpu_custom_call", output_to_operand_aliasing={{2}: (4, {})} | custom-call | tf_op jit(solution)/shard_map/activate/pallas_call | solution.py:290
  38.7 0.3 collective-permute-start.6
  39.0 0.3 collective-permute-start.7
  39.3 0.6 collective-permute-start.4
  39.9 2.3 %collective-permute-done.8.arrived = bf16[96,1536]{1,0:T(8,128)(2,1)S(1)} collective-permute-done((bf16[96,1536]{1,0:T(8,128)(2,1)S(1)}, bf16[96,1536]{1,0:T(8,128)(2,1)S(1)}, u32[]{:S(2)}, u32[]{:S(2)}) %collective-permute-start.8) | collective-permute-done | bytes 294944 | tf_op jit(solution)/shard_map/ppermute | solution.py:35
  42.2 2.0 %activate.4 = (bf16[384,512]{1,0:T(8,128)(2,1)S(1)}, bf16[384,1024]{1,0:T(8,128)(2,1)S(1)}, bf16[384,2560]{1,0:T(8,128)(2,1)S(1)}, bf16[96,1280]{1,0:T(8,128)(2,...) custom-call(s32[1]{0:T(128)} %bitcast.place, ...), custom_call_target="tpu_custom_call", output_to_operand_aliasing={{0}: (4, {}), {1}: (5, {}), {2}: (6, {})} | custom-call | tf_op jit(solution)/shard_map/activate/pallas_call | solution.py:290
  44.2 0.0 collective-permute-done.6
  44.2 0.0 collective-permute-done.7
  44.2 1.7 %collective-permute-start.13 = (bf16[96,640]{1,0:T(8,128)(2,1)S(1)}, bf16[96,640]{1,0:T(8,128)(2,1)S(1)}, u32[]{:S(2)}, u32[]{:S(2)}) collective-permute-start(bf16[96,640]{1,0:T(8,128)(2,1)S(1)} %add_convert_fusion.5), channel_id=1, source_target_pairs={{0,8},{2,10},{4,12},{6,14},{8,0},{10,2},{12,4},{14,6},{16,24},{18,... | collective-permute-start | bytes 368648 | tf_op jit(solution)/shard_map/ppermute | solution.py:35
  45.9 0.1 add_convert_fusion.6
  46.0 1.5 %collective-permute-start.12 = (bf16[96,640]{1,0:T(8,128)(2,1)S(1)}, bf16[96,640]{1,0:T(8,128)(2,1)S(1)}, u32[]{:S(2)}, u32[]{:S(2)}) collective-permute-start(bf16[96,640]{1,0:T(8,128)(2,1)S(1)} %get-tuple-element.122), channel_id=1, source_target_pairs={{0,4},{2,6},{4,0},{6,2},{8,12},{10,14},{12,8},{14,10},{16,20},{18,... | collective-permute-start | bytes 368648 | tf_op jit(solution)/shard_map/ppermute | solution.py:35
  47.5 0.4 collective-permute-start.11
  47.9 0.6 collective-permute-done.4.arrived
  48.5 2.4 %activate.5 = (bf16[384,512]{1,0:T(8,128)(2,1)S(1)}, bf16[384,1024]{1,0:T(8,128)(2,1)S(1)}, bf16[384,2560]{1,0:T(8,128)(2,1)S(1)}, bf16[96,1280]{1,0:T(8,128)(2,...) custom-call(s32[1]{0:T(128)} %bitcast.place, ...), custom_call_target="tpu_custom_call", output_to_operand_aliasing={{0}: (4, {}), {1}: (5, {}), {2}: (6, {}), {3}: (7, {}), {4}... | custom-call | tf_op jit(solution)/shard_map/activate/pallas_call | solution.py:290
  50.9 0.1 collective-permute-start.9
  50.9 0.5 collective-permute-start.10
  51.4 0.0 collective-permute-done.13
  51.4 2.1 %collective-permute-done.12 = bf16[96,640]{1,0:T(8,128)(2,1)S(1)} collective-permute-done((bf16[96,640]{1,0:T(8,128)(2,1)S(1)}, bf16[96,640]{1,0:T(8,128)(2,1)S(1)}, u32[]{:S(2)}, u32[]{:S(2)}) %collective-permute-start.12) | collective-permute-done | bytes 122912 | tf_op jit(solution)/shard_map/ppermute | solution.py:35
  53.6 0.0 collective-permute-done.11
  53.6 0.7 add_convert_fusion.1
  54.3 0.0 collective-permute-done.9
  54.3 0.8 %add_convert_fusion.3 = (bf16[96,640]{1,0:T(8,128)(2,1)}, bf16[96,640]{1,0:T(8,128)(2,1)}) fusion(f32[96,1280]{1,0:T(8,128)S(1)} %get-tuple-element.93, bf16[96,1280]{1,0:T(8,128)(2,1)S(1)} %collective-permute-done.9), kind=kLoop, calls=%fused_computation.8 | loop fusion | flops 368640 | bytes 983040 | tf_op jit(solution)/shard_map/convert_element_type | solution.py:448
  55.1 0.0 collective-permute-done.10
  55.1 0.7 convert_add_fusion.1
  55.8 1.0 %collective-permute-start.15 = (bf16[96,640]{1,0:T(8,128)(2,1)}, bf16[96,640]{1,0:T(8,128)(2,1)}, u32[]{:S(2)}, u32[]{:S(2)}) collective-permute-start(bf16[96,640]{1,0:T(8,128)(2,1)} %get-tuple-element.97), channel_id=1, source_target_pairs={{0,12},{2,14},{4,8},{6,10},{8,4},{10,6},{12,0},{14,2},{16,28},{18,... | collective-permute-start | bytes 368648 | tf_op jit(solution)/shard_map/ppermute | solution.py:35
  56.8 1.3 %collective-permute-start.16 = (bf16[96,640]{1,0:T(8,128)(2,1)}, bf16[96,640]{1,0:T(8,128)(2,1)}, u32[]{:S(2)}, u32[]{:S(2)}) collective-permute-start(bf16[96,640]{1,0:T(8,128)(2,1)} %get-tuple-element.98), channel_id=1, source_target_pairs={{0,4},{2,6},{4,0},{6,2},{8,12},{10,14},{12,8},{14,10},{16,20},{18,... | collective-permute-start | bytes 368648 | tf_op jit(solution)/shard_map/ppermute | solution.py:35
  58.1 1.2 %collective-permute-start.17 = (bf16[96,640]{1,0:T(8,128)(2,1)}, bf16[96,640]{1,0:T(8,128)(2,1)}, u32[]{:S(2)}, u32[]{:S(2)}) collective-permute-start(bf16[96,640]{1,0:T(8,128)(2,1)} %get-tuple-element.99), channel_id=1, source_target_pairs={{0,8},{2,10},{4,12},{6,14},{8,0},{10,2},{12,4},{14,6},{16,24},{18,... | collective-permute-start | bytes 368648 | tf_op jit(solution)/shard_map/ppermute | solution.py:35
  59.3 1.9 %collective-permute-start.14 = (bf16[96,640]{1,0:T(8,128)(2,1)}, bf16[96,640]{1,0:T(8,128)(2,1)}, u32[]{:S(2)}, u32[]{:S(2)}) collective-permute-start(bf16[96,640]{1,0:T(8,128)(2,1)} %add_convert_fusion.1), channel_id=1, source_target_pairs={{0,1},{1,0},{2,3},{3,2},{4,5},{5,4},{6,7},{7,6},{8,9},{9,8},{10,11... | collective-permute-start | bytes 368648 | tf_op jit(solution)/shard_map/ppermute | solution.py:35
  61.2 3.8 %inner_grads.1 = (bf16[2560,512]{1,0:T(8,128)(2,1)}, bf16[2560,512]{1,0:T(8,128)(2,1)}) custom-call(bf16[384,2560]{1,0:T(8,128)(2,1)S(1)} %get-tuple-element.102.tokens, bf16[384,1024]{1,0:T(8,128)(2,1)S(1)} %get-tuple-element.104.d_inner), custom_call_target="tpu_custom_call" | custom-call | tf_op jit(solution)/shard_map/inner_grads/pallas_call | solution.py:328
  65.0 0.0 collective-permute-done.15
  65.0 0.0 collective-permute-done.16
  65.0 0.0 collective-permute-done.17
  65.0 0.0 collective-permute-done.14
  65.0 1.2 %fusion = (bf16[96,640]{1,0:T(8,128)(2,1)S(1)}, f32[96,640]{1,0:T(8,128)S(1)}) fusion(bf16[96,640]{1,0:T(8,128)(2,1)} %collective-permute-done.14, pred[]{:T(512)S(6)} %eq.7, bf16[96,640]{1,0:T(8,128)(2,1)} %collective-permute-done.17, bf16[96,640]{1,0:T(8,128)(2,1)} %collective-permute-done.16, f32[96,640]{1,0:T(8,128)S(1)} %get-tuple-element.101, ...), kind=kLoop, calls=%fused_computation.2 | loop fusion | flops 614400 | bytes 1105922 | tf_op jit(solution)/shard_map/convert_element_type | solution.py:493
  66.2 2.7 %collective-permute-start.18 = (bf16[96,640]{1,0:T(8,128)(2,1)S(1)}, bf16[96,640]{1,0:T(8,128)(2,1)S(1)}, u32[]{:S(2)}, u32[]{:S(2)}) collective-permute-start(bf16[96,640]{1,0:T(8,128)(2,1)S(1)} %get-tuple-element.110), channel_id=1, source_target_pairs={{0,16},{2,18},{4,20},{6,22},{8,24},{10,26},{12,28},{14,30},{16,0},... | collective-permute-start | bytes 368648 | tf_op jit(solution)/shard_map/ppermute | solution.py:35
  68.8 4.3 %down_grads.1 = bf16[512,2560]{1,0:T(8,128)(2,1)} custom-call(bf16[384,2560]{1,0:T(8,128)(2,1)} %get-tuple-element.111.cots, bf16[384,512]{1,0:T(8,128)(2,1)S(1)} %get-tuple-element.113.act), custom_call_target="tpu_custom_call" | custom-call | tf_op jit(solution)/shard_map/down_grads/pallas_call | solution.py:364
  73.2 0.1 collective-permute-done.18
  73.3 0.1 fusion.1
  73.4 0.7 pad_maximum_fusion
  (4 shorter events, 0.1 us)
Async XLA Ops:
  0.6 5.0 %copy-start = (f32[512,40]{0,1:T(8,128)S(1)}, f32[512,40]{0,1:T(8,128)}, u32[]{:S(2)}) copy-start(f32[512,40]{0,1:T(8,128)} %param.15) | copy-start | bytes 245764
  0.7 5.3 %copy-start.1 = (f32[40,512]{1,0:T(8,128)S(1)}, f32[40,512]{1,0:T(8,128)}, u32[]{:S(2)}) copy-start(f32[40,512]{1,0:T(8,128)} %gate_scales.1) | copy-start | bytes 245764
  0.7 5.3 %copy-start.2 = (f32[40,512]{1,0:T(8,128)S(1)}, f32[40,512]{1,0:T(8,128)}, u32[]{:S(2)}) copy-start(f32[40,512]{1,0:T(8,128)} %up_scales.1) | copy-start | bytes 245764
  2.6 14.6 %collective-permute-start = (bf16[96,2560]{1,0:T(8,128)(2,1)}, bf16[96,2560]{1,0:T(8,128)(2,1)}, u32[]{:S(2)}, u32[]{:S(2)}) collective-permute-start(bf16[96,2560]{1,0:T(8,128)(2,1)} %fetch.1), channel_id=1, source_target_pairs={{0,1},{1,0},{2,3},{3,2},{4,5},{5,4},{6,7},{7,6},{8,9},{9,8},{10,11... | collective-permute-start | bytes 1474568 | tf_op jit(solution)/shard_map/ppermute | solution.py:35
  17.1 12.6 %collective-permute-start.1 = (bf16[96,2560]{1,0:T(8,128)(2,1)}, bf16[96,2560]{1,0:T(8,128)(2,1)S(1)}, u32[]{:S(2)}, u32[]{:S(2)}) collective-permute-start(bf16[96,2560]{1,0:T(8,128)(2,1)} %collective-permute-done.held), channel_id=1, source_target_pairs={{0,8},{2,10},{4,12},{6,14},{8,0},{10,2},{12,4},{14,6},{16,24},{18,... | collective-permute-start | bytes 1474568 | tf_op jit(solution)/shard_map/ppermute | solution.py:35
  18.9 17.1 %collective-permute-start.5 = (bf16[192,1536]{1,0:T(8,128)(2,1)S(1)}, bf16[192,1536]{1,0:T(8,128)(2,1)S(1)}, u32[]{:S(2)}, u32[]{:S(2)}) collective-permute-start(bf16[192,1536]{1,0:T(8,128)(2,1)S(1)} %get-tuple-element.62), channel_id=1, source_target_pairs={{0,1},{1,0},{2,3},{3,2},{4,5},{5,4},{6,7},{7,6},{8,9},{9,8},{10,11... | collective-permute-start | bytes 1769480 | tf_op jit(solution)/shard_map/ppermute | solution.py:35
  20.5 9.3 %collective-permute-start.3 = (bf16[96,2560]{1,0:T(8,128)(2,1)}, bf16[96,2560]{1,0:T(8,128)(2,1)S(1)}, u32[]{:S(2)}, u32[]{:S(2)}) collective-permute-start(bf16[96,2560]{1,0:T(8,128)(2,1)} %collective-permute-done.held), channel_id=1, source_target_pairs={{0,2},{2,0},{4,6},{6,4},{8,10},{10,8},{12,14},{14,12},{16,18},{18,... | collective-permute-start | bytes 1474568 | tf_op jit(solution)/shard_map/ppermute | solution.py:35
  29.8 4.4 %collective-permute-start.2 = (bf16[96,2560]{1,0:T(8,128)(2,1)S(1)}, bf16[96,2560]{1,0:T(8,128)(2,1)S(1)}, u32[]{:S(2)}, u32[]{:S(2)}) collective-permute-start(bf16[96,2560]{1,0:T(8,128)(2,1)S(1)} %collective-permute-done.1.held), channel_id=1, source_target_pairs={{0,2},{2,0},{4,6},{6,4},{8,10},{10,8},{12,14},{14,12},{16,18},{18,... | collective-permute-start | bytes 1474568 | tf_op jit(solution)/shard_map/ppermute | solution.py:35
  32.7 9.5 %collective-permute-start.8 = (bf16[96,1536]{1,0:T(8,128)(2,1)S(1)}, bf16[96,1536]{1,0:T(8,128)(2,1)S(1)}, u32[]{:S(2)}, u32[]{:S(2)}) collective-permute-start(bf16[96,1536]{1,0:T(8,128)(2,1)S(1)} %get-tuple-element.77), channel_id=1, source_target_pairs={{0,1},{1,0},{2,3},{3,2},{4,5},{5,4},{6,7},{7,6},{8,9},{9,8},{10,11... | collective-permute-start | bytes 884744 | tf_op jit(solution)/shard_map/ppermute | solution.py:35
  38.7 5.5 %collective-permute-start.6 = (bf16[96,1280]{1,0:T(8,128)(2,1)S(1)}, bf16[96,1280]{1,0:T(8,128)(2,1)S(1)}, u32[]{:S(2)}, u32[]{:S(2)}) collective-permute-start(bf16[96,1280]{1,0:T(8,128)(2,1)S(1)} %get-tuple-element.75), channel_id=1, source_target_pairs={{0,2},{2,0},{4,6},{6,4},{8,10},{10,8},{12,14},{14,12},{16,18},{18,... | collective-permute-start | bytes 737288 | tf_op jit(solution)/shard_map/ppermute | solution.py:35
  39.0 5.2 %collective-permute-start.7 = (bf16[96,1280]{1,0:T(8,128)(2,1)S(1)}, bf16[96,1280]{1,0:T(8,128)(2,1)S(1)}, u32[]{:S(2)}, u32[]{:S(2)}) collective-permute-start(bf16[96,1280]{1,0:T(8,128)(2,1)S(1)} %get-tuple-element.76), channel_id=1, source_target_pairs={{0,2},{2,0},{4,6},{6,4},{8,10},{10,8},{12,14},{14,12},{16,18},{18,... | collective-permute-start | bytes 737288 | tf_op jit(solution)/shard_map/ppermute | solution.py:35
  39.3 9.2 %collective-permute-start.4 = (bf16[96,1536]{1,0:T(8,128)(2,1)S(1)}, bf16[96,1536]{1,0:T(8,128)(2,1)S(1)}, u32[]{:S(2)}, u32[]{:S(2)}) collective-permute-start(bf16[96,1536]{1,0:T(8,128)(2,1)S(1)} %get-tuple-element.70), channel_id=1, source_target_pairs={{0,1},{1,0},{2,3},{3,2},{4,5},{5,4},{6,7},{7,6},{8,9},{9,8},{10,11... | collective-permute-start | bytes 884744 | tf_op jit(solution)/shard_map/ppermute | solution.py:35
  44.2 7.2 %collective-permute-start.13 = (bf16[96,640]{1,0:T(8,128)(2,1)S(1)}, bf16[96,640]{1,0:T(8,128)(2,1)S(1)}, u32[]{:S(2)}, u32[]{:S(2)}) collective-permute-start(bf16[96,640]{1,0:T(8,128)(2,1)S(1)} %add_convert_fusion.5), channel_id=1, source_target_pairs={{0,8},{2,10},{4,12},{6,14},{8,0},{10,2},{12,4},{14,6},{16,24},{18,... | collective-permute-start | bytes 368648 | tf_op jit(solution)/shard_map/ppermute | solution.py:35
  46.0 7.6 %collective-permute-start.12 = (bf16[96,640]{1,0:T(8,128)(2,1)S(1)}, bf16[96,640]{1,0:T(8,128)(2,1)S(1)}, u32[]{:S(2)}, u32[]{:S(2)}) collective-permute-start(bf16[96,640]{1,0:T(8,128)(2,1)S(1)} %get-tuple-element.122), channel_id=1, source_target_pairs={{0,4},{2,6},{4,0},{6,2},{8,12},{10,14},{12,8},{14,10},{16,20},{18,... | collective-permute-start | bytes 368648 | tf_op jit(solution)/shard_map/ppermute | solution.py:35
  47.5 6.0 %collective-permute-start.11 = (bf16[96,640]{1,0:T(8,128)(2,1)S(1)}, bf16[96,640]{1,0:T(8,128)(2,1)S(1)}, u32[]{:S(2)}, u32[]{:S(2)}) collective-permute-start(bf16[96,640]{1,0:T(8,128)(2,1)S(1)} %get-tuple-element.123), channel_id=1, source_target_pairs={{0,12},{2,14},{4,8},{6,10},{8,4},{10,6},{12,0},{14,2},{16,28},{18,... | collective-permute-start | bytes 368648 | tf_op jit(solution)/shard_map/ppermute | solution.py:35
  50.9 3.5 %collective-permute-start.9 = (bf16[96,1280]{1,0:T(8,128)(2,1)S(1)}, bf16[96,1280]{1,0:T(8,128)(2,1)S(1)}, u32[]{:S(2)}, u32[]{:S(2)}) collective-permute-start(bf16[96,1280]{1,0:T(8,128)(2,1)S(1)} %get-tuple-element.94), channel_id=1, source_target_pairs={{0,2},{2,0},{4,6},{6,4},{8,10},{10,8},{12,14},{14,12},{16,18},{18,... | collective-permute-start | bytes 737288 | tf_op jit(solution)/shard_map/ppermute | solution.py:35
  50.9 4.1 %collective-permute-start.10 = (bf16[96,1280]{1,0:T(8,128)(2,1)S(1)}, bf16[96,1280]{1,0:T(8,128)(2,1)S(1)}, u32[]{:S(2)}, u32[]{:S(2)}) collective-permute-start(bf16[96,1280]{1,0:T(8,128)(2,1)S(1)} %get-tuple-element.96), channel_id=1, source_target_pairs={{0,2},{2,0},{4,6},{6,4},{8,10},{10,8},{12,14},{14,12},{16,18},{18,... | collective-permute-start | bytes 737288 | tf_op jit(solution)/shard_map/ppermute | solution.py:35
  55.8 9.2 %collective-permute-start.15 = (bf16[96,640]{1,0:T(8,128)(2,1)}, bf16[96,640]{1,0:T(8,128)(2,1)}, u32[]{:S(2)}, u32[]{:S(2)}) collective-permute-start(bf16[96,640]{1,0:T(8,128)(2,1)} %get-tuple-element.97), channel_id=1, source_target_pairs={{0,12},{2,14},{4,8},{6,10},{8,4},{10,6},{12,0},{14,2},{16,28},{18,... | collective-permute-start | bytes 368648 | tf_op jit(solution)/shard_map/ppermute | solution.py:35
  56.8 8.2 %collective-permute-start.16 = (bf16[96,640]{1,0:T(8,128)(2,1)}, bf16[96,640]{1,0:T(8,128)(2,1)}, u32[]{:S(2)}, u32[]{:S(2)}) collective-permute-start(bf16[96,640]{1,0:T(8,128)(2,1)} %get-tuple-element.98), channel_id=1, source_target_pairs={{0,4},{2,6},{4,0},{6,2},{8,12},{10,14},{12,8},{14,10},{16,20},{18,... | collective-permute-start | bytes 368648 | tf_op jit(solution)/shard_map/ppermute | solution.py:35
  58.1 6.9 %collective-permute-start.17 = (bf16[96,640]{1,0:T(8,128)(2,1)}, bf16[96,640]{1,0:T(8,128)(2,1)}, u32[]{:S(2)}, u32[]{:S(2)}) collective-permute-start(bf16[96,640]{1,0:T(8,128)(2,1)} %get-tuple-element.99), channel_id=1, source_target_pairs={{0,8},{2,10},{4,12},{6,14},{8,0},{10,2},{12,4},{14,6},{16,24},{18,... | collective-permute-start | bytes 368648 | tf_op jit(solution)/shard_map/ppermute | solution.py:35
  59.3 5.8 %collective-permute-start.14 = (bf16[96,640]{1,0:T(8,128)(2,1)}, bf16[96,640]{1,0:T(8,128)(2,1)}, u32[]{:S(2)}, u32[]{:S(2)}) collective-permute-start(bf16[96,640]{1,0:T(8,128)(2,1)} %add_convert_fusion.1), channel_id=1, source_target_pairs={{0,1},{1,0},{2,3},{3,2},{4,5},{5,4},{6,7},{7,6},{8,9},{9,8},{10,11... | collective-permute-start | bytes 368648 | tf_op jit(solution)/shard_map/ppermute | solution.py:35
  66.2 7.1 %collective-permute-start.18 = (bf16[96,640]{1,0:T(8,128)(2,1)S(1)}, bf16[96,640]{1,0:T(8,128)(2,1)S(1)}, u32[]{:S(2)}, u32[]{:S(2)}) collective-permute-start(bf16[96,640]{1,0:T(8,128)(2,1)S(1)} %get-tuple-element.110), channel_id=1, source_target_pairs={{0,16},{2,18},{4,20},{6,22},{8,24},{10,26},{12,28},{14,30},{16,0},... | collective-permute-start | bytes 368648 | tf_op jit(solution)/shard_map/ppermute | solution.py:35

commit v10 on v9

--- a/solution.py
+++ b/solution.py
@@ -408,6 +408,7 @@
         before, near_far = [all_tokens, all_cots], []
         for far, held in enumerate((mine, beside)):
             if far:
+                held = after(held, near_far)
                 given = swap(held, "dp", width, 1)
             *before, short = join(k, far, place_ref, held, given, w_in, w_down, before)
             near_far.append(short)

time: 74.3 us -> 72.6 us (0.977)
  waiting for transfers between devices: 19 us -> 16.3 us
  starting transfers between devices: 21.3 us -> 22.1 us
    ppermute x19, waiting for transfers between devices: 19 us -> 16.3 us  [swap(): return lax.ppermute(value, axis, flipped(size, mask))]
    ppermute x19, starting transfers between devices: 21.3 us -> 22.1 us  [swap(): return lax.ppermute(value, axis, flipped(size, mask))]
  transfers between devices with their start and end apart: 19 -> 19, of which waited for: 6 -> 7; matrix products, arithmetic and copies ran while one was open for 3% -> 3% of each run, Pallas kernels for 36% -> 37%
where the time goes in v10:
time: 72.6 us; the launch traced here: 72.3 us
  Pallas kernels  28.4 us (39%)
  starting transfers between devices  22.1 us (30%)
  waiting for transfers between devices  16.3 us (22%)
  other arithmetic  4.14 us (6%)
  between operations  0.86 us (1%)
    ppermute x19, starting transfers between devices, swap(): return lax.ppermute(value, axis, flipped(size, mask))  22.1 us
    ppermute x19, waiting for transfers between devices, swap(): return lax.ppermute(value, axis, flipped(size, mask))  16.3 us
    pallas_call x3, Pallas kernels, activate(): pl.pallas_call(functools.partial(activate_kernel, group, turns, count, bl...  6.94 us
    pallas_call x1, Pallas kernels, prepare(): pl.pallas_call(prepare_kernel, in_specs=[IN_SMEM] + [IN_HBM] * 5 + [IN_VM...  6.58 us
    pallas_call x2, Pallas kernels, join(): pl.pallas_call(functools.partial(join_kernel, group, far), in_specs=[IN_S...  4.82 us
    pallas_call x1, Pallas kernels, down_grads(): pl.pallas_call(down_grads_kernel, in_specs=[IN_HBM, IN_VMEM], out_specs=I...  4.34 us
    pallas_call x1, Pallas kernels, inner_grads(): pl.pallas_call(inner_grads_kernel, in_specs=[IN_VMEM] * 2, out_specs=[IN_...  3.82 us
    pallas_call x1, Pallas kernels, fetch(): pl.pallas_call(functools.partial(fetch_kernel, mask), in_specs=[IN_SMEM,...  1.89 us
  transfers between devices with their start and end apart: 19, of which 7 were waited for; matrix products, arithmetic and copies ran while one was open for 3% of the time, Pallas kernels for 37%

profile of v10, /device:TPU:0, one launch (start us, length us, event | category | flops | bytes accessed | tf_op | source)
XLA Modules:
  0.0 72.3 jit_solution(1537811082229785321)
XLA Ops:
  0.6 0.0 copy-start
  0.7 0.0 copy-start.1
  0.7 0.0 copy-start.2
  0.7 1.9 %fetch.1 = bf16[96,2560]{1,0:T(8,128)(2,1)} custom-call(s32[1]{0:T(128)} %bitcast.1.node, s32[1]{0:T(128)} %bitcast.place, bf16[192,5120]{1,0:T(8,128)(2,1)} %tokens.3, bf16[192,5120]{1,0:T(8,128)(2,1)} %cot.3), custom_call_target="tpu_custom_call" | custom-call | tf_op jit(solution)/shard_map/fetch/pallas_call | solution.py:78
  2.6 3.0 %collective-permute-start = (bf16[96,2560]{1,0:T(8,128)(2,1)}, bf16[96,2560]{1,0:T(8,128)(2,1)}, u32[]{:S(2)}, u32[]{:S(2)}) collective-permute-start(bf16[96,2560]{1,0:T(8,128)(2,1)} %fetch.1), channel_id=1, source_target_pairs={{0,1},{1,0},{2,3},{3,2},{4,5},{5,4},{6,7},{7,6},{8,9},{9,8},{10,11... | collective-permute-start | bytes 1474568 | tf_op jit(solution)/shard_map/ppermute | solution.py:35
  5.6 0.0 copy-done
  5.6 0.4 copy.28
  6.0 0.0 copy-done.1
  6.0 0.0 copy-done.2
  6.0 6.6 %prepare.1 = (bf16[384,2560]{1,0:T(8,128)(2,1)S(1)}, bf16[384,2560]{1,0:T(8,128)(2,1)S(1)}, bf16[2560,1024]{1,0:T(8,128)(2,1)S(1)}, bf16[512,2560]{1,0:T(8,128)(...) custom-call(s32[1]{0:T(128)} %bitcast.1.node, bf16[192,5120]{1,0:T(8,128)(2,1)} %tokens.3, ...), custom_call_target="tpu_custom_call" | custom-call | tf_op jit(solution)/shard_map/prepare/pallas_call | solution.py:145
  12.6 4.5 %collective-permute-done.held = bf16[96,2560]{1,0:T(8,128)(2,1)} collective-permute-done((bf16[96,2560]{1,0:T(8,128)(2,1)}, bf16[96,2560]{1,0:T(8,128)(2,1)}, u32[]{:S(2)}, u32[]{:S(2)}) %collective-permute-start) | collective-permute-done | bytes 491552 | tf_op jit(solution)/shard_map/ppermute | solution.py:35
  17.1 0.0 collective-permute-start.2
  17.2 1.8 %collective-permute-start.1 = (bf16[96,2560]{1,0:T(8,128)(2,1)}, bf16[96,2560]{1,0:T(8,128)(2,1)S(1)}, u32[]{:S(2)}, u32[]{:S(2)}) collective-permute-start(bf16[96,2560]{1,0:T(8,128)(2,1)} %collective-permute-done.held), channel_id=1, source_target_pairs={{0,8},{2,10},{4,12},{6,14},{8,0},{10,2},{12,4},{14,6},{16,24},{18,... | collective-permute-start | bytes 1474568 | tf_op jit(solution)/shard_map/ppermute | solution.py:35
  18.9 1.5 %collective-permute-start.5 = (bf16[192,1536]{1,0:T(8,128)(2,1)S(1)}, bf16[192,1536]{1,0:T(8,128)(2,1)S(1)}, u32[]{:S(2)}, u32[]{:S(2)}) collective-permute-start(bf16[192,1536]{1,0:T(8,128)(2,1)S(1)} %get-tuple-element.63), channel_id=1, source_target_pairs={{0,1},{1,0},{2,3},{3,2},{4,5},{5,4},{6,7},{7,6},{8,9},{9,8},{10,11... | collective-permute-start | bytes 1769480 | tf_op jit(solution)/shard_map/ppermute | solution.py:35
  20.5 0.0 collective-permute-done.2.given
  20.5 2.9 %join.2 = (bf16[384,2560]{1,0:T(8,128)(2,1)S(1)}, bf16[384,2560]{1,0:T(8,128)(2,1)S(1)}, f32[192,1536]{1,0:T(8,128)S(1)}, bf16[96,1536]{1,0:T(8,128)(2,1)S(1)}) custom-call(s32[1]{0:T(128)} %bitcast.place, bf16[96,2560]{1,0:T(8,128)(2,1)} %collective-permute-done.held, ...), custom_call_target="tpu_custom_call", output_to_operand_aliasing={{0}: (5, {}), {1}: (6, {})} | custom-call | tf_op jit(solution)/shard_map/join/pallas_call | solution.py:202
  23.4 7.7 %collective-permute-done.1.held = bf16[96,2560]{1,0:T(8,128)(2,1)S(1)} collective-permute-done((bf16[96,2560]{1,0:T(8,128)(2,1)}, bf16[96,2560]{1,0:T(8,128)(2,1)S(1)}, u32[]{:S(2)}, u32[]{:S(2)}) %collective-permute-start.1) | collective-permute-done | bytes 491552 | tf_op jit(solution)/shard_map/ppermute | solution.py:35
  31.0 0.0 collective-permute-start.3
  31.1 1.7 %collective-permute-start.8 = (bf16[96,1536]{1,0:T(8,128)(2,1)S(1)}, bf16[96,1536]{1,0:T(8,128)(2,1)S(1)}, u32[]{:S(2)}, u32[]{:S(2)}) collective-permute-start(bf16[96,1536]{1,0:T(8,128)(2,1)S(1)} %get-tuple-element.68), channel_id=1, source_target_pairs={{0,1},{1,0},{2,3},{3,2},{4,5},{5,4},{6,7},{7,6},{8,9},{9,8},{10,11... | collective-permute-start | bytes 884744 | tf_op jit(solution)/shard_map/ppermute | solution.py:35
  32.7 0.2 collective-permute-done.3.given
  32.9 1.9 %join.3 = (bf16[384,2560]{1,0:T(8,128)(2,1)S(1)}, bf16[384,2560]{1,0:T(8,128)(2,1)S(1)}, f32[192,1536]{1,0:T(8,128)S(1)}, bf16[96,1536]{1,0:T(8,128)(2,1)S(1)}) custom-call(s32[1]{0:T(128)} %bitcast.place, bf16[96,2560]{1,0:T(8,128)(2,1)S(1)} %collective-permute-done.1.held, ...), custom_call_target="tpu_custom_call", output_to_operand_aliasing={{0}: (5, {}), {1}: (6, {}), {2}: (7, {})} | custom-call | tf_op jit(solution)/shard_map/join/pallas_call | solution.py:202
  34.8 0.0 collective-permute-done.5.arrived
  34.8 2.6 %activate.3 = (bf16[384,512]{1,0:T(8,128)(2,1)S(1)}, bf16[384,1024]{1,0:T(8,128)(2,1)S(1)}, bf16[384,2560]{1,0:T(8,128)(2,1)S(1)}, bf16[96,1280]{1,0:T(8,128)(2,...) custom-call(s32[1]{0:T(128)} %bitcast.place, ...), custom_call_target="tpu_custom_call", output_to_operand_aliasing={{2}: (4, {})} | custom-call | tf_op jit(solution)/shard_map/activate/pallas_call | solution.py:290
  37.4 0.2 collective-permute-start.6
  37.6 0.4 collective-permute-start.7
  38.0 1.7 %collective-permute-start.4 = (bf16[96,1536]{1,0:T(8,128)(2,1)S(1)}, bf16[96,1536]{1,0:T(8,128)(2,1)S(1)}, u32[]{:S(2)}, u32[]{:S(2)}) collective-permute-start(bf16[96,1536]{1,0:T(8,128)(2,1)S(1)} %get-tuple-element.73), channel_id=1, source_target_pairs={{0,1},{1,0},{2,3},{3,2},{4,5},{5,4},{6,7},{7,6},{8,9},{9,8},{10,11... | collective-permute-start | bytes 884744 | tf_op jit(solution)/shard_map/ppermute | solution.py:35
  39.7 1.0 %collective-permute-done.8.arrived = bf16[96,1536]{1,0:T(8,128)(2,1)S(1)} collective-permute-done((bf16[96,1536]{1,0:T(8,128)(2,1)S(1)}, bf16[96,1536]{1,0:T(8,128)(2,1)S(1)}, u32[]{:S(2)}, u32[]{:S(2)}) %collective-permute-start.8) | collective-permute-done | bytes 294944 | tf_op jit(solution)/shard_map/ppermute | solution.py:35
  40.7 2.0 %activate.4 = (bf16[384,512]{1,0:T(8,128)(2,1)S(1)}, bf16[384,1024]{1,0:T(8,128)(2,1)S(1)}, bf16[384,2560]{1,0:T(8,128)(2,1)S(1)}, bf16[96,1280]{1,0:T(8,128)(2,...) custom-call(s32[1]{0:T(128)} %bitcast.place, ...), custom_call_target="tpu_custom_call", output_to_operand_aliasing={{0}: (4, {}), {1}: (5, {}), {2}: (6, {})} | custom-call | tf_op jit(solution)/shard_map/activate/pallas_call | solution.py:290
  42.7 0.0 collective-permute-done.6
  42.7 0.0 collective-permute-done.7
  42.8 1.7 %collective-permute-start.13 = (bf16[96,640]{1,0:T(8,128)(2,1)S(1)}, bf16[96,640]{1,0:T(8,128)(2,1)S(1)}, u32[]{:S(2)}, u32[]{:S(2)}) collective-permute-start(bf16[96,640]{1,0:T(8,128)(2,1)S(1)} %add_convert_fusion.5), channel_id=1, source_target_pairs={{0,8},{2,10},{4,12},{6,14},{8,0},{10,2},{12,4},{14,6},{16,24},{18,... | collective-permute-start | bytes 368648 | tf_op jit(solution)/shard_map/ppermute | solution.py:35
  44.5 0.1 add_convert_fusion.6
  44.5 1.6 %collective-permute-start.12 = (bf16[96,640]{1,0:T(8,128)(2,1)S(1)}, bf16[96,640]{1,0:T(8,128)(2,1)S(1)}, u32[]{:S(2)}, u32[]{:S(2)}) collective-permute-start(bf16[96,640]{1,0:T(8,128)(2,1)S(1)} %get-tuple-element.124), channel_id=1, source_target_pairs={{0,4},{2,6},{4,0},{6,2},{8,12},{10,14},{12,8},{14,10},{16,20},{18,... | collective-permute-start | bytes 368648 | tf_op jit(solution)/shard_map/ppermute | solution.py:35
  46.1 0.3 collective-permute-start.11
  46.4 0.6 collective-permute-done.4.arrived
  47.0 2.4 %activate.5 = (bf16[384,512]{1,0:T(8,128)(2,1)S(1)}, bf16[384,1024]{1,0:T(8,128)(2,1)S(1)}, bf16[384,2560]{1,0:T(8,128)(2,1)S(1)}, bf16[96,1280]{1,0:T(8,128)(2,...) custom-call(s32[1]{0:T(128)} %bitcast.place, ...), custom_call_target="tpu_custom_call", output_to_operand_aliasing={{0}: (4, {}), {1}: (5, {}), {2}: (6, {}), {3}: (7, {}), {4}... | custom-call | tf_op jit(solution)/shard_map/activate/pallas_call | solution.py:290
  49.4 0.1 collective-permute-start.9
  49.5 0.5 collective-permute-start.10
  50.0 0.0 collective-permute-done.13
  50.0 2.1 %collective-permute-done.12 = bf16[96,640]{1,0:T(8,128)(2,1)S(1)} collective-permute-done((bf16[96,640]{1,0:T(8,128)(2,1)S(1)}, bf16[96,640]{1,0:T(8,128)(2,1)S(1)}, u32[]{:S(2)}, u32[]{:S(2)}) %collective-permute-start.12) | collective-permute-done | bytes 122912 | tf_op jit(solution)/shard_map/ppermute | solution.py:35
  52.1 0.0 collective-permute-done.11
  52.1 0.7 %add_convert_fusion.1 = bf16[96,640]{1,0:T(8,128)(2,1)} fusion(bf16[96,640]{1,0:T(8,128)(2,1)S(1)} %collective-permute-done.13, bf16[96,640]{1,0:T(8,128)(2,1)S(1)} %collective-permute-done.12, bf16[96,640]{1,0:T(8,128)(2,1)S(1)} %collective-permute-done.11, f32[96,1280]{1,0:T(8,128)S(1)} %get-tuple-element.86, bf16[96,1280]{1,0:T(8,128)(2,1)S(1)} %collective-permute-done.7), kind=kLoop, calls=%fused_computation.5 | loop fusion | flops 552960 | bytes 860160 | tf_op jit(solution)/shard_map/convert_element_type | solution.py:480
  52.9 0.0 collective-permute-done.9
  52.9 0.8 %add_convert_fusion.3 = (bf16[96,640]{1,0:T(8,128)(2,1)}, bf16[96,640]{1,0:T(8,128)(2,1)}) fusion(f32[96,1280]{1,0:T(8,128)S(1)} %get-tuple-element.95, bf16[96,1280]{1,0:T(8,128)(2,1)S(1)} %collective-permute-done.9), kind=kLoop, calls=%fused_computation.8 | loop fusion | flops 368640 | bytes 983040 | tf_op jit(solution)/shard_map/convert_element_type | solution.py:449
  53.6 0.0 collective-permute-done.10
  53.6 0.7 convert_add_fusion.1
  54.3 1.2 %collective-permute-start.15 = (bf16[96,640]{1,0:T(8,128)(2,1)}, bf16[96,640]{1,0:T(8,128)(2,1)}, u32[]{:S(2)}, u32[]{:S(2)}) collective-permute-start(bf16[96,640]{1,0:T(8,128)(2,1)} %get-tuple-element.99), channel_id=1, source_target_pairs={{0,12},{2,14},{4,8},{6,10},{8,4},{10,6},{12,0},{14,2},{16,28},{18,... | collective-permute-start | bytes 368648 | tf_op jit(solution)/shard_map/ppermute | solution.py:35
  55.5 1.1 %collective-permute-start.16 = (bf16[96,640]{1,0:T(8,128)(2,1)}, bf16[96,640]{1,0:T(8,128)(2,1)}, u32[]{:S(2)}, u32[]{:S(2)}) collective-permute-start(bf16[96,640]{1,0:T(8,128)(2,1)} %get-tuple-element.100), channel_id=1, source_target_pairs={{0,4},{2,6},{4,0},{6,2},{8,12},{10,14},{12,8},{14,10},{16,20},{18,... | collective-permute-start | bytes 368648 | tf_op jit(solution)/shard_map/ppermute | solution.py:35
  56.7 1.2 %collective-permute-start.17 = (bf16[96,640]{1,0:T(8,128)(2,1)}, bf16[96,640]{1,0:T(8,128)(2,1)}, u32[]{:S(2)}, u32[]{:S(2)}) collective-permute-start(bf16[96,640]{1,0:T(8,128)(2,1)} %get-tuple-element.101), channel_id=1, source_target_pairs={{0,8},{2,10},{4,12},{6,14},{8,0},{10,2},{12,4},{14,6},{16,24},{18,... | collective-permute-start | bytes 368648 | tf_op jit(solution)/shard_map/ppermute | solution.py:35
  57.8 1.5 %collective-permute-start.14 = (bf16[96,640]{1,0:T(8,128)(2,1)}, bf16[96,640]{1,0:T(8,128)(2,1)}, u32[]{:S(2)}, u32[]{:S(2)}) collective-permute-start(bf16[96,640]{1,0:T(8,128)(2,1)} %add_convert_fusion.1), channel_id=1, source_target_pairs={{0,1},{1,0},{2,3},{3,2},{4,5},{5,4},{6,7},{7,6},{8,9},{9,8},{10,11... | collective-permute-start | bytes 368648 | tf_op jit(solution)/shard_map/ppermute | solution.py:35
  59.3 3.8 %inner_grads.1 = (bf16[2560,512]{1,0:T(8,128)(2,1)}, bf16[2560,512]{1,0:T(8,128)(2,1)}) custom-call(bf16[384,2560]{1,0:T(8,128)(2,1)S(1)} %get-tuple-element.104.tokens, bf16[384,1024]{1,0:T(8,128)(2,1)S(1)} %get-tuple-element.106.d_inner), custom_call_target="tpu_custom_call" | custom-call | tf_op jit(solution)/shard_map/inner_grads/pallas_call | solution.py:328
  63.2 0.0 collective-permute-done.15
  63.2 0.0 collective-permute-done.16
  63.2 0.0 collective-permute-done.17
  63.2 0.0 collective-permute-done.14
  63.2 1.2 %fusion = (bf16[96,640]{1,0:T(8,128)(2,1)S(1)}, f32[96,640]{1,0:T(8,128)S(1)}) fusion(bf16[96,640]{1,0:T(8,128)(2,1)} %collective-permute-done.14, pred[]{:T(512)S(6)} %eq.7, bf16[96,640]{1,0:T(8,128)(2,1)} %collective-permute-done.17, bf16[96,640]{1,0:T(8,128)(2,1)} %collective-permute-done.16, f32[96,640]{1,0:T(8,128)S(1)} %get-tuple-element.103, ...), kind=kLoop, calls=%fused_computation.2 | loop fusion | flops 614400 | bytes 1105922 | tf_op jit(solution)/shard_map/convert_element_type | solution.py:494
  64.4 2.7 %collective-permute-start.18 = (bf16[96,640]{1,0:T(8,128)(2,1)S(1)}, bf16[96,640]{1,0:T(8,128)(2,1)S(1)}, u32[]{:S(2)}, u32[]{:S(2)}) collective-permute-start(bf16[96,640]{1,0:T(8,128)(2,1)S(1)} %get-tuple-element.112), channel_id=1, source_target_pairs={{0,16},{2,18},{4,20},{6,22},{8,24},{10,26},{12,28},{14,30},{16,0},... | collective-permute-start | bytes 368648 | tf_op jit(solution)/shard_map/ppermute | solution.py:35
  67.0 4.3 %down_grads.1 = bf16[512,2560]{1,0:T(8,128)(2,1)} custom-call(bf16[384,2560]{1,0:T(8,128)(2,1)} %get-tuple-element.113.cots, bf16[384,512]{1,0:T(8,128)(2,1)S(1)} %get-tuple-element.115.act), custom_call_target="tpu_custom_call" | custom-call | tf_op jit(solution)/shard_map/down_grads/pallas_call | solution.py:364
  71.4 0.2 collective-permute-done.18
  71.6 0.1 fusion.1
  71.7 0.7 pad_maximum_fusion
  (4 shorter events, 0.1 us)
Async XLA Ops:
  0.6 5.0 %copy-start = (f32[512,40]{0,1:T(8,128)S(1)}, f32[512,40]{0,1:T(8,128)}, u32[]{:S(2)}) copy-start(f32[512,40]{0,1:T(8,128)} %param.15) | copy-start | bytes 245764
  0.7 5.3 %copy-start.1 = (f32[40,512]{1,0:T(8,128)S(1)}, f32[40,512]{1,0:T(8,128)}, u32[]{:S(2)}) copy-start(f32[40,512]{1,0:T(8,128)} %gate_scales.1) | copy-start | bytes 245764
  0.7 5.3 %copy-start.2 = (f32[40,512]{1,0:T(8,128)S(1)}, f32[40,512]{1,0:T(8,128)}, u32[]{:S(2)}) copy-start(f32[40,512]{1,0:T(8,128)} %up_scales.1) | copy-start | bytes 245764
  2.6 14.6 %collective-permute-start = (bf16[96,2560]{1,0:T(8,128)(2,1)}, bf16[96,2560]{1,0:T(8,128)(2,1)}, u32[]{:S(2)}, u32[]{:S(2)}) collective-permute-start(bf16[96,2560]{1,0:T(8,128)(2,1)} %fetch.1), channel_id=1, source_target_pairs={{0,1},{1,0},{2,3},{3,2},{4,5},{5,4},{6,7},{7,6},{8,9},{9,8},{10,11... | collective-permute-start | bytes 1474568 | tf_op jit(solution)/shard_map/ppermute | solution.py:35
  17.1 3.3 %collective-permute-start.2 = (bf16[96,2560]{1,0:T(8,128)(2,1)}, bf16[96,2560]{1,0:T(8,128)(2,1)S(1)}, u32[]{:S(2)}, u32[]{:S(2)}) collective-permute-start(bf16[96,2560]{1,0:T(8,128)(2,1)} %collective-permute-done.held), channel_id=1, source_target_pairs={{0,2},{2,0},{4,6},{6,4},{8,10},{10,8},{12,14},{14,12},{16,18},{18,... | collective-permute-start | bytes 1474568 | tf_op jit(solution)/shard_map/ppermute | solution.py:35
  17.2 13.9 %collective-permute-start.1 = (bf16[96,2560]{1,0:T(8,128)(2,1)}, bf16[96,2560]{1,0:T(8,128)(2,1)S(1)}, u32[]{:S(2)}, u32[]{:S(2)}) collective-permute-start(bf16[96,2560]{1,0:T(8,128)(2,1)} %collective-permute-done.held), channel_id=1, source_target_pairs={{0,8},{2,10},{4,12},{6,14},{8,0},{10,2},{12,4},{14,6},{16,24},{18,... | collective-permute-start | bytes 1474568 | tf_op jit(solution)/shard_map/ppermute | solution.py:35
  18.9 15.9 %collective-permute-start.5 = (bf16[192,1536]{1,0:T(8,128)(2,1)S(1)}, bf16[192,1536]{1,0:T(8,128)(2,1)S(1)}, u32[]{:S(2)}, u32[]{:S(2)}) collective-permute-start(bf16[192,1536]{1,0:T(8,128)(2,1)S(1)} %get-tuple-element.63), channel_id=1, source_target_pairs={{0,1},{1,0},{2,3},{3,2},{4,5},{5,4},{6,7},{7,6},{8,9},{9,8},{10,11... | collective-permute-start | bytes 1769480 | tf_op jit(solution)/shard_map/ppermute | solution.py:35
  31.0 1.9 %collective-permute-start.3 = (bf16[96,2560]{1,0:T(8,128)(2,1)S(1)}, bf16[96,2560]{1,0:T(8,128)(2,1)S(1)}, u32[]{:S(2)}, u32[]{:S(2)}) collective-permute-start(bf16[96,2560]{1,0:T(8,128)(2,1)S(1)} %collective-permute-done.1.held), channel_id=1, source_target_pairs={{0,2},{2,0},{4,6},{6,4},{8,10},{10,8},{12,14},{14,12},{16,18},{18,... | collective-permute-start | bytes 1474568 | tf_op jit(solution)/shard_map/ppermute | solution.py:35
  31.1 9.7 %collective-permute-start.8 = (bf16[96,1536]{1,0:T(8,128)(2,1)S(1)}, bf16[96,1536]{1,0:T(8,128)(2,1)S(1)}, u32[]{:S(2)}, u32[]{:S(2)}) collective-permute-start(bf16[96,1536]{1,0:T(8,128)(2,1)S(1)} %get-tuple-element.68), channel_id=1, source_target_pairs={{0,1},{1,0},{2,3},{3,2},{4,5},{5,4},{6,7},{7,6},{8,9},{9,8},{10,11... | collective-permute-start | bytes 884744 | tf_op jit(solution)/shard_map/ppermute | solution.py:35
  37.4 5.3 %collective-permute-start.6 = (bf16[96,1280]{1,0:T(8,128)(2,1)S(1)}, bf16[96,1280]{1,0:T(8,128)(2,1)S(1)}, u32[]{:S(2)}, u32[]{:S(2)}) collective-permute-start(bf16[96,1280]{1,0:T(8,128)(2,1)S(1)} %get-tuple-element.78), channel_id=1, source_target_pairs={{0,2},{2,0},{4,6},{6,4},{8,10},{10,8},{12,14},{14,12},{16,18},{18,... | collective-permute-start | bytes 737288 | tf_op jit(solution)/shard_map/ppermute | solution.py:35
  37.6 5.1 %collective-permute-start.7 = (bf16[96,1280]{1,0:T(8,128)(2,1)S(1)}, bf16[96,1280]{1,0:T(8,128)(2,1)S(1)}, u32[]{:S(2)}, u32[]{:S(2)}) collective-permute-start(bf16[96,1280]{1,0:T(8,128)(2,1)S(1)} %get-tuple-element.79), channel_id=1, source_target_pairs={{0,2},{2,0},{4,6},{6,4},{8,10},{10,8},{12,14},{14,12},{16,18},{18,... | collective-permute-start | bytes 737288 | tf_op jit(solution)/shard_map/ppermute | solution.py:35
  38.0 9.0 %collective-permute-start.4 = (bf16[96,1536]{1,0:T(8,128)(2,1)S(1)}, bf16[96,1536]{1,0:T(8,128)(2,1)S(1)}, u32[]{:S(2)}, u32[]{:S(2)}) collective-permute-start(bf16[96,1536]{1,0:T(8,128)(2,1)S(1)} %get-tuple-element.73), channel_id=1, source_target_pairs={{0,1},{1,0},{2,3},{3,2},{4,5},{5,4},{6,7},{7,6},{8,9},{9,8},{10,11... | collective-permute-start | bytes 884744 | tf_op jit(solution)/shard_map/ppermute | solution.py:35
  42.8 7.2 %collective-permute-start.13 = (bf16[96,640]{1,0:T(8,128)(2,1)S(1)}, bf16[96,640]{1,0:T(8,128)(2,1)S(1)}, u32[]{:S(2)}, u32[]{:S(2)}) collective-permute-start(bf16[96,640]{1,0:T(8,128)(2,1)S(1)} %add_convert_fusion.5), channel_id=1, source_target_pairs={{0,8},{2,10},{4,12},{6,14},{8,0},{10,2},{12,4},{14,6},{16,24},{18,... | collective-permute-start | bytes 368648 | tf_op jit(solution)/shard_map/ppermute | solution.py:35
  44.5 7.6 %collective-permute-start.12 = (bf16[96,640]{1,0:T(8,128)(2,1)S(1)}, bf16[96,640]{1,0:T(8,128)(2,1)S(1)}, u32[]{:S(2)}, u32[]{:S(2)}) collective-permute-start(bf16[96,640]{1,0:T(8,128)(2,1)S(1)} %get-tuple-element.124), channel_id=1, source_target_pairs={{0,4},{2,6},{4,0},{6,2},{8,12},{10,14},{12,8},{14,10},{16,20},{18,... | collective-permute-start | bytes 368648 | tf_op jit(solution)/shard_map/ppermute | solution.py:35
  46.1 6.0 %collective-permute-start.11 = (bf16[96,640]{1,0:T(8,128)(2,1)S(1)}, bf16[96,640]{1,0:T(8,128)(2,1)S(1)}, u32[]{:S(2)}, u32[]{:S(2)}) collective-permute-start(bf16[96,640]{1,0:T(8,128)(2,1)S(1)} %get-tuple-element.125), channel_id=1, source_target_pairs={{0,12},{2,14},{4,8},{6,10},{8,4},{10,6},{12,0},{14,2},{16,28},{18,... | collective-permute-start | bytes 368648 | tf_op jit(solution)/shard_map/ppermute | solution.py:35
  49.4 3.5 %collective-permute-start.9 = (bf16[96,1280]{1,0:T(8,128)(2,1)S(1)}, bf16[96,1280]{1,0:T(8,128)(2,1)S(1)}, u32[]{:S(2)}, u32[]{:S(2)}) collective-permute-start(bf16[96,1280]{1,0:T(8,128)(2,1)S(1)} %get-tuple-element.96), channel_id=1, source_target_pairs={{0,2},{2,0},{4,6},{6,4},{8,10},{10,8},{12,14},{14,12},{16,18},{18,... | collective-permute-start | bytes 737288 | tf_op jit(solution)/shard_map/ppermute | solution.py:35
  49.5 4.1 %collective-permute-start.10 = (bf16[96,1280]{1,0:T(8,128)(2,1)S(1)}, bf16[96,1280]{1,0:T(8,128)(2,1)S(1)}, u32[]{:S(2)}, u32[]{:S(2)}) collective-permute-start(bf16[96,1280]{1,0:T(8,128)(2,1)S(1)} %get-tuple-element.98), channel_id=1, source_target_pairs={{0,2},{2,0},{4,6},{6,4},{8,10},{10,8},{12,14},{14,12},{16,18},{18,... | collective-permute-start | bytes 737288 | tf_op jit(solution)/shard_map/ppermute | solution.py:35
  54.3 8.8 %collective-permute-start.15 = (bf16[96,640]{1,0:T(8,128)(2,1)}, bf16[96,640]{1,0:T(8,128)(2,1)}, u32[]{:S(2)}, u32[]{:S(2)}) collective-permute-start(bf16[96,640]{1,0:T(8,128)(2,1)} %get-tuple-element.99), channel_id=1, source_target_pairs={{0,12},{2,14},{4,8},{6,10},{8,4},{10,6},{12,0},{14,2},{16,28},{18,... | collective-permute-start | bytes 368648 | tf_op jit(solution)/shard_map/ppermute | solution.py:35
  55.5 7.7 %collective-permute-start.16 = (bf16[96,640]{1,0:T(8,128)(2,1)}, bf16[96,640]{1,0:T(8,128)(2,1)}, u32[]{:S(2)}, u32[]{:S(2)}) collective-permute-start(bf16[96,640]{1,0:T(8,128)(2,1)} %get-tuple-element.100), channel_id=1, source_target_pairs={{0,4},{2,6},{4,0},{6,2},{8,12},{10,14},{12,8},{14,10},{16,20},{18,... | collective-permute-start | bytes 368648 | tf_op jit(solution)/shard_map/ppermute | solution.py:35
  56.7 6.5 %collective-permute-start.17 = (bf16[96,640]{1,0:T(8,128)(2,1)}, bf16[96,640]{1,0:T(8,128)(2,1)}, u32[]{:S(2)}, u32[]{:S(2)}) collective-permute-start(bf16[96,640]{1,0:T(8,128)(2,1)} %get-tuple-element.101), channel_id=1, source_target_pairs={{0,8},{2,10},{4,12},{6,14},{8,0},{10,2},{12,4},{14,6},{16,24},{18,... | collective-permute-start | bytes 368648 | tf_op jit(solution)/shard_map/ppermute | solution.py:35
  57.8 5.4 %collective-permute-start.14 = (bf16[96,640]{1,0:T(8,128)(2,1)}, bf16[96,640]{1,0:T(8,128)(2,1)}, u32[]{:S(2)}, u32[]{:S(2)}) collective-permute-start(bf16[96,640]{1,0:T(8,128)(2,1)} %add_convert_fusion.1), channel_id=1, source_target_pairs={{0,1},{1,0},{2,3},{3,2},{4,5},{5,4},{6,7},{7,6},{8,9},{9,8},{10,11... | collective-permute-start | bytes 368648 | tf_op jit(solution)/shard_map/ppermute | solution.py:35
  64.4 7.2 %collective-permute-start.18 = (bf16[96,640]{1,0:T(8,128)(2,1)S(1)}, bf16[96,640]{1,0:T(8,128)(2,1)S(1)}, u32[]{:S(2)}, u32[]{:S(2)}) collective-permute-start(bf16[96,640]{1,0:T(8,128)(2,1)S(1)} %get-tuple-element.112), channel_id=1, source_target_pairs={{0,16},{2,18},{4,20},{6,22},{8,24},{10,26},{12,28},{14,30},{16,0},... | collective-permute-start | bytes 368648 | tf_op jit(solution)/shard_map/ppermute | solution.py:35

commit v11 on v10

--- a/solution.py
+++ b/solution.py
@@ -467,7 +467,7 @@
     *before, parts = passed(activate(0, nodes, (0,), place_ref, sums[0], near_far[0], w_in, owners, before))
     last = []
     for k in range(1, nodes):
-        sending, mine = split(others[k], before[:2])
+        sending, mine = split(others[k], near_far[0])
         last.append([value for _, value in sending])
         blocks[k] = mine, exchange(sending)
     act, d_inner, all_tokens, parts = passed(

time: 72.6 us -> 72.8 us (level)
  transfers between devices with their start and end apart: 19 -> 19, of which waited for: 7 -> 9; matrix products, arithmetic and copies ran while one was open for 3% -> 3% of each run, Pallas kernels for 37% -> 37%
where the time goes in v11:
time: 72.8 us; the launch traced here: 72.6 us
  Pallas kernels  28.4 us (39%)
  starting transfers between devices  22.3 us (31%)
  waiting for transfers between devices  16.5 us (23%)
  other arithmetic  4.12 us (6%)
  between operations  0.82 us (1%)
    ppermute x19, starting transfers between devices, swap(): return lax.ppermute(value, axis, flipped(size, mask))  22.3 us
    ppermute x19, waiting for transfers between devices, swap(): return lax.ppermute(value, axis, flipped(size, mask))  16.5 us
    pallas_call x3, Pallas kernels, activate(): pl.pallas_call(functools.partial(activate_kernel, group, turns, count, bl...  6.94 us
    pallas_call x1, Pallas kernels, prepare(): pl.pallas_call(prepare_kernel, in_specs=[IN_SMEM] + [IN_HBM] * 5 + [IN_VM...  6.58 us
    pallas_call x2, Pallas kernels, join(): pl.pallas_call(functools.partial(join_kernel, group, far), in_specs=[IN_S...  4.82 us
    pallas_call x1, Pallas kernels, down_grads(): pl.pallas_call(down_grads_kernel, in_specs=[IN_HBM, IN_VMEM], out_specs=I...  4.34 us
    pallas_call x1, Pallas kernels, inner_grads(): pl.pallas_call(inner_grads_kernel, in_specs=[IN_VMEM] * 2, out_specs=[IN_...  3.82 us
    pallas_call x1, Pallas kernels, fetch(): pl.pallas_call(functools.partial(fetch_kernel, mask), in_specs=[IN_SMEM,...  1.89 us
  transfers between devices with their start and end apart: 19, of which 9 were waited for; matrix products, arithmetic and copies ran while one was open for 3% of the time, Pallas kernels for 37%

profile of v11, /device:TPU:0, one launch (start us, length us, event | category | flops | bytes accessed | tf_op | source)
XLA Modules:
  0.0 72.6 jit_solution(2476662718520812872)
XLA Ops:
  0.6 0.0 copy-start
  0.7 0.0 copy-start.1
  0.7 0.0 copy-start.2
  0.7 1.9 %fetch.1 = bf16[96,2560]{1,0:T(8,128)(2,1)} custom-call(s32[1]{0:T(128)} %bitcast.1.node, s32[1]{0:T(128)} %bitcast.place, bf16[192,5120]{1,0:T(8,128)(2,1)} %tokens.3, bf16[192,5120]{1,0:T(8,128)(2,1)} %cot.3), custom_call_target="tpu_custom_call" | custom-call | tf_op jit(solution)/shard_map/fetch/pallas_call | solution.py:78
  2.6 3.0 %collective-permute-start = (bf16[96,2560]{1,0:T(8,128)(2,1)}, bf16[96,2560]{1,0:T(8,128)(2,1)}, u32[]{:S(2)}, u32[]{:S(2)}) collective-permute-start(bf16[96,2560]{1,0:T(8,128)(2,1)} %fetch.1), channel_id=1, source_target_pairs={{0,1},{1,0},{2,3},{3,2},{4,5},{5,4},{6,7},{7,6},{8,9},{9,8},{10,11... | collective-permute-start | bytes 1474568 | tf_op jit(solution)/shard_map/ppermute | solution.py:35
  5.6 0.0 copy-done
  5.6 0.4 copy.28
  6.0 0.0 copy-done.1
  6.0 0.0 copy-done.2
  6.0 6.6 %prepare.1 = (bf16[384,2560]{1,0:T(8,128)(2,1)S(1)}, bf16[384,2560]{1,0:T(8,128)(2,1)S(1)}, bf16[2560,1024]{1,0:T(8,128)(2,1)S(1)}, bf16[512,2560]{1,0:T(8,128)(...) custom-call(s32[1]{0:T(128)} %bitcast.1.node, bf16[192,5120]{1,0:T(8,128)(2,1)} %tokens.3, ...), custom_call_target="tpu_custom_call" | custom-call | tf_op jit(solution)/shard_map/prepare/pallas_call | solution.py:145
  12.6 4.5 %collective-permute-done.held = bf16[96,2560]{1,0:T(8,128)(2,1)} collective-permute-done((bf16[96,2560]{1,0:T(8,128)(2,1)}, bf16[96,2560]{1,0:T(8,128)(2,1)}, u32[]{:S(2)}, u32[]{:S(2)}) %collective-permute-start) | collective-permute-done | bytes 491552 | tf_op jit(solution)/shard_map/ppermute | solution.py:35
  17.1 0.0 collective-permute-start.2
  17.2 1.8 %collective-permute-start.1 = (bf16[96,2560]{1,0:T(8,128)(2,1)}, bf16[96,2560]{1,0:T(8,128)(2,1)S(1)}, u32[]{:S(2)}, u32[]{:S(2)}) collective-permute-start(bf16[96,2560]{1,0:T(8,128)(2,1)} %collective-permute-done.held), channel_id=1, source_target_pairs={{0,8},{2,10},{4,12},{6,14},{8,0},{10,2},{12,4},{14,6},{16,24},{18,... | collective-permute-start | bytes 1474568 | tf_op jit(solution)/shard_map/ppermute | solution.py:35
  18.9 1.5 %collective-permute-start.5 = (bf16[192,1536]{1,0:T(8,128)(2,1)S(1)}, bf16[192,1536]{1,0:T(8,128)(2,1)S(1)}, u32[]{:S(2)}, u32[]{:S(2)}) collective-permute-start(bf16[192,1536]{1,0:T(8,128)(2,1)S(1)} %get-tuple-element.63), channel_id=1, source_target_pairs={{0,1},{1,0},{2,3},{3,2},{4,5},{5,4},{6,7},{7,6},{8,9},{9,8},{10,11... | collective-permute-start | bytes 1769480 | tf_op jit(solution)/shard_map/ppermute | solution.py:35
  20.5 0.0 collective-permute-done.2.given
  20.5 2.9 %join.2 = (bf16[384,2560]{1,0:T(8,128)(2,1)S(1)}, bf16[384,2560]{1,0:T(8,128)(2,1)S(1)}, f32[192,1536]{1,0:T(8,128)S(1)}, bf16[96,1536]{1,0:T(8,128)(2,1)S(1)}) custom-call(s32[1]{0:T(128)} %bitcast.place, bf16[96,2560]{1,0:T(8,128)(2,1)} %collective-permute-done.held, ...), custom_call_target="tpu_custom_call", output_to_operand_aliasing={{0}: (5, {}), {1}: (6, {})} | custom-call | tf_op jit(solution)/shard_map/join/pallas_call | solution.py:202
  23.4 7.7 %collective-permute-done.1.held = bf16[96,2560]{1,0:T(8,128)(2,1)S(1)} collective-permute-done((bf16[96,2560]{1,0:T(8,128)(2,1)}, bf16[96,2560]{1,0:T(8,128)(2,1)S(1)}, u32[]{:S(2)}, u32[]{:S(2)}) %collective-permute-start.1) | collective-permute-done | bytes 491552 | tf_op jit(solution)/shard_map/ppermute | solution.py:35
  31.0 0.0 collective-permute-start.3
  31.1 1.7 %collective-permute-start.8 = (bf16[96,1536]{1,0:T(8,128)(2,1)S(1)}, bf16[96,1536]{1,0:T(8,128)(2,1)S(1)}, u32[]{:S(2)}, u32[]{:S(2)}) collective-permute-start(bf16[96,1536]{1,0:T(8,128)(2,1)S(1)} %get-tuple-element.68), channel_id=1, source_target_pairs={{0,1},{1,0},{2,3},{3,2},{4,5},{5,4},{6,7},{7,6},{8,9},{9,8},{10,11... | collective-permute-start | bytes 884744 | tf_op jit(solution)/shard_map/ppermute | solution.py:35
  32.7 0.2 collective-permute-done.3.given
  32.9 1.9 %join.3 = (bf16[384,2560]{1,0:T(8,128)(2,1)S(1)}, bf16[384,2560]{1,0:T(8,128)(2,1)S(1)}, f32[192,1536]{1,0:T(8,128)S(1)}, bf16[96,1536]{1,0:T(8,128)(2,1)S(1)}) custom-call(s32[1]{0:T(128)} %bitcast.place, bf16[96,2560]{1,0:T(8,128)(2,1)S(1)} %collective-permute-done.1.held, ...), custom_call_target="tpu_custom_call", output_to_operand_aliasing={{0}: (5, {}), {1}: (6, {}), {2}: (7, {})} | custom-call | tf_op jit(solution)/shard_map/join/pallas_call | solution.py:202
  34.8 0.0 collective-permute-done.5.arrived
  34.8 2.6 %activate.3 = (bf16[384,512]{1,0:T(8,128)(2,1)S(1)}, bf16[384,1024]{1,0:T(8,128)(2,1)S(1)}, bf16[384,2560]{1,0:T(8,128)(2,1)S(1)}, bf16[96,1280]{1,0:T(8,128)(2,...) custom-call(s32[1]{0:T(128)} %bitcast.place, ...), custom_call_target="tpu_custom_call", output_to_operand_aliasing={{2}: (4, {})} | custom-call | tf_op jit(solution)/shard_map/activate/pallas_call | solution.py:290
  37.4 0.2 collective-permute-start.6
  37.6 0.4 collective-permute-start.7
  38.0 1.7 %collective-permute-start.4 = (bf16[96,1536]{1,0:T(8,128)(2,1)S(1)}, bf16[96,1536]{1,0:T(8,128)(2,1)S(1)}, u32[]{:S(2)}, u32[]{:S(2)}) collective-permute-start(bf16[96,1536]{1,0:T(8,128)(2,1)S(1)} %get-tuple-element.73), channel_id=1, source_target_pairs={{0,1},{1,0},{2,3},{3,2},{4,5},{5,4},{6,7},{7,6},{8,9},{9,8},{10,11... | collective-permute-start | bytes 884744 | tf_op jit(solution)/shard_map/ppermute | solution.py:35
  39.7 1.0 %collective-permute-done.8.arrived = bf16[96,1536]{1,0:T(8,128)(2,1)S(1)} collective-permute-done((bf16[96,1536]{1,0:T(8,128)(2,1)S(1)}, bf16[96,1536]{1,0:T(8,128)(2,1)S(1)}, u32[]{:S(2)}, u32[]{:S(2)}) %collective-permute-start.8) | collective-permute-done | bytes 294944 | tf_op jit(solution)/shard_map/ppermute | solution.py:35
  40.7 0.0 collective-permute-done.6
  40.7 0.0 collective-permute-done.7
  40.8 1.6 %collective-permute-start.13 = (bf16[96,640]{1,0:T(8,128)(2,1)S(1)}, bf16[96,640]{1,0:T(8,128)(2,1)S(1)}, u32[]{:S(2)}, u32[]{:S(2)}) collective-permute-start(bf16[96,640]{1,0:T(8,128)(2,1)S(1)} %add_convert_fusion.5), channel_id=1, source_target_pairs={{0,8},{2,10},{4,12},{6,14},{8,0},{10,2},{12,4},{14,6},{16,24},{18,... | collective-permute-start | bytes 368648 | tf_op jit(solution)/shard_map/ppermute | solution.py:35
  42.4 1.6 %collective-permute-start.12 = (bf16[96,640]{1,0:T(8,128)(2,1)S(1)}, bf16[96,640]{1,0:T(8,128)(2,1)S(1)}, u32[]{:S(2)}, u32[]{:S(2)}) collective-permute-start(bf16[96,640]{1,0:T(8,128)(2,1)S(1)} %get-tuple-element.124), channel_id=1, source_target_pairs={{0,4},{2,6},{4,0},{6,2},{8,12},{10,14},{12,8},{14,10},{16,20},{18,... | collective-permute-start | bytes 368648 | tf_op jit(solution)/shard_map/ppermute | solution.py:35
  43.9 0.5 collective-permute-start.11
  44.4 2.0 %activate.4 = (bf16[384,512]{1,0:T(8,128)(2,1)S(1)}, bf16[384,1024]{1,0:T(8,128)(2,1)S(1)}, bf16[384,2560]{1,0:T(8,128)(2,1)S(1)}, bf16[96,1280]{1,0:T(8,128)(2,...) custom-call(s32[1]{0:T(128)} %bitcast.place, ...), custom_call_target="tpu_custom_call", output_to_operand_aliasing={{0}: (4, {}), {1}: (5, {}), {2}: (6, {})} | custom-call | tf_op jit(solution)/shard_map/activate/pallas_call | solution.py:290
  46.4 0.6 collective-permute-done.4.arrived
  47.0 2.4 %activate.5 = (bf16[384,512]{1,0:T(8,128)(2,1)S(1)}, bf16[384,1024]{1,0:T(8,128)(2,1)S(1)}, bf16[384,2560]{1,0:T(8,128)(2,1)S(1)}, bf16[96,1280]{1,0:T(8,128)(2,...) custom-call(s32[1]{0:T(128)} %bitcast.place, ...), custom_call_target="tpu_custom_call", output_to_operand_aliasing={{0}: (4, {}), {1}: (5, {}), {2}: (6, {}), {3}: (7, {}), {4}... | custom-call | tf_op jit(solution)/shard_map/activate/pallas_call | solution.py:290
  49.4 0.1 collective-permute-start.9
  49.5 0.5 collective-permute-start.10
  50.0 0.0 collective-permute-done.13
  50.0 0.0 collective-permute-done.12
  50.0 0.0 collective-permute-done.11
  50.0 0.7 %add_convert_fusion.1 = bf16[96,640]{1,0:T(8,128)(2,1)} fusion(bf16[96,640]{1,0:T(8,128)(2,1)S(1)} %collective-permute-done.13, bf16[96,640]{1,0:T(8,128)(2,1)S(1)} %collective-permute-done.12, bf16[96,640]{1,0:T(8,128)(2,1)S(1)} %collective-permute-done.11, f32[96,1280]{1,0:T(8,128)S(1)} %get-tuple-element.81, bf16[96,1280]{1,0:T(8,128)(2,1)S(1)} %collective-permute-done.7), kind=kLoop, calls=%fused_computation.5 | loop fusion | flops 552960 | bytes 860160 | tf_op jit(solution)/shard_map/convert_element_type | solution.py:480
  50.7 0.2 collective-permute-done.9
  51.0 0.7 %add_convert_fusion.3 = (bf16[96,640]{1,0:T(8,128)(2,1)}, bf16[96,640]{1,0:T(8,128)(2,1)}) fusion(f32[96,1280]{1,0:T(8,128)S(1)} %get-tuple-element.95, bf16[96,1280]{1,0:T(8,128)(2,1)S(1)} %collective-permute-done.9), kind=kLoop, calls=%fused_computation.8 | loop fusion | flops 368640 | bytes 983040 | tf_op jit(solution)/shard_map/convert_element_type | solution.py:449
  51.7 0.0 collective-permute-done.10
  51.7 0.7 convert_add_fusion.1
  52.4 2.5 %collective-permute-start.15 = (bf16[96,640]{1,0:T(8,128)(2,1)}, bf16[96,640]{1,0:T(8,128)(2,1)}, u32[]{:S(2)}, u32[]{:S(2)}) collective-permute-start(bf16[96,640]{1,0:T(8,128)(2,1)} %get-tuple-element.99), channel_id=1, source_target_pairs={{0,12},{2,14},{4,8},{6,10},{8,4},{10,6},{12,0},{14,2},{16,28},{18,... | collective-permute-start | bytes 368648 | tf_op jit(solution)/shard_map/ppermute | solution.py:35
  54.9 0.5 collective-permute-start.16
  55.4 0.5 collective-permute-start.17
  55.9 1.7 %collective-permute-start.14 = (bf16[96,640]{1,0:T(8,128)(2,1)}, bf16[96,640]{1,0:T(8,128)(2,1)}, u32[]{:S(2)}, u32[]{:S(2)}) collective-permute-start(bf16[96,640]{1,0:T(8,128)(2,1)} %add_convert_fusion.1), channel_id=1, source_target_pairs={{0,1},{1,0},{2,3},{3,2},{4,5},{5,4},{6,7},{7,6},{8,9},{9,8},{10,11... | collective-permute-start | bytes 368648 | tf_op jit(solution)/shard_map/ppermute | solution.py:35
  57.6 3.8 %inner_grads.1 = (bf16[2560,512]{1,0:T(8,128)(2,1)}, bf16[2560,512]{1,0:T(8,128)(2,1)}) custom-call(bf16[384,2560]{1,0:T(8,128)(2,1)S(1)} %get-tuple-element.104.tokens, bf16[384,1024]{1,0:T(8,128)(2,1)S(1)} %get-tuple-element.106.d_inner), custom_call_target="tpu_custom_call" | custom-call | tf_op jit(solution)/shard_map/inner_grads/pallas_call | solution.py:328
  61.5 0.0 collective-permute-done.15
  61.5 0.2 collective-permute-done.16
  61.6 0.2 collective-permute-done.17
  61.9 0.0 collective-permute-done.14
  61.9 1.2 %fusion = (bf16[96,640]{1,0:T(8,128)(2,1)S(1)}, f32[96,640]{1,0:T(8,128)S(1)}) fusion(bf16[96,640]{1,0:T(8,128)(2,1)} %collective-permute-done.14, pred[]{:T(512)S(6)} %eq.7, bf16[96,640]{1,0:T(8,128)(2,1)} %collective-permute-done.17, bf16[96,640]{1,0:T(8,128)(2,1)} %collective-permute-done.16, f32[96,640]{1,0:T(8,128)S(1)} %get-tuple-element.103, ...), kind=kLoop, calls=%fused_computation.2 | loop fusion | flops 614400 | bytes 1105922 | tf_op jit(solution)/shard_map/convert_element_type | solution.py:494
  63.0 2.6 %collective-permute-start.18 = (bf16[96,640]{1,0:T(8,128)(2,1)S(1)}, bf16[96,640]{1,0:T(8,128)(2,1)S(1)}, u32[]{:S(2)}, u32[]{:S(2)}) collective-permute-start(bf16[96,640]{1,0:T(8,128)(2,1)S(1)} %get-tuple-element.112), channel_id=1, source_target_pairs={{0,16},{2,18},{4,20},{6,22},{8,24},{10,26},{12,28},{14,30},{16,0},... | collective-permute-start | bytes 368648 | tf_op jit(solution)/shard_map/ppermute | solution.py:35
  65.7 4.3 %down_grads.1 = bf16[512,2560]{1,0:T(8,128)(2,1)} custom-call(bf16[384,2560]{1,0:T(8,128)(2,1)} %get-tuple-element.113.cots, bf16[384,512]{1,0:T(8,128)(2,1)S(1)} %get-tuple-element.115.act), custom_call_target="tpu_custom_call" | custom-call | tf_op jit(solution)/shard_map/down_grads/pallas_call | solution.py:364
  70.0 1.7 %collective-permute-done.18 = bf16[96,640]{1,0:T(8,128)(2,1)S(1)} collective-permute-done((bf16[96,640]{1,0:T(8,128)(2,1)S(1)}, bf16[96,640]{1,0:T(8,128)(2,1)S(1)}, u32[]{:S(2)}, u32[]{:S(2)}) %collective-permute-start.18) | collective-permute-done | bytes 122912 | tf_op jit(solution)/shard_map/ppermute | solution.py:35
  71.8 0.1 fusion.1
  71.9 0.7 pad_maximum_fusion
  (5 shorter events, 0.1 us)
Async XLA Ops:
  0.6 5.0 %copy-start = (f32[512,40]{0,1:T(8,128)S(1)}, f32[512,40]{0,1:T(8,128)}, u32[]{:S(2)}) copy-start(f32[512,40]{0,1:T(8,128)} %param.15) | copy-start | bytes 245764
  0.7 5.3 %copy-start.1 = (f32[40,512]{1,0:T(8,128)S(1)}, f32[40,512]{1,0:T(8,128)}, u32[]{:S(2)}) copy-start(f32[40,512]{1,0:T(8,128)} %gate_scales.1) | copy-start | bytes 245764
  0.7 5.3 %copy-start.2 = (f32[40,512]{1,0:T(8,128)S(1)}, f32[40,512]{1,0:T(8,128)}, u32[]{:S(2)}) copy-start(f32[40,512]{1,0:T(8,128)} %up_scales.1) | copy-start | bytes 245764
  2.6 14.6 %collective-permute-start = (bf16[96,2560]{1,0:T(8,128)(2,1)}, bf16[96,2560]{1,0:T(8,128)(2,1)}, u32[]{:S(2)}, u32[]{:S(2)}) collective-permute-start(bf16[96,2560]{1,0:T(8,128)(2,1)} %fetch.1), channel_id=1, source_target_pairs={{0,1},{1,0},{2,3},{3,2},{4,5},{5,4},{6,7},{7,6},{8,9},{9,8},{10,11... | collective-permute-start | bytes 1474568 | tf_op jit(solution)/shard_map/ppermute | solution.py:35
  17.1 3.3 %collective-permute-start.2 = (bf16[96,2560]{1,0:T(8,128)(2,1)}, bf16[96,2560]{1,0:T(8,128)(2,1)S(1)}, u32[]{:S(2)}, u32[]{:S(2)}) collective-permute-start(bf16[96,2560]{1,0:T(8,128)(2,1)} %collective-permute-done.held), channel_id=1, source_target_pairs={{0,2},{2,0},{4,6},{6,4},{8,10},{10,8},{12,14},{14,12},{16,18},{18,... | collective-permute-start | bytes 1474568 | tf_op jit(solution)/shard_map/ppermute | solution.py:35
  17.2 13.9 %collective-permute-start.1 = (bf16[96,2560]{1,0:T(8,128)(2,1)}, bf16[96,2560]{1,0:T(8,128)(2,1)S(1)}, u32[]{:S(2)}, u32[]{:S(2)}) collective-permute-start(bf16[96,2560]{1,0:T(8,128)(2,1)} %collective-permute-done.held), channel_id=1, source_target_pairs={{0,8},{2,10},{4,12},{6,14},{8,0},{10,2},{12,4},{14,6},{16,24},{18,... | collective-permute-start | bytes 1474568 | tf_op jit(solution)/shard_map/ppermute | solution.py:35
  18.9 15.9 %collective-permute-start.5 = (bf16[192,1536]{1,0:T(8,128)(2,1)S(1)}, bf16[192,1536]{1,0:T(8,128)(2,1)S(1)}, u32[]{:S(2)}, u32[]{:S(2)}) collective-permute-start(bf16[192,1536]{1,0:T(8,128)(2,1)S(1)} %get-tuple-element.63), channel_id=1, source_target_pairs={{0,1},{1,0},{2,3},{3,2},{4,5},{5,4},{6,7},{7,6},{8,9},{9,8},{10,11... | collective-permute-start | bytes 1769480 | tf_op jit(solution)/shard_map/ppermute | solution.py:35
  31.0 1.9 %collective-permute-start.3 = (bf16[96,2560]{1,0:T(8,128)(2,1)S(1)}, bf16[96,2560]{1,0:T(8,128)(2,1)S(1)}, u32[]{:S(2)}, u32[]{:S(2)}) collective-permute-start(bf16[96,2560]{1,0:T(8,128)(2,1)S(1)} %collective-permute-done.1.held), channel_id=1, source_target_pairs={{0,2},{2,0},{4,6},{6,4},{8,10},{10,8},{12,14},{14,12},{16,18},{18,... | collective-permute-start | bytes 1474568 | tf_op jit(solution)/shard_map/ppermute | solution.py:35
  31.1 9.7 %collective-permute-start.8 = (bf16[96,1536]{1,0:T(8,128)(2,1)S(1)}, bf16[96,1536]{1,0:T(8,128)(2,1)S(1)}, u32[]{:S(2)}, u32[]{:S(2)}) collective-permute-start(bf16[96,1536]{1,0:T(8,128)(2,1)S(1)} %get-tuple-element.68), channel_id=1, source_target_pairs={{0,1},{1,0},{2,3},{3,2},{4,5},{5,4},{6,7},{7,6},{8,9},{9,8},{10,11... | collective-permute-start | bytes 884744 | tf_op jit(solution)/shard_map/ppermute | solution.py:35
  37.4 3.3 %collective-permute-start.6 = (bf16[96,1280]{1,0:T(8,128)(2,1)S(1)}, bf16[96,1280]{1,0:T(8,128)(2,1)S(1)}, u32[]{:S(2)}, u32[]{:S(2)}) collective-permute-start(bf16[96,1280]{1,0:T(8,128)(2,1)S(1)} %get-tuple-element.78), channel_id=1, source_target_pairs={{0,2},{2,0},{4,6},{6,4},{8,10},{10,8},{12,14},{14,12},{16,18},{18,... | collective-permute-start | bytes 737288 | tf_op jit(solution)/shard_map/ppermute | solution.py:35
  37.6 3.1 %collective-permute-start.7 = (bf16[96,1280]{1,0:T(8,128)(2,1)S(1)}, bf16[96,1280]{1,0:T(8,128)(2,1)S(1)}, u32[]{:S(2)}, u32[]{:S(2)}) collective-permute-start(bf16[96,1280]{1,0:T(8,128)(2,1)S(1)} %get-tuple-element.79), channel_id=1, source_target_pairs={{0,2},{2,0},{4,6},{6,4},{8,10},{10,8},{12,14},{14,12},{16,18},{18,... | collective-permute-start | bytes 737288 | tf_op jit(solution)/shard_map/ppermute | solution.py:35
  38.0 9.0 %collective-permute-start.4 = (bf16[96,1536]{1,0:T(8,128)(2,1)S(1)}, bf16[96,1536]{1,0:T(8,128)(2,1)S(1)}, u32[]{:S(2)}, u32[]{:S(2)}) collective-permute-start(bf16[96,1536]{1,0:T(8,128)(2,1)S(1)} %get-tuple-element.73), channel_id=1, source_target_pairs={{0,1},{1,0},{2,3},{3,2},{4,5},{5,4},{6,7},{7,6},{8,9},{9,8},{10,11... | collective-permute-start | bytes 884744 | tf_op jit(solution)/shard_map/ppermute | solution.py:35
  40.8 9.2 %collective-permute-start.13 = (bf16[96,640]{1,0:T(8,128)(2,1)S(1)}, bf16[96,640]{1,0:T(8,128)(2,1)S(1)}, u32[]{:S(2)}, u32[]{:S(2)}) collective-permute-start(bf16[96,640]{1,0:T(8,128)(2,1)S(1)} %add_convert_fusion.5), channel_id=1, source_target_pairs={{0,8},{2,10},{4,12},{6,14},{8,0},{10,2},{12,4},{14,6},{16,24},{18,... | collective-permute-start | bytes 368648 | tf_op jit(solution)/shard_map/ppermute | solution.py:35
  42.4 7.6 %collective-permute-start.12 = (bf16[96,640]{1,0:T(8,128)(2,1)S(1)}, bf16[96,640]{1,0:T(8,128)(2,1)S(1)}, u32[]{:S(2)}, u32[]{:S(2)}) collective-permute-start(bf16[96,640]{1,0:T(8,128)(2,1)S(1)} %get-tuple-element.124), channel_id=1, source_target_pairs={{0,4},{2,6},{4,0},{6,2},{8,12},{10,14},{12,8},{14,10},{16,20},{18,... | collective-permute-start | bytes 368648 | tf_op jit(solution)/shard_map/ppermute | solution.py:35
  43.9 6.1 %collective-permute-start.11 = (bf16[96,640]{1,0:T(8,128)(2,1)S(1)}, bf16[96,640]{1,0:T(8,128)(2,1)S(1)}, u32[]{:S(2)}, u32[]{:S(2)}) collective-permute-start(bf16[96,640]{1,0:T(8,128)(2,1)S(1)} %get-tuple-element.125), channel_id=1, source_target_pairs={{0,12},{2,14},{4,8},{6,10},{8,4},{10,6},{12,0},{14,2},{16,28},{18,... | collective-permute-start | bytes 368648 | tf_op jit(solution)/shard_map/ppermute | solution.py:35
  49.4 1.6 %collective-permute-start.9 = (bf16[96,1280]{1,0:T(8,128)(2,1)S(1)}, bf16[96,1280]{1,0:T(8,128)(2,1)S(1)}, u32[]{:S(2)}, u32[]{:S(2)}) collective-permute-start(bf16[96,1280]{1,0:T(8,128)(2,1)S(1)} %get-tuple-element.96), channel_id=1, source_target_pairs={{0,2},{2,0},{4,6},{6,4},{8,10},{10,8},{12,14},{14,12},{16,18},{18,... | collective-permute-start | bytes 737288 | tf_op jit(solution)/shard_map/ppermute | solution.py:35
  49.5 2.3 %collective-permute-start.10 = (bf16[96,1280]{1,0:T(8,128)(2,1)S(1)}, bf16[96,1280]{1,0:T(8,128)(2,1)S(1)}, u32[]{:S(2)}, u32[]{:S(2)}) collective-permute-start(bf16[96,1280]{1,0:T(8,128)(2,1)S(1)} %get-tuple-element.98), channel_id=1, source_target_pairs={{0,2},{2,0},{4,6},{6,4},{8,10},{10,8},{12,14},{14,12},{16,18},{18,... | collective-permute-start | bytes 737288 | tf_op jit(solution)/shard_map/ppermute | solution.py:35
  52.4 9.0 %collective-permute-start.15 = (bf16[96,640]{1,0:T(8,128)(2,1)}, bf16[96,640]{1,0:T(8,128)(2,1)}, u32[]{:S(2)}, u32[]{:S(2)}) collective-permute-start(bf16[96,640]{1,0:T(8,128)(2,1)} %get-tuple-element.99), channel_id=1, source_target_pairs={{0,12},{2,14},{4,8},{6,10},{8,4},{10,6},{12,0},{14,2},{16,28},{18,... | collective-permute-start | bytes 368648 | tf_op jit(solution)/shard_map/ppermute | solution.py:35
  54.9 6.7 %collective-permute-start.16 = (bf16[96,640]{1,0:T(8,128)(2,1)}, bf16[96,640]{1,0:T(8,128)(2,1)}, u32[]{:S(2)}, u32[]{:S(2)}) collective-permute-start(bf16[96,640]{1,0:T(8,128)(2,1)} %get-tuple-element.100), channel_id=1, source_target_pairs={{0,4},{2,6},{4,0},{6,2},{8,12},{10,14},{12,8},{14,10},{16,20},{18,... | collective-permute-start | bytes 368648 | tf_op jit(solution)/shard_map/ppermute | solution.py:35
  55.4 6.4 %collective-permute-start.17 = (bf16[96,640]{1,0:T(8,128)(2,1)}, bf16[96,640]{1,0:T(8,128)(2,1)}, u32[]{:S(2)}, u32[]{:S(2)}) collective-permute-start(bf16[96,640]{1,0:T(8,128)(2,1)} %get-tuple-element.101), channel_id=1, source_target_pairs={{0,8},{2,10},{4,12},{6,14},{8,0},{10,2},{12,4},{14,6},{16,24},{18,... | collective-permute-start | bytes 368648 | tf_op jit(solution)/shard_map/ppermute | solution.py:35
  55.9 6.0 %collective-permute-start.14 = (bf16[96,640]{1,0:T(8,128)(2,1)}, bf16[96,640]{1,0:T(8,128)(2,1)}, u32[]{:S(2)}, u32[]{:S(2)}) collective-permute-start(bf16[96,640]{1,0:T(8,128)(2,1)} %add_convert_fusion.1), channel_id=1, source_target_pairs={{0,1},{1,0},{2,3},{3,2},{4,5},{5,4},{6,7},{7,6},{8,9},{9,8},{10,11... | collective-permute-start | bytes 368648 | tf_op jit(solution)/shard_map/ppermute | solution.py:35
  63.0 8.7 %collective-permute-start.18 = (bf16[96,640]{1,0:T(8,128)(2,1)S(1)}, bf16[96,640]{1,0:T(8,128)(2,1)S(1)}, u32[]{:S(2)}, u32[]{:S(2)}) collective-permute-start(bf16[96,640]{1,0:T(8,128)(2,1)S(1)} %get-tuple-element.112), channel_id=1, source_target_pairs={{0,16},{2,18},{4,20},{6,22},{8,24},{10,26},{12,28},{14,30},{16,0},... | collective-permute-start | bytes 368648 | tf_op jit(solution)/shard_map/ppermute | solution.py:35
